TPU v7x, 32 devices: a whole 2x2x4 slice. The times are simulated.
32 devices in a mesh: dp: 16 (over z, x, core), seq: 2 (over y).
Axes of the slice: x: 2, y: 2, z: 4, core: 2. Of those that a mesh axis runs over, the one named last changes fastest.
Arguments:
- tokens: bfloat16 [2, 16, 1024, 1152], P(None, 'dp', 'seq'), may hold values from -6 to 6
- conditioning: bfloat16 [2, 16, 1152], P(None, 'dp'), may hold values from -6 to 6
- heights: int32 [2, 16], P(None, 'dp'), may hold values from 8 to 32, as said below
- widths: int32 [2, 16], P(None, 'dp'), may hold values from 8 to 32
- upstream: bfloat16 [2, 16, 1024, 1152], P(None, 'dp', 'seq'), may hold values from -6 to 6
- w_qkv: float32 [1152, 3456], P('seq', 'dp'), may hold values from -0.1875 to 0.1875
- w_proj: float32 [1152, 1152], P('seq', 'dp'), may hold values from -0.5 to 0.5
- w_fc1: float32 [1152, 4608], P('seq', 'dp'), may hold values from -0.1875 to 0.1875
- w_fc2: float32 [4608, 1152], P('seq', 'dp'), may hold values from -0.09375 to 0.09375
- w_ada: float32 [1152, 6912], P('seq', 'dp'), may hold values from -0.25 to 0.25
- mom_qkv: float32 [1152, 3456], P('seq', 'dp')
- mom_proj: float32 [1152, 1152], P('seq', 'dp')
- mom_fc1: float32 [1152, 4608], P('seq', 'dp')
- mom_fc2: float32 [4608, 1152], P('seq', 'dp')
- mom_ada: float32 [1152, 6912], P('seq', 'dp')
- biases: float32 [16128], P(('dp', 'seq')), may hold values from -1.2 to 1.2
- bias_first: float32 [16128], P(('dp', 'seq'))
- bias_second: float32 [16128], P(('dp', 'seq'))
Outputs:
- output: bfloat16 [2, 16, 1024, 1152], P(None, 'dp', 'seq')
- grad_tokens: bfloat16 [2, 16, 1024, 1152], P(None, 'dp', 'seq')
- grad_conditioning: float32 [2, 16, 1152], P(None, 'dp')
- new_qkv: float32 [1152, 3456], P('seq', 'dp')
- new_proj: float32 [1152, 1152], P('seq', 'dp')
- new_fc1: float32 [1152, 4608], P('seq', 'dp')
- new_fc2: float32 [4608, 1152], P('seq', 'dp')
- new_ada: float32 [1152, 6912], P('seq', 'dp')
- next_mom_qkv: float32 [1152, 3456], P('seq', 'dp')
- next_mom_proj: float32 [1152, 1152], P('seq', 'dp')
- next_mom_fc1: float32 [1152, 4608], P('seq', 'dp')
- next_mom_fc2: float32 [4608, 1152], P('seq', 'dp')
- next_mom_ada: float32 [1152, 6912], P('seq', 'dp')
- new_biases: float32 [16128], P(('dp', 'seq'))
- next_first: float32 [16128], P(('dp', 'seq'))
- next_second: float32 [16128], P(('dp', 'seq'))
Inputs may be any that keep to these rules, and one draw needn't show every extreme that they name: `heights`: among the 2 samples that one index of dp holds over all micro-batches, one (drawn from the seed) has a full 32 x 32 grid; the other sides are drawn independently.
All inputs are finite; a program needn't handle non-finite values.
Results may differ from a plain program's by a relative error of at most 0.028.
The roundings to bfloat16 on the way count: a program that leaves them out, or rounds other values in their place, can miss the bound.
Values may be sent and summed in bfloat16 or wider, within the bound.
No kernel may reach another device: no remote copies, remote signals or barrier semaphores. Data moves between devices by JAX's collectives and lax.ppermute only.
A program may use at most 240 MiB of HBM per device.

v0:
```python
import math

import jax
import jax.numpy as jnp
from jax import lax
from jax.sharding import PartitionSpec as P

D = 1152
HEADS = 16
FF = 4608
ROW_BLOCK = 144
NS_STEPS = 5
STEP_COUNT = 10


PRECISE = lax.Precision.HIGHEST
LN_EPS = 1e-06
MASKED = -1e30
NS_A = 3.4445
NS_B = -4.775
NS_C = 2.0315
MUON_DECAY = 0.5
WEIGHT_SHRINK = 0.0001
NORM_EPS = 1e-07
BETA_FIRST = 0.9
BETA_SECOND = 0.999
ADAM_RATE = 0.1
ADAM_DECAY = 0.01
ADAM_EPS = 1e-08


def layer_norm(values):
    centered = values - jnp.mean(values, axis=-1, keepdims=True)
    inverse = lax.rsqrt(jnp.mean(centered * centered, axis=-1, keepdims=True) + LN_EPS)
    return (centered * inverse, inverse)


def norm_back(normed, inverse, grad):
    mean_grad = jnp.mean(grad, axis=-1, keepdims=True)
    mean_cross = jnp.mean(grad * normed, axis=-1, keepdims=True)
    return inverse * (grad - mean_grad - normed * mean_cross)


def sigmoid_linear(values):
    return values * jax.nn.sigmoid(values)


def gelu_tanh(values):
    return jax.nn.gelu(values, approximate=True)


def gather_weights(w_qkv, w_proj, w_fc1, w_fc2, w_ada, biases):
    column_parts = (
        lax.all_gather(w_qkv.astype(jnp.bfloat16), "dp", axis=1, tiled=True),
        lax.all_gather(w_proj.astype(jnp.bfloat16), "dp", axis=1, tiled=True),
        lax.all_gather(w_fc1.astype(jnp.bfloat16), "dp", axis=1, tiled=True),
        lax.all_gather(w_fc2.astype(jnp.bfloat16), "dp", axis=1, tiled=True),
        lax.all_gather(w_ada.astype(jnp.bfloat16), "dp", axis=1, tiled=True),
    )
    part_qkv, part_proj, part_fc1, part_fc2, part_ada = column_parts
    full_parts = (
        lax.all_gather(part_qkv, "seq", axis=0, tiled=True),
        lax.all_gather(part_proj, "seq", axis=0, tiled=True),
        lax.all_gather(part_fc1, "seq", axis=0, tiled=True),
        lax.all_gather(part_fc2, "seq", axis=0, tiled=True),
        lax.all_gather(part_ada, "seq", axis=0, tiled=True),
    )
    bias_full = lax.all_gather(biases, ("dp", "seq"), axis=0, tiled=True)
    return (full_parts, bias_full)


def reduce_terms(terms):
    term_qkv, term_proj, term_fc1, term_fc2, term_ada, term_bias = terms
    cols = (
        lax.psum_scatter(
            term_qkv.astype(jnp.bfloat16), "dp", scatter_dimension=1, tiled=True
        ).astype(jnp.float32),
        lax.psum_scatter(
            term_proj.astype(jnp.bfloat16), "dp", scatter_dimension=1, tiled=True
        ).astype(jnp.float32),
        lax.psum_scatter(
            term_fc1.astype(jnp.bfloat16), "dp", scatter_dimension=1, tiled=True
        ).astype(jnp.float32),
        lax.psum_scatter(
            term_fc2.astype(jnp.bfloat16), "dp", scatter_dimension=1, tiled=True
        ).astype(jnp.float32),
        lax.psum_scatter(
            term_ada.astype(jnp.bfloat16), "dp", scatter_dimension=1, tiled=True
        ).astype(jnp.float32),
        lax.psum_scatter(
            term_bias.astype(jnp.bfloat16), "dp", scatter_dimension=0, tiled=True
        ).astype(jnp.float32),
    )
    col_qkv, col_proj, col_fc1, col_fc2, col_ada, col_bias = cols
    rowed = (
        lax.psum_scatter(
            col_qkv.astype(jnp.bfloat16), "seq", scatter_dimension=0, tiled=True
        ).astype(jnp.float32),
        lax.psum_scatter(
            col_proj.astype(jnp.bfloat16), "seq", scatter_dimension=0, tiled=True
        ).astype(jnp.float32),
        lax.psum_scatter(
            col_fc1.astype(jnp.bfloat16), "seq", scatter_dimension=0, tiled=True
        ).astype(jnp.float32),
        lax.psum_scatter(
            col_fc2.astype(jnp.bfloat16), "seq", scatter_dimension=0, tiled=True
        ).astype(jnp.float32),
        lax.psum_scatter(
            col_bias.astype(jnp.bfloat16), "seq", scatter_dimension=0, tiled=True
        ).astype(jnp.float32),
    )
    return (rowed[0], rowed[1], rowed[2], rowed[3], col_ada, rowed[4])


def micro_batch(tokens, conds, lengths, upstream, full_parts, bias_full):
    w_qkv, w_proj, w_fc1, w_fc2, w_ada = full_parts
    samples, rows, width = tokens.shape
    hidden_width = w_fc1.shape[1]
    head_dim = width // HEADS
    factor_scale = head_dim ** (-0.5)
    bounds = [
        0,
        6 * width,
        7 * width,
        8 * width,
        9 * width,
        9 * width + hidden_width,
        10 * width + hidden_width,
    ]
    b_ada, b_q, b_v, b_proj, b_fc1, b_fc2 = [bias_full[bounds[i] : bounds[i + 1]] for i in range(6)]
    inputs = tokens.astype(jnp.float32)
    cond_values = conds.astype(jnp.float32)
    cond_act, silu_back = jax.vjp(sigmoid_linear, cond_values)
    cond_low = cond_act.astype(jnp.bfloat16)
    modulation = jnp.dot(cond_low, w_ada, preferred_element_type=jnp.float32) + b_ada
    shift_one, scale_one, gate_one, shift_two, scale_two, gate_two = jnp.split(
        modulation[:, None, :], 6, axis=-1
    )
    normed_one, inverse_one = layer_norm(inputs)
    attn_in = (normed_one * (1.0 + scale_one) + shift_one).astype(jnp.bfloat16)
    projected = jnp.einsum("srd,de->sre", attn_in, w_qkv, preferred_element_type=jnp.float32)
    queries = (projected[..., :width] + b_q).astype(jnp.bfloat16)
    keys = projected[..., width : 2 * width].astype(jnp.bfloat16)
    values = (projected[..., 2 * width :] + b_v).astype(jnp.bfloat16)
    query_heads = queries.reshape(samples, rows, HEADS, head_dim)

    def piece_scores(key_piece):
        count = key_piece.shape[1]
        key_heads = key_piece.reshape(samples, count, HEADS, head_dim)
        scores = (
            jnp.einsum(
                "sqhd,skhd->shqk", query_heads, key_heads, preferred_element_type=jnp.float32
            )
            * factor_scale
        )
        places = jnp.arange(count, dtype=jnp.int32)
        valid = places[None, :] < lengths[:, None]
        return (jnp.where(valid[:, None, None, :], scores, MASKED), key_heads)

    run_max = jnp.full((samples, HEADS, rows), MASKED, jnp.float32)
    key_piece = lax.all_gather(keys, "seq", axis=1, tiled=True)
    value_piece = lax.all_gather(values, "seq", axis=1, tiled=True)
    count = key_piece.shape[1]
    scores, key_heads = piece_scores(key_piece)
    value_heads = value_piece.reshape(samples, count, HEADS, head_dim)
    new_max = jnp.maximum(run_max, jnp.max(scores, axis=-1))
    weights_exp = jnp.exp(scores - new_max[..., None])
    new_total = jnp.sum(weights_exp, axis=-1)
    new_acc = jnp.einsum(
        "shqk,skhd->shqd",
        weights_exp.astype(jnp.bfloat16),
        value_heads,
        preferred_element_type=jnp.float32,
    )
    attn_heads = new_acc / new_total[..., None]
    log_total = new_max + jnp.log(new_total)
    attended = jnp.transpose(attn_heads, (0, 2, 1, 3)).reshape(samples, rows, width)
    attended_low = attended.astype(jnp.bfloat16)
    branch_one = (
        jnp.einsum("srd,de->sre", attended_low, w_proj, preferred_element_type=jnp.float32) + b_proj
    )
    mixed_one = inputs + gate_one * branch_one
    normed_two, inverse_two = layer_norm(mixed_one)
    ffn_in = (normed_two * (1.0 + scale_two) + shift_two).astype(jnp.bfloat16)
    pre_act = jnp.einsum("srd,df->srf", ffn_in, w_fc1, preferred_element_type=jnp.float32) + b_fc1
    activated, gelu_back = jax.vjp(gelu_tanh, pre_act)
    activated_low = activated.astype(jnp.bfloat16)
    branch_two = (
        jnp.einsum("srf,fd->srd", activated_low, w_fc2, preferred_element_type=jnp.float32) + b_fc2
    )
    result = mixed_one + gate_two * branch_two
    grad_out = upstream.astype(jnp.float32)
    grad_branch_two = (gate_two * grad_out).astype(jnp.bfloat16)
    grad_gate_two = jnp.sum(branch_two * grad_out, axis=1)
    term_fc2 = jnp.einsum(
        "srf,srd->fd", activated_low, grad_branch_two, preferred_element_type=jnp.float32
    )
    bias_fc2 = jnp.sum(grad_branch_two.astype(jnp.float32), axis=(0, 1))
    grad_act = jnp.einsum("srd,fd->srf", grad_branch_two, w_fc2, preferred_element_type=jnp.float32)
    grad_pre = gelu_back(grad_act)[0].astype(jnp.bfloat16)
    term_fc1 = jnp.einsum("srd,srf->df", ffn_in, grad_pre, preferred_element_type=jnp.float32)
    bias_fc1 = jnp.sum(grad_pre.astype(jnp.float32), axis=(0, 1))
    grad_ffn_in = jnp.einsum("srf,df->srd", grad_pre, w_fc1, preferred_element_type=jnp.float32)
    grad_shift_two = jnp.sum(grad_ffn_in, axis=1)
    grad_scale_two = jnp.sum(grad_ffn_in * normed_two, axis=1)
    grad_mixed = grad_out + norm_back(normed_two, inverse_two, grad_ffn_in * (1.0 + scale_two))
    grad_gate_one = jnp.sum(branch_one * grad_mixed, axis=1)
    grad_branch_one = (gate_one * grad_mixed).astype(jnp.bfloat16)
    term_proj = jnp.einsum(
        "srd,sre->de", attended_low, grad_branch_one, preferred_element_type=jnp.float32
    )
    bias_proj = jnp.sum(grad_branch_one.astype(jnp.float32), axis=(0, 1))
    grad_attended = jnp.einsum(
        "sre,de->srd", grad_branch_one, w_proj, preferred_element_type=jnp.float32
    ).astype(jnp.bfloat16)
    grad_heads = grad_attended.reshape(samples, rows, HEADS, head_dim)
    delta = jnp.einsum(
        "sqhd,sqhd->shq",
        grad_heads.astype(jnp.float32),
        attended.reshape(samples, rows, HEADS, head_dim),
    )
    key_piece = lax.all_gather(keys, "seq", axis=1, tiled=True)
    value_piece = lax.all_gather(values, "seq", axis=1, tiled=True)
    count = key_piece.shape[1]
    scores, key_heads = piece_scores(key_piece)
    value_heads = value_piece.reshape(samples, count, HEADS, head_dim)
    probs = jnp.exp(scores - log_total[..., None])
    grad_probs = jnp.einsum(
        "sqhd,skhd->shqk", grad_heads, value_heads, preferred_element_type=jnp.float32
    )
    grad_scores = (probs * (grad_probs - delta[..., None])).astype(jnp.bfloat16)
    grad_query = (
        jnp.einsum("shqk,skhd->sqhd", grad_scores, key_heads, preferred_element_type=jnp.float32)
        * factor_scale
    )
    key_part = (
        jnp.einsum("shqk,sqhd->skhd", grad_scores, query_heads, preferred_element_type=jnp.float32)
        * factor_scale
    ).reshape(samples, count, width)
    value_part = jnp.einsum(
        "shqk,sqhd->skhd",
        probs.astype(jnp.bfloat16),
        grad_heads,
        preferred_element_type=jnp.float32,
    ).reshape(samples, count, width)
    grad_query, grad_keys, grad_values = (grad_query, key_part, value_part)
    grad_key_rows, grad_value_rows = (
        lax.psum_scatter(
            grad_keys.astype(jnp.bfloat16), "seq", scatter_dimension=1, tiled=True
        ).astype(jnp.float32),
        lax.psum_scatter(
            grad_values.astype(jnp.bfloat16), "seq", scatter_dimension=1, tiled=True
        ).astype(jnp.float32),
    )
    grad_projected = jnp.concatenate(
        [grad_query.reshape(samples, rows, width), grad_key_rows, grad_value_rows], axis=-1
    ).astype(jnp.bfloat16)
    term_qkv = jnp.einsum(
        "srd,sre->de", attn_in, grad_projected, preferred_element_type=jnp.float32
    )
    grad_sums = jnp.sum(grad_projected.astype(jnp.float32), axis=(0, 1))
    bias_q = grad_sums[:width]
    bias_v = grad_sums[2 * width :]
    grad_attn_in = jnp.einsum(
        "sre,de->srd", grad_projected, w_qkv, preferred_element_type=jnp.float32
    )
    grad_shift_one = jnp.sum(grad_attn_in, axis=1)
    grad_scale_one = jnp.sum(grad_attn_in * normed_one, axis=1)
    grad_inputs = grad_mixed + norm_back(normed_one, inverse_one, grad_attn_in * (1.0 + scale_one))
    grad_mod_local = jnp.concatenate(
        [
            grad_shift_one,
            grad_scale_one,
            grad_gate_one,
            grad_shift_two,
            grad_scale_two,
            grad_gate_two,
        ],
        axis=-1,
    )
    bias_ada = jnp.sum(grad_mod_local, axis=0)
    grad_mod = lax.psum(grad_mod_local, "seq")
    grad_mod_low = grad_mod.astype(jnp.bfloat16)
    row_count = width // lax.axis_size("seq")
    cond_rows = lax.dynamic_slice_in_dim(cond_low, lax.axis_index("seq") * row_count, row_count, 1)
    term_ada = jnp.dot(cond_rows.T, grad_mod_low, preferred_element_type=jnp.float32)
    grad_cond_act = jnp.dot(grad_mod_low, w_ada.T, preferred_element_type=jnp.float32)
    grad_cond = silu_back(grad_cond_act)[0]
    term_bias = jnp.concatenate([bias_ada, bias_q, bias_v, bias_proj, bias_fc1, bias_fc2])
    terms = (term_qkv, term_proj, term_fc1, term_fc2, term_ada, term_bias)
    return (result.astype(jnp.bfloat16), grad_inputs.astype(jnp.bfloat16), grad_cond, terms)


def gram_sums(blocks):
    gram_qkv, gram_proj, gram_fc1, gram_fc2, gram_ada = [
        jnp.einsum("nrc,nsc->nrs", block, block, precision=PRECISE) for block in blocks
    ]
    return (
        lax.psum(gram_qkv.astype(jnp.bfloat16), "dp").astype(jnp.float32),
        lax.psum(gram_proj.astype(jnp.bfloat16), "dp").astype(jnp.float32),
        lax.psum(gram_fc1.astype(jnp.bfloat16), "dp").astype(jnp.float32),
        lax.psum(gram_fc2.astype(jnp.bfloat16), "dp").astype(jnp.float32),
        lax.psum(gram_ada.astype(jnp.bfloat16), "dp").astype(jnp.float32),
    )


def newton_schulz(moments):
    blocks = [
        moment.reshape(moment.shape[0] // ROW_BLOCK, ROW_BLOCK, moment.shape[1])
        for moment in moments
    ]
    squares = [jnp.sum(block * block, axis=(1, 2)) for block in blocks]
    totals = lax.psum((squares[0], squares[1], squares[2], squares[3], squares[4]), "dp")
    current = [
        block / (jnp.sqrt(total) + NORM_EPS)[:, None, None] for block, total in zip(blocks, totals)
    ]
    grams = gram_sums(current)
    for step in range(NS_STEPS):
        if step > 0:
            grams = gram_sums(current)
        current = [
            NS_A * block
            + jnp.einsum(
                "nrs,nsc->nrc",
                NS_B * gram + NS_C * jnp.einsum("nrs,nst->nrt", gram, gram, precision=PRECISE),
                block,
                precision=PRECISE,
            )
            for block, gram in zip(current, grams)
        ]
    return [block.reshape(moment.shape) for block, moment in zip(current, moments)]


def body(
    tokens,
    conditioning,
    heights,
    widths,
    upstream,
    w_qkv,
    w_proj,
    w_fc1,
    w_fc2,
    w_ada,
    mom_qkv,
    mom_proj,
    mom_fc1,
    mom_fc2,
    mom_ada,
    biases,
    bias_first,
    bias_second,
):
    lengths = heights * widths
    outputs = []
    input_grads = []
    cond_grads = []
    reduced = None
    for micro in range(tokens.shape[0]):
        full_parts, bias_full = gather_weights(w_qkv, w_proj, w_fc1, w_fc2, w_ada, biases)
        result, grad_in, grad_cond, terms = micro_batch(
            tokens[micro],
            conditioning[micro],
            lengths[micro],
            upstream[micro],
            full_parts,
            bias_full,
        )
        shards = reduce_terms(terms)
        reduced = (
            shards
            if reduced is None
            else tuple((left + right for left, right in zip(reduced, shards)))
        )
        outputs.append(result)
        input_grads.append(grad_in)
        cond_grads.append(grad_cond)
    grad_qkv, grad_proj, grad_fc1, grad_fc2, grad_ada, grad_bias = reduced
    masters = (w_qkv, w_proj, w_fc1, w_fc2, w_ada)
    moments = [
        MUON_DECAY * previous + grad
        for previous, grad in zip(
            (mom_qkv, mom_proj, mom_fc1, mom_fc2, mom_ada),
            (grad_qkv, grad_proj, grad_fc1, grad_fc2, grad_ada),
        )
    ]
    ortho = newton_schulz(moments)
    rates = (math.sqrt(3.0), 1.0, math.sqrt(FF / D), math.sqrt(D / FF), math.sqrt(6.0))
    new_weights = [
        weight * (1.0 - WEIGHT_SHRINK) - rate * direction
        for weight, rate, direction in zip(masters, rates, ortho)
    ]
    next_first = BETA_FIRST * bias_first + (1.0 - BETA_FIRST) * grad_bias
    next_second = BETA_SECOND * bias_second + (1.0 - BETA_SECOND) * grad_bias * grad_bias
    first_hat = next_first / (1.0 - BETA_FIRST**STEP_COUNT)
    second_hat = next_second / (1.0 - BETA_SECOND**STEP_COUNT)
    new_biases = biases * (1.0 - ADAM_RATE * ADAM_DECAY) - ADAM_RATE * first_hat / (
        jnp.sqrt(second_hat) + ADAM_EPS
    )
    return (
        jnp.stack(outputs),
        jnp.stack(input_grads),
        jnp.stack(cond_grads),
        new_weights[0],
        new_weights[1],
        new_weights[2],
        new_weights[3],
        new_weights[4],
        moments[0],
        moments[1],
        moments[2],
        moments[3],
        moments[4],
        new_biases,
        next_first,
        next_second,
    )


def solution(mesh):
    in_specs = (
        P(None, "dp", "seq", None),
        P(None, "dp", None),
        P(None, "dp"),
        P(None, "dp"),
        P(None, "dp", "seq", None),
        P("seq", "dp"),
        P("seq", "dp"),
        P("seq", "dp"),
        P("seq", "dp"),
        P("seq", "dp"),
        P("seq", "dp"),
        P("seq", "dp"),
        P("seq", "dp"),
        P("seq", "dp"),
        P("seq", "dp"),
        P(("dp", "seq")),
        P(("dp", "seq")),
        P(("dp", "seq")),
    )
    out_specs = (
        P(None, "dp", "seq", None),
        P(None, "dp", "seq", None),
        P(None, "dp", None),
        P("seq", "dp"),
        P("seq", "dp"),
        P("seq", "dp"),
        P("seq", "dp"),
        P("seq", "dp"),
        P("seq", "dp"),
        P("seq", "dp"),
        P("seq", "dp"),
        P("seq", "dp"),
        P("seq", "dp"),
        P(("dp", "seq")),
        P(("dp", "seq")),
        P(("dp", "seq")),
    )
    return jax.shard_map(body, mesh=mesh, in_specs=in_specs, out_specs=out_specs, check_vma=False)
```

profile of v0, /device:TPU:11, one launch (start us, length us, event | category | flops | bytes accessed | tf_op | source)
XLA Modules:
  0.0 3193.9 jit_solution(10255348421277705080)
XLA Ops:
  10.3 78.2 %all-gather.15.cloned.1.call-done = bf16[576,6912]{0,1:T(8,128)(2,1)} async-done(((bf16[576,432]{0,1:T(8,128)(2,1)}), bf16[576,6912]{0,1:T(8,128)(2,1)}) %all-gather.15.cloned.1.call-update) | async-done | bytes 7962640 | tf_op jit(solution)/shard_map/all_gather | solution.py:58
  100.0 42.0 %all-gather.19.cloned.1.call-done = bf16[576,3456]{0,1:T(8,128)(2,1)} async-done(((bf16[576,216]{0,1:T(8,128)(2,1)}), bf16[576,3456]{0,1:T(8,128)(2,1)}) %all-gather.19.cloned.1.call-update) | async-done | bytes 3981328 | tf_op jit(solution)/shard_map/all_gather | solution.py:54
  154.1 39.6 %all-reduce = f32[16128]{0:T(1024)S(1)} all-reduce(f32[16128]{0:T(1024)S(1)} %dynamic-update-slice), channel_id=1, replica_groups=mesh['dp'=16,'seq'=2] {'dp','seq'}, use_global_device_ids=true, to_apply=%add | all-reduce | flops 16128 | bytes 129024
  194.9 138.1 %all-gather.17.cloned.1.call-done = bf16[1152,6912]{1,0:T(8,128)(2,1)} async-done(((bf16[576,6912]{1,0:T(8,128)(2,1)}), bf16[1152,6912]{1,0:T(8,128)(2,1)}) %all-gather.17.cloned.1.call-update) | async-done | bytes 15925264 | tf_op jit(solution)/shard_map/all_gather | solution.py:66
  346.9 86.8 %all-gather.21.cloned.1.call-done = bf16[1152,3456]{1,0:T(8,128)(2,1)} async-done(((bf16[576,3456]{1,0:T(8,128)(2,1)}), bf16[1152,3456]{1,0:T(8,128)(2,1)}) %all-gather.21.cloned.1.call-update) | async-done | bytes 7962640 | tf_op jit(solution)/shard_map/all_gather | solution.py:62
  477.0 59.5 %all-gather.31.cloned.1.call-done = bf16[576,4608]{0,1:T(8,128)(2,1)} async-done(((bf16[576,288]{0,1:T(8,128)(2,1)}), bf16[576,4608]{0,1:T(8,128)(2,1)}) %all-gather.31.cloned.1.call-update) | async-done | bytes 5308432 | tf_op jit(solution)/shard_map/all_gather | solution.py:56
  548.5 45.8 %all-gather.35.cloned.1.call-done = bf16[2304,1152]{0,1:T(8,128)(2,1)} async-done(((bf16[2304,72]{0,1:T(8,128)(2,1)}), bf16[2304,1152]{0,1:T(8,128)(2,1)}) %all-gather.35.cloned.1.call-update) | async-done | bytes 5308432 | tf_op jit(solution)/shard_map/all_gather | solution.py:57
  835.0 83.3 %all-gather.33.cloned.1.call-done = bf16[1152,4608]{1,0:T(8,128)(2,1)} async-done(((bf16[576,4608]{1,0:T(8,128)(2,1)}), bf16[1152,4608]{1,0:T(8,128)(2,1)}) %all-gather.33.cloned.1.call-update) | async-done | bytes 10616848 | tf_op jit(solution)/shard_map/all_gather | solution.py:64
  931.4 119.2 %all-gather.37.cloned.1.call-done = bf16[4608,1152]{0,1:T(8,128)(2,1)} async-done(((bf16[2304,1152]{0,1:T(8,128)(2,1)}), bf16[4608,1152]{0,1:T(8,128)(2,1)}) %all-gather.37.cloned.1.call-update) | async-done | bytes 10616848 | tf_op jit(solution)/shard_map/all_gather | solution.py:65
  1422.9 36.9 %reduce-scatter.43.cloned.1.call-done = bf16[1,512,1152]{1,2,0:T(8,128)(2,1)} async-done(((bf16[1,1024,1152]{1,2,0:T(8,128)(2,1)}), bf16[1,512,1152]{1,2,0:T(8,128)(2,1)}) %reduce-scatter.43.cloned.1.call-update) | async-done | bytes 1179664 | tf_op jit(solution)/shard_map/reduce_scatter | solution.py:248
  1525.0 59.0 %reduce-scatter.55.cloned.1.call-done = bf16[4608,72]{0,1:T(8,128)(2,1)} async-done(((bf16[4608,1152]{0,1:T(8,128)(2,1)}), bf16[4608,72]{0,1:T(8,128)(2,1)}) %reduce-scatter.55.cloned.1.call-update) | async-done | bytes 663568 | tf_op jit(solution)/shard_map/reduce_scatter | solution.py:84
  1584.1 124.0 %reduce-scatter.59.cloned.1.call-done = bf16[4608,72]{0,1:T(8,128)(2,1)} async-done(((bf16[4608,1152]{0,1:T(8,128)(2,1)}), bf16[4608,72]{0,1:T(8,128)(2,1)}) %reduce-scatter.59.cloned.1.call-update) | async-done | bytes 663568 | tf_op jit(solution)/shard_map/reduce_scatter | solution.py:84
  1708.2 124.0 %reduce-scatter.51.cloned.1.call-done = bf16[1152,288]{0,1:T(8,128)(2,1)} async-done(((bf16[1152,4608]{0,1:T(8,128)(2,1)}), bf16[1152,288]{0,1:T(8,128)(2,1)}) %reduce-scatter.51.cloned.1.call-update) | async-done | bytes 663568 | tf_op jit(solution)/shard_map/reduce_scatter | solution.py:81
  1834.6 121.6 %reduce-scatter.53.cloned.1.call-done = bf16[1152,288]{0,1:T(8,128)(2,1)} async-done(((bf16[1152,4608]{0,1:T(8,128)(2,1)}), bf16[1152,288]{0,1:T(8,128)(2,1)}) %reduce-scatter.53.cloned.1.call-update) | async-done | bytes 663568 | tf_op jit(solution)/shard_map/reduce_scatter | solution.py:81
  1958.6 102.3 %reduce-scatter.81.cloned.1.call-done = bf16[1152,216]{0,1:T(8,128)(2,1)} async-done(((bf16[1152,3456]{0,1:T(8,128)(2,1)}), bf16[1152,216]{0,1:T(8,128)(2,1)}) %reduce-scatter.81.cloned.1.call-update) | async-done | bytes 497680
  2092.7 103.2 %reduce-scatter.79.cloned.1.call-done = bf16[1152,216]{0,1:T(8,128)(2,1)} async-done(((bf16[1152,3456]{0,1:T(8,128)(2,1)}), bf16[1152,216]{0,1:T(8,128)(2,1)}) %reduce-scatter.79.cloned.1.call-update) | async-done | bytes 497680
  2201.2 105.6 %reduce-scatter.63.cloned.1.call-done = bf16[576,432]{0,1:T(8,128)(2,1)} async-done(((bf16[576,6912]{0,1:T(8,128)(2,1)}), bf16[576,432]{0,1:T(8,128)(2,1)}) %reduce-scatter.63.cloned.1.call-update) | async-done | bytes 497680 | tf_op jit(solution)/shard_map/reduce_scatter | solution.py:87
  2306.7 111.4 %reduce-scatter.65.cloned.1.call-done = bf16[576,432]{0,1:T(8,128)(2,1)} async-done(((bf16[576,6912]{0,1:T(8,128)(2,1)}), bf16[576,432]{0,1:T(8,128)(2,1)}) %reduce-scatter.65.cloned.1.call-update) | async-done | bytes 497680 | tf_op jit(solution)/shard_map/reduce_scatter | solution.py:87
  2578.2 98.0 %all-reduce.32.cloned.1.call-done = (bf16[4,144,144]{2,1,0:T(8,128)(2,1)}, bf16[4,144,144]{2,1,0:T(8,128)(2,1)}, bf16[4,144,144]{2,1,0:T(8,128)(2,1)}, bf16[16,144,144]{2,1,0:T(8,128)(2,1)}, bf16[4,144,144]{2,1,0:T(8,128)(2,1)}) async-done(((bf16[4,144,144]{2,1,0:T(8,128)(2,1)}, bf16[4,144,144]{2,1,0:T(8,128)(2,1)}, bf16[4,144,144]{2,1,0:T(8,128)(2,1)}, bf16[16,144,144]{2,1,0:T(8,128)(2,1)}, ...) | async-done | bytes 1327120 | tf_op jit(solution)/shard_map/psum | solution.py:299
  2707.2 89.7 %all-reduce.30.cloned.1.call-done = (bf16[4,144,144]{2,1,0:T(8,128)(2,1)}, bf16[4,144,144]{2,1,0:T(8,128)(2,1)}, bf16[4,144,144]{2,1,0:T(8,128)(2,1)}, bf16[16,144,144]{2,1,0:T(8,128)(2,1)}, bf16[4,144,144]{2,1,0:T(8,128)(2,1)}) async-done(((bf16[4,144,144]{2,1,0:T(8,128)(2,1)}, bf16[4,144,144]{2,1,0:T(8,128)(2,1)}, bf16[4,144,144]{2,1,0:T(8,128)(2,1)}, bf16[16,144,144]{2,1,0:T(8,128)(2,1)}, ...) | async-done | bytes 1327120 | tf_op jit(solution)/shard_map/psum | solution.py:299
  2826.5 89.7 %all-reduce.28.cloned.1.call-done = (bf16[4,144,144]{2,1,0:T(8,128)(2,1)}, bf16[4,144,144]{2,1,0:T(8,128)(2,1)}, bf16[4,144,144]{2,1,0:T(8,128)(2,1)}, bf16[16,144,144]{2,1,0:T(8,128)(2,1)}, bf16[4,144,144]{2,1,0:T(8,128)(2,1)}) async-done(((bf16[4,144,144]{2,1,0:T(8,128)(2,1)}, bf16[4,144,144]{2,1,0:T(8,128)(2,1)}, bf16[4,144,144]{2,1,0:T(8,128)(2,1)}, bf16[16,144,144]{2,1,0:T(8,128)(2,1)}, ...) | async-done | bytes 1327120 | tf_op jit(solution)/shard_map/psum | solution.py:299
  2939.1 46.8 %all-reduce.11 = (bf16[16128]{0:T(1024)(128)(2,1)S(1)}, bf16[16128]{0:T(1024)(128)(2,1)S(1)}) all-reduce(bf16[16128]{0:T(1024)(128)(2,1)S(1)} %dynamic-update-slice.6, bf16[16128]{0:T(1024)(128)(2,1)S(1)} %dynamic-update-slice.12), channel_id=26, replica_groups=mesh['dp'=16,'seq'=2] {'dp'}, use_global_device_ids=true, to_apply=%region_106.107.clone | all-reduce | flops 32256 | bytes 129024
  2991.1 45.1 %all-reduce.26.cloned.1.call-done = (bf16[4,144,144]{2,1,0:T(8,128)(2,1)}, bf16[4,144,144]{2,1,0:T(8,128)(2,1)}, bf16[4,144,144]{2,1,0:T(8,128)(2,1)}, bf16[16,144,144]{2,1,0:T(8,128)(2,1)}, bf16[4,144,144]{2,1,0:T(8,128)(2,1)}) async-done(((bf16[4,144,144]{2,1,0:T(8,128)(2,1)}, bf16[4,144,144]{2,1,0:T(8,128)(2,1)}, bf16[4,144,144]{2,1,0:T(8,128)(2,1)}, bf16[16,144,144]{2,1,0:T(8,128)(2,1)}, ...) | async-done | bytes 1327120 | tf_op jit(solution)/shard_map/psum | solution.py:299
  3064.7 90.0 %all-reduce.24.cloned.1.call-done = (bf16[4,144,144]{2,1,0:T(8,128)(2,1)}, bf16[4,144,144]{2,1,0:T(8,128)(2,1)}, bf16[4,144,144]{2,1,0:T(8,128)(2,1)}, bf16[16,144,144]{2,1,0:T(8,128)(2,1)}, bf16[4,144,144]{2,1,0:T(8,128)(2,1)}) async-done(((bf16[4,144,144]{2,1,0:T(8,128)(2,1)}, bf16[4,144,144]{2,1,0:T(8,128)(2,1)}, bf16[4,144,144]{2,1,0:T(8,128)(2,1)}, bf16[16,144,144]{2,1,0:T(8,128)(2,1)}, ...) | async-done | bytes 1327120 | tf_op jit(solution)/shard_map/psum | solution.py:299
  (754 shorter events, 1135.4 us)
Async XLA Ops:
  100.0 333.7 %all-gather.21.cloned.1.call-start = ((), (), s32[]{:S(2)}) async-start(), calls=%async_computation.25 | async-start | bytes 11943936 | tf_op jit(solution)/shard_map/all_gather | solution.py:62
  148.5 325.9 %all-gather.27.cloned.1.call-start = ((), (), s32[]{:S(2)}) async-start(), calls=%async_computation.28 | async-start | bytes 1566720 | tf_op jit(solution)/shard_map/all_gather | solution.py:55
  150.1 386.5 %all-gather.31.cloned.1.call-start = ((), (), s32[]{:S(2)}) async-start(), calls=%async_computation.30 | async-start | bytes 6266880 | tf_op jit(solution)/shard_map/all_gather | solution.py:56
  150.9 443.3 %all-gather.35.cloned.1.call-start = ((), (), s32[]{:S(2)}) async-start(), calls=%async_computation.32 | async-start | bytes 5640192 | tf_op jit(solution)/shard_map/all_gather | solution.py:57
  153.0 477.9 %all-gather.23.cloned.1.call-start = ((), (), s32[]{:S(2)}) async-start(), calls=%async_computation.26 | async-start | bytes 3538944 | tf_op jit(solution)/shard_map/all_gather | solution.py:161
  477.0 441.3 %all-gather.33.cloned.1.call-start = ((), (), s32[]{:S(2)}) async-start(), calls=%async_computation.31 | async-start | bytes 15925248 | tf_op jit(solution)/shard_map/all_gather | solution.py:64
  544.8 505.9 %all-gather.37.cloned.1.call-start = ((), (), s32[]{:S(2)}) async-start(), calls=%async_computation.33 | async-start | bytes 15925248 | tf_op jit(solution)/shard_map/all_gather | solution.py:65
  594.3 753.5 %reduce-scatter.49.cloned.1.call-start = ((), (), s32[]{:S(2)}) async-start(), calls=%async_computation.39 | async-start | bytes 3538944 | tf_op jit(solution)/shard_map/reduce_scatter | solution.py:251
  1294.9 413.2 %reduce-scatter.59.cloned.1.call-start = ((), (), s32[]{:S(2)}) async-start(), calls=%async_computation.44 | async-start | bytes 11280384 | tf_op jit(solution)/shard_map/reduce_scatter | solution.py:84
  1307.0 525.2 %reduce-scatter.51.cloned.1.call-start = ((), (), s32[]{:S(2)}) async-start(), calls=%async_computation.40 | async-start | bytes 11280384 | tf_op jit(solution)/shard_map/reduce_scatter | solution.py:81
  1320.3 635.9 %reduce-scatter.53.cloned.1.call-start = ((), (), s32[]{:S(2)}) async-start(), calls=%async_computation.41 | async-start | bytes 11280384 | tf_op jit(solution)/shard_map/reduce_scatter | solution.py:81
  1334.5 726.4 %reduce-scatter.81.cloned.1.call-start = ((), (), s32[]{:S(2)}) async-start(), calls=%async_computation.55 | async-start | bytes 8460288
  1358.1 717.6 %reduce-scatter.73.cloned.1.call-start = ((), (), s32[]{:S(2)}) async-start(), calls=%async_computation.51 | async-start | bytes 442368
  1360.1 730.3 %reduce-scatter.71.cloned.1.call-start = ((), (), s32[]{:S(2)}) async-start(), calls=%async_computation.50 | async-start | bytes 442368
  1386.8 809.0 %reduce-scatter.79.cloned.1.call-start = ((), (), s32[]{:S(2)}) async-start(), calls=%async_computation.54 | async-start | bytes 8460288
  1470.4 836.3 %reduce-scatter.63.cloned.1.call-start = ((), (), s32[]{:S(2)}) async-start(), calls=%async_computation.46 | async-start | bytes 9400320 | tf_op jit(solution)/shard_map/reduce_scatter | solution.py:87
  1520.0 898.2 %reduce-scatter.65.cloned.1.call-start = ((), (), s32[]{:S(2)}) async-start(), calls=%async_computation.47 | async-start | bytes 9400320 | tf_op jit(solution)/shard_map/reduce_scatter | solution.py:87
  1525.0 911.6 %reduce-scatter.57.cloned.1.call-start = ((), (), s32[]{:S(2)}) async-start(), calls=%async_computation.43 | async-start | bytes 995328 | tf_op jit(solution)/shard_map/reduce_scatter | solution.py:105
  1584.1 871.0 %reduce-scatter.61.cloned.1.call-start = ((), (), s32[]{:S(2)}) async-start(), calls=%async_computation.45 | async-start | bytes 995328 | tf_op jit(solution)/shard_map/reduce_scatter | solution.py:105
  1708.1 768.2 %reduce-scatter.75.cloned.1.call-start = ((), (), s32[]{:S(2)}) async-start(), calls=%async_computation.52 | async-start | bytes 1327104 | tf_op jit(solution)/shard_map/reduce_scatter | solution.py:102
  1834.5 663.2 %reduce-scatter.77.cloned.1.call-start = ((), (), s32[]{:S(2)}) async-start(), calls=%async_computation.53 | async-start | bytes 1327104 | tf_op jit(solution)/shard_map/reduce_scatter | solution.py:102
  1958.5 557.4 %reduce-scatter.69.cloned.1.call-start = ((), (), s32[]{:S(2)}) async-start(), calls=%async_computation.49 | async-start | bytes 884736 | tf_op jit(solution)/shard_map/reduce_scatter | solution.py:96
  2063.0 471.0 %reduce-scatter.67.cloned.1.call-start = ((), (), s32[]{:S(2)}) async-start(), calls=%async_computation.48 | async-start | bytes 884736 | tf_op jit(solution)/shard_map/reduce_scatter | solution.py:96
  2197.9 478.2 %all-reduce.32.cloned.1.call-start = ((), (), s32[]{:S(2)}) async-start(), calls=%async_computation.62 | async-start | bytes 4718592 | tf_op jit(solution)/shard_map/psum | solution.py:299
  (202 other events, 9250.2 us)
Sparse Core Ops, SparseCore 0:
  10.8 77.6 all-gather.14
  91.2 50.7 all-gather.18
  143.6 189.3 all-gather.16
  334.3 99.3 all-gather.20
  477.1 59.3 all-gather.30
  539.3 54.9 all-gather.34
  746.3 39.3 all-gather.28
  787.3 130.9 all-gather.32
  919.7 130.9 all-gather.36
  1256.2 61.7 reduce-scatter.84
  1322.2 62.6 reduce-scatter.82
  1463.9 120.0 reduce-scatter.54
  1588.1 119.9 reduce-scatter.58
  1712.2 119.9 reduce-scatter.50
  1836.1 120.0 reduce-scatter.52
  1960.2 100.5 reduce-scatter.80
  2095.1 100.6 reduce-scatter.78
  2200.0 106.6 reduce-scatter.62
  2311.3 106.8 reduce-scatter.64
  2570.5 105.6 all-reduce.31
  2697.5 99.3 all-reduce.29
  2816.8 99.3 all-reduce.27
  2936.6 99.5 all-reduce.25
  3055.3 99.3 all-reduce.23
  (17 shorter events, 444.0 us)
where the time goes:
time: 3210 us; the launch traced here: 3190 us
  waiting for transfers between devices  2250 us (70%)
  matrix products  561 us (17%)
  local copies, waits for them, and re-layouts  128 us (4%)
  blocking collectives  126 us (4%)
  other arithmetic  111 us (3%)
    psum x5, waiting for transfers between devices, gram_sums(): lax.psum(gram_qkv.astype(jnp.bfloat16), 'dp').astype(jnp.float32)  412 us
    reduce_scatter x2, waiting for transfers between devices, reduce_terms(): lax.psum_scatter(term_fc1.astype(jnp.bfloat16), 'dp', scatter_dimension=1...  246 us
    unnamed x47, waiting for transfers between devices  234 us
    reduce_scatter x2, waiting for transfers between devices, reduce_terms(): lax.psum_scatter(term_ada.astype(jnp.bfloat16), 'dp', scatter_dimension=1...  217 us
    reduce_scatter x2, waiting for transfers between devices, reduce_terms(): lax.psum_scatter(term_fc2.astype(jnp.bfloat16), 'dp', scatter_dimension=1...  183 us
    all_gather x1, waiting for transfers between devices, gather_weights(): lax.all_gather(part_ada, 'seq', axis=0, tiled=True)  138 us
    all_gather x1, waiting for transfers between devices, gather_weights(): lax.all_gather(part_fc2, 'seq', axis=0, tiled=True)  119 us
    unnamed x3, blocking collectives  90.7 us
  transfers between devices with their start and end apart: 41, of which 38 were waited for; matrix products, arithmetic and copies ran while one was open for 16% of the time, Pallas kernels for 0%

commit v1 on v0

v1 whole, which is shorter than its diff:
```python
import functools
import math

import jax
import jax.numpy as jnp
from jax import lax
from jax.experimental import pallas as pl
from jax.experimental.pallas import tpu as pltpu
from jax.sharding import PartitionSpec as P

HEADS = 16
ROW_BLOCK = 144
NS_STEPS = 5
STEP_COUNT = 10

PRECISE = lax.Precision.HIGHEST
LN_EPS = 1e-06
MASKED = -1e30
NS_A = 3.4445
NS_B = -4.775
NS_C = 2.0315
MUON_DECAY = 0.5
WEIGHT_SHRINK = 0.0001
NORM_EPS = 1e-07
BETA_FIRST = 0.9
BETA_SECOND = 0.999
ADAM_RATE = 0.1
ADAM_DECAY = 0.01
ADAM_EPS = 1e-08
BF = jnp.bfloat16
F32 = jnp.float32


class Ring:
    def __init__(self, name, total, stride, size):
        self.name, self.total, self.stride, self.size = name, total, stride, size

    def digit(self):
        return (lax.axis_index(self.name) // self.stride) % self.size

    def send(self, value, shift):
        pairs = []
        for i in range(self.total):
            d = (i // self.stride) % self.size
            pairs.append((i, i + ((d + shift) % self.size - d) * self.stride))
        return lax.ppermute(value, self.name, pairs)

    def gather(self, value):
        n, rows = self.size, value.shape[0]
        pieces = [(0, 0, rows, value)]
        if n == 1:
            return pieces
        if n == 2:
            return pieces + [(1, 0, rows, self.send(value, 1))]
        low = high = value
        for t in range(1, n // 2):
            low, high = self.send(low, 1), self.send(high, -1)
            pieces += [(n - t, 0, rows, low), (t, 0, rows, high)]
        cut = rows // 2
        pieces.append((n // 2, 0, cut, self.send(low[:cut], 1)))
        pieces.append((n // 2, cut, rows, self.send(high[cut:], -1)))
        return pieces

    def gather_list(self, value):
        blocks = [[] for _ in range(self.size)]
        for shift, start, _, array in self.gather(value):
            blocks[shift].append((start, array))
        merged = []
        for block in blocks:
            arrays = [array for _, array in sorted(block, key=lambda item: item[0])]
            merged.append(arrays[0] if len(arrays) == 1 else jnp.concatenate(arrays, axis=0))
        return merged

    def scatter_sum(self, block_of):
        n = self.size
        own = block_of(0).astype(F32)
        if n == 1:
            return own
        if n == 2:
            return own + self.send(block_of(1), 1).astype(F32)
        far = block_of(n // 2)
        kind, cut = far.dtype, far.shape[0] // 2
        low, high = self.send(far[:cut], 1), self.send(far[cut:], -1)
        for t in range(n // 2 - 1, 0, -1):
            up, down = block_of(t), block_of(n - t)
            if t == n // 2 - 1:
                up = jnp.concatenate([(up[:cut].astype(F32) + low.astype(F32)).astype(kind), up[cut:]], axis=0)
                down = jnp.concatenate(
                    [down[:cut], (down[cut:].astype(F32) + high.astype(F32)).astype(kind)], axis=0
                )
            else:
                up = (up.astype(F32) + low.astype(F32)).astype(kind)
                down = (down.astype(F32) + high.astype(F32)).astype(kind)
            low, high = self.send(up, 1), self.send(down, -1)
        return own + low.astype(F32) + high.astype(F32)


def place_kernel(moves, count, *refs):
    spots, sources, out, sems = refs[0], refs[1 : 1 + count], refs[1 + count], refs[2 + count]
    copies = []
    for n, (source, index, target) in enumerate(moves):
        copies.append(
            pltpu.make_async_copy(sources[source].at[index], out.at[target(spots)], sems.at[n])
        )
    for copy in copies:
        copy.start()
    for copy in copies:
        copy.wait()


def place(spots, sources, moves, shape, dtype):
    return pl.pallas_call(
        functools.partial(place_kernel, moves, len(sources)),
        out_shape=jax.ShapeDtypeStruct(shape, dtype),
        in_specs=[pl.BlockSpec(memory_space=pltpu.SMEM)]
        + [pl.BlockSpec(memory_space=pl.ANY)] * len(sources),
        out_specs=pl.BlockSpec(memory_space=pl.ANY),
        scratch_shapes=[pltpu.SemaphoreType.DMA((len(moves),))],
        cost_estimate=pl.CostEstimate(
            flops=0, bytes_accessed=2 * math.prod(shape) * jnp.dtype(dtype).itemsize, transcendentals=0
        ),
        name="place",
    )(spots, *sources)


class Net:
    def __init__(self, mesh):
        dp, seq = mesh.shape["dp"], mesh.shape["seq"]
        self.dp, self.seq = dp, seq
        self.core = Ring("dp", dp, 1, 2)
        self.x = Ring("dp", dp, 2, 2)
        self.z = Ring("dp", dp, 4, dp // 4)
        self.y = Ring("seq", seq, 1, seq)

    def spots(self):
        return jnp.stack([self.z.digit(), self.x.digit(), self.core.digit()]).astype(jnp.int32)


    def rows_joined(self, shard):
        turned = shard.astype(BF).T
        blocks = self.y.gather_list(turned)
        if self.seq == 2:
            own, other = blocks
            full = jnp.where(
                self.y.digit() == 0,
                jnp.concatenate([own, other], axis=1),
                jnp.concatenate([other, own], axis=1),
            )
        else:
            order = (jnp.arange(self.seq) - self.y.digit()) % self.seq
            full = jnp.take(jnp.stack(blocks), order, axis=0)
            full = jnp.transpose(full, (1, 0, 2)).reshape(turned.shape[0], -1)
        unit = math.gcd(full.shape[0], 8)
        return full.reshape(full.shape[0] // unit, unit, full.shape[1])

    def gather_weight(self, units):
        g, unit, depth = units.shape
        zs = self.z.size
        ga = max(1, (4 * g) // 9)
        gb = g - ga
        first, second = units[:ga], units[ga:]
        line = jnp.stack(self.z.gather_list(first))
        line_x = self.x.send(line, 1)
        pair = jnp.stack([second, self.x.send(second, 1)])
        pieces = self.z.gather(pair)
        sources, moves = [], []

        def spot(sz, sx, sc, start, stop):
            def target(spots):
                return (
                    lax.rem(spots[0] + sz, zs),
                    lax.rem(spots[1] + sx, 2),
                    lax.rem(spots[2] + sc, 2),
                    pl.ds(start, stop - start),
                )

            return target

        for sc in range(2):
            for sx, array in ((0, line), (1, line_x)):
                array = array if sc == 0 else self.core.send(array, 1)
                for sz in range(zs):
                    moves.append((len(sources), (sz,), spot(sz, sx, sc, 0, ga)))
                sources.append(array)
            for sz, start, stop, array in pieces:
                array = array if sc == 0 else self.core.send(array, 1)
                for sx in range(start, stop):
                    moves.append((len(sources), (sx - start,), spot(sz, sx, sc, ga, g)))
                sources.append(array)
        full = place(self.spots(), sources, moves, (zs, 2, 2, g, unit, depth), BF)
        return full.reshape(self.dp * g * unit, depth)

    def scatter_weight(self, term, rows):
        depth = term.shape[1]
        n = term.shape[0] // self.dp
        unit = math.gcd(n, 8)
        g = n // unit
        zs = self.z.size
        ga = max(1, (4 * g) // 9)
        blocks = term.reshape(zs, 2, 2, g, unit, depth)
        core, x, z = self.core.digit(), self.x.digit(), self.z.digit()
        half = self.core.scatter_sum(
            lambda s: lax.dynamic_index_in_dim(blocks, (core + s) % 2, 2, keepdims=False)
        ).astype(BF)
        first, second = half[:, :, :ga], half[:, :, ga:]
        line = self.x.scatter_sum(
            lambda s: lax.dynamic_index_in_dim(first, (x + s) % 2, 1, keepdims=False)
        ).astype(BF)
        first = self.z.scatter_sum(
            lambda s: lax.dynamic_index_in_dim(line, (z + s) % zs, 0, keepdims=False)
        )
        pair = self.z.scatter_sum(
            lambda s: lax.dynamic_index_in_dim(second, (z + s) % zs, 0, keepdims=False)
        ).astype(BF)
        second = self.x.scatter_sum(
            lambda s: lax.dynamic_index_in_dim(pair, (x + s) % 2, 0, keepdims=False)
        )
        joined = jnp.concatenate([first, second], axis=0).astype(BF).reshape(n, depth)
        y = self.y.digit()
        total = self.y.scatter_sum(
            lambda s: lax.dynamic_slice_in_dim(joined, ((y + s) % self.seq) * rows, rows, 1)
        )
        return total.T


    def gather_dp(self, value):
        z, x, core = self.z.digit(), self.x.digit(), self.core.digit()
        blocks = self.z.gather_list(value)
        line = jnp.zeros((self.z.size,) + value.shape, value.dtype)
        for s, block in enumerate(blocks):
            line = lax.dynamic_update_index_in_dim(line, block, (z + s) % self.z.size, 0)
        other = self.x.send(line, 1)
        plane = jnp.where(x == 0, jnp.stack([line, other], 1), jnp.stack([other, line], 1))
        other = self.core.send(plane, 1)
        both = jnp.where(core == 0, jnp.stack([plane, other], 2), jnp.stack([other, plane], 2))
        return both.reshape((self.dp,) + value.shape)

    def scatter_dp(self, value):
        z, x, core, zs = self.z.digit(), self.x.digit(), self.core.digit(), self.z.size
        blocks = value.reshape((zs, 2, 2) + value.shape[1:])
        half = self.core.scatter_sum(
            lambda s: lax.dynamic_index_in_dim(blocks, (core + s) % 2, 2, keepdims=False)
        )
        line = self.x.scatter_sum(
            lambda s: lax.dynamic_index_in_dim(half, (x + s) % 2, 1, keepdims=False)
        )
        return self.z.scatter_sum(
            lambda s: lax.dynamic_index_in_dim(line, (z + s) % zs, 0, keepdims=False)
        )


def layer_norm(values):
    centered = values - jnp.mean(values, axis=-1, keepdims=True)
    inverse = lax.rsqrt(jnp.mean(centered * centered, axis=-1, keepdims=True) + LN_EPS)
    return (centered * inverse, inverse)


def norm_back(normed, inverse, grad):
    mean_grad = jnp.mean(grad, axis=-1, keepdims=True)
    mean_cross = jnp.mean(grad * normed, axis=-1, keepdims=True)
    return inverse * (grad - mean_grad - normed * mean_cross)


def sigmoid_linear(values):
    return values * jax.nn.sigmoid(values)


def gelu_tanh(values):
    return jax.nn.gelu(values, approximate=True)


def dot_t(left, right):
    return jnp.einsum("srk,nk->srn", left, right, preferred_element_type=F32)


def dot(left, right):
    return jnp.einsum("srn,nk->srk", left, right, preferred_element_type=F32)


def outer(left, right):
    return jnp.einsum("srn,srk->nk", left, right, preferred_element_type=F32).astype(BF)


def attention_scores(queries, keys, valid):
    head_dim = queries.shape[-1]
    scores = jnp.einsum("qhd,khd->hqk", queries, keys, preferred_element_type=F32) * head_dim**-0.5
    return jnp.where(valid[None, None, :], scores, MASKED)


def attention_one(queries, keys, values, valid):
    scores = attention_scores(queries, keys, valid)
    peak = jnp.max(scores, axis=-1)
    weights = jnp.exp(scores - peak[..., None])
    total = jnp.sum(weights, axis=-1)
    mixed = jnp.einsum("hqk,khd->hqd", weights.astype(BF), values, preferred_element_type=F32)
    heads = jnp.transpose(mixed / total[..., None], (1, 0, 2))
    return heads, peak + jnp.log(total)


def attention_one_back(queries, keys, values, valid, heads, log_total, grad_heads):
    head_dim = queries.shape[-1]
    delta = jnp.einsum("qhd,qhd->hq", grad_heads.astype(F32), heads)
    scores = attention_scores(queries, keys, valid)
    probs = jnp.exp(scores - log_total[..., None])
    grad_probs = jnp.einsum("qhd,khd->hqk", grad_heads, values, preferred_element_type=F32)
    grad_scores = (probs * (grad_probs - delta[..., None])).astype(BF)
    scale = head_dim**-0.5
    grad_q = jnp.einsum("hqk,khd->qhd", grad_scores, keys, preferred_element_type=F32) * scale
    grad_k = jnp.einsum("hqk,qhd->khd", grad_scores, queries, preferred_element_type=F32) * scale
    grad_v = jnp.einsum("hqk,qhd->khd", probs.astype(BF), grad_heads, preferred_element_type=F32)
    return grad_q.astype(BF), grad_k.astype(BF), grad_v.astype(BF)


def gram_of(moment):
    block = moment.reshape(moment.shape[0] // ROW_BLOCK, ROW_BLOCK, moment.shape[1])
    return jnp.einsum("nrc,nsc->nrs", block, block, precision=PRECISE)


def polynomial(gram):
    eye = jnp.eye(ROW_BLOCK, dtype=F32)
    square = jnp.sum(gram * eye, axis=(1, 2))
    scale = 1.0 / (jnp.sqrt(square) + NORM_EPS)
    current = gram * (scale * scale)[:, None, None]
    mul = functools.partial(jnp.einsum, "nrs,nst->nrt", precision=PRECISE)
    total = None
    for step in range(NS_STEPS):
        factor = NS_A * eye + NS_B * current + NS_C * mul(current, current)
        total = factor if total is None else mul(factor, total)
        if step + 1 < NS_STEPS:
            current = mul(mul(factor, current), factor)
    return total * scale[:, None, None]


def body(net, tokens, conditioning, heights, widths, upstream, *state):
    masters, momenta = state[0:5], state[5:10]
    biases, bias_first, bias_second = state[10:13]
    w_qkv, w_proj, w_fc1, w_fc2, w_ada = masters
    micro, local, rows, width = tokens.shape
    count = micro * local
    head_dim = width // HEADS
    hidden = w_fc1.shape[1] * net.dp
    seq, dp = net.seq, net.dp
    y = net.y.digit()

    units_qkv = net.rows_joined(w_qkv)
    units_proj = net.rows_joined(w_proj)
    units_fc1 = net.rows_joined(w_fc1)
    units_fc2 = net.rows_joined(w_fc2)
    own_tokens = tokens.reshape(count, rows, width)
    all_tokens = jnp.concatenate(net.y.gather_list(own_tokens), axis=1)
    t_qkv = net.gather_weight(units_qkv)
    t_proj = net.gather_weight(units_proj)
    t_fc1 = net.gather_weight(units_fc1)
    t_fc2 = net.gather_weight(units_fc2)

    low_ada = w_ada.astype(BF)
    ada_rows, ada_cols = w_ada.shape
    cond = conditioning.astype(F32).reshape(count, width)
    cond_act, silu_back = jax.vjp(sigmoid_linear, cond)
    cond_low = cond_act.astype(BF)
    cond_rows = lax.dynamic_slice_in_dim(cond_low, y * ada_rows, ada_rows, 1)
    cond_all = net.gather_dp(cond_rows).reshape(dp * count, ada_rows)
    partial = jnp.dot(cond_all, low_ada, preferred_element_type=F32)
    partial = lax.psum(partial, "seq").reshape(dp, count, ada_cols)
    received = lax.all_to_all(partial, "dp", 0, 0, tiled=True)
    bias_full = lax.all_to_all(
        jnp.broadcast_to(biases[None], (dp * seq,) + biases.shape), ("dp", "seq"), 0, 0, tiled=True
    ).reshape(-1)
    bounds = [0, 6 * width, 7 * width, 8 * width, 9 * width, 9 * width + hidden, 10 * width + hidden]
    b_ada, b_q, b_v, b_proj, b_fc1, b_fc2 = [bias_full[bounds[i] : bounds[i + 1]] for i in range(6)]
    modulation = jnp.transpose(received, (1, 0, 2)).reshape(count, dp * ada_cols) + b_ada
    shift_one, scale_one, gate_one, shift_two, scale_two, gate_two = jnp.split(
        modulation[:, None, :], 6, axis=-1
    )

    lengths = (heights * widths).reshape(count)
    places = jnp.concatenate([((y + s) % seq) * rows + jnp.arange(rows) for s in range(seq)])
    valid = places[None, :] < lengths[:, None]
    normed_all, inverse_all = layer_norm(all_tokens.astype(F32))
    attn_all = (normed_all * (1.0 + scale_one) + shift_one).astype(BF)
    attn_own = attn_all[:, :rows]
    queries = (dot_t(attn_own, t_qkv[:width]) + b_q).astype(BF)
    keys = dot_t(attn_all, t_qkv[width : 2 * width]).astype(BF)
    values = (dot_t(attn_all, t_qkv[2 * width :]) + b_v).astype(BF)
    queries = queries.reshape(count, rows, HEADS, head_dim)
    keys = keys.reshape(count, rows * seq, HEADS, head_dim)
    values = values.reshape(count, rows * seq, HEADS, head_dim)
    mixed_heads = [attention_one(queries[i], keys[i], values[i], valid[i]) for i in range(count)]
    attended_low = jnp.stack([heads for heads, _ in mixed_heads]).reshape(count, rows, width).astype(BF)
    inputs = own_tokens.astype(F32)
    branch_one = dot_t(attended_low, t_proj) + b_proj
    mixed_one = inputs + gate_one * branch_one
    normed_two, inverse_two = layer_norm(mixed_one)
    ffn_in = (normed_two * (1.0 + scale_two) + shift_two).astype(BF)
    pre_act = dot_t(ffn_in, t_fc1) + b_fc1
    activated, gelu_back = jax.vjp(gelu_tanh, pre_act)
    activated_low = activated.astype(BF)
    branch_two = dot_t(activated_low, t_fc2) + b_fc2
    result = (mixed_one + gate_two * branch_two).astype(BF)

    grad_out = upstream.reshape(count, rows, width).astype(F32)
    grad_branch_two = (gate_two * grad_out).astype(BF)
    grad_gate_two = jnp.sum(branch_two * grad_out, axis=1)
    shard_fc2 = net.scatter_weight(outer(grad_branch_two, activated_low), w_fc2.shape[0])
    bias_fc2 = jnp.sum(grad_branch_two.astype(F32), axis=(0, 1))
    grad_pre = gelu_back(dot(grad_branch_two, t_fc2))[0].astype(BF)
    shard_fc1 = net.scatter_weight(outer(grad_pre, ffn_in), w_fc1.shape[0])
    bias_fc1 = jnp.sum(grad_pre.astype(F32), axis=(0, 1))
    grad_ffn_in = dot(grad_pre, t_fc1)
    grad_shift_two = jnp.sum(grad_ffn_in, axis=1)
    grad_scale_two = jnp.sum(grad_ffn_in * normed_two, axis=1)
    grad_mixed = grad_out + norm_back(normed_two, inverse_two, grad_ffn_in * (1.0 + scale_two))
    grad_gate_one = jnp.sum(branch_one * grad_mixed, axis=1)
    grad_branch_one = (gate_one * grad_mixed).astype(BF)
    shard_proj = net.scatter_weight(outer(grad_branch_one, attended_low), w_proj.shape[0])
    bias_proj = jnp.sum(grad_branch_one.astype(F32), axis=(0, 1))
    grad_attended = dot(grad_branch_one, t_proj).astype(BF).reshape(count, rows, HEADS, head_dim)

    parts = [
        attention_one_back(
            queries[i], keys[i], values[i], valid[i], mixed_heads[i][0], mixed_heads[i][1], grad_attended[i]
        )
        for i in range(count)
    ]
    grad_q = jnp.stack([part[0] for part in parts]).reshape(count, rows, width)
    grad_kv = jnp.concatenate(
        [jnp.stack([part[k] for part in parts]).reshape(count, rows * seq, width) for k in (1, 2)], axis=-1
    )
    term_qkv = jnp.concatenate([outer(grad_q, attn_own), outer(grad_kv, attn_all)], axis=0)
    shard_qkv = net.scatter_weight(term_qkv, w_qkv.shape[0])
    bias_q = jnp.sum(grad_q.astype(F32), axis=(0, 1))
    bias_v = jnp.sum(grad_kv[..., width:].astype(F32), axis=(0, 1))
    part_in = dot(grad_kv, t_qkv[width:])
    own_part = part_in[:, :rows] + dot(grad_q, t_qkv[:width])
    grad_attn_in = net.y.scatter_sum(
        lambda s: own_part if s == 0 else part_in[:, s * rows : (s + 1) * rows].astype(BF)
    )
    normed_one, inverse_one = normed_all[:, :rows], inverse_all[:, :rows]
    grad_shift_one = jnp.sum(grad_attn_in, axis=1)
    grad_scale_one = jnp.sum(grad_attn_in * normed_one, axis=1)
    grad_inputs = grad_mixed + norm_back(normed_one, inverse_one, grad_attn_in * (1.0 + scale_one))

    grad_mod_local = jnp.concatenate(
        [grad_shift_one, grad_scale_one, grad_gate_one, grad_shift_two, grad_scale_two, grad_gate_two], axis=-1
    )
    bias_ada = jnp.sum(grad_mod_local, axis=0)
    grad_mod = lax.psum(grad_mod_local, "seq").astype(BF)
    grad_mod = jnp.transpose(grad_mod.reshape(count, dp, ada_cols), (1, 0, 2))
    mod_cols = lax.all_to_all(grad_mod, "dp", 0, 0, tiled=True).reshape(dp * count, ada_cols)
    shard_ada = jnp.einsum("sr,sc->rc", cond_all, mod_cols, preferred_element_type=F32)
    cond_part = jnp.einsum("sc,rc->sr", mod_cols, low_ada, preferred_element_type=F32)
    cond_part = lax.all_to_all(cond_part.reshape(dp, count, ada_rows), "dp", 0, 0, tiled=True)
    cond_part = jnp.sum(cond_part, axis=0)
    grad_cond_act = lax.all_gather(cond_part, "seq", axis=1, tiled=True)
    grad_cond = silu_back(grad_cond_act)[0]

    term_bias = jnp.concatenate([bias_ada, bias_q, bias_v, bias_proj, bias_fc1, bias_fc2])
    grad_bias = jnp.sum(
        lax.all_to_all(term_bias.reshape(dp * seq, -1), ("dp", "seq"), 0, 0, tiled=True), axis=0
    )
    next_first = BETA_FIRST * bias_first + (1.0 - BETA_FIRST) * grad_bias
    next_second = BETA_SECOND * bias_second + (1.0 - BETA_SECOND) * grad_bias * grad_bias
    first_hat = next_first / (1.0 - BETA_FIRST**STEP_COUNT)
    second_hat = next_second / (1.0 - BETA_SECOND**STEP_COUNT)
    new_biases = biases * (1.0 - ADAM_RATE * ADAM_DECAY) - ADAM_RATE * first_hat / (
        jnp.sqrt(second_hat) + ADAM_EPS
    )

    shards = (shard_qkv, shard_proj, shard_fc1, shard_fc2, shard_ada)
    moments = [MUON_DECAY * momentum + shard for momentum, shard in zip(momenta, shards)]
    grams = [gram_of(moment) for moment in moments]
    directions = [None] * 5
    for group in ((3, 2, 1), (0, 4)):
        stack = jnp.concatenate([grams[i] for i in group], axis=0)
        blocks = stack.shape[0]
        each = -(-blocks // dp)
        stack = jnp.pad(stack, ((0, each * dp - blocks), (0, 0), (0, 0)))
        mine = net.scatter_dp(stack.reshape(dp, each, ROW_BLOCK, ROW_BLOCK))
        factors = net.gather_dp(polynomial(mine)).reshape(dp * each, ROW_BLOCK, ROW_BLOCK)
        start = 0
        for i in group:
            size = grams[i].shape[0]
            block = moments[i].reshape(size, ROW_BLOCK, -1)
            direction = jnp.einsum("nrs,nsc->nrc", factors[start : start + size], block, precision=PRECISE)
            directions[i] = direction.reshape(moments[i].shape)
            start += size
    rates = (math.sqrt(3.0), 1.0, math.sqrt(hidden / width), math.sqrt(width / hidden), math.sqrt(6.0))
    new_weights = [
        weight * (1.0 - WEIGHT_SHRINK) - rate * direction
        for weight, rate, direction in zip(masters, rates, directions)
    ]
    return (
        result.reshape(tokens.shape),
        grad_inputs.astype(BF).reshape(tokens.shape),
        grad_cond.reshape(conditioning.shape),
        *new_weights,
        *moments,
        new_biases,
        next_first,
        next_second,
    )


def solution(mesh):
    rows = P(None, "dp", "seq", None)
    matrix = P("seq", "dp")
    flat = P(("dp", "seq"))
    in_specs = (rows, P(None, "dp", None), P(None, "dp"), P(None, "dp"), rows) + (matrix,) * 10 + (flat,) * 3
    out_specs = (rows, rows, P(None, "dp", None)) + (matrix,) * 10 + (flat,) * 3
    return jax.shard_map(
        functools.partial(body, Net(mesh)), mesh=mesh, in_specs=in_specs, out_specs=out_specs, check_vma=False
    )
```

time: 3210 us -> 2300 us (0.72)
  waiting for transfers between devices: 2250 us -> 363 us
  Pallas kernels: 0 us -> 973 us
  starting transfers between devices: 3.81 us -> 193 us
  matrix products: 561 us -> 447 us
  blocking collectives: 126 us -> 16.6 us
  other arithmetic: 111 us -> 148 us
    pallas_call x0 -> x4, Pallas kernels: none -> 973 us  [place(): pl.pallas_call(functools.partial(place_kernel, moves, len(sources)), out_...]
    reduce_scatter x16 -> x0, waiting for transfers between devices: 827 us -> none  [the longest x2 246 us: reduce_terms(): lax.psum_scatter(term_fc1.astype(jnp.bfloat16), 'dp', scatter_dimension=1...]
    all_gather x14 -> x0, waiting for transfers between devices: 772 us -> none  [the longest x1 138 us: gather_weights(): lax.all_gather(part_ada, 'seq', axis=0, tiled=True)]
    psum x5 -> x0, waiting for transfers between devices: 412 us -> none  [gram_sums(): lax.psum(gram_qkv.astype(jnp.bfloat16), 'dp').astype(jnp.float32)]
    ppermute x0 -> x150, waiting for transfers between devices: none -> 360 us  [send(): return lax.ppermute(value, self.name, pairs)]
    unnamed x47 -> x0, waiting for transfers between devices: 234 us -> none
    ppermute x0 -> x150, starting transfers between devices: none -> 149 us  [send(): return lax.ppermute(value, self.name, pairs)]
    dot_general x115 -> x75, matrix products: 561 us -> 447 us  [the longest x5 81.7 us: dot(): return jnp.einsum('srn,nk->srk', left, right, preferred_element_type=F32)]
  transfers between devices with their start and end apart: 41 -> 155, of which waited for: 38 -> 63; matrix products, arithmetic and copies ran while one was open for 16% -> 18% of each run, Pallas kernels for 0% -> 28%
where the time goes in v1:
time: 2300 us; the launch traced here: 2290 us
  Pallas kernels  973 us (42%)
  matrix products  447 us (19%)
  waiting for transfers between devices  363 us (16%)
  starting transfers between devices  193 us (8%)
  other arithmetic  148 us (6%)
  local copies, waits for them, and re-layouts  141 us (6%)
    pallas_call x4, Pallas kernels, place(): pl.pallas_call(functools.partial(place_kernel, moves, len(sources)), out_...  973 us
    ppermute x150, waiting for transfers between devices, send(): return lax.ppermute(value, self.name, pairs)  360 us
    ppermute x150, starting transfers between devices, send(): return lax.ppermute(value, self.name, pairs)  149 us
    dot_general x5, matrix products, dot(): return jnp.einsum('srn,nk->srk', left, right, preferred_element_type=F32)  81.7 us
    dot_general x6, matrix products, dot_t(): return jnp.einsum('srk,nk->srn', left, right, preferred_element_type=F32)  76.9 us
    dot_general x5, matrix products, outer(): jnp.einsum('srn,srk->nk', left, right, preferred_element_type=F32)  67.5 us
  transfers between devices with their start and end apart: 155, of which 63 were waited for; matrix products, arithmetic and copies ran while one was open for 18% of the time, Pallas kernels for 28%

profile of v1, /device:TPU:11, one launch (start us, length us, event | category | flops | bytes accessed | tf_op | source)
XLA Modules:
  0.0 2285.6 jit_solution(4912911559822627389)
XLA Ops:
  173.1 34.3 %collective-permute-done.17.refs_7_ = bf16[1,15,8,1152]{3,2,1,0:T(8,128)(2,1)S(1)} collective-permute-done((bf16[1,15,8,1152]{3,2,1,0:T(8,128)(2,1)S(1)}, bf16[1,15,8,1152]{3,2,1,0:T(8,128)(2,1)S(1)}, u32[]{:S(2)}, u32[]{:S(2)}) %collective-permute-start.17) | collective-permute-done | bytes 276512 | tf_op jit(solution)/shard_map/ppermute | solution.py:46
  253.3 82.5 %place.5 = bf16[4,2,2,9,8,1152]{5,4,3,2,1,0:T(8,128)(2,1)} custom-call(s32[3]{0:T(128)} %pad_add_fusion.1.refs_0_, bf16[4,4,8,1152]{3,2,1,0:T(8,128)(2,1)} %copy-done.79, bf16[4,4,8,1152]{3,2,1,0:T(8,128)(2,1)} %copy-done.117, bf16[2,5,8,1152]{3,2,1,0:T(8,128)(2,1)} %copy-done.87, bf16[2,5,8,1152]{3,2,1,0:T(8,128)(2,1)} %copy-done.103, ...), custom_call_target="tpu_custom_call" | custom-call | bytes 5308416 | tf_op jit(solution)/shard_map/place/pallas_call | solution.py:112
  344.7 243.3 %place.4 = bf16[4,2,2,27,8,1152]{5,4,3,2,1,0:T(8,128)(2,1)} custom-call(s32[3]{0:T(128)} %pad_add_fusion.1.refs_0_, bf16[4,12,8,1152]{3,2,1,0:T(8,128)(2,1)} %copy-done.43, bf16[4,12,8,1152]{3,2,1,0:T(8,128)(2,1)} %collective-permute-done.12.refs_2_, bf16[2,15,8,1152]{3,2,1,0:T(8,128)(2,1)} %copy-done.64, ...), custom_call_target="tpu_custom_call" | custom-call | bytes 15925248 | tf_op jit(solution)/shard_map/place/pallas_call | solution.py:112
  647.8 16.0 fusion.16
  663.8 15.3 fusion.2
  679.2 16.5 fusion.188
  727.0 16.9 fusion.189
  762.1 323.7 %place.6 = bf16[4,2,2,36,8,1152]{5,4,3,2,1,0:T(8,128)(2,1)} custom-call(s32[3]{0:T(128)} %pad_add_fusion.1.refs_0_, bf16[4,16,8,1152]{3,2,1,0:T(8,128)(2,1)} %pad_maximum_fusion.6.refs_1_, bf16[4,16,8,1152]{3,2,1,0:T(8,128)(2,1)} %collective-permute-done.48.refs_2_, bf16[2,20,8,1152]{3,2,1,0:T(8,128)(2,1)} %copy-done.51, ...), custom_call_target="tpu_custom_call" | custom-call | bytes 21233664 | tf_op jit(solution)/shard_map/place/pallas_call | solution.py:112
  1085.8 21.0 fusion.150
  1108.3 18.9 fusion.6
  1130.2 323.8 %place.7 = bf16[4,2,2,9,8,4608]{5,4,3,2,1,0:T(8,128)(2,1)} custom-call(s32[3]{0:T(128)} %pad_add_fusion.1.refs_0_, bf16[4,4,8,4608]{3,2,1,0:T(8,128)(2,1)} %pad_maximum_fusion.7.refs_1_, bf16[4,4,8,4608]{3,2,1,0:T(8,128)(2,1)} %collective-permute-done.66.refs_2_, bf16[2,5,8,4608]{3,2,1,0:T(8,128)(2,1)} %copy-done.49, bf16[2,5,8,4608]{3,2,1,0:T(8,128)(2,1)} %copy-done.68, ...), custom_call_target="tpu_custom_call" | custom-call | bytes 21233664 | tf_op jit(solution)/shard_map/place/pallas_call | solution.py:112
  1454.1 30.6 %convert_reduce_fusion = (f32[4608]{0:T(1024)}, bf16[2,512,4608]{2,1,0:T(8,128)(2,1)}) fusion(f32[2,512,4608]{2,1,0:T(8,128)} %fusion.150, f32[4608]{0:T(1024)S(1)} %copy-done.141, bf16[1152,4608,1]{1,0,2:T(8,128)(2,1)} %bitcast.798, bf16[2,1,512,1152]{3,2,1,0:T(8,128)(2,1)} %param.22, f32[2,1152]{1,0:T(2,128)S(1)} %copy-done.149), kind=kOutput, calls=%fused_computation.27 | convolution fusion | flops 10983698432 | bytes 41333760 | tf_op jit(solution)/shard_map/srn,nk->srk/dot_general | solution.py:277
  1484.6 18.2 multiply_reduce_fusion
  1502.9 19.3 fusion.7
  1522.3 26.1 %convert_reduce_fusion.3 = (f32[1152]{0:T(1024)}, f32[2,1152]{1,0:T(2,128)}, bf16[2,1,512,1152]{3,2,1,0:T(8,128)(2,1)}, f32[1152]{0:T(1024)}, bf16[2,512,1152]{2,1,0:T(8,128)(2,1)}, /*index=5*/f32[2,512,1152]{2,1,0:T(8,128)}) fusion(bf16[2,1,512,1152]{3,2,1,0:T(8,128)(2,1)} %param.22, f32[2,1152]{1,0:T(2,128)S(1)} %copy-done.149, ...), kind=kOutput, calls=%fused_computation.83 | convolution fusion | flops 10945949696 | bytes 50810368 | tf_op jit(solution)/shard_map/srk,nk->srn/dot_general | solution.py:273
  1563.0 15.5 fusion.63
  1578.5 22.0 multiply_convert_fusion
  1626.3 15.5 fusion.60
  1641.9 21.8 multiply_convert_fusion.1
  1700.3 18.1 fusion.29
  1718.4 17.5 fusion.41
  1990.7 19.5 collective-permute-done.121
  2014.1 27.7 %collective-permute-done.109 = bf16[2,5,8,4608]{3,2,1,0:T(8,128)(2,1)S(1)} collective-permute-done((bf16[2,5,8,4608]{3,2,1,0:T(8,128)(2,1)S(1)}, bf16[2,5,8,4608]{3,2,1,0:T(8,128)(2,1)S(1)}, u32[]{:S(2)}, u32[]{:S(2)}) %collective-permute-start.109) | collective-permute-done | bytes 737312 | tf_op jit(solution)/shard_map/ppermute | solution.py:46
  2218.2 22.8 collective-permute-done.148
  (1015 shorter events, 893.8 us)
Async XLA Ops:
  172.1 416.3 %collective-permute-start.6 = (bf16[2,512,1152]{2,1,0:T(8,128)(2,1)S(1)}, bf16[2,512,1152]{2,1,0:T(8,128)(2,1)}, u32[]{:S(2)}, u32[]{:S(2)}) collective-permute-start(bf16[2,512,1152]{2,1,0:T(8,128)(2,1)S(1)} %bitcast.770), channel_id=1, source_target_pairs={{0,1},{1,0},{2,3},{3,2},{4,5},{5,4},{6,7},{7,6},{8,9},{9,8},{10,11... | collective-permute-start | bytes 7077896 | tf_op jit(solution)/shard_map/ppermute | solution.py:46
  231.7 356.3 %collective-permute-start.48 = (bf16[4,16,8,1152]{3,2,1,0:T(8,128)(2,1)}, bf16[4,16,8,1152]{3,2,1,0:T(8,128)(2,1)}, u32[]{:S(2)}, u32[]{:S(2)}) collective-permute-start(bf16[4,16,8,1152]{3,2,1,0:T(8,128)(2,1)} %pad_maximum_fusion.6.refs_1_), channel_id=1, source_target_pairs={{0,4},{2,6},{4,0},{6,2},{8,12},{10,14},{12,8},{14,10},{16,20},{18,... | collective-permute-start | bytes 3538952 | tf_op jit(solution)/shard_map/ppermute | solution.py:46
  248.6 94.8 %collective-permute-start.19 = (bf16[4,12,8,1152]{3,2,1,0:T(8,128)(2,1)}, bf16[4,12,8,1152]{3,2,1,0:T(8,128)(2,1)}, u32[]{:S(2)}, u32[]{:S(2)}) collective-permute-start(bf16[4,12,8,1152]{3,2,1,0:T(8,128)(2,1)} %collective-permute-done.12.refs_2_), channel_id=1, source_target_pairs={{0,2},{2,0},{4,6},{6,4},{8,10},{10,8},{12,14},{14,12},{16,18},{18,... | collective-permute-start | bytes 2654216 | tf_op jit(solution)/shard_map/ppermute | solution.py:46
  250.8 92.1 %collective-permute-start.21 = (bf16[2,15,8,1152]{3,2,1,0:T(8,128)(2,1)}, bf16[2,15,8,1152]{3,2,1,0:T(8,128)(2,1)}, u32[]{:S(2)}, u32[]{:S(2)}) collective-permute-start(bf16[2,15,8,1152]{3,2,1,0:T(8,128)(2,1)} %collective-permute-done.14.refs_4_), channel_id=1, source_target_pairs={{0,2},{2,0},{4,6},{6,4},{8,10},{10,8},{12,14},{14,12},{16,18},{18,... | collective-permute-start | bytes 1658888 | tf_op jit(solution)/shard_map/ppermute | solution.py:46
  251.2 91.6 %collective-permute-start.23 = (bf16[1,15,8,1152]{3,2,1,0:T(8,128)(2,1)}, bf16[1,15,8,1152]{3,2,1,0:T(8,128)(2,1)}, u32[]{:S(2)}, u32[]{:S(2)}) collective-permute-start(bf16[1,15,8,1152]{3,2,1,0:T(8,128)(2,1)} %collective-permute-done.16.refs_6_), channel_id=1, source_target_pairs={{0,2},{2,0},{4,6},{6,4},{8,10},{10,8},{12,14},{14,12},{16,18},{18,... | collective-permute-start | bytes 829448 | tf_op jit(solution)/shard_map/ppermute | solution.py:46
  342.8 412.7 %collective-permute-start.56 = (bf16[2,20,8,1152]{3,2,1,0:T(8,128)(2,1)}, bf16[2,20,8,1152]{3,2,1,0:T(8,128)(2,1)}, u32[]{:S(2)}, u32[]{:S(2)}) collective-permute-start(bf16[2,20,8,1152]{3,2,1,0:T(8,128)(2,1)} %copy-done.51), channel_id=1, source_target_pairs={{0,2},{2,0},{4,6},{6,4},{8,10},{10,8},{12,14},{14,12},{16,18},{18,... | collective-permute-start | bytes 2211848 | tf_op jit(solution)/shard_map/ppermute | solution.py:46
  343.0 413.9 %collective-permute-start.54 = (bf16[4,16,8,1152]{3,2,1,0:T(8,128)(2,1)}, bf16[4,16,8,1152]{3,2,1,0:T(8,128)(2,1)}, u32[]{:S(2)}, u32[]{:S(2)}) collective-permute-start(bf16[4,16,8,1152]{3,2,1,0:T(8,128)(2,1)} %pad_maximum_fusion.6.refs_1_), channel_id=1, source_target_pairs={{0,2},{2,0},{4,6},{6,4},{8,10},{10,8},{12,14},{14,12},{16,18},{18,... | collective-permute-start | bytes 3538952 | tf_op jit(solution)/shard_map/ppermute | solution.py:46
  343.3 412.3 %collective-permute-start.53 = (bf16[1,20,8,1152]{3,2,1,0:T(8,128)(2,1)}, bf16[1,20,8,1152]{3,2,1,0:T(8,128)(2,1)}, u32[]{:S(2)}, u32[]{:S(2)}) collective-permute-start(bf16[1,20,8,1152]{3,2,1,0:T(8,128)(2,1)} %slice.745), channel_id=1, source_target_pairs={{0,24},{2,26},{4,28},{6,30},{8,0},{10,2},{12,4},{14,6},{16,8},{18,... | collective-permute-start | bytes 1105928 | tf_op jit(solution)/shard_map/ppermute | solution.py:46
  588.0 168.7 %collective-permute-start.52 = (bf16[1,20,8,1152]{3,2,1,0:T(8,128)(2,1)}, bf16[1,20,8,1152]{3,2,1,0:T(8,128)(2,1)}, u32[]{:S(2)}, u32[]{:S(2)}) collective-permute-start(bf16[1,20,8,1152]{3,2,1,0:T(8,128)(2,1)} %slice.744), channel_id=1, source_target_pairs={{0,8},{2,10},{4,12},{6,14},{8,16},{10,18},{12,20},{14,22},{16,24},... | collective-permute-start | bytes 1105928 | tf_op jit(solution)/shard_map/ppermute | solution.py:46
  588.4 173.6 %collective-permute-start.55 = (bf16[4,16,8,1152]{3,2,1,0:T(8,128)(2,1)}, bf16[4,16,8,1152]{3,2,1,0:T(8,128)(2,1)}, u32[]{:S(2)}, u32[]{:S(2)}) collective-permute-start(bf16[4,16,8,1152]{3,2,1,0:T(8,128)(2,1)} %collective-permute-done.48.refs_2_), channel_id=1, source_target_pairs={{0,2},{2,0},{4,6},{6,4},{8,10},{10,8},{12,14},{14,12},{16,18},{18,... | collective-permute-start | bytes 3538952 | tf_op jit(solution)/shard_map/ppermute | solution.py:46
  759.6 347.2 %collective-permute-start.74 = (bf16[2,5,8,4608]{3,2,1,0:T(8,128)(2,1)S(1)}, bf16[2,5,8,4608]{3,2,1,0:T(8,128)(2,1)}, u32[]{:S(2)}, u32[]{:S(2)}) collective-permute-start(bf16[2,5,8,4608]{3,2,1,0:T(8,128)(2,1)S(1)} %copy-done.50), channel_id=1, source_target_pairs={{0,2},{2,0},{4,6},{6,4},{8,10},{10,8},{12,14},{14,12},{16,18},{18,... | collective-permute-start | bytes 2211848 | tf_op jit(solution)/shard_map/ppermute | solution.py:46
  759.7 348.1 %collective-permute-start.72 = (bf16[4,4,8,4608]{3,2,1,0:T(8,128)(2,1)S(1)}, bf16[4,4,8,4608]{3,2,1,0:T(8,128)(2,1)}, u32[]{:S(2)}, u32[]{:S(2)}) collective-permute-start(bf16[4,4,8,4608]{3,2,1,0:T(8,128)(2,1)S(1)} %copy-done.31), channel_id=1, source_target_pairs={{0,2},{2,0},{4,6},{6,4},{8,10},{10,8},{12,14},{14,12},{16,18},{18,... | collective-permute-start | bytes 3538952 | tf_op jit(solution)/shard_map/ppermute | solution.py:46
  760.2 347.7 %collective-permute-start.66 = (bf16[4,4,8,4608]{3,2,1,0:T(8,128)(2,1)S(1)}, bf16[4,4,8,4608]{3,2,1,0:T(8,128)(2,1)}, u32[]{:S(2)}, u32[]{:S(2)}) collective-permute-start(bf16[4,4,8,4608]{3,2,1,0:T(8,128)(2,1)S(1)} %copy-done.31), channel_id=1, source_target_pairs={{0,4},{2,6},{4,0},{6,2},{8,12},{10,14},{12,8},{14,10},{16,20},{18,... | collective-permute-start | bytes 3538952 | tf_op jit(solution)/shard_map/ppermute | solution.py:46
  760.3 347.0 %collective-permute-start.71 = (bf16[1,5,8,4608]{3,2,1,0:T(8,128)(2,1)}, bf16[1,5,8,4608]{3,2,1,0:T(8,128)(2,1)}, u32[]{:S(2)}, u32[]{:S(2)}) collective-permute-start(bf16[1,5,8,4608]{3,2,1,0:T(8,128)(2,1)} %slice.752), channel_id=1, source_target_pairs={{0,24},{2,26},{4,28},{6,30},{8,0},{10,2},{12,4},{14,6},{16,8},{18,... | collective-permute-start | bytes 1105928 | tf_op jit(solution)/shard_map/ppermute | solution.py:46
  762.0 345.4 %collective-permute-start.70 = (bf16[1,5,8,4608]{3,2,1,0:T(8,128)(2,1)}, bf16[1,5,8,4608]{3,2,1,0:T(8,128)(2,1)}, u32[]{:S(2)}, u32[]{:S(2)}) collective-permute-start(bf16[1,5,8,4608]{3,2,1,0:T(8,128)(2,1)} %slice.751), channel_id=1, source_target_pairs={{0,8},{2,10},{4,12},{6,14},{8,16},{10,18},{12,20},{14,22},{16,24},... | collective-permute-start | bytes 1105928 | tf_op jit(solution)/shard_map/ppermute | solution.py:46
  1745.2 73.4 %collective-permute-start.79 = (bf16[2,512,1152]{2,1,0:T(8,128)(2,1)}, bf16[2,512,1152]{2,1,0:T(8,128)(2,1)}, u32[]{:S(2)}, u32[]{:S(2)}) collective-permute-start(bf16[2,512,1152]{2,1,0:T(8,128)(2,1)} %slice.815), channel_id=1, source_target_pairs={{0,1},{1,0},{2,3},{3,2},{4,5},{5,4},{6,7},{7,6},{8,9},{9,8},{10,11... | collective-permute-start | bytes 7077896 | tf_op jit(solution)/shard_map/ppermute | solution.py:46
  1763.5 90.7 %collective-permute-start.80 = (bf16[4,2,27,8,1152]{4,3,2,1,0:T(8,128)(2,1)}, bf16[4,2,27,8,1152]{4,3,2,1,0:T(8,128)(2,1)}, u32[]{:S(2)}, u32[]{:S(2)}) collective-permute-start(bf16[4,2,27,8,1152]{4,3,2,1,0:T(8,128)(2,1)} %dynamic-slice_bitcast_fusion.2), channel_id=1, source_target_pairs={{0,2},{2,0},{4,6},{6,4},{8,10},{10,8},{12,14},{14,12},{16,18},{18,... | collective-permute-start | bytes 11943944 | tf_op jit(solution)/shard_map/ppermute | solution.py:46
  1779.7 149.3 %collective-permute-start.114 = (bf16[4,2,36,8,1152]{4,3,2,1,0:T(8,128)(2,1)}, bf16[4,2,36,8,1152]{4,3,2,1,0:T(8,128)(2,1)}, u32[]{:S(2)}, u32[]{:S(2)}) collective-permute-start(bf16[4,2,36,8,1152]{4,3,2,1,0:T(8,128)(2,1)} %dynamic-slice_bitcast_fusion), channel_id=1, source_target_pairs={{0,2},{2,0},{4,6},{6,4},{8,10},{10,8},{12,14},{14,12},{16,18},{18,... | collective-permute-start | bytes 15925256 | tf_op jit(solution)/shard_map/ppermute | solution.py:46
  1806.1 130.6 %collective-permute-start.102 = (bf16[4,2,9,8,4608]{4,3,2,1,0:T(8,128)(2,1)}, bf16[4,2,9,8,4608]{4,3,2,1,0:T(8,128)(2,1)}, u32[]{:S(2)}, u32[]{:S(2)}) collective-permute-start(bf16[4,2,9,8,4608]{4,3,2,1,0:T(8,128)(2,1)} %dynamic-slice_bitcast_fusion.1), channel_id=1, source_target_pairs={{0,2},{2,0},{4,6},{6,4},{8,10},{10,8},{12,14},{14,12},{16,18},{18,... | collective-permute-start | bytes 15925256 | tf_op jit(solution)/shard_map/ppermute | solution.py:46
  1863.9 263.8 %all-to-all-start.4 = ((f32[32,1,504]{2,1,0:T(1,128)}), f32[32,1,504]{2,1,0:T(1,128)}, u32[]{:S(2)}, u32[]{:S(2)}) async-start(f32[32,1,504]{2,1,0:T(1,128)} %all_to_all.23), calls=%async_computation.4 | async-start | bytes 131072 | tf_op jit(solution)/shard_map/all_to_all | solution.py:459
  1943.7 102.0 %collective-permute-start.115 = (bf16[4,16,8,1152]{3,2,1,0:T(8,128)(2,1)}, bf16[4,16,8,1152]{3,2,1,0:T(8,128)(2,1)}, u32[]{:S(2)}, u32[]{:S(2)}) collective-permute-start(bf16[4,16,8,1152]{3,2,1,0:T(8,128)(2,1)} %dynamic-slice_bitcast_fusion.6), channel_id=1, source_target_pairs={{0,4},{2,6},{4,0},{6,2},{8,12},{10,14},{12,8},{14,10},{16,20},{18,... | collective-permute-start | bytes 3538952 | tf_op jit(solution)/shard_map/ppermute | solution.py:46
  1950.7 97.3 %collective-permute-start.103 = (bf16[4,4,8,4608]{3,2,1,0:T(8,128)(2,1)}, bf16[4,4,8,4608]{3,2,1,0:T(8,128)(2,1)}, u32[]{:S(2)}, u32[]{:S(2)}) collective-permute-start(bf16[4,4,8,4608]{3,2,1,0:T(8,128)(2,1)} %dynamic-slice_bitcast_fusion.7), channel_id=1, source_target_pairs={{0,4},{2,6},{4,0},{6,2},{8,12},{10,14},{12,8},{14,10},{16,20},{18,... | collective-permute-start | bytes 3538952 | tf_op jit(solution)/shard_map/ppermute | solution.py:46
  2014.1 62.1 %collective-permute-start.124 = (bf16[20,8,1152]{2,1,0:T(8,128)(2,1)}, bf16[20,8,1152]{2,1,0:T(8,128)(2,1)}, u32[]{:S(2)}, u32[]{:S(2)}) collective-permute-start(bf16[20,8,1152]{2,1,0:T(8,128)(2,1)} %dynamic-slice_bitcast_fusion.23), channel_id=1, source_target_pairs={{0,4},{2,6},{4,0},{6,2},{8,12},{10,14},{12,8},{14,10},{16,20},{18,... | collective-permute-start | bytes 1105928 | tf_op jit(solution)/shard_map/ppermute | solution.py:46
  2127.7 61.2 %all-to-all-start.3 = ((f32[16,2,576]{2,1,0:T(2,128)}), f32[16,2,576]{2,1,0:T(2,128)}, u32[]{:S(2)}, u32[]{:S(2)}) async-start(f32[16,2,576]{2,1,0:T(2,128)} %copy.416), calls=%async_computation.3 | async-start | bytes 163840 | tf_op jit(solution)/shard_map/all_to_all | solution.py:452
  (310 other events, 7466.1 us)

commit v2 on v1

v2 whole, which is shorter than its diff:
```python
import functools
import math

import jax
import jax.numpy as jnp
from jax import lax
from jax.experimental import pallas as pl
from jax.experimental.pallas import tpu as pltpu
from jax.sharding import PartitionSpec as P

HEADS = 16
ROW_BLOCK = 144
NS_STEPS = 5
STEP_COUNT = 10

PRECISE = lax.Precision.HIGHEST
LN_EPS = 1e-06
MASKED = -1e30
NS_A = 3.4445
NS_B = -4.775
NS_C = 2.0315
MUON_DECAY = 0.5
WEIGHT_SHRINK = 0.0001
NORM_EPS = 1e-07
BETA_FIRST = 0.9
BETA_SECOND = 0.999
ADAM_RATE = 0.1
ADAM_DECAY = 0.01
ADAM_EPS = 1e-08
BF = jnp.bfloat16
F32 = jnp.float32
VMEM_LIMIT = 60 * 2**20


class Ring:
    def __init__(self, name, total, stride, size):
        self.name, self.total, self.stride, self.size = name, total, stride, size

    def digit(self):
        return (lax.axis_index(self.name) // self.stride) % self.size

    def send(self, value, shift):
        pairs = []
        for i in range(self.total):
            d = (i // self.stride) % self.size
            pairs.append((i, i + ((d + shift) % self.size - d) * self.stride))
        return lax.ppermute(value, self.name, pairs)

    def gather(self, value, far=1):
        n = self.size
        blocks = [value] + [None] * (n - 1)
        if n == 2:
            blocks[1] = self.send(value, 1)
        elif n > 2:
            low = high = value
            for t in range(1, n // 2):
                low, high = self.send(low, 1), self.send(high, -1)
                blocks[n - t], blocks[t] = low, high
            blocks[n // 2] = self.send(low, 1) if far == 1 else self.send(high, -1)
        return blocks

    def scatter_sum(self, block_of, far=1):
        n = self.size
        own = block_of(0).astype(F32)
        if n == 1:
            return own
        if n == 2:
            return own + self.send(block_of(1), 1).astype(F32)
        low = high = None
        if far == 1:
            low = self.send(block_of(n // 2), 1)
        else:
            high = self.send(block_of(n // 2), -1)
        for t in range(n // 2 - 1, 0, -1):
            up, down = block_of(t), block_of(n - t)
            if low is not None:
                up = (up.astype(F32) + low.astype(F32)).astype(up.dtype)
            if high is not None:
                down = (down.astype(F32) + high.astype(F32)).astype(down.dtype)
            low, high = self.send(up, 1), self.send(down, -1)
        return own + low.astype(F32) + high.astype(F32)


def place_kernel(moves, outs, count, parts, *refs):
    spots, sources = refs[0], refs[1 : 1 + count]
    outputs, (full, in_sems, out_sems) = refs[1 + count : 1 + count + parts], refs[1 + count + parts :]
    arrivals = []
    for n, (source, index, target) in enumerate(moves):
        arrivals.append(
            pltpu.make_async_copy(sources[source].at[index], full.at[target(spots)], in_sems.at[n])
        )
    for copy in arrivals:
        copy.start()
    for copy in arrivals:
        copy.wait()
    exits = []
    for n, (start, output, target) in enumerate(outs):
        exits.append(pltpu.make_async_copy(full.at[start], outputs[output].at[target], out_sems.at[n]))
    for copy in exits:
        copy.start()
    for copy in exits:
        copy.wait()


def place(spots, sources, moves, shape, outs, shapes):
    moved = math.prod(shape) * 2
    return pl.pallas_call(
        functools.partial(place_kernel, moves, outs, len(sources), len(shapes)),
        out_shape=[jax.ShapeDtypeStruct(each, BF) for each in shapes],
        in_specs=[pl.BlockSpec(memory_space=pltpu.SMEM)]
        + [pl.BlockSpec(memory_space=pl.ANY)] * len(sources),
        out_specs=[pl.BlockSpec(memory_space=pl.ANY)] * len(shapes),
        scratch_shapes=[
            pltpu.VMEM(shape, BF),
            pltpu.SemaphoreType.DMA((len(moves),)),
            pltpu.SemaphoreType.DMA((len(outs),)),
        ],
        compiler_params=pltpu.CompilerParams(vmem_limit_bytes=VMEM_LIMIT),
        cost_estimate=pl.CostEstimate(flops=0, bytes_accessed=2 * moved, transcendentals=0),
        name="place",
    )(spots, *sources)


class Net:
    def __init__(self, mesh):
        dp, seq = mesh.shape["dp"], mesh.shape["seq"]
        self.dp, self.seq = dp, seq
        self.core = Ring("dp", dp, 1, 2)
        self.x = Ring("dp", dp, 2, 2)
        self.z = Ring("dp", dp, 4, dp // 4)
        self.y = Ring("seq", seq, 1, seq)

    def spots(self):
        return jnp.stack([self.z.digit(), self.x.digit(), self.core.digit()]).astype(jnp.int32)


    def rows_joined(self, shards, unit, depth):
        turned = [shard.astype(BF).T for shard in shards]
        wire = jnp.concatenate([t.reshape(-1) for t in turned]) if len(turned) > 1 else turned[0]
        wires = self.y.gather(wire)
        joined = []
        start = 0
        for t in turned:
            if len(turned) > 1:
                blocks = [w[start : start + t.size].reshape(t.shape) for w in wires]
            else:
                blocks = wires
            start += t.size
            if self.seq == 2:
                own, other = blocks
                full = jnp.where(
                    self.y.digit() == 0,
                    jnp.concatenate([own, other], axis=1),
                    jnp.concatenate([other, own], axis=1),
                )
            else:
                order = (jnp.arange(self.seq) - self.y.digit()) % self.seq
                full = jnp.take(jnp.stack(blocks), order, axis=0)
                full = jnp.transpose(full, (1, 0, 2)).reshape(t.shape[0], -1)
            full = full.reshape(t.shape[0] // unit, unit, full.shape[1] // depth, depth)
            joined.append(jnp.transpose(full, (2, 0, 1, 3)).reshape(-1, unit, depth))
        return joined[0] if len(joined) == 1 else jnp.concatenate(joined, axis=0)

    def gather_weights(self, units, layout):
        g, unit, depth = units.shape
        zs = self.z.size
        ga = max(1, (4 * g) // 9)
        first, second = units[:ga], units[ga:]
        line = jnp.stack(self.z.gather(first, 1))
        pair = jnp.stack([second, self.x.send(second, 1)])
        line_x = self.x.send(line, 1)
        pieces = self.z.gather(pair, -1)
        arrived = [line_x] + pieces[1:]
        sources, moves = [], []

        def spot(sz, sx, sc, start, stop):
            def target(spots):
                return (
                    lax.rem(spots[0] + sz, zs),
                    lax.rem(spots[1] + sx, 2),
                    lax.rem(spots[2] + sc, 2),
                    pl.ds(start, stop - start),
                )

            return target

        for sc in range(2):
            for sx, array in ((0, line), (1, line_x)):
                array = array if sc == 0 else self.core.send(array, 1)
                for sz in range(zs):
                    moves.append((len(sources), (sz,), spot(sz, sx, sc, 0, ga)))
                sources.append(array)
            for sz, array in enumerate(pieces):
                array = array if sc == 0 else self.core.send(array, 1)
                for sx in range(2):
                    moves.append((len(sources), (sx,), spot(sz, sx, sc, ga, g)))
                sources.append(array)
        outs, shapes, start = [], [], 0
        for n, (rows, blocks) in enumerate(layout):
            size = rows // unit
            shapes.append((zs, 2, 2, size, unit, blocks * depth))
            for j in range(blocks):
                window = (slice(None),) * 3 + (pl.ds(start, size),)
                target = (slice(None),) * 5 + (pl.ds(j * depth, depth),)
                outs.append((window, n, target))
                start += size
        full = place(self.spots(), sources, moves, (zs, 2, 2, g, unit, depth), outs, shapes)
        return [f.reshape(-1, f.shape[-1]) for f in full], arrived

    def scatter_weights(self, terms, unit, depth, layout):
        zs = self.z.size
        blocks = [term.reshape(zs, 2, 2, -1, unit, depth) for term in terms]
        g = sum(block.shape[3] for block in blocks)
        ga = max(1, (4 * g) // 9)
        core, x, z = self.core.digit(), self.x.digit(), self.z.digit()

        def half_of(s):
            parts = [lax.dynamic_index_in_dim(block, (core + s) % 2, 2, keepdims=False) for block in blocks]
            return parts[0] if len(parts) == 1 else jnp.concatenate(parts, axis=2)

        half = self.core.scatter_sum(half_of).astype(BF)
        first, second = half[:, :, :ga], half[:, :, ga:]
        line = self.x.scatter_sum(
            lambda s: lax.dynamic_index_in_dim(first, (x + s) % 2, 1, keepdims=False)
        ).astype(BF)
        pair = self.z.scatter_sum(
            lambda s: lax.dynamic_index_in_dim(second, (z + s) % zs, 0, keepdims=False), -1
        ).astype(BF)
        first = self.z.scatter_sum(
            lambda s: lax.dynamic_index_in_dim(line, (z + s) % zs, 0, keepdims=False), 1
        )
        second = self.x.scatter_sum(
            lambda s: lax.dynamic_index_in_dim(pair, (x + s) % 2, 0, keepdims=False)
        )
        joined = jnp.concatenate([first, second], axis=0).astype(BF)
        y = self.y.digit()
        wire, start = [], 0
        for rows, count in layout:
            size = rows // unit * count
            full = joined[start : start + size].reshape(count, rows // unit, unit, depth)
            full = jnp.transpose(full, (1, 2, 0, 3)).reshape(rows, count * depth)
            wire.append(full.reshape(rows, self.seq, -1))
            start += size
        own = [lax.dynamic_index_in_dim(w, y, 1, keepdims=False).astype(F32) for w in wire]
        if len(wire) == 1:
            total = [
                self.y.scatter_sum(
                    lambda s: lax.dynamic_index_in_dim(wire[0], (y + s) % self.seq, 1, keepdims=False)
                )
            ]
        else:

            def flat_of(s):
                parts = [lax.dynamic_index_in_dim(w, (y + s) % self.seq, 1, keepdims=False) for w in wire]
                return jnp.concatenate([part.reshape(-1) for part in parts])

            summed = self.y.scatter_sum(flat_of)
            total, start = [], 0
            for part in own:
                total.append(summed[start : start + part.size].reshape(part.shape))
                start += part.size
        return [t.T for t in total]


    def to_all(self, value):
        flat = value.reshape((self.dp * self.seq,) + value.shape[2:])
        return lax.all_to_all(flat, ("dp", "seq"), 0, 0, tiled=True).reshape(value.shape)

    def to_dp(self, value):
        return lax.all_to_all(value, "dp", 0, 0, tiled=True)


def after(value, *earlier):
    return lax.optimization_barrier((value,) + earlier)[0]


def layer_norm(values):
    centered = values - jnp.mean(values, axis=-1, keepdims=True)
    inverse = lax.rsqrt(jnp.mean(centered * centered, axis=-1, keepdims=True) + LN_EPS)
    return (centered * inverse, inverse)


def norm_back(normed, inverse, grad):
    mean_grad = jnp.mean(grad, axis=-1, keepdims=True)
    mean_cross = jnp.mean(grad * normed, axis=-1, keepdims=True)
    return inverse * (grad - mean_grad - normed * mean_cross)


def sigmoid_linear(values):
    return values * jax.nn.sigmoid(values)


def gelu_tanh(values):
    return jax.nn.gelu(values, approximate=True)


def dot_t(left, right):
    return jnp.einsum("srk,nk->srn", left, right, preferred_element_type=F32)


def dot(left, right):
    return jnp.einsum("srn,nk->srk", left, right, preferred_element_type=F32)


def outer(left, right):
    return jnp.einsum("srn,srk->nk", left, right, preferred_element_type=F32).astype(BF)


LANES = 128
LOG2E = math.log2(math.e)


def padded(block, column=None):
    rows, depth = block.shape
    if column is None:
        return jnp.concatenate([block, jnp.zeros((rows, LANES - depth), block.dtype)], axis=1)
    rest = jnp.zeros((rows, LANES - depth - 1), block.dtype)
    return jnp.concatenate([block, column.astype(block.dtype), rest], axis=1)


def mask_column(lengths_ref, offsets_ref, sample, total, rows):
    place = lax.broadcasted_iota(jnp.int32, (total, 1), 0)
    position = place
    for s in range(total // rows):
        position = jnp.where(place // rows == s, place - s * rows + offsets_ref[s], position)
    return jnp.where(position < lengths_ref[sample], 0.0, MASKED)


def nt(left, right):
    return lax.dot_general(left, right, (((1,), (1,)), ((), ())), preferred_element_type=F32)


def nn(left, right):
    return jnp.dot(left, right, preferred_element_type=F32)


def attend_kernel(heads, chunk, lengths_ref, offsets_ref, q_ref, k_ref, v_ref, o_ref, lse_ref, q_s, k_s, vt_s, o_s):
    rows, width = q_ref.shape[1:]
    total = k_ref.shape[1]
    depth = width // heads
    factor = depth**-0.5 * LOG2E
    mask = mask_column(lengths_ref, offsets_ref, pl.program_id(0), total, rows)
    ones = jnp.ones((rows, 1), F32)
    for h in range(heads):
        span = slice(h * depth, (h + 1) * depth)
        q_s[h] = padded(q_ref[0, :, span], ones)
        k_s[h] = padded(k_ref[0, :, span], mask)
        vt_s[h] = jnp.transpose(v_ref[0, :, span])

    def one_head(h, carry):
        peak = jnp.full((1, rows), MASKED, F32)
        sums = jnp.zeros((1, rows), F32)
        mixed = jnp.zeros((depth, rows), F32)
        for c in range(total // chunk):
            part = slice(c * chunk, (c + 1) * chunk)
            scores = nt(k_s[h, part], q_s[h])
            higher = jnp.maximum(peak, jnp.max(scores, axis=0, keepdims=True))
            weights = jnp.exp2((scores - higher) * factor)
            if c == 0:
                sums = jnp.sum(weights, axis=0, keepdims=True)
                mixed = nn(vt_s[h, :, part], weights.astype(BF))
            else:
                shrink = jnp.exp2((peak - higher) * factor)
                sums = sums * shrink + jnp.sum(weights, axis=0, keepdims=True)
                mixed = mixed * shrink + nn(vt_s[h, :, part], weights.astype(BF))
            peak = higher
        o_s[h] = jnp.transpose(mixed / sums)
        lse_ref[0, h] = peak * factor + jnp.log2(sums)
        return carry

    lax.fori_loop(0, heads, one_head, 0)
    for h in range(heads):
        o_ref[0, :, h * depth : (h + 1) * depth] = o_s[h].astype(BF)


def attend(lengths, offsets, queries, keys, values, heads, tile):
    count, rows, width = queries.shape
    total = keys.shape[1]
    depth = width // heads
    tile = min(tile, total)
    pick = lambda i, *_: (i, 0, 0)
    return pl.pallas_call(
        functools.partial(attend_kernel, heads, tile),
        grid_spec=pltpu.PrefetchScalarGridSpec(
            num_scalar_prefetch=2,
            grid=(count,),
            in_specs=[
                pl.BlockSpec((1, rows, width), pick),
                pl.BlockSpec((1, total, width), pick),
                pl.BlockSpec((1, total, width), pick),
            ],
            out_specs=[
                pl.BlockSpec((1, rows, width), pick),
                pl.BlockSpec((1, heads, 1, rows), lambda i, *_: (i, 0, 0, 0)),
            ],
            scratch_shapes=[
                pltpu.VMEM((heads, rows, LANES), BF),
                pltpu.VMEM((heads, total, LANES), BF),
                pltpu.VMEM((heads, depth, total), BF),
                pltpu.VMEM((heads, rows, depth), F32),
            ],
        ),
        out_shape=[
            jax.ShapeDtypeStruct((count, rows, width), BF),
            jax.ShapeDtypeStruct((count, heads, 1, rows), F32),
        ],
        compiler_params=pltpu.CompilerParams(vmem_limit_bytes=VMEM_LIMIT),
        cost_estimate=pl.CostEstimate(
            flops=4 * count * heads * rows * total * LANES,
            bytes_accessed=2 * count * width * (2 * rows + 2 * total),
            transcendentals=count * heads * rows * total,
        ),
        name="attend",
    )(lengths, offsets, queries, keys, values)


def attend_back_kernel(
    heads, chunk, lengths_ref, offsets_ref, q_ref, k_ref, v_ref, o_ref, g_ref, lse_ref,
    dq_ref, dk_ref, dv_ref, q_s, k_s, kt_s, v_s, g_s, delta_s, dq_s, dk_s, dv_s
):
    rows, width = q_ref.shape[1:]
    total = k_ref.shape[1]
    depth = width // heads
    scale = depth**-0.5
    factor = scale * LOG2E
    mask = mask_column(lengths_ref, offsets_ref, pl.program_id(0), total, rows)
    ones = jnp.ones((rows, 1), F32)
    cross = jnp.transpose(g_ref[0].astype(F32) * o_ref[0].astype(F32))
    for h in range(heads):
        span = slice(h * depth, (h + 1) * depth)
        delta_s[h] = jnp.sum(cross[span], axis=0, keepdims=True)
        q_s[h] = padded(q_ref[0, :, span], ones)
        k_s[h] = padded(k_ref[0, :, span], mask)
        kt_s[h] = jnp.transpose(k_ref[0, :, span])
        g_s[h] = padded(g_ref[0, :, span])
        v_s[h] = padded(v_ref[0, :, span])

    def one_head(h, carry):
        dq = jnp.zeros((depth, rows), F32)
        for c in range(total // chunk):
            part = slice(c * chunk, (c + 1) * chunk)
            probs = jnp.exp2(nt(k_s[h, part], q_s[h]) * factor - lse_ref[0, h])
            slopes = (probs * (nt(v_s[h, part], g_s[h]) - delta_s[h])).astype(BF)
            dv_s[h, part] = nn(probs.astype(BF), g_s[h]).astype(BF)
            dk_s[h, part] = (nn(slopes, q_s[h]) * scale).astype(BF)
            dq = dq + nn(kt_s[h, :, part], slopes)
        dq_s[h] = jnp.transpose(dq * scale)
        return carry

    lax.fori_loop(0, heads, one_head, 0)
    for h in range(heads):
        span = slice(h * depth, (h + 1) * depth)
        dq_ref[0, :, span] = dq_s[h].astype(BF)
        dk_ref[0, :, span] = dk_s[h][:, :depth]
        dv_ref[0, :, span] = dv_s[h][:, :depth]


def attend_back(lengths, offsets, queries, keys, values, mixed, grads, lse, heads, tile):
    count, rows, width = queries.shape
    total = keys.shape[1]
    depth = width // heads
    tile = min(tile, total)
    pick = lambda i, *_: (i, 0, 0)
    near = pl.BlockSpec((1, rows, width), pick)
    far = pl.BlockSpec((1, total, width), pick)
    return pl.pallas_call(
        functools.partial(attend_back_kernel, heads, tile),
        grid_spec=pltpu.PrefetchScalarGridSpec(
            num_scalar_prefetch=2,
            grid=(count,),
            in_specs=[near, far, far, near, near, pl.BlockSpec((1, heads, 1, rows), lambda i, *_: (i, 0, 0, 0))],
            out_specs=[near, far, far],
            scratch_shapes=[
                pltpu.VMEM((heads, rows, LANES), BF),
                pltpu.VMEM((heads, total, LANES), BF),
                pltpu.VMEM((heads, depth, total), BF),
                pltpu.VMEM((heads, total, LANES), BF),
                pltpu.VMEM((heads, rows, LANES), BF),
                pltpu.VMEM((heads, 1, rows), F32),
                pltpu.VMEM((heads, rows, depth), F32),
                pltpu.VMEM((heads, total, LANES), BF),
                pltpu.VMEM((heads, total, LANES), BF),
            ],
        ),
        out_shape=[
            jax.ShapeDtypeStruct((count, rows, width), BF),
            jax.ShapeDtypeStruct((count, total, width), BF),
            jax.ShapeDtypeStruct((count, total, width), BF),
        ],
        compiler_params=pltpu.CompilerParams(vmem_limit_bytes=VMEM_LIMIT),
        cost_estimate=pl.CostEstimate(
            flops=10 * count * heads * rows * total * LANES,
            bytes_accessed=2 * count * width * (4 * rows + 4 * total),
            transcendentals=count * heads * rows * total,
        ),
        name="attend_back",
    )(lengths, offsets, queries, keys, values, mixed, grads, lse)


def gram_of(moment):
    block = moment.reshape(moment.shape[0] // ROW_BLOCK, ROW_BLOCK, moment.shape[1])
    return jnp.einsum("nrc,nsc->nrs", block, block, precision=PRECISE)


def polynomial(gram):
    eye = jnp.eye(ROW_BLOCK, dtype=F32)
    square = jnp.sum(gram * eye, axis=(1, 2))
    scale = 1.0 / (jnp.sqrt(square) + NORM_EPS)
    current = gram * (scale * scale)[:, None, None]
    mul = functools.partial(jnp.einsum, "nrs,nst->nrt", precision=PRECISE)
    total = None
    for step in range(NS_STEPS):
        factor = NS_A * eye + NS_B * current + NS_C * mul(current, current)
        total = factor if total is None else mul(factor, total)
        if step + 1 < NS_STEPS:
            current = mul(mul(factor, current), factor)
    return total * scale[:, None, None]


def body(net, tokens, conditioning, heights, widths, upstream, *state):
    masters, momenta = state[0:5], state[5:10]
    biases, bias_first, bias_second = state[10:13]
    w_qkv, w_proj, w_fc1, w_fc2, w_ada = masters
    micro, local, rows, width = tokens.shape
    count = micro * local
    head_dim = width // HEADS
    hidden = w_fc1.shape[1] * net.dp
    seq, dp = net.seq, net.dp
    y = net.y.digit()

    bounds = [0, 6 * width, 7 * width, 8 * width, 9 * width, 9 * width + hidden, 10 * width + hidden]

    ada_rows, ada_cols = w_ada.shape
    cond = conditioning.astype(F32).reshape(count, width)
    cond_act, silu_back = jax.vjp(sigmoid_linear, cond)
    cond_low = cond_act.astype(BF)
    cond_rows = lax.dynamic_slice_in_dim(cond_low, y * ada_rows, ada_rows, 1)
    cond_all = net.to_dp(jnp.broadcast_to(cond_rows[None], (dp,) + cond_rows.shape))
    cond_all = cond_all.reshape(dp * count, ada_rows)
    bias_full = net.to_all(jnp.broadcast_to(biases, (dp, seq) + biases.shape)).reshape(-1)
    b_ada, b_q, b_v, b_proj, b_fc1, b_fc2 = [bias_full[bounds[i] : bounds[i + 1]] for i in range(6)]

    n_qkv, n_proj, n_fc1, n_fc2 = [w.shape[1] for w in (w_qkv, w_proj, w_fc1, w_fc2)]
    unit_qkv = math.gcd(n_qkv, 8)
    unit = math.gcd(math.gcd(n_proj, n_fc1), math.gcd(n_fc2, 8))
    fold = hidden // width
    layout_qkv = [(n_qkv, 1)]
    layout = [(n_proj, 1), (n_fc1, 1), (n_fc2, fold)]
    own_tokens = tokens.reshape(count, rows, width)
    units_qkv = net.rows_joined([w_qkv], unit_qkv, width)
    first_tokens = net.y.gather(after(own_tokens[0], units_qkv))
    units = net.rows_joined(
        [after(w, first_tokens[-1]) for w in (w_proj, w_fc1, w_fc2)], unit, width
    )
    other_tokens = [net.y.gather(after(own_tokens[i], units)) for i in range(1, count)]
    all_tokens = jnp.stack([jnp.concatenate(t, axis=0) for t in [first_tokens] + other_tokens])
    (t_qkv,), arrived = net.gather_weights(units_qkv, layout_qkv)
    (t_proj, t_fc1, t_fc2), _ = net.gather_weights(after(units, *arrived), layout)

    low_ada = w_ada.astype(BF)
    partial = jnp.dot(cond_all, low_ada, preferred_element_type=F32).reshape(dp, 1, count, ada_cols)
    received = jnp.sum(net.to_all(jnp.broadcast_to(partial, (dp, seq, count, ada_cols))), axis=1)
    modulation = jnp.transpose(received, (1, 0, 2)).reshape(count, dp * ada_cols) + b_ada
    shift_one, scale_one, gate_one, shift_two, scale_two, gate_two = jnp.split(
        modulation[:, None, :], 6, axis=-1
    )

    lengths = (heights * widths).reshape(count).astype(jnp.int32)
    offsets = jnp.stack([((y + s) % seq) * rows for s in range(seq)]).astype(jnp.int32)
    normed_all, inverse_all, attn_all, queries, keys, values, attended_low, log_total = [[] for _ in range(8)]
    for i in range(count):
        normed, inverse = layer_norm(all_tokens[i].astype(F32))
        attn = (normed * (1.0 + scale_one[i]) + shift_one[i]).astype(BF)
        queries.append((dot_t(attn[None, :rows], t_qkv[:width]) + b_q).astype(BF))
        keys.append(dot_t(attn[None], t_qkv[width : 2 * width]).astype(BF))
        values.append((dot_t(attn[None], t_qkv[2 * width :]) + b_v).astype(BF))
        mixed, lse = attend(lengths[i : i + 1], offsets, queries[i], keys[i], values[i], HEADS, 512)
        normed_all.append(normed[:rows])
        inverse_all.append(inverse[:rows])
        attn_all.append(attn)
        attended_low.append(mixed[0])
        log_total.append(lse)
    attended_low = jnp.stack(attended_low)
    attn_all = jnp.stack(attn_all)
    attn_own = attn_all[:, :rows]
    inputs = own_tokens.astype(F32)
    branch_one = dot_t(attended_low, t_proj) + b_proj
    mixed_one = inputs + gate_one * branch_one
    normed_two, inverse_two = layer_norm(mixed_one)
    ffn_in = (normed_two * (1.0 + scale_two) + shift_two).astype(BF)
    pre_act = dot_t(ffn_in, t_fc1) + b_fc1
    activated, gelu_back = jax.vjp(gelu_tanh, pre_act)
    activated_low = activated.astype(BF)
    branch_two = dot_t(activated_low, t_fc2) + b_fc2
    result = (mixed_one + gate_two * branch_two).astype(BF)

    grad_out = upstream.reshape(count, rows, width).astype(F32)
    grad_branch_two = (gate_two * grad_out).astype(BF)
    grad_gate_two = jnp.sum(branch_two * grad_out, axis=1)
    terms_fc2 = [
        outer(grad_branch_two, activated_low[..., j * width : (j + 1) * width]) for j in range(fold)
    ]
    bias_fc2 = jnp.sum(grad_branch_two.astype(F32), axis=(0, 1))
    grad_pre = gelu_back(dot(grad_branch_two, t_fc2))[0].astype(BF)
    term_fc1 = outer(grad_pre, ffn_in)
    bias_fc1 = jnp.sum(grad_pre.astype(F32), axis=(0, 1))
    grad_ffn_in = dot(grad_pre, t_fc1)
    grad_shift_two = jnp.sum(grad_ffn_in, axis=1)
    grad_scale_two = jnp.sum(grad_ffn_in * normed_two, axis=1)
    grad_mixed = grad_out + norm_back(normed_two, inverse_two, grad_ffn_in * (1.0 + scale_two))
    grad_gate_one = jnp.sum(branch_one * grad_mixed, axis=1)
    grad_branch_one = (gate_one * grad_mixed).astype(BF)
    term_proj = outer(grad_branch_one, attended_low)
    shard_proj, shard_fc1, shard_fc2 = net.scatter_weights([term_proj, term_fc1, *terms_fc2], unit, width, layout)
    bias_proj = jnp.sum(grad_branch_one.astype(F32), axis=(0, 1))
    grad_attended = dot(grad_branch_one, t_proj).astype(BF)

    parts = [
        attend_back(
            lengths[i : i + 1], offsets, queries[i], keys[i], values[i], attended_low[i : i + 1],
            grad_attended[i : i + 1], log_total[i], HEADS, 512,
        )
        for i in range(count)
    ]
    grad_q, grad_k, grad_v = [jnp.concatenate([part[k] for part in parts], axis=0) for k in range(3)]
    term_qkv = jnp.concatenate(
        [outer(grad_q, attn_own), outer(grad_k, attn_all), outer(grad_v, attn_all)], axis=0
    )
    (shard_qkv,) = net.scatter_weights([term_qkv], unit_qkv, width, layout_qkv)
    bias_q = jnp.sum(grad_q.astype(F32), axis=(0, 1))
    bias_v = jnp.sum(grad_v.astype(F32), axis=(0, 1))
    part_in = dot(grad_k, t_qkv[width : 2 * width]) + dot(grad_v, t_qkv[2 * width :])
    own_part = part_in[:, :rows] + dot(grad_q, t_qkv[:width])
    grad_attn_in = net.y.scatter_sum(
        lambda s: own_part if s == 0 else part_in[:, s * rows : (s + 1) * rows].astype(BF)
    )
    normed_one, inverse_one = jnp.stack(normed_all), jnp.stack(inverse_all)
    grad_shift_one = jnp.sum(grad_attn_in, axis=1)
    grad_scale_one = jnp.sum(grad_attn_in * normed_one, axis=1)
    grad_inputs = grad_mixed + norm_back(normed_one, inverse_one, grad_attn_in * (1.0 + scale_one))

    grad_mod_local = jnp.concatenate(
        [grad_shift_one, grad_scale_one, grad_gate_one, grad_shift_two, grad_scale_two, grad_gate_two], axis=-1
    )
    bias_ada = jnp.sum(grad_mod_local, axis=0)
    sent = jnp.transpose(grad_mod_local.reshape(count, dp, 1, ada_cols), (1, 2, 0, 3))
    sent = jnp.broadcast_to(sent, (dp, seq, count, ada_cols))
    mod_cols = jnp.sum(net.to_all(sent), axis=1).astype(BF).reshape(dp * count, ada_cols)
    shard_ada = jnp.einsum("sr,sc->rc", cond_all, mod_cols, preferred_element_type=F32)
    cond_part = jnp.einsum("sc,rc->sr", mod_cols, low_ada, preferred_element_type=F32)
    cond_part = cond_part.reshape(dp, 1, count, ada_rows)
    cond_part = jnp.sum(net.to_all(jnp.broadcast_to(cond_part, (dp, seq, count, ada_rows))), axis=0)
    grad_cond = silu_back(jnp.transpose(cond_part, (1, 0, 2)).reshape(count, width))[0]

    term_bias = jnp.concatenate([bias_ada, bias_q, bias_v, bias_proj, bias_fc1, bias_fc2])
    grad_bias = jnp.sum(net.to_all(term_bias.reshape(dp, seq, -1)), axis=(0, 1))
    next_first = BETA_FIRST * bias_first + (1.0 - BETA_FIRST) * grad_bias
    next_second = BETA_SECOND * bias_second + (1.0 - BETA_SECOND) * grad_bias * grad_bias
    first_hat = next_first / (1.0 - BETA_FIRST**STEP_COUNT)
    second_hat = next_second / (1.0 - BETA_SECOND**STEP_COUNT)
    new_biases = biases * (1.0 - ADAM_RATE * ADAM_DECAY) - ADAM_RATE * first_hat / (
        jnp.sqrt(second_hat) + ADAM_EPS
    )

    shards = (shard_qkv, shard_proj, shard_fc1, shard_fc2, shard_ada)
    moments = [MUON_DECAY * momentum + shard for momentum, shard in zip(momenta, shards)]
    grams = [gram_of(moment) for moment in moments]
    directions = [None] * 5
    for group in ((3, 2, 1), (0, 4)):
        stack = jnp.concatenate([grams[i] for i in group], axis=0)
        blocks = stack.shape[0]
        each = -(-blocks // dp)
        stack = jnp.pad(stack, ((0, each * dp - blocks), (0, 0), (0, 0)))
        mine = jnp.sum(net.to_dp(stack.reshape(dp, each, ROW_BLOCK, ROW_BLOCK)), axis=0)
        factors = jnp.broadcast_to(polynomial(mine)[None], (dp, each, ROW_BLOCK, ROW_BLOCK))
        factors = net.to_dp(factors).reshape(dp * each, ROW_BLOCK, ROW_BLOCK)
        start = 0
        for i in group:
            size = grams[i].shape[0]
            block = moments[i].reshape(size, ROW_BLOCK, -1)
            direction = jnp.einsum("nrs,nsc->nrc", factors[start : start + size], block, precision=PRECISE)
            directions[i] = direction.reshape(moments[i].shape)
            start += size
    rates = (math.sqrt(3.0), 1.0, math.sqrt(hidden / width), math.sqrt(width / hidden), math.sqrt(6.0))
    new_weights = [
        weight * (1.0 - WEIGHT_SHRINK) - rate * direction
        for weight, rate, direction in zip(masters, rates, directions)
    ]
    return (
        result.reshape(tokens.shape),
        grad_inputs.astype(BF).reshape(tokens.shape),
        grad_cond.reshape(conditioning.shape),
        *new_weights,
        *moments,
        new_biases,
        next_first,
        next_second,
    )


def solution(mesh):
    rows = P(None, "dp", "seq", None)
    matrix = P("seq", "dp")
    flat = P(("dp", "seq"))
    in_specs = (rows, P(None, "dp", None), P(None, "dp"), P(None, "dp"), rows) + (matrix,) * 10 + (flat,) * 3
    out_specs = (rows, rows, P(None, "dp", None)) + (matrix,) * 10 + (flat,) * 3
    return jax.shard_map(
        functools.partial(body, Net(mesh)), mesh=mesh, in_specs=in_specs, out_specs=out_specs, check_vma=False
    )
```

time: 2300 us -> 1380 us (0.60)
  Pallas kernels: 973 us -> 142 us
  matrix products: 447 us -> 269 us
  waiting for transfers between devices: 363 us -> 510 us
  starting transfers between devices: 193 us -> 106 us
  other arithmetic: 148 us -> 185 us
    pallas_call x4 -> x5, Pallas kernels: 973 us -> 142 us  [the longest x2 72.6 us: attend(): pl.pallas_call(functools.partial(attend_kernel, heads, tile), grid_spec=p...]
    all_to_all x5 -> x10, waiting for transfers between devices: 2.78 us -> 294 us  [the longest x5 260 us: to_dp(): return lax.all_to_all(value, 'dp', 0, 0, tiled=True)]
    dot_general x13 -> x1, matrix products: 183 us -> 1.54 us  [body(): jnp.dot(cond_all, low_ada, preferred_element_type=F32)]
    ppermute x150 -> x53, waiting for transfers between devices: 360 us -> 215 us  [send(): return lax.ppermute(value, self.name, pairs)]
    ppermute x150 -> x53, starting transfers between devices: 149 us -> 47.4 us  [send(): return lax.ppermute(value, self.name, pairs)]
    pallas_call x0 -> x1, other arithmetic: none -> 44.6 us  [attend_back(): pl.pallas_call(functools.partial(attend_back_kernel, heads, tile), grid_s...]
    slice x49 -> x19, local copies, waits for them, and re-layouts: 45.1 us -> 15.3 us  [the longest x4 6.29 us: scatter_weights(): first, second = (half[:, :, :ga], half[:, :, ga:])]
    unnamed x366 -> x250, local copies, waits for them, and re-layouts: 14.7 us -> 44.2 us
  transfers between devices with their start and end apart: 155 -> 63, of which waited for: 63 -> 21; matrix products, arithmetic and copies ran while one was open for 18% -> 25% of each run, Pallas kernels for 28% -> 6%
where the time goes in v2:
time: 1380 us; the launch traced here: 1370 us
  waiting for transfers between devices  510 us (37%)
  matrix products  269 us (19%)
  other arithmetic  185 us (13%)
  local copies, waits for them, and re-layouts  153 us (11%)
  Pallas kernels  142 us (10%)
  starting transfers between devices  106 us (8%)
    all_to_all x5, waiting for transfers between devices, to_dp(): return lax.all_to_all(value, 'dp', 0, 0, tiled=True)  260 us
    ppermute x53, waiting for transfers between devices, send(): return lax.ppermute(value, self.name, pairs)  215 us
    dot_general x9, matrix products, dot_t(): return jnp.einsum('srk,nk->srn', left, right, preferred_element_type=F32)  85.1 us
    dot_general x6, matrix products, dot(): return jnp.einsum('srn,nk->srk', left, right, preferred_element_type=F32)  78.9 us
    pallas_call x2, Pallas kernels, attend(): pl.pallas_call(functools.partial(attend_kernel, heads, tile), grid_spec=p...  72.6 us
    dot_general x9, matrix products, outer(): jnp.einsum('srn,srk->nk', left, right, preferred_element_type=F32)  63.5 us
    ppermute x53, starting transfers between devices, send(): return lax.ppermute(value, self.name, pairs)  47.4 us
    pallas_call x1, Pallas kernels, attend_back(): pl.pallas_call(functools.partial(attend_back_kernel, heads, tile), grid_s...  44.9 us
  transfers between devices with their start and end apart: 63, of which 21 were waited for; matrix products, arithmetic and copies ran while one was open for 25% of the time, Pallas kernels for 6%

profile of v2, /device:TPU:11, one launch (start us, length us, event | category | flops | bytes accessed | tf_op | source)
XLA Modules:
  0.0 1367.8 jit_solution(17165282554489316993)
XLA Ops:
  26.3 19.0 %all-to-all-done.2 = f32[32,1,504]{2,1,0:T(1,128)} async-done(((f32[32,1,504]{2,1,0:T(1,128)}), f32[32,1,504]{2,1,0:T(1,128)}, u32[]{:S(2)}, u32[]{:S(2)}) %all-to-all-start.2) | async-done | bytes 64544 | tf_op jit(solution)/shard_map/all_to_all | solution.py:267
  196.2 56.4 %collective-permute-done.23.refs_4_ = bf16[2,45,8,1152]{3,2,1,0:T(8,128)(2,1)} collective-permute-done((bf16[2,45,8,1152]{3,2,1,0:T(8,128)(2,1)}, bf16[2,45,8,1152]{3,2,1,0:T(8,128)(2,1)}, u32[]{:S(2)}, u32[]{:S(2)}) %collective-permute-start.23) | collective-permute-done | bytes 1658912 | tf_op jit(solution)/shard_map/ppermute | solution.py:47
  253.8 40.6 %attend.2 = (bf16[1,512,1152]{2,1,0:T(8,128)(2,1)}, f32[1,16,1,512]{3,2,1,0:T(1,128)}) custom-call(s32[1]{0:T(128)} %bitcast.8.lengths_ref, s32[2]{0:T(128)} %pad_add_fusion.offsets_ref, bf16[1,512,1152]{2,1,0:T(8,128)(2,1)} %fusion.41.q_ref, bf16[1,1024,1152]{2,1,0:T(8,128)(2,1)} %fusion.36.k_ref, bf16[1,1024,1152]{2,1,0:T(8,128)(2,1)} %fusion.34.v_ref), custom_call_target="tpu_custom_call" | custom-call | flops 4294967296 | bytes 7077888 | tf_op jit(solution)/shard_map/attend/pallas_call | solution.py:382
  306.3 32.0 %attend.3 = (bf16[1,512,1152]{2,1,0:T(8,128)(2,1)}, f32[1,16,1,512]{3,2,1,0:T(1,128)}) custom-call(s32[1]{0:T(128)} %bitcast.28.lengths_ref, s32[2]{0:T(128)} %pad_add_fusion.offsets_ref, bf16[1,512,1152]{2,1,0:T(8,128)(2,1)} %fusion.40.q_ref, bf16[1,1024,1152]{2,1,0:T(8,128)(2,1)} %fusion.37.k_ref, bf16[1,1024,1152]{2,1,0:T(8,128)(2,1)} %fusion.35.v_ref), custom_call_target="tpu_custom_call" | custom-call | flops 4294967296 | bytes 7077888 | tf_op jit(solution)/shard_map/attend/pallas_call | solution.py:382
  353.7 16.8 %place.3 = (bf16[4,2,2,9,8,1152]{5,4,3,2,1,0:T(8,128)(2,1)}, bf16[4,2,2,36,8,1152]{5,4,3,2,1,0:T(8,128)(2,1)}, bf16[4,2,2,9,8,4608]{5,4,3,2,1,0:T(8,128)(2,1)}) custom-call(s32[3]{0:T(128)} %pad_add_fusion.1.refs_0_, bf16[4,36,8,1152]{3,2,1,0:T(8,128)(2,1)} %pad_maximum_fusion.5.refs_1_, bf16[4,36,8,1152]{3,2,1,0:T(8,128)(2,1)} %collective-permute-done.21.refs_2_, ...), custom_call_target="tpu_custom_call" | custom-call | bytes 47775744 | tf_op jit(solution)/shard_map/place/pallas_call | solution.py:107
  381.5 25.0 %multiply_convert_fusion = (bf16[2,512,4608]{2,1,0:T(8,128)(2,1)}, f32[2,512,4608]{2,1,0:T(8,128)}) fusion(f32[4608]{0:T(1024)S(1)} %copy-done.65, bf16[4608,1152,1]{1,0,2:T(8,128)(2,1)} %bitcast.569, f32[2,512,1152]{2,1,0:T(8,128)} %copy-done.11, f32[2,1152]{1,0:T(2,128)S(1)} %copy-done.71, f32[2,1152]{1,0:T(2,128)S(1)} %copy-done.69, ...), kind=kOutput, calls=%fused_computation.13 | convolution fusion | flops 10924720128 | bytes 43692032 | tf_op jit(solution)/shard_map/srk,nk->srn/dot_general | solution.py:298
  406.5 28.2 %convert_reduce_fusion = (f32[4608]{0:T(1024)}, bf16[2,512,4608]{2,1,0:T(8,128)(2,1)S(1)}) fusion(f32[2,512,4608]{2,1,0:T(8,128)} %get-tuple-element.269, f32[4608]{0:T(1024)S(1)} %copy-done.65, bf16[1152,4608,1]{1,0,2:T(8,128)(2,1)} %bitcast.567, bf16[2,1,512,1152]{3,2,1,0:T(8,128)(2,1)S(1)} %copy-done.87, f32[2,1152]{1,0:T(2,128)S(1)} %copy-done.68), kind=kOutput, calls=%fused_computation.12 | convolution fusion | flops 10983698432 | bytes 41333760 | tf_op jit(solution)/shard_map/srn,nk->srk/dot_general | solution.py:302
  438.4 19.2 %multiply_reduce_fusion = (f32[2,1152]{1,0:T(2,128)}, f32[2,512]{1,0:T(2,128)S(1)}, f32[2,512]{1,0:T(2,128)S(1)}, f32[2,1152]{1,0:T(2,128)}, f32[2,512,1152]{2,1,0:T(8,128)}) fusion(f32[2,512,1152]{2,1,0:T(8,128)S(1)} %bitcast.535, f32[2,512]{1,0:T(2,128)S(1)} %add_rsqrt_fusion, f32[2,512]{1,0:T(2,128)S(1)} %broadcast_multiply_fusion.4, ...), kind=kOutput, calls=%fused_computation.72 | convolution fusion | flops 10882246656 | bytes 29535232 | tf_op jit(solution)/shard_map/srn,nk->srk/dot_general | solution.py:302
  457.6 20.1 %fusion = bf16[4608,1152]{1,0:T(8,128)(2,1)} fusion(bf16[2,512,4608]{2,1,0:T(8,128)(2,1)} %copy-done.93, f32[2,512,1152]{2,1,0:T(8,128)S(1)} %bitcast.535, f32[2,1152]{1,0:T(2,128)S(1)} %copy-done.71, f32[2,1152]{1,0:T(2,128)S(1)} %copy-done.69, f32[2,512]{1,0:T(2,128)S(1)} %add_rsqrt_fusion, f32[2,512]{1,0:T(2,128)S(1)} %broadcast_multiply_fusion.4), kind=kOutput, calls=%fused_computation.4 | convolution fusion | flops 10882842624 | bytes 24799232 | tf_op jit(solution)/shard_map/srn,srk->nk/dot_general | solution.py:306
  477.7 23.4 %convert_reduce_fusion.4 = (f32[1152]{0:T(1024)}, f32[2,1152]{1,0:T(2,128)}, bf16[2,1,512,1152]{3,2,1,0:T(8,128)(2,1)}, f32[1152]{0:T(1024)}, bf16[2,512,1152]{2,1,0:T(8,128)(2,1)}, /*index=5*/f32[2,512,1152]{2,1,0:T(8,128)}) fusion(bf16[2,1,512,1152]{3,2,1,0:T(8,128)(2,1)} %param.22, f32[2,1152]{1,0:T(2,128)S(1)} %copy-done.68, ...), kind=kOutput, calls=%fused_computation.67 | convolution fusion | flops 10898763776 | bytes 41354752 | tf_op jit(solution)/shard_map/srk,nk->srn/dot_general | solution.py:298
  534.5 44.9 %attend_back.2 = (bf16[1,512,1152]{2,1,0:T(8,128)(2,1)}, bf16[1,1024,1152]{2,1,0:T(8,128)(2,1)}, bf16[1,1024,1152]{2,1,0:T(8,128)(2,1)}) custom-call(s32[1]{0:T(128)} %bitcast.8.lengths_ref, s32[2]{0:T(128)} %pad_add_fusion.offsets_ref, bf16[1,512,1152]{2,1,0:T(8,128)(2,1)} %fusion.41.q_ref, bf16[1,1024,1152]{2,1,0:T(8,128)(2,1)} %fusion.36.k_ref, ...), custom_call_target="tpu_custom_call" | custom-call | flops 10737418240 | bytes 14155776 | tf_op jit(solution)/shard_map/attend_back/pallas_call | solution.py:466
  584.6 44.6 %attend_back.3 = (bf16[2,1024,1152]{2,1,0:T(8,128)(2,1)}, bf16[1,1024,1152]{2,1,0:T(8,128)(2,1)}, bf16[1,512,1152]{2,1,0:T(8,128)(2,1)}) fusion(bf16[2,1024,1152]{2,1,0:T(8,128)(2,1)} %constant_dynamic-update-slice_fusion.3, s32[1]{0:T(128)} %bitcast.28.lengths_ref, s32[2]{0:T(128)S(1)} %copy-done.91, bf16[1,512,1152]{2,1,0:T(8,128)(2,1)} %fusion.40.q_ref, ...), kind=kCustom, calls=%fused_computation.292 | custom fusion | flops 10737418240 | bytes 14189064 | tf_op jit(solution)/shard_map/attend_back/pallas_call | solution.py:466
  632.6 9.9 fusion.43
  656.8 8.9 bitcast_dynamic-update-slice_fusion.1
  694.6 14.5 %pad_maximum_fusion = bf16[3456,1152]{1,0:T(8,128)(2,1)S(1)} fusion(bf16[1152,1152]{1,0:T(8,128)(2,1)S(1)} %fusion.16, bf16[1152,1152]{1,0:T(8,128)(2,1)S(1)} %fusion.15, bf16[1152,1152]{1,0:T(8,128)(2,1)S(1)} %fusion.9), kind=kLoop, calls=%fused_computation.23 | loop fusion | flops 23887872 | bytes 15925248 | tf_op jit(solution)/shard_map/concatenate | solution.py:626
  741.4 12.6 all-to-all-done.3
  759.1 9.9 add_convert_fusion
  788.9 38.3 %collective-permute-done.35 = bf16[12,8,1152]{2,1,0:T(8,128)(2,1)} collective-permute-done((bf16[12,8,1152]{2,1,0:T(8,128)(2,1)}, bf16[12,8,1152]{2,1,0:T(8,128)(2,1)}, u32[]{:S(2)}, u32[]{:S(2)}) %collective-permute-start.35) | collective-permute-done | bytes 221216 | tf_op jit(solution)/shard_map/ppermute | solution.py:47
  845.7 80.2 %collective-permute-done.45 = bf16[36,8,1152]{2,1,0:T(8,128)(2,1)S(1)} collective-permute-done((bf16[36,8,1152]{2,1,0:T(8,128)(2,1)S(1)}, bf16[36,8,1152]{2,1,0:T(8,128)(2,1)S(1)}, u32[]{:S(2)}, u32[]{:S(2)}) %collective-permute-start.45) | collective-permute-done | bytes 663584 | tf_op jit(solution)/shard_map/ppermute | solution.py:47
  941.7 11.4 collective-permute-done.46
  1007.2 36.1 %all-to-all-done.5 = f32[16,1,144,144]{3,2,1,0:T(8,128)} async-done(((f32[16,1,144,144]{3,2,1,0:T(8,128)}), f32[16,1,144,144]{3,2,1,0:T(8,128)}, u32[]{:S(2)}, u32[]{:S(2)}) %all-to-all-start.5) | async-done | bytes 1327136 | tf_op jit(solution)/shard_map/all_to_all | solution.py:270
  1060.1 91.9 %all-to-all-done.7 = f32[16,2,144,144]{3,2,1,0:T(8,128)} async-done(((f32[16,2,144,144]{3,2,1,0:T(8,128)}), f32[16,2,144,144]{3,2,1,0:T(8,128)}, u32[]{:S(2)}, u32[]{:S(2)}) %all-to-all-start.7) | async-done | bytes 2654240 | tf_op jit(solution)/shard_map/all_to_all | solution.py:270
  1196.7 46.3 %all-to-all-done.6 = f32[16,1,144,144]{3,2,1,0:T(8,128)} async-done(((f32[16,1,144,144]{3,2,1,0:T(8,128)}), f32[16,1,144,144]{3,2,1,0:T(8,128)}, u32[]{:S(2)}, u32[]{:S(2)}) %all-to-all-start.6) | async-done | bytes 1327136 | tf_op jit(solution)/shard_map/all_to_all | solution.py:270
  1268.8 86.0 %all-to-all-done.8 = f32[16,2,144,144]{3,2,1,0:T(8,128)} async-done(((f32[16,2,144,144]{3,2,1,0:T(8,128)}), f32[16,2,144,144]{3,2,1,0:T(8,128)}, u32[]{:S(2)}, u32[]{:S(2)}) %all-to-all-start.8) | async-done | bytes 2654240 | tf_op jit(solution)/shard_map/all_to_all | solution.py:270
  (622 shorter events, 547.9 us)
Async XLA Ops:
  10.5 49.7 %collective-permute-start.1 = (bf16[216,576]{1,0:T(8,128)(2,1)}, bf16[216,576]{1,0:T(8,128)(2,1)}, u32[]{:S(2)}, u32[]{:S(2)}) collective-permute-start(bf16[216,576]{1,0:T(8,128)(2,1)} %convert_bitcast_fusion.2), channel_id=1, source_target_pairs={{0,1},{1,0},{2,3},{3,2},{4,5},{5,4},{6,7},{7,6},{8,9},{9,8},{10,11... | collective-permute-start | bytes 746504 | tf_op jit(solution)/shard_map/ppermute | solution.py:47
  13.5 63.6 %collective-permute-start = (bf16[512,1152]{1,0:T(8,128)(2,1)S(1)}, bf16[512,1152]{1,0:T(8,128)(2,1)S(1)}, u32[]{:S(2)}, u32[]{:S(2)}) collective-permute-start(bf16[512,1152]{1,0:T(8,128)(2,1)S(1)} %get-tuple-element.231), channel_id=1, source_target_pairs={{0,1},{1,0},{2,3},{3,2},{4,5},{5,4},{6,7},{7,6},{8,9},{9,8},{10,11... | collective-permute-start | bytes 3538952 | tf_op jit(solution)/shard_map/ppermute | solution.py:47
  74.1 57.9 %collective-permute-start.12 = (bf16[2,15,8,1152]{3,2,1,0:T(8,128)(2,1)}, bf16[2,15,8,1152]{3,2,1,0:T(8,128)(2,1)}, u32[]{:S(2)}, u32[]{:S(2)}) collective-permute-start(bf16[2,15,8,1152]{3,2,1,0:T(8,128)(2,1)} %pad_maximum_fusion.14.refs_3_), channel_id=1, source_target_pairs={{0,2},{2,0},{4,6},{6,4},{8,10},{10,8},{12,14},{14,12},{16,18},{18,... | collective-permute-start | bytes 1658888 | tf_op jit(solution)/shard_map/ppermute | solution.py:47
  76.0 52.6 %collective-permute-start.9 = (bf16[2,15,8,1152]{3,2,1,0:T(8,128)(2,1)}, bf16[2,15,8,1152]{3,2,1,0:T(8,128)(2,1)}, u32[]{:S(2)}, u32[]{:S(2)}) collective-permute-start(bf16[2,15,8,1152]{3,2,1,0:T(8,128)(2,1)} %pad_maximum_fusion.14.refs_3_), channel_id=1, source_target_pairs={{0,8},{2,10},{4,12},{6,14},{8,16},{10,18},{12,20},{14,22},{16,24},... | collective-permute-start | bytes 1658888 | tf_op jit(solution)/shard_map/ppermute | solution.py:47
  156.0 182.2 %collective-permute-start.28 = (bf16[2,45,8,1152]{3,2,1,0:T(8,128)(2,1)}, bf16[2,45,8,1152]{3,2,1,0:T(8,128)(2,1)}, u32[]{:S(2)}, u32[]{:S(2)}) collective-permute-start(bf16[2,45,8,1152]{3,2,1,0:T(8,128)(2,1)} %pad_maximum_fusion.8.refs_3_), channel_id=1, source_target_pairs={{0,2},{2,0},{4,6},{6,4},{8,10},{10,8},{12,14},{14,12},{16,18},{18,... | collective-permute-start | bytes 4976648 | tf_op jit(solution)/shard_map/ppermute | solution.py:47
  157.2 181.6 %collective-permute-start.25 = (bf16[2,45,8,1152]{3,2,1,0:T(8,128)(2,1)}, bf16[2,45,8,1152]{3,2,1,0:T(8,128)(2,1)}, u32[]{:S(2)}, u32[]{:S(2)}) collective-permute-start(bf16[2,45,8,1152]{3,2,1,0:T(8,128)(2,1)} %pad_maximum_fusion.8.refs_3_), channel_id=1, source_target_pairs={{0,8},{2,10},{4,12},{6,14},{8,16},{10,18},{12,20},{14,22},{16,24},... | collective-permute-start | bytes 4976648 | tf_op jit(solution)/shard_map/ppermute | solution.py:47
  159.7 92.9 %collective-permute-start.23 = (bf16[2,45,8,1152]{3,2,1,0:T(8,128)(2,1)}, bf16[2,45,8,1152]{3,2,1,0:T(8,128)(2,1)}, u32[]{:S(2)}, u32[]{:S(2)}) collective-permute-start(bf16[2,45,8,1152]{3,2,1,0:T(8,128)(2,1)} %pad_maximum_fusion.8.refs_3_), channel_id=1, source_target_pairs={{0,24},{2,26},{4,28},{6,30},{8,0},{10,2},{12,4},{14,6},{16,8},{18,... | collective-permute-start | bytes 4976648 | tf_op jit(solution)/shard_map/ppermute | solution.py:47
  182.5 119.1 %collective-permute-start.21 = (bf16[4,36,8,1152]{3,2,1,0:T(8,128)(2,1)}, bf16[4,36,8,1152]{3,2,1,0:T(8,128)(2,1)}, u32[]{:S(2)}, u32[]{:S(2)}) collective-permute-start(bf16[4,36,8,1152]{3,2,1,0:T(8,128)(2,1)} %pad_maximum_fusion.5.refs_1_), channel_id=1, source_target_pairs={{0,4},{2,6},{4,0},{6,2},{8,12},{10,14},{12,8},{14,10},{16,20},{18,... | collective-permute-start | bytes 7962632 | tf_op jit(solution)/shard_map/ppermute | solution.py:47
  252.6 86.2 %collective-permute-start.24 = (bf16[2,45,8,1152]{3,2,1,0:T(8,128)(2,1)}, bf16[2,45,8,1152]{3,2,1,0:T(8,128)(2,1)}, u32[]{:S(2)}, u32[]{:S(2)}) collective-permute-start(bf16[2,45,8,1152]{3,2,1,0:T(8,128)(2,1)} %collective-permute-done.23.refs_4_), channel_id=1, source_target_pairs={{0,24},{2,26},{4,28},{6,30},{8,0},{10,2},{12,4},{14,6},{16,8},{18,... | collective-permute-start | bytes 4976648 | tf_op jit(solution)/shard_map/ppermute | solution.py:47
  300.9 49.9 %collective-permute-start.26 = (bf16[4,36,8,1152]{3,2,1,0:T(8,128)(2,1)}, bf16[4,36,8,1152]{3,2,1,0:T(8,128)(2,1)}, u32[]{:S(2)}, u32[]{:S(2)}) collective-permute-start(bf16[4,36,8,1152]{3,2,1,0:T(8,128)(2,1)} %pad_maximum_fusion.5.refs_1_), channel_id=1, source_target_pairs={{0,2},{2,0},{4,6},{6,4},{8,10},{10,8},{12,14},{14,12},{16,18},{18,... | collective-permute-start | bytes 7962632 | tf_op jit(solution)/shard_map/ppermute | solution.py:47
  301.6 51.5 %collective-permute-start.27 = (bf16[4,36,8,1152]{3,2,1,0:T(8,128)(2,1)}, bf16[4,36,8,1152]{3,2,1,0:T(8,128)(2,1)}, u32[]{:S(2)}, u32[]{:S(2)}) collective-permute-start(bf16[4,36,8,1152]{3,2,1,0:T(8,128)(2,1)} %collective-permute-done.21.refs_2_), channel_id=1, source_target_pairs={{0,2},{2,0},{4,6},{6,4},{8,10},{10,8},{12,14},{14,12},{16,18},{18,... | collective-permute-start | bytes 7962632 | tf_op jit(solution)/shard_map/ppermute | solution.py:47
  652.8 60.5 %collective-permute-start.32 = (bf16[2,512,1152]{2,1,0:T(8,128)(2,1)}, bf16[2,512,1152]{2,1,0:T(8,128)(2,1)}, u32[]{:S(2)}, u32[]{:S(2)}) collective-permute-start(bf16[2,512,1152]{2,1,0:T(8,128)(2,1)} %slice.437), channel_id=1, source_target_pairs={{0,1},{1,0},{2,3},{3,2},{4,5},{5,4},{6,7},{7,6},{8,9},{9,8},{10,11... | collective-permute-start | bytes 7077896 | tf_op jit(solution)/shard_map/ppermute | solution.py:47
  675.7 83.4 %collective-permute-start.43 = (bf16[4,2,81,8,1152]{4,3,2,1,0:T(8,128)(2,1)}, bf16[4,2,81,8,1152]{4,3,2,1,0:T(8,128)(2,1)}, u32[]{:S(2)}, u32[]{:S(2)}) collective-permute-start(bf16[4,2,81,8,1152]{4,3,2,1,0:T(8,128)(2,1)} %get-tuple-element.215), channel_id=1, source_target_pairs={{0,2},{2,0},{4,6},{6,4},{8,10},{10,8},{12,14},{14,12},{16,18},{18,... | collective-permute-start | bytes 35831816 | tf_op jit(solution)/shard_map/ppermute | solution.py:47
  754.0 74.3 %collective-permute-start.38 = (bf16[2,15,8,1152]{3,2,1,0:T(8,128)(2,1)}, bf16[2,15,8,1152]{3,2,1,0:T(8,128)(2,1)}, u32[]{:S(2)}, u32[]{:S(2)}) collective-permute-start(bf16[2,15,8,1152]{3,2,1,0:T(8,128)(2,1)} %get-tuple-element.232), channel_id=1, source_target_pairs={{0,8},{2,10},{4,12},{6,14},{8,16},{10,18},{12,20},{14,22},{16,24},... | collective-permute-start | bytes 1658888 | tf_op jit(solution)/shard_map/ppermute | solution.py:47
  756.5 74.1 %collective-permute-start.40 = (bf16[2,15,8,1152]{3,2,1,0:T(8,128)(2,1)}, bf16[2,15,8,1152]{3,2,1,0:T(8,128)(2,1)}, u32[]{:S(2)}, u32[]{:S(2)}) collective-permute-start(bf16[2,15,8,1152]{3,2,1,0:T(8,128)(2,1)} %fusion.91), channel_id=1, source_target_pairs={{0,24},{2,26},{4,28},{6,30},{8,0},{10,2},{12,4},{14,6},{16,8},{18,... | collective-permute-start | bytes 1658888 | tf_op jit(solution)/shard_map/ppermute | solution.py:47
  778.4 58.3 %collective-permute-start.44 = (bf16[4,36,8,1152]{3,2,1,0:T(8,128)(2,1)}, bf16[4,36,8,1152]{3,2,1,0:T(8,128)(2,1)}, u32[]{:S(2)}, u32[]{:S(2)}) collective-permute-start(bf16[4,36,8,1152]{3,2,1,0:T(8,128)(2,1)} %dynamic-slice_bitcast_fusion.1), channel_id=1, source_target_pairs={{0,4},{2,6},{4,0},{6,2},{8,12},{10,14},{12,8},{14,10},{16,20},{18,... | collective-permute-start | bytes 7962632 | tf_op jit(solution)/shard_map/ppermute | solution.py:47
  832.6 97.2 %collective-permute-start.48 = (bf16[2,45,8,1152]{3,2,1,0:T(8,128)(2,1)S(1)}, bf16[2,45,8,1152]{3,2,1,0:T(8,128)(2,1)S(1)}, u32[]{:S(2)}, u32[]{:S(2)}) collective-permute-start(bf16[2,45,8,1152]{3,2,1,0:T(8,128)(2,1)S(1)} %copy-done.35), channel_id=1, source_target_pairs={{0,8},{2,10},{4,12},{6,14},{8,16},{10,18},{12,20},{14,22},{16,24},... | collective-permute-start | bytes 4976648 | tf_op jit(solution)/shard_map/ppermute | solution.py:47
  836.8 93.0 %collective-permute-start.50 = (bf16[2,45,8,1152]{3,2,1,0:T(8,128)(2,1)S(1)}, bf16[2,45,8,1152]{3,2,1,0:T(8,128)(2,1)S(1)}, u32[]{:S(2)}, u32[]{:S(2)}) collective-permute-start(bf16[2,45,8,1152]{3,2,1,0:T(8,128)(2,1)S(1)} %fusion.31), channel_id=1, source_target_pairs={{0,24},{2,26},{4,28},{6,30},{8,0},{10,2},{12,4},{14,6},{16,8},{18,... | collective-permute-start | bytes 4976648 | tf_op jit(solution)/shard_map/ppermute | solution.py:47
  843.1 82.9 %collective-permute-start.45 = (bf16[36,8,1152]{2,1,0:T(8,128)(2,1)S(1)}, bf16[36,8,1152]{2,1,0:T(8,128)(2,1)S(1)}, u32[]{:S(2)}, u32[]{:S(2)}) collective-permute-start(bf16[36,8,1152]{2,1,0:T(8,128)(2,1)S(1)} %get-tuple-element.212), channel_id=1, source_target_pairs={{0,8},{2,10},{4,12},{6,14},{8,16},{10,18},{12,20},{14,22},{16,24},... | collective-permute-start | bytes 1990664 | tf_op jit(solution)/shard_map/ppermute | solution.py:47
  844.2 97.5 %collective-permute-start.47 = (bf16[36,8,1152]{2,1,0:T(8,128)(2,1)}, bf16[36,8,1152]{2,1,0:T(8,128)(2,1)}, u32[]{:S(2)}, u32[]{:S(2)}) collective-permute-start(bf16[36,8,1152]{2,1,0:T(8,128)(2,1)} %get-tuple-element.213), channel_id=1, source_target_pairs={{0,24},{2,26},{4,28},{6,30},{8,0},{10,2},{12,4},{14,6},{16,8},{18,... | collective-permute-start | bytes 1990664 | tf_op jit(solution)/shard_map/ppermute | solution.py:47
  981.6 61.7 %all-to-all-start.5 = ((f32[16,1,144,144]{3,2,1,0:T(8,128)}), f32[16,1,144,144]{3,2,1,0:T(8,128)}, u32[]{:S(2)}, u32[]{:S(2)}) async-start(f32[16,1,144,144]{3,2,1,0:T(8,128)} %fusion.53), calls=%async_computation.5 | async-start | bytes 4718592 | tf_op jit(solution)/shard_map/all_to_all | solution.py:270
  1043.3 108.7 %all-to-all-start.7 = ((f32[16,2,144,144]{3,2,1,0:T(8,128)}), f32[16,2,144,144]{3,2,1,0:T(8,128)}, u32[]{:S(2)}, u32[]{:S(2)}) async-start(f32[16,2,144,144]{3,2,1,0:T(8,128)} %bitcast.507), calls=%async_computation.7 | async-start | bytes 9437184 | tf_op jit(solution)/shard_map/all_to_all | solution.py:270
  1182.9 60.1 %all-to-all-start.6 = ((f32[16,1,144,144]{3,2,1,0:T(8,128)}), f32[16,1,144,144]{3,2,1,0:T(8,128)}, u32[]{:S(2)}, u32[]{:S(2)}) async-start(f32[16,1,144,144]{3,2,1,0:T(8,128)} %broadcast_in_dim.19), calls=%async_computation.6 | async-start | bytes 4718592 | tf_op jit(solution)/shard_map/all_to_all | solution.py:270
  1245.7 109.0 %all-to-all-start.8 = ((f32[16,2,144,144]{3,2,1,0:T(8,128)}), f32[16,2,144,144]{3,2,1,0:T(8,128)}, u32[]{:S(2)}, u32[]{:S(2)}) async-start(f32[16,2,144,144]{3,2,1,0:T(8,128)} %broadcast_in_dim.20), calls=%async_computation.8 | async-start | bytes 9437184 | tf_op jit(solution)/shard_map/all_to_all | solution.py:270
  (155 other events, 2375.2 us)

commit v3 on v2

--- a/solution.py
+++ b/solution.py
@@ -59,18 +59,40 @@
             blocks[n // 2] = self.send(low, 1) if far == 1 else self.send(high, -1)
         return blocks
 
-    def scatter_sum(self, block_of, far=1):
+    def gather_steps(self, value, far=1):
         n = self.size
-        own = block_of(0).astype(F32)
+        blocks = [value] + [None] * (n - 1)
+        if n == 2:
+            blocks[1] = self.send(value, 1)
+            anchor = yield [value]
+            blocks[1] = tie(blocks[1], anchor)
+            return blocks
+        low = high = value
+        for t in range(1, n // 2):
+            sent = [low, high]
+            low, high = self.send(low, 1), self.send(high, -1)
+            anchor = yield sent
+            low, high = tie(low, anchor), tie(high, anchor)
+            blocks[n - t], blocks[t] = low, high
+        sent = [low if far == 1 else high]
+        last = self.send(sent[0], far)
+        anchor = yield sent
+        blocks[n // 2] = tie(last, anchor)
+        return blocks
+
+    def scatter_steps(self, block_of, far=1):
+        n = self.size
         if n == 1:
-            return own
+            return block_of(0).astype(F32)
         if n == 2:
-            return own + self.send(block_of(1), 1).astype(F32)
-        low = high = None
-        if far == 1:
-            low = self.send(block_of(n // 2), 1)
-        else:
-            high = self.send(block_of(n // 2), -1)
+            sent = block_of(1)
+            got = self.send(sent, 1)
+            anchor = yield [sent]
+            return block_of(0).astype(F32) + tie(got, anchor).astype(F32)
+        sent = block_of(n // 2)
+        got = self.send(sent, far)
+        anchor = yield [sent]
+        low, high = (tie(got, anchor), None) if far == 1 else (None, tie(got, anchor))
         for t in range(n // 2 - 1, 0, -1):
             up, down = block_of(t), block_of(n - t)
             if low is not None:
@@ -78,7 +100,62 @@
             if high is not None:
                 down = (down.astype(F32) + high.astype(F32)).astype(down.dtype)
             low, high = self.send(up, 1), self.send(down, -1)
-        return own + low.astype(F32) + high.astype(F32)
+            anchor = yield [up, down]
+            low, high = tie(low, anchor), tie(high, anchor)
+        return block_of(0).astype(F32) + low.astype(F32) + high.astype(F32)
+
+
+def tie(value, *earlier):
+    earlier = [array for array in earlier if array is not None]
+    if not earlier:
+        return value
+    anywhere = pl.BlockSpec(memory_space=pl.ANY)
+    return pl.pallas_call(
+        lambda *refs: None,
+        out_shape=jax.ShapeDtypeStruct(value.shape, value.dtype),
+        in_specs=[anywhere] * (1 + len(earlier)),
+        out_specs=anywhere,
+        input_output_aliases={0: 0},
+        name="tie",
+    )(value, *earlier)
+
+
+def lockstep(*steps):
+    results = [None] * len(steps)
+    alive = dict(enumerate(steps))
+    anchor = None
+    while alive:
+        sent = []
+        for n, step in list(alive.items()):
+            try:
+                sent += step.send(anchor)
+            except StopIteration as stop:
+                results[n] = stop.value
+                del alive[n]
+        if alive:
+            anchor = yield sent
+    return results
+
+
+class Staged:
+    def __init__(self, steps):
+        self.steps, self.result, self.started, self.done = steps, None, False, False
+
+    def advance(self, anchor=None):
+        if self.done:
+            return []
+        try:
+            sent = self.steps.send(anchor if self.started else None)
+            self.started = True
+            return sent
+        except StopIteration as stop:
+            self.result, self.done = stop.value, True
+            return []
+
+    def finish(self, anchor=None):
+        while not self.done:
+            self.advance(anchor)
+        return self.result
 
 
 def place_kernel(moves, outs, count, parts, *refs):
@@ -134,44 +211,45 @@
         return jnp.stack([self.z.digit(), self.x.digit(), self.core.digit()]).astype(jnp.int32)
 
 
-    def rows_joined(self, shards, unit, depth):
+    def wire(self, shards):
         turned = [shard.astype(BF).T for shard in shards]
-        wire = jnp.concatenate([t.reshape(-1) for t in turned]) if len(turned) > 1 else turned[0]
-        wires = self.y.gather(wire)
-        joined = []
-        start = 0
-        for t in turned:
-            if len(turned) > 1:
-                blocks = [w[start : start + t.size].reshape(t.shape) for w in wires]
-            else:
-                blocks = wires
-            start += t.size
-            if self.seq == 2:
-                own, other = blocks
-                full = jnp.where(
-                    self.y.digit() == 0,
-                    jnp.concatenate([own, other], axis=1),
-                    jnp.concatenate([other, own], axis=1),
-                )
-            else:
-                order = (jnp.arange(self.seq) - self.y.digit()) % self.seq
-                full = jnp.take(jnp.stack(blocks), order, axis=0)
-                full = jnp.transpose(full, (1, 0, 2)).reshape(t.shape[0], -1)
-            full = full.reshape(t.shape[0] // unit, unit, full.shape[1] // depth, depth)
-            joined.append(jnp.transpose(full, (2, 0, 1, 3)).reshape(-1, unit, depth))
-        return joined[0] if len(joined) == 1 else jnp.concatenate(joined, axis=0)
-
-    def gather_weights(self, units, layout):
+        return turned[0] if len(turned) == 1 else jnp.concatenate(turned, axis=0)
+
+    def joined(self, wires, unit, depth):
+        if self.seq == 2:
+            own, other = wires
+            full = jnp.where(
+                self.y.digit() == 0,
+                jnp.concatenate([own, other], axis=1),
+                jnp.concatenate([other, own], axis=1),
+            )
+        else:
+            order = (jnp.arange(self.seq) - self.y.digit()) % self.seq
+            full = jnp.take(jnp.stack(wires), order, axis=0)
+            full = jnp.transpose(full, (1, 0, 2)).reshape(full.shape[1], -1)
+        full = full.reshape(full.shape[0] // unit, unit, full.shape[1] // depth, depth)
+        return jnp.transpose(full, (2, 0, 1, 3)).reshape(-1, unit, depth)
+
+    def gather_steps(self, units, layout, part):
         g, unit, depth = units.shape
         zs = self.z.size
-        ga = max(1, (4 * g) // 9)
+        ga = max(1, int(part * g))
         first, second = units[:ga], units[ga:]
-        line = jnp.stack(self.z.gather(first, 1))
-        pair = jnp.stack([second, self.x.send(second, 1)])
-        line_x = self.x.send(line, 1)
-        pieces = self.z.gather(pair, -1)
-        arrived = [line_x] + pieces[1:]
-        sources, moves = [], []
+
+        def line_steps():
+            blocks = yield from self.z.gather_steps(first, 1)
+            line = jnp.stack(blocks)
+            return (yield from self.x.gather_steps(line))
+
+        def pair_steps():
+            blocks = yield from self.x.gather_steps(second)
+            return (yield from self.z.gather_steps(jnp.stack(blocks), -1))
+
+        lines, pairs = yield from lockstep(line_steps(), pair_steps())
+        pieces = lines + pairs
+        others = [self.core.send(piece, 1) for piece in pieces]
+        anchor = yield pieces
+        sources, moves = pieces + [tie(other, anchor) for other in others], []
 
         def spot(sz, sx, sc, start, stop):
             def target(spots):
@@ -185,16 +263,11 @@
             return target
 
         for sc in range(2):
-            for sx, array in ((0, line), (1, line_x)):
-                array = array if sc == 0 else self.core.send(array, 1)
+            base = sc * len(pieces)
+            for sx in range(2):
                 for sz in range(zs):
-                    moves.append((len(sources), (sz,), spot(sz, sx, sc, 0, ga)))
-                sources.append(array)
-            for sz, array in enumerate(pieces):
-                array = array if sc == 0 else self.core.send(array, 1)
-                for sx in range(2):
-                    moves.append((len(sources), (sx,), spot(sz, sx, sc, ga, g)))
-                sources.append(array)
+                    moves.append((base + sx, (sz,), spot(sz, sx, sc, 0, ga)))
+                    moves.append((base + 2 + sz, (sx,), spot(sz, sx, sc, ga, g)))
         outs, shapes, start = [], [], 0
         for n, (rows, blocks) in enumerate(layout):
             size = rows // unit
@@ -205,61 +278,75 @@
                 outs.append((window, n, target))
                 start += size
         full = place(self.spots(), sources, moves, (zs, 2, 2, g, unit, depth), outs, shapes)
-        return [f.reshape(-1, f.shape[-1]) for f in full], arrived
-
-    def scatter_weights(self, terms, unit, depth, layout):
+        return [f.reshape(-1, f.shape[-1]) for f in full], lines[1:] + pairs[1:]
+
+    def scatter_steps(self, terms, unit, depth, layout, part):
         zs = self.z.size
         blocks = [term.reshape(zs, 2, 2, -1, unit, depth) for term in terms]
         g = sum(block.shape[3] for block in blocks)
-        ga = max(1, (4 * g) // 9)
+        ga = max(1, int(part * g))
         core, x, z = self.core.digit(), self.x.digit(), self.z.digit()
 
         def half_of(s):
             parts = [lax.dynamic_index_in_dim(block, (core + s) % 2, 2, keepdims=False) for block in blocks]
             return parts[0] if len(parts) == 1 else jnp.concatenate(parts, axis=2)
 
-        half = self.core.scatter_sum(half_of).astype(BF)
-        first, second = half[:, :, :ga], half[:, :, ga:]
-        line = self.x.scatter_sum(
-            lambda s: lax.dynamic_index_in_dim(first, (x + s) % 2, 1, keepdims=False)
-        ).astype(BF)
-        pair = self.z.scatter_sum(
-            lambda s: lax.dynamic_index_in_dim(second, (z + s) % zs, 0, keepdims=False), -1
-        ).astype(BF)
-        first = self.z.scatter_sum(
-            lambda s: lax.dynamic_index_in_dim(line, (z + s) % zs, 0, keepdims=False), 1
+        half = (yield from self.core.scatter_steps(half_of)).astype(BF)
+
+        def line_steps():
+            line = yield from self.x.scatter_steps(
+                lambda s: lax.dynamic_index_in_dim(half[:, :, :ga], (x + s) % 2, 1, keepdims=False)
+            )
+            line = line.astype(BF)
+            return (
+                yield from self.z.scatter_steps(
+                    lambda s: lax.dynamic_index_in_dim(line, (z + s) % zs, 0, keepdims=False), 1
+                )
+            )
+
+        def pair_steps():
+            pair = yield from self.z.scatter_steps(
+                lambda s: lax.dynamic_index_in_dim(half[:, :, ga:], (z + s) % zs, 0, keepdims=False), -1
+            )
+            pair = pair.astype(BF)
+            return (
+                yield from self.x.scatter_steps(
+                    lambda s: lax.dynamic_index_in_dim(pair, (x + s) % 2, 0, keepdims=False)
+                )
+            )
+
+        line, pair = yield from lockstep(line_steps(), pair_steps())
+        joined = jnp.concatenate([line, pair], axis=0).astype(BF)
+        count = layout[0][1]
+        if count > 1:
+            joined = jnp.transpose(joined.reshape(count, -1, unit, depth), (1, 2, 0, 3))
+        joined = joined.reshape(-1, self.seq, count * depth // self.seq)
+        y = self.y.digit()
+        return (
+            yield from self.y.scatter_steps(
+                lambda s: lax.dynamic_index_in_dim(joined, (y + s) % self.seq, 1, keepdims=False)
+            )
         )
-        second = self.x.scatter_sum(
-            lambda s: lax.dynamic_index_in_dim(pair, (x + s) % 2, 0, keepdims=False)
-        )
-        joined = jnp.concatenate([first, second], axis=0).astype(BF)
-        y = self.y.digit()
-        wire, start = [], 0
-        for rows, count in layout:
-            size = rows // unit * count
-            full = joined[start : start + size].reshape(count, rows // unit, unit, depth)
-            full = jnp.transpose(full, (1, 2, 0, 3)).reshape(rows, count * depth)
-            wire.append(full.reshape(rows, self.seq, -1))
-            start += size
-        own = [lax.dynamic_index_in_dim(w, y, 1, keepdims=False).astype(F32) for w in wire]
-        if len(wire) == 1:
-            total = [
-                self.y.scatter_sum(
-                    lambda s: lax.dynamic_index_in_dim(wire[0], (y + s) % self.seq, 1, keepdims=False)
-                )
-            ]
-        else:
-
-            def flat_of(s):
-                parts = [lax.dynamic_index_in_dim(w, (y + s) % self.seq, 1, keepdims=False) for w in wire]
-                return jnp.concatenate([part.reshape(-1) for part in parts])
-
-            summed = self.y.scatter_sum(flat_of)
-            total, start = [], 0
-            for part in own:
-                total.append(summed[start : start + part.size].reshape(part.shape))
-                start += part.size
-        return [t.T for t in total]
+
+
+    def muon_steps(self, groups, masters, rates):
+        momenta, own, other = muon_gram(self.spots(), groups)
+        got = self.core.send(other, 1)
+        anchor = yield [other]
+        half = own + tie(got, anchor)
+        sent, kept = half[1], half[0]
+        got = self.x.send(sent, 1)
+        anchor = yield [sent]
+        blocks = yield from self.z.gather_steps(kept + tie(got, anchor))
+        factor = polynomial(blocks)
+        got = self.x.send(factor, 1)
+        anchor = yield [factor]
+        got = tie(got, anchor)
+        pair = [factor, got]
+        others = [self.core.send(each, 1) for each in pair]
+        anchor = yield pair
+        factors = pair + [tie(each, anchor) for each in others]
+        return momenta, muon_apply(self.spots(), factors, momenta, masters, rates)
 
 
     def to_all(self, value):
@@ -268,10 +355,6 @@
 
     def to_dp(self, value):
         return lax.all_to_all(value, "dp", 0, 0, tiled=True)
-
-
-def after(value, *earlier):
-    return lax.optimization_barrier((value,) + earlier)[0]
 
 
 def layer_norm(values):
@@ -332,6 +415,13 @@
 
 def nn(left, right):
     return jnp.dot(left, right, preferred_element_type=F32)
+
+
+def without(kernel, start, count, *fixed):
+    def run(*refs):
+        kernel(*fixed, *refs[:start], *refs[start + count :])
+
+    return run
 
 
 def attend_kernel(heads, chunk, lengths_ref, offsets_ref, q_ref, k_ref, v_ref, o_ref, lse_ref, q_s, k_s, vt_s, o_s):
@@ -373,14 +463,14 @@
         o_ref[0, :, h * depth : (h + 1) * depth] = o_s[h].astype(BF)
 
 
-def attend(lengths, offsets, queries, keys, values, heads, tile):
+def attend(lengths, offsets, queries, keys, values, heads, tile, deps=()):
     count, rows, width = queries.shape
     total = keys.shape[1]
     depth = width // heads
     tile = min(tile, total)
     pick = lambda i, *_: (i, 0, 0)
     return pl.pallas_call(
-        functools.partial(attend_kernel, heads, tile),
+        without(attend_kernel, 5, len(deps), heads, tile),
         grid_spec=pltpu.PrefetchScalarGridSpec(
             num_scalar_prefetch=2,
             grid=(count,),
@@ -388,7 +478,8 @@
                 pl.BlockSpec((1, rows, width), pick),
                 pl.BlockSpec((1, total, width), pick),
                 pl.BlockSpec((1, total, width), pick),
-            ],
+            ]
+            + [pl.BlockSpec(memory_space=pl.ANY)] * len(deps),
             out_specs=[
                 pl.BlockSpec((1, rows, width), pick),
                 pl.BlockSpec((1, heads, 1, rows), lambda i, *_: (i, 0, 0, 0)),
@@ -411,7 +502,7 @@
             transcendentals=count * heads * rows * total,
         ),
         name="attend",
-    )(lengths, offsets, queries, keys, values)
+    )(lengths, offsets, queries, keys, values, *deps)
 
 
 def attend_back_kernel(
@@ -455,7 +546,7 @@
         dv_ref[0, :, span] = dv_s[h][:, :depth]
 
 
-def attend_back(lengths, offsets, queries, keys, values, mixed, grads, lse, heads, tile):
+def attend_back(lengths, offsets, queries, keys, values, mixed, grads, lse, heads, tile, deps=()):
     count, rows, width = queries.shape
     total = keys.shape[1]
     depth = width // heads
@@ -464,11 +555,12 @@
     near = pl.BlockSpec((1, rows, width), pick)
     far = pl.BlockSpec((1, total, width), pick)
     return pl.pallas_call(
-        functools.partial(attend_back_kernel, heads, tile),
+        without(attend_back_kernel, 8, len(deps), heads, tile),
         grid_spec=pltpu.PrefetchScalarGridSpec(
             num_scalar_prefetch=2,
             grid=(count,),
-            in_specs=[near, far, far, near, near, pl.BlockSpec((1, heads, 1, rows), lambda i, *_: (i, 0, 0, 0))],
+            in_specs=[near, far, far, near, near, pl.BlockSpec((1, heads, 1, rows), lambda i, *_: (i, 0, 0, 0))]
+            + [pl.BlockSpec(memory_space=pl.ANY)] * len(deps),
             out_specs=[near, far, far],
             scratch_shapes=[
                 pltpu.VMEM((heads, rows, LANES), BF),
@@ -494,27 +586,134 @@
             transcendentals=count * heads * rows * total,
         ),
         name="attend_back",
-    )(lengths, offsets, queries, keys, values, mixed, grads, lse)
-
-
-def gram_of(moment):
-    block = moment.reshape(moment.shape[0] // ROW_BLOCK, ROW_BLOCK, moment.shape[1])
-    return jnp.einsum("nrc,nsc->nrs", block, block, precision=PRECISE)
-
-
-def polynomial(gram):
-    eye = jnp.eye(ROW_BLOCK, dtype=F32)
-    square = jnp.sum(gram * eye, axis=(1, 2))
-    scale = 1.0 / (jnp.sqrt(square) + NORM_EPS)
-    current = gram * (scale * scale)[:, None, None]
-    mul = functools.partial(jnp.einsum, "nrs,nst->nrt", precision=PRECISE)
-    total = None
+    )(lengths, offsets, queries, keys, values, mixed, grads, lse, *deps)
+
+
+def block_spots(counts):
+    total = sum(counts)
+    per = -(-total // 4)
+    spots = []
+    for matrix, count in enumerate(counts):
+        for block in range(count):
+            n = len(spots)
+            spots.append((matrix, block, n // per // 2, n // per % 2, n % per))
+    return spots, per
+
+
+def precise(left, right, dims):
+    return lax.dot_general(left, right, (dims, ((), ())), precision=PRECISE, preferred_element_type=F32)
+
+
+def muon_gram_kernel(groups, spots_ref, *refs):
+    count = sum(matrices for _, matrices in groups)
+    sums, momenta = refs[: len(groups)], refs[len(groups) : len(groups) + count]
+    outs = refs[len(groups) + count : len(groups) + 2 * count]
+    own_ref, other_ref = refs[len(groups) + 2 * count :]
+    n = 0
+    for (turned, matrices), sum_ref in zip(groups, sums):
+        grads = jnp.transpose(sum_ref[...]) if turned else sum_ref[...]
+        start = 0
+        for _ in range(matrices):
+            width = momenta[n].shape[1]
+            outs[n][...] = MUON_DECAY * momenta[n][...] + grads[:, start : start + width]
+            start += width
+            n += 1
+    spots, per = block_spots([out.shape[0] // ROW_BLOCK for out in outs])
+    if len(spots) < 4 * per:
+        own_ref[...] = jnp.zeros_like(own_ref)
+        other_ref[...] = jnp.zeros_like(other_ref)
+    for matrix, block, core, x, place_in in spots:
+        rows = outs[matrix][block * ROW_BLOCK : (block + 1) * ROW_BLOCK]
+        gram = precise(rows, rows, ((1,), (1,)))
+        away = lax.rem(spots_ref[1] + x, 2)
+
+        @pl.when(spots_ref[2] == core)
+        def _():
+            own_ref[away, place_in] = gram
+
+        @pl.when(spots_ref[2] != core)
+        def _():
+            other_ref[away, place_in] = gram
+
+
+def muon_gram(spots, groups):
+    momenta = [momentum for _, _, each in groups for momentum in each]
+    _, per = block_spots([momentum.shape[0] // ROW_BLOCK for momentum in momenta])
+    grams = jax.ShapeDtypeStruct((2, per, ROW_BLOCK, ROW_BLOCK), F32)
+    vmem = pl.BlockSpec(memory_space=pltpu.VMEM)
+    outs = pl.pallas_call(
+        functools.partial(muon_gram_kernel, [(turned, len(each)) for _, turned, each in groups]),
+        out_shape=[jax.ShapeDtypeStruct(momentum.shape, F32) for momentum in momenta] + [grams, grams],
+        in_specs=[pl.BlockSpec(memory_space=pltpu.SMEM)] + [vmem] * (len(groups) + len(momenta)),
+        out_specs=[vmem] * (len(momenta) + 2),
+        compiler_params=pltpu.CompilerParams(vmem_limit_bytes=VMEM_LIMIT),
+        name="muon_gram",
+    )(spots, *[group[0] for group in groups], *momenta)
+    return outs[:-2], outs[-2], outs[-1]
+
+
+def polynomial_kernel(count, *refs):
+    out = refs[count]
+    shape = (ROW_BLOCK, ROW_BLOCK)
+    eye = (lax.broadcasted_iota(jnp.int32, shape, 0) == lax.broadcasted_iota(jnp.int32, shape, 1)).astype(F32)
+    mul = lambda left, right: precise(left, right, ((1,), (0,)))
+    blocks = range(out.shape[0])
+    currents, scales, totals = [], [], []
+    for n in blocks:
+        gram = refs[0][n]
+        for ref in refs[1:count]:
+            gram = gram + ref[n]
+        square = jnp.sum(jnp.sum(gram * eye, axis=1, keepdims=True), axis=0, keepdims=True)
+        scale = 1.0 / (jnp.sqrt(square) + NORM_EPS)
+        scales.append(scale)
+        currents.append(gram * (scale * scale))
     for step in range(NS_STEPS):
-        factor = NS_A * eye + NS_B * current + NS_C * mul(current, current)
-        total = factor if total is None else mul(factor, total)
+        factors = [NS_A * eye + NS_B * a + NS_C * mul(a, a) for a in currents]
+        totals = factors if step == 0 else [mul(f, t) for f, t in zip(factors, totals)]
         if step + 1 < NS_STEPS:
-            current = mul(mul(factor, current), factor)
-    return total * scale[:, None, None]
+            currents = [mul(f, a) for f, a in zip(factors, currents)]
+            currents = [mul(a, f) for f, a in zip(factors, currents)]
+    for n in blocks:
+        out[n] = totals[n] * scales[n]
+
+
+def polynomial(parts):
+    vmem = pl.BlockSpec(memory_space=pltpu.VMEM)
+    return pl.pallas_call(
+        functools.partial(polynomial_kernel, len(parts)),
+        out_shape=jax.ShapeDtypeStruct(parts[0].shape, F32),
+        in_specs=[vmem] * len(parts),
+        out_specs=vmem,
+        compiler_params=pltpu.CompilerParams(vmem_limit_bytes=VMEM_LIMIT),
+        name="polynomial",
+    )(*parts)
+
+
+def muon_apply_kernel(rates, spots_ref, *refs):
+    count = len(rates)
+    parts, momenta, masters = refs[:4], refs[4 : 4 + count], refs[4 + count : 4 + 2 * count]
+    outs, factors = refs[4 + 2 * count : 4 + 3 * count], refs[4 + 3 * count]
+    for n in range(4):
+        factors[n] = parts[n][...]
+    spots, _ = block_spots([momentum.shape[0] // ROW_BLOCK for momentum in momenta])
+    for matrix, block, core, x, place_in in spots:
+        rows = slice(block * ROW_BLOCK, (block + 1) * ROW_BLOCK)
+        away = 2 * lax.rem(spots_ref[2] + core, 2) + lax.rem(spots_ref[1] + x, 2)
+        direction = precise(factors[away, place_in], momenta[matrix][rows], ((1,), (0,)))
+        outs[matrix][rows] = masters[matrix][rows] * (1.0 - WEIGHT_SHRINK) - rates[matrix] * direction
+
+
+def muon_apply(spots, factors, momenta, masters, rates):
+    vmem = pl.BlockSpec(memory_space=pltpu.VMEM)
+    return pl.pallas_call(
+        functools.partial(muon_apply_kernel, rates),
+        out_shape=[jax.ShapeDtypeStruct(master.shape, F32) for master in masters],
+        in_specs=[pl.BlockSpec(memory_space=pltpu.SMEM)] + [vmem] * (4 + 2 * len(masters)),
+        out_specs=[vmem] * len(masters),
+        scratch_shapes=[pltpu.VMEM((4,) + factors[0].shape, F32)],
+        compiler_params=pltpu.CompilerParams(vmem_limit_bytes=VMEM_LIMIT),
+        name="muon_apply",
+    )(spots, *factors, *momenta, *masters)
 
 
 def body(net, tokens, conditioning, heights, widths, upstream, *state):
@@ -530,32 +729,32 @@
 
     bounds = [0, 6 * width, 7 * width, 8 * width, 9 * width, 9 * width + hidden, 10 * width + hidden]
 
+    n_qkv, n_proj, n_fc1, n_fc2 = [w.shape[1] for w in (w_qkv, w_proj, w_fc1, w_fc2)]
+    unit_qkv, unit_fc2 = math.gcd(n_qkv, 8), math.gcd(n_fc2, 8)
+    unit_mid = math.gcd(math.gcd(n_proj, n_fc1), 8)
+    fold = hidden // width
+    layout_qkv, layout_mid, layout_fc2 = [(n_qkv, 1)], [(n_proj, 1), (n_fc1, 1)], [(n_fc2, fold)]
+    own_tokens = tokens.reshape(count, rows, width)
+    wires = net.y.gather(net.wire([w_qkv]))
+    units_qkv = net.joined(wires, unit_qkv, width)
+    token_pieces = [net.y.gather(tie(own_tokens[0], wires[-1]))]
+    wires = net.y.gather(tie(net.wire([w_proj, w_fc1]), token_pieces[0][-1]))
+    units_mid = net.joined(wires, unit_mid, width)
+    for i in range(1, count):
+        token_pieces.append(net.y.gather(tie(own_tokens[i], wires[-1])))
+    wires = net.y.gather(tie(net.wire([w_fc2]), token_pieces[-1][-1]))
+    units_fc2 = net.joined(wires, unit_fc2, width)
+
     ada_rows, ada_cols = w_ada.shape
     cond = conditioning.astype(F32).reshape(count, width)
     cond_act, silu_back = jax.vjp(sigmoid_linear, cond)
-    cond_low = cond_act.astype(BF)
-    cond_rows = lax.dynamic_slice_in_dim(cond_low, y * ada_rows, ada_rows, 1)
-    cond_all = net.to_dp(jnp.broadcast_to(cond_rows[None], (dp,) + cond_rows.shape))
-    cond_all = cond_all.reshape(dp * count, ada_rows)
-    bias_full = net.to_all(jnp.broadcast_to(biases, (dp, seq) + biases.shape)).reshape(-1)
+    cond_low = cond_act.astype(BF).astype(F32)
+    cond_parts = jnp.transpose(cond_low.reshape(count, seq, ada_rows), (1, 0, 2)).reshape(seq, -1)
+    parcel = jnp.concatenate([jnp.broadcast_to(biases, (seq,) + biases.shape), cond_parts], axis=1)
+    parcel = net.to_all(jnp.broadcast_to(parcel[None], (dp,) + parcel.shape))
+    bias_full = parcel[:, :, : biases.shape[0]].reshape(-1)
+    cond_all = parcel[:, 0, biases.shape[0] :].reshape(dp * count, ada_rows).astype(BF)
     b_ada, b_q, b_v, b_proj, b_fc1, b_fc2 = [bias_full[bounds[i] : bounds[i + 1]] for i in range(6)]
-
-    n_qkv, n_proj, n_fc1, n_fc2 = [w.shape[1] for w in (w_qkv, w_proj, w_fc1, w_fc2)]
-    unit_qkv = math.gcd(n_qkv, 8)
-    unit = math.gcd(math.gcd(n_proj, n_fc1), math.gcd(n_fc2, 8))
-    fold = hidden // width
-    layout_qkv = [(n_qkv, 1)]
-    layout = [(n_proj, 1), (n_fc1, 1), (n_fc2, fold)]
-    own_tokens = tokens.reshape(count, rows, width)
-    units_qkv = net.rows_joined([w_qkv], unit_qkv, width)
-    first_tokens = net.y.gather(after(own_tokens[0], units_qkv))
-    units = net.rows_joined(
-        [after(w, first_tokens[-1]) for w in (w_proj, w_fc1, w_fc2)], unit, width
-    )
-    other_tokens = [net.y.gather(after(own_tokens[i], units)) for i in range(1, count)]
-    all_tokens = jnp.stack([jnp.concatenate(t, axis=0) for t in [first_tokens] + other_tokens])
-    (t_qkv,), arrived = net.gather_weights(units_qkv, layout_qkv)
-    (t_proj, t_fc1, t_fc2), _ = net.gather_weights(after(units, *arrived), layout)
 
     low_ada = w_ada.astype(BF)
     partial = jnp.dot(cond_all, low_ada, preferred_element_type=F32).reshape(dp, 1, count, ada_cols)
@@ -565,44 +764,75 @@
         modulation[:, None, :], 6, axis=-1
     )
 
+    (t_qkv,), arrived = Staged(net.gather_steps(units_qkv, layout_qkv, 0.45)).finish()
+    mid = Staged(net.gather_steps(tie(units_mid, *arrived), layout_mid, 0.4))
+    late = None
+
     lengths = (heights * widths).reshape(count).astype(jnp.int32)
     offsets = jnp.stack([((y + s) % seq) * rows for s in range(seq)]).astype(jnp.int32)
     normed_all, inverse_all, attn_all, queries, keys, values, attended_low, log_total = [[] for _ in range(8)]
+    sent = mid.advance()
     for i in range(count):
-        normed, inverse = layer_norm(all_tokens[i].astype(F32))
+        normed, inverse = layer_norm(jnp.concatenate(token_pieces[i], axis=0).astype(F32))
         attn = (normed * (1.0 + scale_one[i]) + shift_one[i]).astype(BF)
+        attn = tie(attn, *sent)
         queries.append((dot_t(attn[None, :rows], t_qkv[:width]) + b_q).astype(BF))
         keys.append(dot_t(attn[None], t_qkv[width : 2 * width]).astype(BF))
         values.append((dot_t(attn[None], t_qkv[2 * width :]) + b_v).astype(BF))
-        mixed, lse = attend(lengths[i : i + 1], offsets, queries[i], keys[i], values[i], HEADS, 512)
+        if i == 0:
+            sent = mid.advance(keys[i])
+        elif late is None:
+            late = Staged(net.gather_steps(tie(units_fc2, keys[i]), layout_fc2, 0.4))
+            sent = late.advance()
+        mixed, lse = attend(lengths[i : i + 1], offsets, queries[i], keys[i], values[i], HEADS, 512, sent)
+        sent = mid.advance(mixed)
         normed_all.append(normed[:rows])
         inverse_all.append(inverse[:rows])
         attn_all.append(attn)
         attended_low.append(mixed[0])
         log_total.append(lse)
+    if late is None:
+        late = Staged(net.gather_steps(tie(units_fc2, keys[-1]), layout_fc2, 0.4))
+        late.advance()
     attended_low = jnp.stack(attended_low)
     attn_all = jnp.stack(attn_all)
     attn_own = attn_all[:, :rows]
+    t_proj, t_fc1 = mid.finish(log_total[-1])[0]
+    sent = late.advance(attended_low)
+
     inputs = own_tokens.astype(F32)
-    branch_one = dot_t(attended_low, t_proj) + b_proj
+    branch_one = dot_t(tie(attended_low, *sent), t_proj) + b_proj
     mixed_one = inputs + gate_one * branch_one
     normed_two, inverse_two = layer_norm(mixed_one)
     ffn_in = (normed_two * (1.0 + scale_two) + shift_two).astype(BF)
+    sent = late.advance(ffn_in)
+    ffn_in = tie(ffn_in, *sent)
     pre_act = dot_t(ffn_in, t_fc1) + b_fc1
     activated, gelu_back = jax.vjp(gelu_tanh, pre_act)
     activated_low = activated.astype(BF)
-    branch_two = dot_t(activated_low, t_fc2) + b_fc2
-    result = (mixed_one + gate_two * branch_two).astype(BF)
-
+    sent = late.advance(activated_low)
     grad_out = upstream.reshape(count, rows, width).astype(F32)
     grad_branch_two = (gate_two * grad_out).astype(BF)
-    grad_gate_two = jnp.sum(branch_two * grad_out, axis=1)
+    activated_low = tie(activated_low, *sent)
     terms_fc2 = [
         outer(grad_branch_two, activated_low[..., j * width : (j + 1) * width]) for j in range(fold)
     ]
+    back_fc2 = Staged(net.scatter_steps(terms_fc2, unit_fc2, width, layout_fc2, 0.4))
+    sent = back_fc2.advance()
+    (t_fc2,) = late.finish(terms_fc2[-1])[0]
+    branch_two = dot_t(tie(activated_low, *sent), t_fc2) + b_fc2
+    result = (mixed_one + gate_two * branch_two).astype(BF)
+
+    grad_gate_two = jnp.sum(branch_two * grad_out, axis=1)
+    sent = back_fc2.advance(branch_two)
+    grad_branch_two = tie(grad_branch_two, *sent)
     bias_fc2 = jnp.sum(grad_branch_two.astype(F32), axis=(0, 1))
     grad_pre = gelu_back(dot(grad_branch_two, t_fc2))[0].astype(BF)
+    sent = back_fc2.advance(grad_pre)
+    grad_pre = tie(grad_pre, *sent)
     term_fc1 = outer(grad_pre, ffn_in)
+    sent = back_fc2.advance(term_fc1)
+    grad_pre = tie(grad_pre, *sent)
     bias_fc1 = jnp.sum(grad_pre.astype(F32), axis=(0, 1))
     grad_ffn_in = dot(grad_pre, t_fc1)
     grad_shift_two = jnp.sum(grad_ffn_in, axis=1)
@@ -611,33 +841,58 @@
     grad_gate_one = jnp.sum(branch_one * grad_mixed, axis=1)
     grad_branch_one = (gate_one * grad_mixed).astype(BF)
     term_proj = outer(grad_branch_one, attended_low)
-    shard_proj, shard_fc1, shard_fc2 = net.scatter_weights([term_proj, term_fc1, *terms_fc2], unit, width, layout)
+    back_mid = Staged(net.scatter_steps([term_proj, term_fc1], unit_mid, width, layout_mid, 0.4))
+    sent = back_mid.advance() + back_fc2.advance(term_proj)
+    grad_branch_one = tie(grad_branch_one, *sent)
     bias_proj = jnp.sum(grad_branch_one.astype(F32), axis=(0, 1))
     grad_attended = dot(grad_branch_one, t_proj).astype(BF)
 
-    parts = [
-        attend_back(
+    grad_q, grad_k, grad_v, far_parts = [], [], [], []
+    sent = back_mid.advance(grad_attended)
+    for i in range(count):
+        dq, dk, dv = attend_back(
             lengths[i : i + 1], offsets, queries[i], keys[i], values[i], attended_low[i : i + 1],
-            grad_attended[i : i + 1], log_total[i], HEADS, 512,
+            grad_attended[i : i + 1], log_total[i], HEADS, 512, sent,
         )
-        for i in range(count)
-    ]
-    grad_q, grad_k, grad_v = [jnp.concatenate([part[k] for part in parts], axis=0) for k in range(3)]
+        sent = back_mid.advance(dq) + back_fc2.advance(dq)
+        grad_q.append(dq)
+        grad_k.append(dk)
+        grad_v.append(dv)
+        far_part = (
+            dot(dk[:, rows:], t_qkv[width : 2 * width]) + dot(dv[:, rows:], t_qkv[2 * width :])
+        ).astype(BF)[0]
+        far_steps = Staged(
+            net.y.scatter_steps(
+                lambda s, p=far_part: (
+                    jnp.zeros((rows, width), BF) if s == 0 else p[(s - 1) * rows : s * rows]
+                )
+            )
+        )
+        sent = sent + far_steps.advance()
+        far_parts.append(far_steps)
+    grad_q, grad_k, grad_v = [jnp.concatenate(each, axis=0) for each in (grad_q, grad_k, grad_v)]
+    grad_q = tie(grad_q, *sent)
     term_qkv = jnp.concatenate(
         [outer(grad_q, attn_own), outer(grad_k, attn_all), outer(grad_v, attn_all)], axis=0
     )
-    (shard_qkv,) = net.scatter_weights([term_qkv], unit_qkv, width, layout_qkv)
+    back_qkv = Staged(net.scatter_steps([term_qkv], unit_qkv, width, layout_qkv, 0.45))
+    sent = back_qkv.advance() + back_mid.advance(term_qkv)
+    grad_q = tie(grad_q, *sent)
     bias_q = jnp.sum(grad_q.astype(F32), axis=(0, 1))
     bias_v = jnp.sum(grad_v.astype(F32), axis=(0, 1))
-    part_in = dot(grad_k, t_qkv[width : 2 * width]) + dot(grad_v, t_qkv[2 * width :])
-    own_part = part_in[:, :rows] + dot(grad_q, t_qkv[:width])
-    grad_attn_in = net.y.scatter_sum(
-        lambda s: own_part if s == 0 else part_in[:, s * rows : (s + 1) * rows].astype(BF)
+    own_part = (
+        dot(grad_q, t_qkv[:width])
+        + dot(grad_k[:, :rows], t_qkv[width : 2 * width])
+        + dot(grad_v[:, :rows], t_qkv[2 * width :])
     )
+    sent = back_qkv.advance(own_part) + back_mid.advance(own_part)
+    far_sum = jnp.stack([steps.finish() for steps in far_parts])
+    grad_attn_in = tie(own_part, *sent) + far_sum
     normed_one, inverse_one = jnp.stack(normed_all), jnp.stack(inverse_all)
     grad_shift_one = jnp.sum(grad_attn_in, axis=1)
     grad_scale_one = jnp.sum(grad_attn_in * normed_one, axis=1)
     grad_inputs = grad_mixed + norm_back(normed_one, inverse_one, grad_attn_in * (1.0 + scale_one))
+    grad_inputs = grad_inputs.astype(BF).reshape(tokens.shape)
 
     grad_mod_local = jnp.concatenate(
         [grad_shift_one, grad_scale_one, grad_gate_one, grad_shift_two, grad_scale_two, grad_gate_two], axis=-1
@@ -647,6 +902,30 @@
     sent = jnp.broadcast_to(sent, (dp, seq, count, ada_cols))
     mod_cols = jnp.sum(net.to_all(sent), axis=1).astype(BF).reshape(dp * count, ada_cols)
     shard_ada = jnp.einsum("sr,sc->rc", cond_all, mod_cols, preferred_element_type=F32)
+
+    rate_of = {
+        "qkv": math.sqrt(3.0), "proj": 1.0, "fc1": math.sqrt(hidden / width),
+        "fc2": math.sqrt(width / hidden), "ada": math.sqrt(6.0),
+    }
+    sum_mid, sum_fc2 = back_mid.finish(), back_fc2.finish()
+    early = Staged(
+        net.muon_steps(
+            [(sum_mid, True, [momenta[1], momenta[2]]), (sum_fc2, True, [momenta[3]])],
+            [w_proj, w_fc1, w_fc2],
+            [rate_of["proj"], rate_of["fc1"], rate_of["fc2"]],
+        )
+    )
+    (next_proj, next_fc1, next_fc2), (new_proj, new_fc1, new_fc2) = early.finish()
+    sum_qkv = back_qkv.finish()
+    last = Staged(
+        net.muon_steps(
+            [(sum_qkv, True, [momenta[0]]), (shard_ada, False, [momenta[4]])],
+            [w_qkv, w_ada],
+            [rate_of["qkv"], rate_of["ada"]],
+        )
+    )
+    (next_qkv, next_ada), (new_qkv, new_ada) = last.finish()
+
     cond_part = jnp.einsum("sc,rc->sr", mod_cols, low_ada, preferred_element_type=F32)
     cond_part = cond_part.reshape(dp, 1, count, ada_rows)
     cond_part = jnp.sum(net.to_all(jnp.broadcast_to(cond_part, (dp, seq, count, ada_rows))), axis=0)
@@ -661,37 +940,12 @@
     new_biases = biases * (1.0 - ADAM_RATE * ADAM_DECAY) - ADAM_RATE * first_hat / (
         jnp.sqrt(second_hat) + ADAM_EPS
     )
-
-    shards = (shard_qkv, shard_proj, shard_fc1, shard_fc2, shard_ada)
-    moments = [MUON_DECAY * momentum + shard for momentum, shard in zip(momenta, shards)]
-    grams = [gram_of(moment) for moment in moments]
-    directions = [None] * 5
-    for group in ((3, 2, 1), (0, 4)):
-        stack = jnp.concatenate([grams[i] for i in group], axis=0)
-        blocks = stack.shape[0]
-        each = -(-blocks // dp)
-        stack = jnp.pad(stack, ((0, each * dp - blocks), (0, 0), (0, 0)))
-        mine = jnp.sum(net.to_dp(stack.reshape(dp, each, ROW_BLOCK, ROW_BLOCK)), axis=0)
-        factors = jnp.broadcast_to(polynomial(mine)[None], (dp, each, ROW_BLOCK, ROW_BLOCK))
-        factors = net.to_dp(factors).reshape(dp * each, ROW_BLOCK, ROW_BLOCK)
-        start = 0
-        for i in group:
-            size = grams[i].shape[0]
-            block = moments[i].reshape(size, ROW_BLOCK, -1)
-            direction = jnp.einsum("nrs,nsc->nrc", factors[start : start + size], block, precision=PRECISE)
-            directions[i] = direction.reshape(moments[i].shape)
-            start += size
-    rates = (math.sqrt(3.0), 1.0, math.sqrt(hidden / width), math.sqrt(width / hidden), math.sqrt(6.0))
-    new_weights = [
-        weight * (1.0 - WEIGHT_SHRINK) - rate * direction
-        for weight, rate, direction in zip(masters, rates, directions)
-    ]
     return (
         result.reshape(tokens.shape),
-        grad_inputs.astype(BF).reshape(tokens.shape),
+        grad_inputs,
         grad_cond.reshape(conditioning.shape),
-        *new_weights,
-        *moments,
+        new_qkv, new_proj, new_fc1, new_fc2, new_ada,
+        next_qkv, next_proj, next_fc1, next_fc2, next_ada,
         new_biases,
         next_first,
         next_second,

time: 1380 us -> 1110 us (0.80)
  waiting for transfers between devices: 510 us -> 138 us
  Pallas kernels: 142 us -> 242 us
  other arithmetic: 185 us -> 148 us
  starting transfers between devices: 106 us -> 141 us
  matrix products: 269 us -> 241 us
  local copies, waits for them, and re-layouts: 153 us -> 181 us
    all_to_all x5 -> x0, waiting for transfers between devices: 260 us -> none  [to_dp(): return lax.all_to_all(value, 'dp', 0, 0, tiled=True)]
    pallas_call x3 -> x78, Pallas kernels: 117 us -> 215 us  [the longest x2 90 us: attend_back(): pl.pallas_call(without(attend_back_kernel, 8, len(deps), heads, tile), gr...]
    ppermute x53 -> x95, waiting for transfers between devices: 215 us -> 124 us  [send(): return lax.ppermute(value, self.name, pairs)]
    unnamed x250 -> x359, local copies, waits for them, and re-layouts: 44.2 us -> 102 us
    ppermute x53 -> x95, starting transfers between devices: 47.4 us -> 105 us  [send(): return lax.ppermute(value, self.name, pairs)]
    pallas_call x1 -> x0, other arithmetic: 44.6 us -> none  [attend_back(): pl.pallas_call(functools.partial(attend_back_kernel, heads, tile), grid_s...]
    dot_general x44 -> x0, matrix products: 37.1 us -> none  [the longest x5 9.95 us: body(): jnp.einsum('nrs,nsc->nrc', factors[start:start + size], block, precision=...]
    all_to_all x5 -> x0, starting transfers between devices: 32.6 us -> none  [to_dp(): return lax.all_to_all(value, 'dp', 0, 0, tiled=True)]
  transfers between devices with their start and end apart: 63 -> 100, of which waited for: 21 -> 23; matrix products, arithmetic and copies ran while one was open for 25% -> 41% of each run, Pallas kernels for 6% -> 20%
where the time goes in v3:
time: 1110 us; the launch traced here: 1090 us
  Pallas kernels  242 us (22%)
  matrix products  241 us (22%)
  local copies, waits for them, and re-layouts  181 us (16%)
  other arithmetic  148 us (13%)
  starting transfers between devices  141 us (13%)
  waiting for transfers between devices  138 us (12%)
    ppermute x95, waiting for transfers between devices, send(): return lax.ppermute(value, self.name, pairs)  124 us
    ppermute x95, starting transfers between devices, send(): return lax.ppermute(value, self.name, pairs)  105 us
    unnamed x359, local copies, waits for them, and re-layouts  102 us
    dot_general x10, matrix products, dot(): return jnp.einsum('srn,nk->srk', left, right, preferred_element_type=F32)  90.4 us
    pallas_call x2, Pallas kernels, attend_back(): pl.pallas_call(without(attend_back_kernel, 8, len(deps), heads, tile), gr...  90 us
    dot_general x9, matrix products, dot_t(): return jnp.einsum('srk,nk->srn', left, right, preferred_element_type=F32)  89.7 us
    pallas_call x2, Pallas kernels, attend(): pl.pallas_call(without(attend_kernel, 5, len(deps), heads, tile), grid_sp...  64.2 us
    dot_general x9, matrix products, outer(): jnp.einsum('srn,srk->nk', left, right, preferred_element_type=F32)  58.7 us
  transfers between devices with their start and end apart: 100, of which 23 were waited for; matrix products, arithmetic and copies ran while one was open for 41% of the time, Pallas kernels for 20%

profile of v3, /device:TPU:11, one launch (start us, length us, event | category | flops | bytes accessed | tf_op | source)
XLA Modules:
  0.0 1093.2 jit_solution(9409143516985481797)
XLA Ops:
  37.9 13.7 %all-to-all-done.1 = f32[32,2,432]{2,1,0:T(2,128)S(1)} async-done(((f32[32,2,432]{2,1,0:T(2,128)}), f32[32,2,432]{2,1,0:T(2,128)S(1)}, u32[]{:S(2)}, u32[]{:S(2)}) %all-to-all-start.1) | async-done | bytes 110624 | tf_op jit(solution)/shard_map/all_to_all | solution.py:354
  123.3 32.2 %attend.2 = (bf16[1,512,1152]{2,1,0:T(8,128)(2,1)}, f32[1,16,1,512]{3,2,1,0:T(1,128)}) custom-call(s32[1]{0:T(128)} %bitcast.8.refs_0_, s32[2]{0:T(128)} %pad_add_fusion.refs_1_, bf16[1,512,1152]{2,1,0:T(8,128)(2,1)} %fusion.34.refs_2_, bf16[1,1024,1152]{2,1,0:T(8,128)(2,1)} %fusion.27.refs_1_.refs_3_, bf16[1,1024,1152]{2,1,0:T(8,128)(2,1)} %fusion.25.refs_4_, ...), custom_call_target="tpu_custom_call" | custom-call | flops 4294967296 | bytes 7077888 | tf_op jit(solution)/shard_map/attend/pallas_call | solution.py:472
  199.6 32.0 %attend.3 = (bf16[1,512,1152]{2,1,0:T(8,128)(2,1)}, f32[1,16,1,512]{3,2,1,0:T(1,128)}) custom-call(s32[1]{0:T(128)} %bitcast.34.refs_0_, s32[2]{0:T(128)} %pad_add_fusion.refs_1_, bf16[1,512,1152]{2,1,0:T(8,128)(2,1)} %fusion.33.refs_2_, bf16[1,1024,1152]{2,1,0:T(8,128)(2,1)} %fusion.28.refs_1_.refs_3_, bf16[1,1024,1152]{2,1,0:T(8,128)(2,1)} %fusion.26.refs_4_, ...), custom_call_target="tpu_custom_call" | custom-call | flops 4294967296 | bytes 7077888 | tf_op jit(solution)/shard_map/attend/pallas_call | solution.py:472
  247.4 10.5 place.4
  257.9 9.0 fusion.123
  276.5 10.7 collective-permute-done.40.refs_0_
  288.0 24.0 %multiply_convert_fusion = (bf16[2,512,4608]{2,1,0:T(8,128)(2,1)}, f32[2,512,4608]{2,1,0:T(8,128)}) fusion(f32[4608]{0:T(1024)S(1)} %copy-done.133, bf16[2,512,1152]{2,1,0:T(8,128)(2,1)} %tie.96, bf16[4608,1152,1]{1,0,2:T(8,128)(2,1)} %bitcast.482), kind=kOutput, calls=%fused_computation.12 | convolution fusion | flops 10918821888 | bytes 41306112 | tf_op jit(solution)/shard_map/srk,nk->srn/dot_general | solution.py:381
  357.1 9.2 place.5
  366.2 18.2 %convolution_add_fusion.refs_1_ = f32[2,512,1152]{2,1,0:T(8,128)} fusion(bf16[2,512,4608]{2,1,0:T(8,128)(2,1)} %tie.101, bf16[1152,4608,1]{1,0,2:T(8,128)(2,1)} %bitcast.427, f32[1152]{0:T(1024)S(1)} %copy-done.140), kind=kOutput, calls=%fused_computation.50 | convolution fusion | flops 10872815616 | bytes 24777216 | tf_op jit(solution)/shard_map/srk,nk->srn/dot_general | solution.py:381
  398.6 28.6 %fusion.7.refs_1_.refs_0_ = bf16[2,512,4608]{2,1,0:T(8,128)(2,1)} fusion(f32[2,512,4608]{2,1,0:T(8,128)} %get-tuple-element.268, bf16[2,512,1152]{2,1,0:T(8,128)(2,1)} %tie.109, bf16[1152,4608,1]{1,0,2:T(8,128)(2,1)} %bitcast.428, f32[4608]{0:T(1024)S(1)} %copy-done.133), kind=kOutput, calls=%fused_computation.10 | convolution fusion | flops 10970726400 | bytes 41306112 | tf_op jit(solution)/shard_map/srn,nk->srk/dot_general | solution.py:385
  439.7 18.4 %fusion.refs_1_ = bf16[4608,1152]{1,0:T(8,128)(2,1)} fusion(bf16[2,512,4608]{2,1,0:T(8,128)(2,1)} %tie.112.refs_0_, bf16[2,512,1152]{2,1,0:T(8,128)(2,1)S(1)} %copy-done.3), kind=kOutput, calls=%fused_computation.3 | convolution fusion | flops 10876944384 | bytes 22413312 | tf_op jit(solution)/shard_map/srn,srk->nk/dot_general | solution.py:389
  458.1 8.9 constant_dynamic-slice_fusion.6
  472.1 20.2 %multiply_reduce_fusion = (f32[2,1152]{1,0:T(2,128)}, f32[2,512]{1,0:T(2,128)S(1)}, f32[2,512]{1,0:T(2,128)S(1)}, f32[2,1152]{1,0:T(2,128)}, f32[2,512,1152]{2,1,0:T(8,128)S(1)}) fusion(f32[2,512,1152]{2,1,0:T(8,128)} %copy-done.6, f32[2,512]{1,0:T(2,128)S(1)} %copy-done.125, f32[2,512]{1,0:T(2,128)S(1)} %copy-done.123, f32[2,1152]{1,0:T(2,128)S(1)} %copy-done.119, ...), kind=kOutput, calls=%fused_computation.61 | convolution fusion | flops 10882246656 | bytes 29535232 | tf_op jit(solution)/shard_map/srn,nk->srk/dot_general | solution.py:385
  562.1 45.0 %attend_back.2 = (bf16[1,512,1152]{2,1,0:T(8,128)(2,1)}, bf16[1,1024,1152]{2,1,0:T(8,128)(2,1)}, bf16[1,1024,1152]{2,1,0:T(8,128)(2,1)}) custom-call(s32[1]{0:T(128)} %bitcast.8.refs_0_, s32[2]{0:T(128)} %pad_add_fusion.refs_1_, bf16[1,512,1152]{2,1,0:T(8,128)(2,1)} %fusion.34.refs_2_, bf16[1,1024,1152]{2,1,0:T(8,128)(2,1)} %fusion.27.refs_1_.refs_3_, ...), custom_call_target="tpu_custom_call" | custom-call | flops 10737418240 | bytes 14155776 | tf_op jit(solution)/shard_map/attend_back/pallas_call | solution.py:557
  630.2 45.0 %attend_back.3 = (bf16[1,512,1152]{2,1,0:T(8,128)(2,1)}, bf16[1,1024,1152]{2,1,0:T(8,128)(2,1)}, bf16[1,1024,1152]{2,1,0:T(8,128)(2,1)}) custom-call(s32[1]{0:T(128)} %bitcast.34.refs_0_, s32[2]{0:T(128)} %pad_add_fusion.refs_1_, bf16[1,512,1152]{2,1,0:T(8,128)(2,1)} %fusion.33.refs_2_, bf16[1,1024,1152]{2,1,0:T(8,128)(2,1)} %fusion.28.refs_1_.refs_3_, ...), custom_call_target="tpu_custom_call" | custom-call | flops 10737418240 | bytes 14155776 | tf_op jit(solution)/shard_map/attend_back/pallas_call | solution.py:557
  695.3 8.3 fusion.16
  725.1 14.9 %pad_maximum_fusion.refs_1_ = bf16[3456,1152]{1,0:T(8,128)(2,1)S(1)} fusion(bf16[1152,1152]{1,0:T(8,128)(2,1)S(1)} %copy-done.69, bf16[1152,1152]{1,0:T(8,128)(2,1)S(1)} %copy-done.68, bf16[1152,1152]{1,0:T(8,128)(2,1)S(1)} %fusion.14), kind=kLoop, calls=%fused_computation.24 | loop fusion | flops 23887872 | bytes 15925248 | tf_op jit(solution)/shard_map/concatenate | solution.py:875
  769.1 15.4 %muon_gram.3 = (f32[576,72]{1,0:T(8,128)}, f32[576,288]{1,0:T(8,128)}, f32[2304,72]{1,0:T(8,128)}, f32[2,6,144,144]{3,2,1,0:T(8,128)}, f32[2,6,144,144]{3,2,1,0:T(8,128)}) custom-call(s32[3]{0:T(128)} %pad_add_fusion.1.refs_0_.spots_ref, f32[360,576]{1,0:T(8,128)} %convert_add_fusion.14.refs_0_, f32[72,2304]{1,0:T(8,128)} %convert_add_fusion.16.refs_1_, ...), custom_call_target="tpu_custom_call" | custom-call | tf_op jit(solution)/shard_map/muon_gram/pallas_call | solution.py:644
  828.3 12.2 %collective-permute-done.90.refs_3_ = f32[6,144,144]{2,1,0:T(8,128)S(1)} collective-permute-done((f32[6,144,144]{2,1,0:T(8,128)S(1)}, f32[6,144,144]{2,1,0:T(8,128)S(1)}, u32[]{:S(2)}, u32[]{:S(2)}) %collective-permute-start.90) | collective-permute-done | bytes 497696 | tf_op jit(solution)/shard_map/ppermute | solution.py:47
  850.8 13.7 %collective-permute-done.89.refs_1_ = f32[6,144,144]{2,1,0:T(8,128)S(1)} collective-permute-done((f32[6,144,144]{2,1,0:T(8,128)S(1)}, f32[6,144,144]{2,1,0:T(8,128)S(1)}, u32[]{:S(2)}, u32[]{:S(2)}) %collective-permute-start.89) | collective-permute-done | bytes 497696 | tf_op jit(solution)/shard_map/ppermute | solution.py:47
  865.4 10.3 collective-permute-done.91.refs_2_
  875.7 16.3 %polynomial.3.refs_0_ = f32[6,144,144]{2,1,0:T(8,128)} custom-call(f32[6,144,144]{2,1,0:T(8,128)} %copy-done.60, f32[6,144,144]{2,1,0:T(8,128)} %copy-done.98, f32[6,144,144]{2,1,0:T(8,128)} %collective-permute-done.91.refs_2_, f32[6,144,144]{2,1,0:T(8,128)} %copy-done.97), custom_call_target="tpu_custom_call" | custom-call | tf_op jit(solution)/shard_map/polynomial/pallas_call | solution.py:682
  963.6 10.0 collective-permute-done.74
  1035.2 10.6 all-to-all-start.3
  (827 shorter events, 653.2 us)
Async XLA Ops:
  86.0 75.1 %collective-permute-start.19 = (bf16[512,1152]{1,0:T(8,128)(2,1)}, bf16[512,1152]{1,0:T(8,128)(2,1)S(1)}, u32[]{:S(2)}, u32[]{:S(2)}) collective-permute-start(bf16[512,1152]{1,0:T(8,128)(2,1)} %tie.74), channel_id=1, source_target_pairs={{0,1},{1,0},{2,3},{3,2},{4,5},{5,4},{6,7},{7,6},{8,9},{9,8},{10,11... | collective-permute-start | bytes 3538952 | tf_op jit(solution)/shard_map/ppermute | solution.py:47
  105.0 91.7 %collective-permute-start.28 = (bf16[2,27,8,1152]{3,2,1,0:T(8,128)(2,1)S(1)}, bf16[2,27,8,1152]{3,2,1,0:T(8,128)(2,1)}, u32[]{:S(2)}, u32[]{:S(2)}) collective-permute-start(bf16[2,27,8,1152]{3,2,1,0:T(8,128)(2,1)S(1)} %pad_maximum_fusion.12.refs_6_.refs_7_.refs_3_), channel_id=1, source_target_pairs={{0,8},{2,10},{4,12},{6,14},{8,16},{10,18},{12,20},{14,22},{16,24},... | collective-permute-start | bytes 2985992 | tf_op jit(solution)/shard_map/ppermute | solution.py:47
  105.6 65.0 %collective-permute-start.22 = (bf16[2,27,8,1152]{3,2,1,0:T(8,128)(2,1)S(1)}, bf16[2,27,8,1152]{3,2,1,0:T(8,128)(2,1)}, u32[]{:S(2)}, u32[]{:S(2)}) collective-permute-start(bf16[2,27,8,1152]{3,2,1,0:T(8,128)(2,1)S(1)} %pad_maximum_fusion.12.refs_6_.refs_7_.refs_3_), channel_id=1, source_target_pairs={{0,24},{2,26},{4,28},{6,30},{8,0},{10,2},{12,4},{14,6},{16,8},{18,... | collective-permute-start | bytes 2985992 | tf_op jit(solution)/shard_map/ppermute | solution.py:47
  115.9 119.2 %collective-permute-start.31 = (bf16[2,27,8,1152]{3,2,1,0:T(8,128)(2,1)S(1)}, bf16[2,27,8,1152]{3,2,1,0:T(8,128)(2,1)}, u32[]{:S(2)}, u32[]{:S(2)}) collective-permute-start(bf16[2,27,8,1152]{3,2,1,0:T(8,128)(2,1)S(1)} %pad_maximum_fusion.12.refs_6_.refs_7_.refs_3_), channel_id=1, source_target_pairs={{0,2},{2,0},{4,6},{6,4},{8,10},{10,8},{12,14},{14,12},{16,18},{18,... | collective-permute-start | bytes 2985992 | tf_op jit(solution)/shard_map/ppermute | solution.py:47
  117.6 40.3 %collective-permute-start.21 = (bf16[18,8,1152]{2,1,0:T(8,128)(2,1)}, bf16[18,8,1152]{2,1,0:T(8,128)(2,1)}, u32[]{:S(2)}, u32[]{:S(2)}) collective-permute-start(bf16[18,8,1152]{2,1,0:T(8,128)(2,1)} %tie.72.refs_5_), channel_id=1, source_target_pairs={{0,8},{2,10},{4,12},{6,14},{8,16},{10,18},{12,20},{14,22},{16,24},... | collective-permute-start | bytes 995336 | tf_op jit(solution)/shard_map/ppermute | solution.py:47
  184.7 46.9 %collective-permute-start.27 = (bf16[2,27,8,1152]{3,2,1,0:T(8,128)(2,1)}, bf16[2,27,8,1152]{3,2,1,0:T(8,128)(2,1)}, u32[]{:S(2)}, u32[]{:S(2)}) collective-permute-start(bf16[2,27,8,1152]{3,2,1,0:T(8,128)(2,1)} %tie.77.refs_2_.refs_4_), channel_id=1, source_target_pairs={{0,24},{2,26},{4,28},{6,30},{8,0},{10,2},{12,4},{14,6},{16,8},{18,... | collective-permute-start | bytes 2985992 | tf_op jit(solution)/shard_map/ppermute | solution.py:47
  191.2 44.5 %collective-permute-start.25 = (bf16[22,8,1152]{2,1,0:T(8,128)(2,1)}, bf16[22,8,1152]{2,1,0:T(8,128)(2,1)}, u32[]{:S(2)}, u32[]{:S(2)}) collective-permute-start(bf16[22,8,1152]{2,1,0:T(8,128)(2,1)} %get-tuple-element.248.refs_7_), channel_id=1, source_target_pairs={{0,4},{2,6},{4,0},{6,2},{8,12},{10,14},{12,8},{14,10},{16,20},{18,... | collective-permute-start | bytes 1216520 | tf_op jit(solution)/shard_map/ppermute | solution.py:47
  196.7 38.9 %collective-permute-start.35 = (bf16[14,8,1152]{2,1,0:T(8,128)(2,1)}, bf16[14,8,1152]{2,1,0:T(8,128)(2,1)}, u32[]{:S(2)}, u32[]{:S(2)}) collective-permute-start(bf16[14,8,1152]{2,1,0:T(8,128)(2,1)} %get-tuple-element.246.refs_5_.refs_6_), channel_id=1, source_target_pairs={{0,24},{2,26},{4,28},{6,30},{8,0},{10,2},{12,4},{14,6},{16,8},{18,... | collective-permute-start | bytes 774152 | tf_op jit(solution)/shard_map/ppermute | solution.py:47
  247.2 40.1 %collective-permute-start.40 = (bf16[2,22,8,1152]{3,2,1,0:T(8,128)(2,1)S(1)}, bf16[2,22,8,1152]{3,2,1,0:T(8,128)(2,1)}, u32[]{:S(2)}, u32[]{:S(2)}) collective-permute-start(bf16[2,22,8,1152]{3,2,1,0:T(8,128)(2,1)S(1)} %copy-done.16), channel_id=1, source_target_pairs={{0,8},{2,10},{4,12},{6,14},{8,16},{10,18},{12,20},{14,22},{16,24},... | collective-permute-start | bytes 2433032 | tf_op jit(solution)/shard_map/ppermute | solution.py:47
  271.1 40.9 %collective-permute-start.39 = (bf16[2,22,8,1152]{3,2,1,0:T(8,128)(2,1)}, bf16[2,22,8,1152]{3,2,1,0:T(8,128)(2,1)S(1)}, u32[]{:S(2)}, u32[]{:S(2)}) collective-permute-start(bf16[2,22,8,1152]{3,2,1,0:T(8,128)(2,1)} %tie.95.refs_2_.refs_4_), channel_id=1, source_target_pairs={{0,24},{2,26},{4,28},{6,30},{8,0},{10,2},{12,4},{14,6},{16,8},{18,... | collective-permute-start | bytes 2433032 | tf_op jit(solution)/shard_map/ppermute | solution.py:47
  336.8 47.6 %collective-permute-start.47 = (bf16[4,2,36,8,1152]{4,3,2,1,0:T(8,128)(2,1)}, bf16[4,2,36,8,1152]{4,3,2,1,0:T(8,128)(2,1)}, u32[]{:S(2)}, u32[]{:S(2)}) collective-permute-start(bf16[4,2,36,8,1152]{4,3,2,1,0:T(8,128)(2,1)} %pad_maximum_fusion.2.refs_1_), channel_id=1, source_target_pairs={{0,2},{2,0},{4,6},{6,4},{8,10},{10,8},{12,14},{14,12},{16,18},{18,... | collective-permute-start | bytes 15925256 | tf_op jit(solution)/shard_map/ppermute | solution.py:47
  398.6 59.5 %collective-permute-start.51 = (bf16[2,22,8,1152]{3,2,1,0:T(8,128)(2,1)}, bf16[2,22,8,1152]{3,2,1,0:T(8,128)(2,1)}, u32[]{:S(2)}, u32[]{:S(2)}) collective-permute-start(bf16[2,22,8,1152]{3,2,1,0:T(8,128)(2,1)} %get-tuple-element.209.refs_2_), channel_id=1, source_target_pairs={{0,8},{2,10},{4,12},{6,14},{8,16},{10,18},{12,20},{14,22},{16,24},... | collective-permute-start | bytes 2433032 | tf_op jit(solution)/shard_map/ppermute | solution.py:47
  539.8 80.1 %collective-permute-start.86 = (bf16[72,2304]{1,0:T(8,128)(2,1)}, bf16[72,2304]{1,0:T(8,128)(2,1)}, u32[]{:S(2)}, u32[]{:S(2)}) collective-permute-start(bf16[72,2304]{1,0:T(8,128)(2,1)} %bitcast.415.refs_2_), channel_id=1, source_target_pairs={{0,1},{1,0},{2,3},{3,2},{4,5},{5,4},{6,7},{7,6},{8,9},{9,8},{10,11... | collective-permute-start | bytes 995336 | tf_op jit(solution)/shard_map/ppermute | solution.py:47
  557.8 68.2 %collective-permute-start.57 = (bf16[4,18,8,1152]{3,2,1,0:T(8,128)(2,1)}, bf16[4,18,8,1152]{3,2,1,0:T(8,128)(2,1)}, u32[]{:S(2)}, u32[]{:S(2)}) collective-permute-start(bf16[4,18,8,1152]{3,2,1,0:T(8,128)(2,1)} %dynamic-slice_bitcast_fusion.2.refs_8_), channel_id=1, source_target_pairs={{0,4},{2,6},{4,0},{6,2},{8,12},{10,14},{12,8},{14,10},{16,20},{18,... | collective-permute-start | bytes 3981320 | tf_op jit(solution)/shard_map/ppermute | solution.py:47
  559.0 62.8 %collective-permute-start.58 = (bf16[2,27,8,1152]{3,2,1,0:T(8,128)(2,1)}, bf16[2,27,8,1152]{3,2,1,0:T(8,128)(2,1)}, u32[]{:S(2)}, u32[]{:S(2)}) collective-permute-start(bf16[2,27,8,1152]{3,2,1,0:T(8,128)(2,1)} %get-tuple-element.208.refs_9_), channel_id=1, source_target_pairs={{0,24},{2,26},{4,28},{6,30},{8,0},{10,2},{12,4},{14,6},{16,8},{18,... | collective-permute-start | bytes 2985992 | tf_op jit(solution)/shard_map/ppermute | solution.py:47
  619.9 90.4 %collective-permute-start.60 = (bf16[2,27,8,1152]{3,2,1,0:T(8,128)(2,1)}, bf16[2,27,8,1152]{3,2,1,0:T(8,128)(2,1)}, u32[]{:S(2)}, u32[]{:S(2)}) collective-permute-start(bf16[2,27,8,1152]{3,2,1,0:T(8,128)(2,1)} %get-tuple-element.207.refs_9_), channel_id=1, source_target_pairs={{0,8},{2,10},{4,12},{6,14},{8,16},{10,18},{12,20},{14,22},{16,24},... | collective-permute-start | bytes 2985992 | tf_op jit(solution)/shard_map/ppermute | solution.py:47
  624.5 90.5 %collective-permute-start.61 = (bf16[2,27,8,1152]{3,2,1,0:T(8,128)(2,1)}, bf16[2,27,8,1152]{3,2,1,0:T(8,128)(2,1)}, u32[]{:S(2)}, u32[]{:S(2)}) collective-permute-start(bf16[2,27,8,1152]{3,2,1,0:T(8,128)(2,1)} %fusion.58.refs_10_), channel_id=1, source_target_pairs={{0,24},{2,26},{4,28},{6,30},{8,0},{10,2},{12,4},{14,6},{16,8},{18,... | collective-permute-start | bytes 2985992 | tf_op jit(solution)/shard_map/ppermute | solution.py:47
  629.5 82.5 %collective-permute-start.59 = (bf16[18,8,1152]{2,1,0:T(8,128)(2,1)S(1)}, bf16[18,8,1152]{2,1,0:T(8,128)(2,1)S(1)}, u32[]{:S(2)}, u32[]{:S(2)}) collective-permute-start(bf16[18,8,1152]{2,1,0:T(8,128)(2,1)S(1)} %get-tuple-element.232.refs_8_), channel_id=1, source_target_pairs={{0,8},{2,10},{4,12},{6,14},{8,16},{10,18},{12,20},{14,22},{16,24},... | collective-permute-start | bytes 995336 | tf_op jit(solution)/shard_map/ppermute | solution.py:47
  787.9 126.4 %collective-permute-start.65 = (bf16[4,2,27,8,1152]{4,3,2,1,0:T(8,128)(2,1)}, bf16[4,2,27,8,1152]{4,3,2,1,0:T(8,128)(2,1)}, u32[]{:S(2)}, u32[]{:S(2)}) collective-permute-start(bf16[4,2,27,8,1152]{4,3,2,1,0:T(8,128)(2,1)} %get-tuple-element.202.refs_1_), channel_id=1, source_target_pairs={{0,2},{2,0},{4,6},{6,4},{8,10},{10,8},{12,14},{14,12},{16,18},{18,... | collective-permute-start | bytes 11943944 | tf_op jit(solution)/shard_map/ppermute | solution.py:47
  849.3 72.3 %collective-permute-start.66 = (bf16[512,1152]{1,0:T(8,128)(2,1)}, bf16[512,1152]{1,0:T(8,128)(2,1)}, u32[]{:S(2)}, u32[]{:S(2)}) collective-permute-start(bf16[512,1152]{1,0:T(8,128)(2,1)} %fusion.31.refs_11_), channel_id=1, source_target_pairs={{0,1},{1,0},{2,3},{3,2},{4,5},{5,4},{6,7},{7,6},{8,9},{9,8},{10,11... | collective-permute-start | bytes 3538952 | tf_op jit(solution)/shard_map/ppermute | solution.py:47
  849.7 74.8 %collective-permute-start.67 = (bf16[512,1152]{1,0:T(8,128)(2,1)}, bf16[512,1152]{1,0:T(8,128)(2,1)}, u32[]{:S(2)}, u32[]{:S(2)}) collective-permute-start(bf16[512,1152]{1,0:T(8,128)(2,1)} %fusion.32.refs_4_), channel_id=1, source_target_pairs={{0,1},{1,0},{2,3},{3,2},{4,5},{5,4},{6,7},{7,6},{8,9},{9,8},{10,11... | collective-permute-start | bytes 3538952 | tf_op jit(solution)/shard_map/ppermute | solution.py:47
  903.6 161.0 %collective-permute-start.93 = (f32[6,144,144]{2,1,0:T(8,128)}, f32[6,144,144]{2,1,0:T(8,128)}, u32[]{:S(2)}, u32[]{:S(2)}) collective-permute-start(f32[6,144,144]{2,1,0:T(8,128)} %polynomial.3.refs_0_), channel_id=1, source_target_pairs={{0,2},{2,0},{4,6},{6,4},{8,10},{10,8},{12,14},{14,12},{16,18},{18,... | collective-permute-start | bytes 1493000 | tf_op jit(solution)/shard_map/ppermute | solution.py:47
  908.7 155.9 %collective-permute-start.94 = (f32[6,144,144]{2,1,0:T(8,128)}, f32[6,144,144]{2,1,0:T(8,128)}, u32[]{:S(2)}, u32[]{:S(2)}) collective-permute-start(f32[6,144,144]{2,1,0:T(8,128)} %collective-permute-done.92.refs_1_), channel_id=1, source_target_pairs={{0,2},{2,0},{4,6},{6,4},{8,10},{10,8},{12,14},{14,12},{16,18},{18,... | collective-permute-start | bytes 1493000 | tf_op jit(solution)/shard_map/ppermute | solution.py:47
  1035.2 43.5 %all-to-all-start.3 = ((f32[32,2,576]{2,1,0:T(2,128)}), f32[32,2,576]{2,1,0:T(2,128)S(1)}, u32[]{:S(2)}, u32[]{:S(2)}) async-start(f32[32,2,576]{2,1,0:T(2,128)} %bitcast.154), calls=%async_computation.3 | async-start | bytes 327680 | tf_op jit(solution)/shard_map/all_to_all | solution.py:354
  (235 other events, 3084.2 us)

commit v4 on v3

--- a/solution.py
+++ b/solution.py
@@ -158,39 +158,53 @@
         return self.result
 
 
-def place_kernel(moves, outs, count, parts, *refs):
+def place_kernel(zs, ga, parts, count, outs, *refs):
     spots, sources = refs[0], refs[1 : 1 + count]
-    outputs, (full, in_sems, out_sems) = refs[1 + count : 1 + count + parts], refs[1 + count + parts :]
-    arrivals = []
-    for n, (source, index, target) in enumerate(moves):
-        arrivals.append(
-            pltpu.make_async_copy(sources[source].at[index], full.at[target(spots)], in_sems.at[n])
-        )
-    for copy in arrivals:
-        copy.start()
-    for copy in arrivals:
-        copy.wait()
+    outputs, (full, in_sems, out_sems) = refs[1 + count : 1 + count + outs], refs[1 + count + outs :]
+    g = full.shape[3]
+    half = count // 2
+    shards = []
+    for sc in range(2):
+        for sx in range(2):
+            for sz in range(zs):
+                where = (lax.rem(spots[0] + sz, zs), lax.rem(spots[1] + sx, 2), lax.rem(spots[2] + sc, 2))
+                n = 2 * len(shards)
+                line, pair = sources[sc * half + sx].at[sz], sources[sc * half + 2 + sz].at[sx]
+                copies = [
+                    pltpu.make_async_copy(line, full.at[(*where, pl.ds(0, ga))], in_sems.at[n]),
+                    pltpu.make_async_copy(pair, full.at[(*where, pl.ds(ga, g - ga))], in_sems.at[n + 1]),
+                ]
+                for copy in copies:
+                    copy.start()
+                shards.append((where, copies))
     exits = []
-    for n, (start, output, target) in enumerate(outs):
-        exits.append(pltpu.make_async_copy(full.at[start], outputs[output].at[target], out_sems.at[n]))
-    for copy in exits:
-        copy.start()
+    for where, copies in shards:
+        for copy in copies:
+            copy.wait()
+        for output, start, size, column, depth in parts:
+            target = outputs[output].at[(*where, slice(None), slice(None), pl.ds(column, depth))]
+            copy = pltpu.make_async_copy(
+                full.at[(*where, pl.ds(start, size))], target, out_sems.at[len(exits)]
+            )
+            copy.start()
+            exits.append(copy)
     for copy in exits:
         copy.wait()
 
 
-def place(spots, sources, moves, shape, outs, shapes):
+def place(spots, sources, shape, ga, parts, shapes):
+    zs = shape[0]
     moved = math.prod(shape) * 2
     return pl.pallas_call(
-        functools.partial(place_kernel, moves, outs, len(sources), len(shapes)),
+        functools.partial(place_kernel, zs, ga, parts, len(sources), len(shapes)),
         out_shape=[jax.ShapeDtypeStruct(each, BF) for each in shapes],
         in_specs=[pl.BlockSpec(memory_space=pltpu.SMEM)]
         + [pl.BlockSpec(memory_space=pl.ANY)] * len(sources),
         out_specs=[pl.BlockSpec(memory_space=pl.ANY)] * len(shapes),
         scratch_shapes=[
             pltpu.VMEM(shape, BF),
-            pltpu.SemaphoreType.DMA((len(moves),)),
-            pltpu.SemaphoreType.DMA((len(outs),)),
+            pltpu.SemaphoreType.DMA((8 * zs,)),
+            pltpu.SemaphoreType.DMA((4 * zs * len(parts),)),
         ],
         compiler_params=pltpu.CompilerParams(vmem_limit_bytes=VMEM_LIMIT),
         cost_estimate=pl.CostEstimate(flops=0, bytes_accessed=2 * moved, transcendentals=0),
@@ -215,20 +229,33 @@
         turned = [shard.astype(BF).T for shard in shards]
         return turned[0] if len(turned) == 1 else jnp.concatenate(turned, axis=0)
 
-    def joined(self, wires, unit, depth):
+    def rows(self, wires):
         if self.seq == 2:
             own, other = wires
-            full = jnp.where(
+            return jnp.where(
                 self.y.digit() == 0,
                 jnp.concatenate([own, other], axis=1),
                 jnp.concatenate([other, own], axis=1),
             )
-        else:
-            order = (jnp.arange(self.seq) - self.y.digit()) % self.seq
-            full = jnp.take(jnp.stack(wires), order, axis=0)
-            full = jnp.transpose(full, (1, 0, 2)).reshape(full.shape[1], -1)
-        full = full.reshape(full.shape[0] // unit, unit, full.shape[1] // depth, depth)
-        return jnp.transpose(full, (2, 0, 1, 3)).reshape(-1, unit, depth)
+        order = (jnp.arange(self.seq) - self.y.digit()) % self.seq
+        full = jnp.take(jnp.stack(wires), order, axis=0)
+        return jnp.transpose(full, (1, 0, 2)).reshape(full.shape[1], -1)
+
+    def joined(self, wires, unit, depth):
+        full = self.rows(wires)
+        return full.reshape(full.shape[0] // unit, unit, depth)
+
+    def scatter(self, term):
+        return lax.psum_scatter(term, "dp", scatter_dimension=0, tiled=True)
+
+    def halves_steps(self, term):
+        y = self.y.digit()
+        blocks = term.reshape(term.shape[0], self.seq, -1)
+        return (
+            yield from self.y.scatter_steps(
+                lambda s: lax.dynamic_index_in_dim(blocks, (y + s) % self.seq, 1, keepdims=False)
+            )
+        )
 
     def gather_steps(self, units, layout, part):
         g, unit, depth = units.shape
@@ -249,100 +276,37 @@
         pieces = lines + pairs
         others = [self.core.send(piece, 1) for piece in pieces]
         anchor = yield pieces
-        sources, moves = pieces + [tie(other, anchor) for other in others], []
-
-        def spot(sz, sx, sc, start, stop):
-            def target(spots):
-                return (
-                    lax.rem(spots[0] + sz, zs),
-                    lax.rem(spots[1] + sx, 2),
-                    lax.rem(spots[2] + sc, 2),
-                    pl.ds(start, stop - start),
-                )
-
-            return target
-
-        for sc in range(2):
-            base = sc * len(pieces)
-            for sx in range(2):
-                for sz in range(zs):
-                    moves.append((base + sx, (sz,), spot(sz, sx, sc, 0, ga)))
-                    moves.append((base + 2 + sz, (sx,), spot(sz, sx, sc, ga, g)))
-        outs, shapes, start = [], [], 0
+        sources = pieces + [tie(other, anchor) for other in others]
+        parts, shapes, start = [], [], 0
         for n, (rows, blocks) in enumerate(layout):
             size = rows // unit
             shapes.append((zs, 2, 2, size, unit, blocks * depth))
             for j in range(blocks):
-                window = (slice(None),) * 3 + (pl.ds(start, size),)
-                target = (slice(None),) * 5 + (pl.ds(j * depth, depth),)
-                outs.append((window, n, target))
+                parts.append((n, start, size, j * depth, depth))
                 start += size
-        full = place(self.spots(), sources, moves, (zs, 2, 2, g, unit, depth), outs, shapes)
+        full = place(self.spots(), sources, (zs, 2, 2, g, unit, depth), ga, parts, shapes)
         return [f.reshape(-1, f.shape[-1]) for f in full], lines[1:] + pairs[1:]
 
-    def scatter_steps(self, terms, unit, depth, layout, part):
-        zs = self.z.size
-        blocks = [term.reshape(zs, 2, 2, -1, unit, depth) for term in terms]
-        g = sum(block.shape[3] for block in blocks)
-        ga = max(1, int(part * g))
-        core, x, z = self.core.digit(), self.x.digit(), self.z.digit()
-
-        def half_of(s):
-            parts = [lax.dynamic_index_in_dim(block, (core + s) % 2, 2, keepdims=False) for block in blocks]
-            return parts[0] if len(parts) == 1 else jnp.concatenate(parts, axis=2)
-
-        half = (yield from self.core.scatter_steps(half_of)).astype(BF)
-
-        def line_steps():
-            line = yield from self.x.scatter_steps(
-                lambda s: lax.dynamic_index_in_dim(half[:, :, :ga], (x + s) % 2, 1, keepdims=False)
-            )
-            line = line.astype(BF)
-            return (
-                yield from self.z.scatter_steps(
-                    lambda s: lax.dynamic_index_in_dim(line, (z + s) % zs, 0, keepdims=False), 1
-                )
-            )
-
-        def pair_steps():
-            pair = yield from self.z.scatter_steps(
-                lambda s: lax.dynamic_index_in_dim(half[:, :, ga:], (z + s) % zs, 0, keepdims=False), -1
-            )
-            pair = pair.astype(BF)
-            return (
-                yield from self.x.scatter_steps(
-                    lambda s: lax.dynamic_index_in_dim(pair, (x + s) % 2, 0, keepdims=False)
-                )
-            )
-
-        line, pair = yield from lockstep(line_steps(), pair_steps())
-        joined = jnp.concatenate([line, pair], axis=0).astype(BF)
-        count = layout[0][1]
-        if count > 1:
-            joined = jnp.transpose(joined.reshape(count, -1, unit, depth), (1, 2, 0, 3))
-        joined = joined.reshape(-1, self.seq, count * depth // self.seq)
-        y = self.y.digit()
-        return (
-            yield from self.y.scatter_steps(
-                lambda s: lax.dynamic_index_in_dim(joined, (y + s) % self.seq, 1, keepdims=False)
-            )
-        )
-
 
     def muon_steps(self, groups, masters, rates):
-        momenta, own, other = muon_gram(self.spots(), groups)
+        momenta, own, other = muon_gram(self.spots(), self.z.size, groups)
         got = self.core.send(other, 1)
         anchor = yield [other]
         half = own + tie(got, anchor)
-        sent, kept = half[1], half[0]
+        sent = half[1]
         got = self.x.send(sent, 1)
         anchor = yield [sent]
-        blocks = yield from self.z.gather_steps(kept + tie(got, anchor))
-        factor = polynomial(blocks)
-        got = self.x.send(factor, 1)
+        kept = half[0] + tie(got, anchor)
+        blocks = [kept[shift] for shift in range(self.z.size)]
+        got = [self.z.send(blocks[shift], shift) for shift in range(1, self.z.size)]
+        anchor = yield blocks[1:]
+        factor = polynomial([blocks[0]] + [tie(each, anchor) for each in got])
+        got = [self.z.send(factor, -shift) for shift in range(1, self.z.size)]
         anchor = yield [factor]
-        got = tie(got, anchor)
-        pair = [factor, got]
+        line = jnp.stack([factor] + [tie(each, anchor) for each in got])
+        got = self.x.send(line, 1)
+        anchor = yield [line]
+        pair = [line, tie(got, anchor)]
         others = [self.core.send(each, 1) for each in pair]
         anchor = yield pair
         factors = pair + [tie(each, anchor) for each in others]
@@ -387,6 +351,75 @@
 
 def outer(left, right):
     return jnp.einsum("srn,srk->nk", left, right, preferred_element_type=F32).astype(BF)
+
+
+def joined_outer_kernel(loads, parts, counts, tile, *refs):
+    inputs, out = refs[: counts[0]], refs[counts[1]]
+    buffers = refs[counts[1] + 1 : counts[1] + 1 + len(loads)]
+    acc, in_sems, out_sems = refs[counts[1] + 1 + len(loads) :]
+    arrivals = []
+    for n, (sources, start, size) in enumerate(loads):
+        row, copies = 0, []
+        for m, source in enumerate(sources):
+            rows = inputs[source].shape[0]
+            window = inputs[source].at[:, pl.ds(start, size)]
+            copies.append(pltpu.make_async_copy(window, buffers[n].at[pl.ds(row, rows)], in_sems.at[n, m]))
+            row += rows
+        arrivals.append(copies)
+    order = [n for part in parts for n in part]
+    for n in sorted(range(len(loads)), key=order.index):
+        for copy in arrivals[n]:
+            copy.start()
+    ready, exits = set(), []
+    for n, (left, right) in enumerate(parts):
+        for m in (left, right):
+            if m not in ready:
+                for copy in arrivals[m]:
+                    copy.wait()
+                ready.add(m)
+        width = buffers[left].shape[1]
+        step = tile if width % tile == 0 else width
+
+        @pl.loop(0, width // step)
+        def _(t):
+            spot = pl.multiple_of(t * step, step)
+            product = lax.dot_general(
+                buffers[left][:, pl.ds(spot, step)],
+                buffers[right][...],
+                (((0,), (0,)), ((), ())),
+                preferred_element_type=F32,
+            )
+            acc[n, pl.ds(spot, step)] = product.astype(BF)
+
+        exits.append(pltpu.make_async_copy(acc.at[n], out.at[pl.ds(n * width, width)], out_sems.at[n]))
+        exits[-1].start()
+    for copy in exits:
+        copy.wait()
+
+
+def joined_outer(inputs, loads, parts, deps=(), tile=384):
+    heights = [sum(inputs[source].shape[0] for source in sources) for sources, _, _ in loads]
+    width, depth = loads[parts[0][0]][2], loads[parts[0][1]][2]
+    anywhere = pl.BlockSpec(memory_space=pl.ANY)
+    return pl.pallas_call(
+        functools.partial(joined_outer_kernel, loads, parts, (len(inputs), len(inputs) + len(deps)), tile),
+        out_shape=jax.ShapeDtypeStruct((len(parts) * width, depth), BF),
+        in_specs=[anywhere] * (len(inputs) + len(deps)),
+        out_specs=anywhere,
+        scratch_shapes=[pltpu.VMEM((height, load[2]), BF) for height, load in zip(heights, loads)]
+        + [
+            pltpu.VMEM((len(parts), width, depth), BF),
+            pltpu.SemaphoreType.DMA((len(loads), max(len(load[0]) for load in loads))),
+            pltpu.SemaphoreType.DMA((len(parts),)),
+        ],
+        compiler_params=pltpu.CompilerParams(vmem_limit_bytes=VMEM_LIMIT),
+        cost_estimate=pl.CostEstimate(
+            flops=sum(2 * heights[left] * width * depth for left, _ in parts),
+            bytes_accessed=2 * sum(heights) * width + 2 * len(parts) * width * depth,
+            transcendentals=0,
+        ),
+        name="joined_outer",
+    )(*inputs, *deps)
 
 
 LANES = 128
@@ -589,14 +622,13 @@
     )(lengths, offsets, queries, keys, values, mixed, grads, lse, *deps)
 
 
-def block_spots(counts):
-    total = sum(counts)
-    per = -(-total // 4)
+def block_spots(counts, zs):
+    per = -(-sum(counts) // (4 * zs))
     spots = []
     for matrix, count in enumerate(counts):
         for block in range(count):
-            n = len(spots)
-            spots.append((matrix, block, n // per // 2, n // per % 2, n % per))
+            device, place_in = divmod(len(spots), per)
+            spots.append((matrix, block, device // 4, device // 2 % 2, device % 2, place_in))
     return spots, per
 
 
@@ -605,44 +637,44 @@
 
 
 def muon_gram_kernel(groups, spots_ref, *refs):
-    count = sum(matrices for _, matrices in groups)
+    count = sum(groups)
     sums, momenta = refs[: len(groups)], refs[len(groups) : len(groups) + count]
     outs = refs[len(groups) + count : len(groups) + 2 * count]
     own_ref, other_ref = refs[len(groups) + 2 * count :]
     n = 0
-    for (turned, matrices), sum_ref in zip(groups, sums):
-        grads = jnp.transpose(sum_ref[...]) if turned else sum_ref[...]
+    for matrices, sum_ref in zip(groups, sums):
         start = 0
         for _ in range(matrices):
-            width = momenta[n].shape[1]
-            outs[n][...] = MUON_DECAY * momenta[n][...] + grads[:, start : start + width]
-            start += width
+            size = momenta[n].shape[0]
+            outs[n][...] = MUON_DECAY * momenta[n][...] + sum_ref[start : start + size]
+            start += size
             n += 1
-    spots, per = block_spots([out.shape[0] // ROW_BLOCK for out in outs])
-    if len(spots) < 4 * per:
+    zs = own_ref.shape[1]
+    spots, per = block_spots([out.shape[1] // ROW_BLOCK for out in outs], zs)
+    if len(spots) < 4 * zs * per:
         own_ref[...] = jnp.zeros_like(own_ref)
         other_ref[...] = jnp.zeros_like(other_ref)
-    for matrix, block, core, x, place_in in spots:
-        rows = outs[matrix][block * ROW_BLOCK : (block + 1) * ROW_BLOCK]
-        gram = precise(rows, rows, ((1,), (1,)))
-        away = lax.rem(spots_ref[1] + x, 2)
+    for matrix, block, z, x, core, place_in in spots:
+        turned = outs[matrix][:, block * ROW_BLOCK : (block + 1) * ROW_BLOCK]
+        gram = precise(turned, turned, ((0,), (0,)))
+        away = (lax.rem(spots_ref[1] + x, 2), lax.rem(zs + z - spots_ref[0], zs), place_in)
 
         @pl.when(spots_ref[2] == core)
         def _():
-            own_ref[away, place_in] = gram
+            own_ref[away] = gram
 
         @pl.when(spots_ref[2] != core)
         def _():
-            other_ref[away, place_in] = gram
-
-
-def muon_gram(spots, groups):
-    momenta = [momentum for _, _, each in groups for momentum in each]
-    _, per = block_spots([momentum.shape[0] // ROW_BLOCK for momentum in momenta])
-    grams = jax.ShapeDtypeStruct((2, per, ROW_BLOCK, ROW_BLOCK), F32)
+            other_ref[away] = gram
+
+
+def muon_gram(spots, zs, groups):
+    momenta = [momentum for _, each in groups for momentum in each]
+    _, per = block_spots([momentum.shape[1] // ROW_BLOCK for momentum in momenta], zs)
+    grams = jax.ShapeDtypeStruct((2, zs, per, ROW_BLOCK, ROW_BLOCK), F32)
     vmem = pl.BlockSpec(memory_space=pltpu.VMEM)
     outs = pl.pallas_call(
-        functools.partial(muon_gram_kernel, [(turned, len(each)) for _, turned, each in groups]),
+        functools.partial(muon_gram_kernel, [len(each) for _, each in groups]),
         out_shape=[jax.ShapeDtypeStruct(momentum.shape, F32) for momentum in momenta] + [grams, grams],
         in_specs=[pl.BlockSpec(memory_space=pltpu.SMEM)] + [vmem] * (len(groups) + len(momenta)),
         out_specs=[vmem] * (len(momenta) + 2),
@@ -695,12 +727,14 @@
     outs, factors = refs[4 + 2 * count : 4 + 3 * count], refs[4 + 3 * count]
     for n in range(4):
         factors[n] = parts[n][...]
-    spots, _ = block_spots([momentum.shape[0] // ROW_BLOCK for momentum in momenta])
-    for matrix, block, core, x, place_in in spots:
-        rows = slice(block * ROW_BLOCK, (block + 1) * ROW_BLOCK)
+    zs = factors.shape[1]
+    spots, _ = block_spots([momentum.shape[1] // ROW_BLOCK for momentum in momenta], zs)
+    for matrix, block, z, x, core, place_in in spots:
+        part = slice(block * ROW_BLOCK, (block + 1) * ROW_BLOCK)
         away = 2 * lax.rem(spots_ref[2] + core, 2) + lax.rem(spots_ref[1] + x, 2)
-        direction = precise(factors[away, place_in], momenta[matrix][rows], ((1,), (0,)))
-        outs[matrix][rows] = masters[matrix][rows] * (1.0 - WEIGHT_SHRINK) - rates[matrix] * direction
+        factor = factors[away, lax.rem(zs + z - spots_ref[0], zs), place_in]
+        direction = precise(momenta[matrix][:, part], factor, ((1,), (1,)))
+        outs[matrix][:, part] = masters[matrix][:, part] * (1.0 - WEIGHT_SHRINK) - rates[matrix] * direction
 
 
 def muon_apply(spots, factors, momenta, masters, rates):
@@ -730,20 +764,19 @@
     bounds = [0, 6 * width, 7 * width, 8 * width, 9 * width, 9 * width + hidden, 10 * width + hidden]
 
     n_qkv, n_proj, n_fc1, n_fc2 = [w.shape[1] for w in (w_qkv, w_proj, w_fc1, w_fc2)]
-    unit_qkv, unit_fc2 = math.gcd(n_qkv, 8), math.gcd(n_fc2, 8)
-    unit_mid = math.gcd(math.gcd(n_proj, n_fc1), 8)
-    fold = hidden // width
-    layout_qkv, layout_mid, layout_fc2 = [(n_qkv, 1)], [(n_proj, 1), (n_fc1, 1)], [(n_fc2, fold)]
+    unit_qkv, layout_qkv = math.gcd(n_qkv, 8), [(n_qkv, 1)]
     own_tokens = tokens.reshape(count, rows, width)
     wires = net.y.gather(net.wire([w_qkv]))
     units_qkv = net.joined(wires, unit_qkv, width)
     token_pieces = [net.y.gather(tie(own_tokens[0], wires[-1]))]
     wires = net.y.gather(tie(net.wire([w_proj, w_fc1]), token_pieces[0][-1]))
-    units_mid = net.joined(wires, unit_mid, width)
     for i in range(1, count):
         token_pieces.append(net.y.gather(tie(own_tokens[i], wires[-1])))
+    rows_mid = net.rows(wires)
+    t_proj = lax.all_gather(rows_mid[:n_proj], "dp", axis=0, tiled=True)
+    t_fc1 = lax.all_gather(rows_mid[n_proj:], "dp", axis=0, tiled=True)
     wires = net.y.gather(tie(net.wire([w_fc2]), token_pieces[-1][-1]))
-    units_fc2 = net.joined(wires, unit_fc2, width)
+    t_fc2 = lax.all_gather(net.rows(wires), "dp", axis=0, tiled=True)
 
     ada_rows, ada_cols = w_ada.shape
     cond = conditioning.astype(F32).reshape(count, width)
@@ -759,80 +792,50 @@
     low_ada = w_ada.astype(BF)
     partial = jnp.dot(cond_all, low_ada, preferred_element_type=F32).reshape(dp, 1, count, ada_cols)
     received = jnp.sum(net.to_all(jnp.broadcast_to(partial, (dp, seq, count, ada_cols))), axis=1)
+    (t_qkv,), _ = Staged(net.gather_steps(units_qkv, layout_qkv, 0.45)).finish()
     modulation = jnp.transpose(received, (1, 0, 2)).reshape(count, dp * ada_cols) + b_ada
     shift_one, scale_one, gate_one, shift_two, scale_two, gate_two = jnp.split(
         modulation[:, None, :], 6, axis=-1
     )
 
-    (t_qkv,), arrived = Staged(net.gather_steps(units_qkv, layout_qkv, 0.45)).finish()
-    mid = Staged(net.gather_steps(tie(units_mid, *arrived), layout_mid, 0.4))
-    late = None
-
     lengths = (heights * widths).reshape(count).astype(jnp.int32)
     offsets = jnp.stack([((y + s) % seq) * rows for s in range(seq)]).astype(jnp.int32)
     normed_all, inverse_all, attn_all, queries, keys, values, attended_low, log_total = [[] for _ in range(8)]
-    sent = mid.advance()
     for i in range(count):
         normed, inverse = layer_norm(jnp.concatenate(token_pieces[i], axis=0).astype(F32))
         attn = (normed * (1.0 + scale_one[i]) + shift_one[i]).astype(BF)
-        attn = tie(attn, *sent)
         queries.append((dot_t(attn[None, :rows], t_qkv[:width]) + b_q).astype(BF))
         keys.append(dot_t(attn[None], t_qkv[width : 2 * width]).astype(BF))
         values.append((dot_t(attn[None], t_qkv[2 * width :]) + b_v).astype(BF))
-        if i == 0:
-            sent = mid.advance(keys[i])
-        elif late is None:
-            late = Staged(net.gather_steps(tie(units_fc2, keys[i]), layout_fc2, 0.4))
-            sent = late.advance()
-        mixed, lse = attend(lengths[i : i + 1], offsets, queries[i], keys[i], values[i], HEADS, 512, sent)
-        sent = mid.advance(mixed)
+        mixed, lse = attend(lengths[i : i + 1], offsets, queries[i], keys[i], values[i], HEADS, 512)
         normed_all.append(normed[:rows])
         inverse_all.append(inverse[:rows])
         attn_all.append(attn)
         attended_low.append(mixed[0])
         log_total.append(lse)
-    if late is None:
-        late = Staged(net.gather_steps(tie(units_fc2, keys[-1]), layout_fc2, 0.4))
-        late.advance()
     attended_low = jnp.stack(attended_low)
-    attn_all = jnp.stack(attn_all)
-    attn_own = attn_all[:, :rows]
-    t_proj, t_fc1 = mid.finish(log_total[-1])[0]
-    sent = late.advance(attended_low)
 
     inputs = own_tokens.astype(F32)
-    branch_one = dot_t(tie(attended_low, *sent), t_proj) + b_proj
+    branch_one = dot_t(attended_low, t_proj) + b_proj
     mixed_one = inputs + gate_one * branch_one
     normed_two, inverse_two = layer_norm(mixed_one)
     ffn_in = (normed_two * (1.0 + scale_two) + shift_two).astype(BF)
-    sent = late.advance(ffn_in)
-    ffn_in = tie(ffn_in, *sent)
     pre_act = dot_t(ffn_in, t_fc1) + b_fc1
     activated, gelu_back = jax.vjp(gelu_tanh, pre_act)
     activated_low = activated.astype(BF)
-    sent = late.advance(activated_low)
     grad_out = upstream.reshape(count, rows, width).astype(F32)
     grad_branch_two = (gate_two * grad_out).astype(BF)
-    activated_low = tie(activated_low, *sent)
-    terms_fc2 = [
-        outer(grad_branch_two, activated_low[..., j * width : (j + 1) * width]) for j in range(fold)
-    ]
-    back_fc2 = Staged(net.scatter_steps(terms_fc2, unit_fc2, width, layout_fc2, 0.4))
-    sent = back_fc2.advance()
-    (t_fc2,) = late.finish(terms_fc2[-1])[0]
-    branch_two = dot_t(tie(activated_low, *sent), t_fc2) + b_fc2
+    flat = lambda array: array.reshape(-1, array.shape[-1])
+    sum_fc2 = net.scatter(outer(grad_branch_two, activated_low))
+    branch_two = dot_t(activated_low, t_fc2) + b_fc2
     result = (mixed_one + gate_two * branch_two).astype(BF)
 
     grad_gate_two = jnp.sum(branch_two * grad_out, axis=1)
-    sent = back_fc2.advance(branch_two)
-    grad_branch_two = tie(grad_branch_two, *sent)
     bias_fc2 = jnp.sum(grad_branch_two.astype(F32), axis=(0, 1))
     grad_pre = gelu_back(dot(grad_branch_two, t_fc2))[0].astype(BF)
-    sent = back_fc2.advance(grad_pre)
-    grad_pre = tie(grad_pre, *sent)
     term_fc1 = outer(grad_pre, ffn_in)
-    sent = back_fc2.advance(term_fc1)
-    grad_pre = tie(grad_pre, *sent)
+    sum_fc1 = net.scatter(term_fc1)
+    grad_pre = tie(grad_pre, term_fc1)
     bias_fc1 = jnp.sum(grad_pre.astype(F32), axis=(0, 1))
     grad_ffn_in = dot(grad_pre, t_fc1)
     grad_shift_two = jnp.sum(grad_ffn_in, axis=1)
@@ -841,20 +844,24 @@
     grad_gate_one = jnp.sum(branch_one * grad_mixed, axis=1)
     grad_branch_one = (gate_one * grad_mixed).astype(BF)
     term_proj = outer(grad_branch_one, attended_low)
-    back_mid = Staged(net.scatter_steps([term_proj, term_fc1], unit_mid, width, layout_mid, 0.4))
-    sent = back_mid.advance() + back_fc2.advance(term_proj)
-    grad_branch_one = tie(grad_branch_one, *sent)
+    sum_proj = net.scatter(term_proj)
+    grad_branch_one = tie(grad_branch_one, term_proj)
     bias_proj = jnp.sum(grad_branch_one.astype(F32), axis=(0, 1))
     grad_attended = dot(grad_branch_one, t_proj).astype(BF)
 
     grad_q, grad_k, grad_v, far_parts = [], [], [], []
-    sent = back_mid.advance(grad_attended)
+    turned = [momentum.T for momentum in momenta]
+    sent = []
     for i in range(count):
         dq, dk, dv = attend_back(
             lengths[i : i + 1], offsets, queries[i], keys[i], values[i], attended_low[i : i + 1],
             grad_attended[i : i + 1], log_total[i], HEADS, 512, sent,
         )
-        sent = back_mid.advance(dq) + back_fc2.advance(dq)
+        if i == 0:
+            early = Staged(lockstep(*[net.halves_steps(tie(each, dq)) for each in (sum_proj, sum_fc1, sum_fc2)]))
+            sent = early.advance()
+        else:
+            sent = early.advance(dq)
         grad_q.append(dq)
         grad_k.append(dk)
         grad_v.append(dv)
@@ -870,23 +877,36 @@
         )
         sent = sent + far_steps.advance()
         far_parts.append(far_steps)
-    grad_q, grad_k, grad_v = [jnp.concatenate(each, axis=0) for each in (grad_q, grad_k, grad_v)]
-    grad_q = tie(grad_q, *sent)
-    term_qkv = jnp.concatenate(
-        [outer(grad_q, attn_own), outer(grad_k, attn_all), outer(grad_v, attn_all)], axis=0
+    term_qkv = joined_outer(
+        [flat(each) for each in grad_q + grad_k + grad_v] + [attn[:rows] for attn in attn_all] + attn_all,
+        [([n * count + i for i in range(count)], 0, width) for n in range(5)],
+        [(0, 3), (1, 4), (2, 4)],
+        sent,
     )
-    back_qkv = Staged(net.scatter_steps([term_qkv], unit_qkv, width, layout_qkv, 0.45))
-    sent = back_qkv.advance() + back_mid.advance(term_qkv)
-    grad_q = tie(grad_q, *sent)
-    bias_q = jnp.sum(grad_q.astype(F32), axis=(0, 1))
-    bias_v = jnp.sum(grad_v.astype(F32), axis=(0, 1))
-    own_part = (
-        dot(grad_q, t_qkv[:width])
-        + dot(grad_k[:, :rows], t_qkv[width : 2 * width])
-        + dot(grad_v[:, :rows], t_qkv[2 * width :])
+    sum_qkv = net.scatter(term_qkv)
+    sums = early.finish(term_qkv)
+    chain = Staged(
+        net.muon_steps(
+            [(sums[0], [turned[1]]), (sums[1], [turned[2]]), (sums[2], [turned[3]])],
+            [w_proj.T, w_fc1.T, w_fc2.T],
+            [1.0, math.sqrt(hidden / width), math.sqrt(width / hidden)],
+        )
     )
-    sent = back_qkv.advance(own_part) + back_mid.advance(own_part)
-    far_sum = jnp.stack([steps.finish() for steps in far_parts])
+    sent = chain.advance()
+    grad_q[0] = tie(grad_q[0], *sent)
+    bias_q = sum(jnp.sum(each.astype(F32), axis=(0, 1)) for each in grad_q)
+    bias_v = sum(jnp.sum(each.astype(F32), axis=(0, 1)) for each in grad_v)
+    own_part = jnp.concatenate(
+        [
+            dot(grad_q[i], t_qkv[:width])
+            + dot(grad_k[i][:, :rows], t_qkv[width : 2 * width])
+            + dot(grad_v[i][:, :rows], t_qkv[2 * width :])
+            for i in range(count)
+        ],
+        axis=0,
+    )
+    sent = chain.advance(own_part)
+    far_sum = jnp.stack([steps_of.finish() for steps_of in far_parts])
     grad_attn_in = tie(own_part, *sent) + far_sum
     normed_one, inverse_one = jnp.stack(normed_all), jnp.stack(inverse_all)
     grad_shift_one = jnp.sum(grad_attn_in, axis=1)
@@ -900,39 +920,44 @@
     bias_ada = jnp.sum(grad_mod_local, axis=0)
     sent = jnp.transpose(grad_mod_local.reshape(count, dp, 1, ada_cols), (1, 2, 0, 3))
     sent = jnp.broadcast_to(sent, (dp, seq, count, ada_cols))
-    mod_cols = jnp.sum(net.to_all(sent), axis=1).astype(BF).reshape(dp * count, ada_cols)
-    shard_ada = jnp.einsum("sr,sc->rc", cond_all, mod_cols, preferred_element_type=F32)
-
-    rate_of = {
-        "qkv": math.sqrt(3.0), "proj": 1.0, "fc1": math.sqrt(hidden / width),
-        "fc2": math.sqrt(width / hidden), "ada": math.sqrt(6.0),
-    }
-    sum_mid, sum_fc2 = back_mid.finish(), back_fc2.finish()
-    early = Staged(
+    mod_parts = net.to_all(sent)
+    anchor = grad_mod_local
+    while not chain.done:
+        anchor = (chain.advance(anchor) or [None])[0]
+        if anchor is not None:
+            mod_parts = tie(mod_parts, anchor)
+    halves = Staged(net.halves_steps(tie(sum_qkv, mod_parts)))
+    halves.advance()
+    mod_cols = jnp.sum(mod_parts, axis=1).astype(BF).reshape(dp * count, ada_cols)
+    shard_ada = jnp.einsum("sr,sc->cr", cond_all, mod_cols, preferred_element_type=F32)
+
+    last = Staged(
         net.muon_steps(
-            [(sum_mid, True, [momenta[1], momenta[2]]), (sum_fc2, True, [momenta[3]])],
-            [w_proj, w_fc1, w_fc2],
-            [rate_of["proj"], rate_of["fc1"], rate_of["fc2"]],
+            [
+                (halves.finish(), [turned[0]]),
+                (shard_ada, [turned[4]]),
+            ],
+            [w_qkv.T, w_ada.T],
+            [math.sqrt(3.0), math.sqrt(6.0)],
         )
     )
-    (next_proj, next_fc1, next_fc2), (new_proj, new_fc1, new_fc2) = early.finish()
-    sum_qkv = back_qkv.finish()
-    last = Staged(
-        net.muon_steps(
-            [(sum_qkv, True, [momenta[0]]), (shard_ada, False, [momenta[4]])],
-            [w_qkv, w_ada],
-            [rate_of["qkv"], rate_of["ada"]],
-        )
-    )
-    (next_qkv, next_ada), (new_qkv, new_ada) = last.finish()
+    sent = last.advance()
 
     cond_part = jnp.einsum("sc,rc->sr", mod_cols, low_ada, preferred_element_type=F32)
-    cond_part = cond_part.reshape(dp, 1, count, ada_rows)
-    cond_part = jnp.sum(net.to_all(jnp.broadcast_to(cond_part, (dp, seq, count, ada_rows))), axis=0)
+    cond_part = jnp.broadcast_to(cond_part.reshape(dp, 1, -1), (dp, seq, count * ada_rows))
+    term_bias = jnp.concatenate([bias_ada, bias_q, bias_v, bias_proj, bias_fc1, bias_fc2])
+    parcel = jnp.concatenate([term_bias.reshape(dp, seq, -1), cond_part], axis=-1)
+    parcel = net.to_all(tie(parcel, *sent))
+    while not last.done:
+        anchor = sent[0] if sent else None
+        sent = last.advance(anchor)
+    (next_qkv, next_ada), (new_qkv, new_ada) = last.result
+    (next_proj, next_fc1, next_fc2), (new_proj, new_fc1, new_fc2) = chain.result
+
+    size = biases.shape[0]
+    grad_bias = jnp.sum(parcel[..., :size], axis=(0, 1))
+    cond_part = jnp.sum(parcel[..., size:], axis=0).reshape(seq, count, ada_rows)
     grad_cond = silu_back(jnp.transpose(cond_part, (1, 0, 2)).reshape(count, width))[0]
-
-    term_bias = jnp.concatenate([bias_ada, bias_q, bias_v, bias_proj, bias_fc1, bias_fc2])
-    grad_bias = jnp.sum(net.to_all(term_bias.reshape(dp, seq, -1)), axis=(0, 1))
     next_first = BETA_FIRST * bias_first + (1.0 - BETA_FIRST) * grad_bias
     next_second = BETA_SECOND * bias_second + (1.0 - BETA_SECOND) * grad_bias * grad_bias
     first_hat = next_first / (1.0 - BETA_FIRST**STEP_COUNT)
@@ -944,8 +969,8 @@
         result.reshape(tokens.shape),
         grad_inputs,
         grad_cond.reshape(conditioning.shape),
-        new_qkv, new_proj, new_fc1, new_fc2, new_ada,
-        next_qkv, next_proj, next_fc1, next_fc2, next_ada,
+        new_qkv.T, new_proj.T, new_fc1.T, new_fc2.T, new_ada.T,
+        next_qkv.T, next_proj.T, next_fc1.T, next_fc2.T, next_ada.T,
         new_biases,
         next_first,
         next_second,

time: 1110 us -> 1210 us (1.090); the launches traced: 1090 us -> 1210 us
  waiting for transfers between devices: 138 us -> 481 us
  local copies, waits for them, and re-layouts: 181 us -> 89.2 us
  other arithmetic: 148 us -> 75.5 us
  starting transfers between devices: 141 us -> 76.3 us
  matrix products: 241 us -> 228 us
  between operations: 2.83 us -> 15.6 us
    reduce_scatter x0 -> x2, waiting for transfers between devices: none -> 215 us  [scatter(): return lax.psum_scatter(term, 'dp', scatter_dimension=0, tiled=True)]
    ppermute x95 -> x47, waiting for transfers between devices: 124 us -> 260 us  [send(): return lax.ppermute(value, self.name, pairs)]
    unnamed x359 -> x227, local copies, waits for them, and re-layouts: 102 us -> 39.4 us
    ppermute x95 -> x47, starting transfers between devices: 105 us -> 46.7 us  [send(): return lax.ppermute(value, self.name, pairs)]
    convert_element_type x17 -> x0, other arithmetic: 41.3 us -> none  [the longest x3 15 us: scatter_steps(): half = (yield from self.core.scatter_steps(half_of)).astype(BF)]
    concatenate x7 -> x2, other arithmetic: 24.2 us -> 4.32 us  [the longest x1 2.56 us: body(): jnp.concatenate([dot(grad_q[i], t_qkv[:width]) + dot(grad_k[i][:, :rows],...]
    dot_general x9 -> x3, matrix products: 58.7 us -> 39.6 us  [outer(): jnp.einsum('srn,srk->nk', left, right, preferred_element_type=F32)]
    dynamic_slice x8 -> x4, local copies, waits for them, and re-layouts: 24.5 us -> 6.81 us  [halves_steps(): lax.dynamic_index_in_dim(blocks, (y + s) % self.seq, 1, keepdims=False)]
  transfers between devices with their start and end apart: 100 -> 58, of which waited for: 23 -> 30; matrix products, arithmetic and copies ran while one was open for 41% -> 20% of each run, Pallas kernels for 20% -> 13%
where the time goes in v4:
time: 1210 us
  waiting for transfers between devices  481 us (40%)
  Pallas kernels  241 us (20%)
  matrix products  228 us (19%)
  local copies, waits for them, and re-layouts  89.2 us (7%)
  starting transfers between devices  76.3 us (6%)
  other arithmetic  75.5 us (6%)
  between operations  15.6 us (1%)
    ppermute x47, waiting for transfers between devices, send(): return lax.ppermute(value, self.name, pairs)  260 us
    reduce_scatter x2, waiting for transfers between devices, scatter(): return lax.psum_scatter(term, 'dp', scatter_dimension=0, tiled=True)  215 us
    dot_general x13, matrix products, dot(): return jnp.einsum('srn,nk->srk', left, right, preferred_element_type=F32)  102 us
    pallas_call x2, Pallas kernels, attend_back(): pl.pallas_call(without(attend_back_kernel, 8, len(deps), heads, tile), gr...  90.5 us
    dot_general x9, matrix products, dot_t(): return jnp.einsum('srk,nk->srn', left, right, preferred_element_type=F32)  82.7 us
    pallas_call x2, Pallas kernels, attend(): pl.pallas_call(without(attend_kernel, 5, len(deps), heads, tile), grid_sp...  65.3 us
    ppermute x47, starting transfers between devices, send(): return lax.ppermute(value, self.name, pairs)  46.7 us
    dot_general x3, matrix products, outer(): jnp.einsum('srn,srk->nk', left, right, preferred_element_type=F32)  39.6 us
  transfers between devices with their start and end apart: 58, of which 30 were waited for; matrix products, arithmetic and copies ran while one was open for 20% of the time, Pallas kernels for 13%

profile of v4, /device:TPU:11, one launch (start us, length us, event | category | flops | bytes accessed | tf_op | source)
XLA Modules:
  0.0 1206.5 jit_solution(9484434258875673019)
XLA Ops:
  19.4 24.0 %collective-permute-done.1.refs_1_ = bf16[512,1152]{1,0:T(8,128)(2,1)S(1)} collective-permute-done((bf16[512,1152]{1,0:T(8,128)(2,1)}, bf16[512,1152]{1,0:T(8,128)(2,1)S(1)}, u32[]{:S(2)}, u32[]{:S(2)}) %collective-permute-start.1) | collective-permute-done | bytes 1179680 | tf_op jit(solution)/shard_map/ppermute | solution.py:47
  60.0 22.3 %collective-permute-done.17.refs_1_ = bf16[512,1152]{1,0:T(8,128)(2,1)S(1)} collective-permute-done((bf16[512,1152]{1,0:T(8,128)(2,1)}, bf16[512,1152]{1,0:T(8,128)(2,1)S(1)}, u32[]{:S(2)}, u32[]{:S(2)}) %collective-permute-start.17) | collective-permute-done | bytes 1179680 | tf_op jit(solution)/shard_map/ppermute | solution.py:47
  93.4 10.7 all-to-all-start
  146.9 26.4 %collective-permute-done.7.refs_4_ = bf16[2,15,8,1152]{3,2,1,0:T(8,128)(2,1)} collective-permute-done((bf16[2,15,8,1152]{3,2,1,0:T(8,128)(2,1)}, bf16[2,15,8,1152]{3,2,1,0:T(8,128)(2,1)}, u32[]{:S(2)}, u32[]{:S(2)}) %collective-permute-start.7) | collective-permute-done | bytes 552992 | tf_op jit(solution)/shard_map/ppermute | solution.py:47
  175.9 35.5 %collective-permute-done.8.refs_5_ = bf16[2,15,8,1152]{3,2,1,0:T(8,128)(2,1)S(1)} collective-permute-done((bf16[2,15,8,1152]{3,2,1,0:T(8,128)(2,1)}, bf16[2,15,8,1152]{3,2,1,0:T(8,128)(2,1)S(1)}, u32[]{:S(2)}, u32[]{:S(2)}) %collective-permute-start.8) | collective-permute-done | bytes 552992 | tf_op jit(solution)/shard_map/ppermute | solution.py:47
  240.8 33.1 %attend.2 = (bf16[1,512,1152]{2,1,0:T(8,128)(2,1)}, f32[1,16,1,512]{3,2,1,0:T(1,128)}) custom-call(s32[1]{0:T(128)} %bitcast.8.refs_0_, s32[2]{0:T(128)} %pad_add_fusion.refs_1_, bf16[1,512,1152]{2,1,0:T(8,128)(2,1)} %fusion.41.refs_2_, bf16[1,1024,1152]{2,1,0:T(8,128)(2,1)} %fusion.34.refs_3_, bf16[1,1024,1152]{2,1,0:T(8,128)(2,1)} %fusion.32.refs_4_), custom_call_target="tpu_custom_call" | custom-call | flops 4294967296 | bytes 7077888 | tf_op jit(solution)/shard_map/attend/pallas_call | solution.py:505
  293.7 32.2 %attend.3 = (bf16[1,512,1152]{2,1,0:T(8,128)(2,1)}, f32[1,16,1,512]{3,2,1,0:T(1,128)}) custom-call(s32[1]{0:T(128)} %bitcast.28.refs_0_, s32[2]{0:T(128)} %pad_add_fusion.refs_1_, bf16[1,512,1152]{2,1,0:T(8,128)(2,1)} %fusion.40.refs_2_, bf16[1,1024,1152]{2,1,0:T(8,128)(2,1)} %fusion.35.refs_3_, bf16[1,1024,1152]{2,1,0:T(8,128)(2,1)} %fusion.33.refs_4_), custom_call_target="tpu_custom_call" | custom-call | flops 4294967296 | bytes 7077888 | tf_op jit(solution)/shard_map/attend/pallas_call | solution.py:505
  339.3 21.0 %fusion.14 = f32[2,512,4608]{2,1,0:T(8,128)} fusion(bf16[4608,1152]{1,0:T(8,128)(2,1)} %all-gather.6.cloned.1.call-done, f32[2,512,1152]{2,1,0:T(8,128)} %copy-done.26, f32[2,1152]{1,0:T(2,128)S(1)} %get-tuple-element.220, f32[2,1152]{1,0:T(2,128)S(1)} %get-tuple-element.221, f32[2,512]{1,0:T(2,128)S(1)} %add_rsqrt_fusion, ...), kind=kOutput, calls=%fused_computation.20 | convolution fusion | flops 10877534208 | bytes 34236416 | tf_op jit(solution)/shard_map/srk,nk->srn/dot_general | solution.py:345
  360.4 27.0 %fusion.8.refs_0_ = bf16[2,512,4608]{2,1,0:T(8,128)(2,1)S(1)} fusion(f32[2,512,4608]{2,1,0:T(8,128)} %fusion.14, bf16[1152,4608]{1,0:T(8,128)(2,1)} %all-gather.8.cloned.1.call-done, f32[4608]{0:T(1024)S(1)} %slice.272, bf16[2,1,512,1152]{3,2,1,0:T(8,128)(2,1)} %param.22, f32[2,1152]{1,0:T(2,128)S(1)} %get-tuple-element.219), kind=kOutput, calls=%fused_computation.12 | convolution fusion | flops 10974265344 | bytes 41315328 | tf_op jit(solution)/shard_map/srn,nk->srk/dot_general | solution.py:349
  391.0 16.6 %fusion.1.refs_1_ = bf16[4608,1152]{1,0:T(8,128)(2,1)} fusion(bf16[2,512,4608]{2,1,0:T(8,128)(2,1)S(1)} %fusion.8.refs_0_, f32[2,512,1152]{2,1,0:T(8,128)S(1)} %bitcast.319, f32[2,1152]{1,0:T(2,128)S(1)} %get-tuple-element.220, f32[2,1152]{1,0:T(2,128)S(1)} %get-tuple-element.221, f32[2,512]{1,0:T(2,128)S(1)} %add_rsqrt_fusion, ...), kind=kOutput, calls=%fused_computation.5 | convolution fusion | flops 10882842624 | bytes 24799232 | tf_op jit(solution)/shard_map/srn,srk->nk/dot_general | solution.py:353
  407.6 21.3 %multiply_reduce_fusion = (f32[2,1152]{1,0:T(2,128)}, f32[2,512]{1,0:T(2,128)S(1)}, f32[2,512]{1,0:T(2,128)S(1)}, f32[2,1152]{1,0:T(2,128)}, f32[2,512,1152]{2,1,0:T(8,128)}) fusion(f32[2,512,1152]{2,1,0:T(8,128)} %copy-done.26, f32[2,512]{1,0:T(2,128)S(1)} %add_rsqrt_fusion, f32[2,512]{1,0:T(2,128)S(1)} %broadcast_multiply_fusion.4, ...), kind=kOutput, calls=%fused_computation.47 | convolution fusion | flops 10882246656 | bytes 29535232 | tf_op jit(solution)/shard_map/srn,nk->srk/dot_general | solution.py:349
  428.9 26.5 %convert_reduce_fusion.3 = (f32[1152]{0:T(1024)}, f32[2,1152]{1,0:T(2,128)}, bf16[2,1,512,1152]{3,2,1,0:T(8,128)(2,1)}, f32[2,1152]{1,0:T(2,128)}, f32[2,512,1152]{2,1,0:T(8,128)}) fusion(bf16[2,1,512,1152]{3,2,1,0:T(8,128)(2,1)} %param.22, f32[2,1152]{1,0:T(2,128)S(1)} %get-tuple-element.219, f32[2,512,1152]{2,1,0:T(8,128)} %copy-done.26, ...), kind=kOutput, calls=%fused_computation.43 | convolution fusion | flops 10943589376 | bytes 53165056 | tf_op jit(solution)/shard_map/srk,nk->srn/dot_general | solution.py:345
  465.0 18.2 %fusion = bf16[1152,4608]{1,0:T(8,128)(2,1)} fusion(bf16[2,1,512,1152]{3,2,1,0:T(8,128)(2,1)S(1)} %copy-done.93, f32[2,1152]{1,0:T(2,128)S(1)} %get-tuple-element.219, f32[2,512,4608]{2,1,0:T(8,128)} %fusion.14, f32[4608]{0:T(1024)S(1)} %slice.272), kind=kOutput, calls=%fused_computation.4 | convolution fusion | flops 10927669248 | bytes 31878144 | tf_op jit(solution)/shard_map/srn,srk->nk/dot_general | solution.py:353
  496.9 45.5 %attend_back.2 = (bf16[1,512,1152]{2,1,0:T(8,128)(2,1)}, bf16[1,1024,1152]{2,1,0:T(8,128)(2,1)}, bf16[1,1024,1152]{2,1,0:T(8,128)(2,1)}) custom-call(s32[1]{0:T(128)} %bitcast.8.refs_0_, s32[2]{0:T(128)} %pad_add_fusion.refs_1_, bf16[1,512,1152]{2,1,0:T(8,128)(2,1)} %fusion.41.refs_2_, bf16[1,1024,1152]{2,1,0:T(8,128)(2,1)} %fusion.34.refs_3_, ...), custom_call_target="tpu_custom_call" | custom-call | flops 10737418240 | bytes 14155776 | tf_op jit(solution)/shard_map/attend_back/pallas_call | solution.py:590
  554.8 95.1 %reduce-scatter.11.cloned.1.call-done.refs_0_ = bf16[72,4608]{1,0:T(8,128)(2,1)} async-done(((bf16[1152,4608]{1,0:T(8,128)(2,1)}), bf16[72,4608]{1,0:T(8,128)(2,1)}) %reduce-scatter.11.cloned.1.call-update) | async-done | bytes 663568 | tf_op jit(solution)/shard_map/reduce_scatter | solution.py:249
  655.1 119.4 %reduce-scatter.9.cloned.1.call-done.refs_0_ = bf16[288,1152]{1,0:T(8,128)(2,1)} async-done(((bf16[4608,1152]{1,0:T(8,128)(2,1)}), bf16[288,1152]{1,0:T(8,128)(2,1)}) %reduce-scatter.9.cloned.1.call-update) | async-done | bytes 663568 | tf_op jit(solution)/shard_map/reduce_scatter | solution.py:249
  780.1 45.0 %attend_back.3 = (bf16[1,512,1152]{2,1,0:T(8,128)(2,1)}, bf16[1,1024,1152]{2,1,0:T(8,128)(2,1)}, bf16[1,1024,1152]{2,1,0:T(8,128)(2,1)}) custom-call(s32[1]{0:T(128)} %bitcast.28.refs_0_, s32[2]{0:T(128)} %pad_add_fusion.refs_1_, bf16[1,512,1152]{2,1,0:T(8,128)(2,1)} %fusion.40.refs_2_, bf16[1,1024,1152]{2,1,0:T(8,128)(2,1)} %fusion.35.refs_3_, ...), custom_call_target="tpu_custom_call" | custom-call | flops 10737418240 | bytes 14155776 | tf_op jit(solution)/shard_map/attend_back/pallas_call | solution.py:590
  833.8 21.6 %joined_outer.1 = bf16[3456,1152]{1,0:T(8,128)(2,1)} custom-call(bf16[512,1152]{1,0:T(8,128)(2,1)} %bitcast.295, bf16[512,1152]{1,0:T(8,128)(2,1)} %bitcast.296, bf16[1024,1152]{1,0:T(8,128)(2,1)} %bitcast.356, bf16[1024,1152]{1,0:T(8,128)(2,1)} %bitcast.357, bf16[1024,1152]{1,0:T(8,128)(2,1)} %bitcast.323, bf16[1024,1152]{1,0:T(8,128)(2,1)} %bitcast.324, ...), custom_call_target="tpu_custom_call" | custom-call | flops 13589544960 | bytes 26836992 | tf_op jit(solution)/shard_map/joined_outer/pallas_call | solution.py:404
  920.2 17.7 %muon_gram.2 = (f32[72,576]{1,0:T(8,128)}, f32[288,576]{1,0:T(8,128)}, f32[72,2304]{1,0:T(8,128)}, f32[2,4,2,144,144]{4,3,2,1,0:T(8,128)}, f32[2,4,2,144,144]{4,3,2,1,0:T(8,128)}) custom-call(s32[3]{0:T(128)} %pad_add_fusion.1.refs_0_.spots_ref, f32[72,576]{1,0:T(8,128)} %convert_add_fusion.6.refs_0_, f32[288,576]{1,0:T(8,128)} %convert_add_fusion.3.refs_1_, ...), custom_call_target="tpu_custom_call" | custom-call | tf_op jit(solution)/shard_map/muon_gram/pallas_call | solution.py:676
  969.0 16.4 %collective-permute-done.25.refs_0_ = f32[4,2,144,144]{3,2,1,0:T(8,128)} collective-permute-done((f32[4,2,144,144]{3,2,1,0:T(8,128)}, f32[4,2,144,144]{3,2,1,0:T(8,128)}, u32[]{:S(2)}, u32[]{:S(2)}) %collective-permute-start.25) | collective-permute-done | bytes 663584 | tf_op jit(solution)/shard_map/ppermute | solution.py:47
  995.9 13.1 %collective-permute-done.27.refs_0_ = f32[2,144,144]{2,1,0:T(8,128)S(1)} collective-permute-done((f32[2,144,144]{2,1,0:T(8,128)}, f32[2,144,144]{2,1,0:T(8,128)S(1)}, u32[]{:S(2)}, u32[]{:S(2)}) %collective-permute-start.27) | collective-permute-done | bytes 165920 | tf_op jit(solution)/shard_map/ppermute | solution.py:47
  1034.0 17.4 %collective-permute-done.30.refs_0_ = f32[2,144,144]{2,1,0:T(8,128)S(1)} collective-permute-done((f32[2,144,144]{2,1,0:T(8,128)}, f32[2,144,144]{2,1,0:T(8,128)S(1)}, u32[]{:S(2)}, u32[]{:S(2)}) %collective-permute-start.30) | collective-permute-done | bytes 165920 | tf_op jit(solution)/shard_map/ppermute | solution.py:47
  1095.3 17.4 %collective-permute-done.44.refs_0_ = f32[4,2,144,144]{3,2,1,0:T(8,128)} collective-permute-done((f32[4,2,144,144]{3,2,1,0:T(8,128)S(1)}, f32[4,2,144,144]{3,2,1,0:T(8,128)}, u32[]{:S(2)}, u32[]{:S(2)}) %collective-permute-start.44) | collective-permute-done | bytes 663584 | tf_op jit(solution)/shard_map/ppermute | solution.py:47
  1175.2 12.9 %collective-permute-done.41.refs_0_ = f32[4,1,144,144]{3,2,1,0:T(8,128)S(1)} collective-permute-done((f32[4,1,144,144]{3,2,1,0:T(8,128)S(1)}, f32[4,1,144,144]{3,2,1,0:T(8,128)S(1)}, u32[]{:S(2)}, u32[]{:S(2)}) %collective-permute-start.41) | collective-permute-done | bytes 331808 | tf_op jit(solution)/shard_map/ppermute | solution.py:47
  (537 shorter events, 454.5 us)
Async XLA Ops:
  7.2 321.1 %all-gather.4.cloned.1.call-start = ((), (), s32[]{:S(2)}) async-start(), calls=%async_computation.8 | async-start | bytes 2820096 | tf_op jit(solution)/shard_map/all_gather | solution.py:776
  56.9 282.5 %all-gather.6.cloned.1.call-start = ((), (), s32[]{:S(2)}) async-start(), calls=%async_computation.9 | async-start | bytes 11280384 | tf_op jit(solution)/shard_map/all_gather | solution.py:777
  57.8 302.6 %all-gather.8.cloned.1.call-start = ((), (), s32[]{:S(2)}) async-start(), calls=%async_computation.10 | async-start | bytes 11280384 | tf_op jit(solution)/shard_map/all_gather | solution.py:779
  125.2 426.7 %reduce-scatter.13.cloned.1.call-start = ((), (), s32[]{:S(2)}) async-start(), calls=%async_computation.13 | async-start | bytes 2820096
  129.1 46.2 %collective-permute-start.12 = (bf16[2,15,8,1152]{3,2,1,0:T(8,128)(2,1)}, bf16[2,15,8,1152]{3,2,1,0:T(8,128)(2,1)}, u32[]{:S(2)}, u32[]{:S(2)}) collective-permute-start(bf16[2,15,8,1152]{3,2,1,0:T(8,128)(2,1)} %pad_maximum_fusion.7.refs_3_), channel_id=1, source_target_pairs={{0,2},{2,0},{4,6},{6,4},{8,10},{10,8},{12,14},{14,12},{16,18},{18,... | collective-permute-start | bytes 1658888 | tf_op jit(solution)/shard_map/ppermute | solution.py:47
  129.7 45.7 %collective-permute-start.9 = (bf16[2,15,8,1152]{3,2,1,0:T(8,128)(2,1)}, bf16[2,15,8,1152]{3,2,1,0:T(8,128)(2,1)}, u32[]{:S(2)}, u32[]{:S(2)}) collective-permute-start(bf16[2,15,8,1152]{3,2,1,0:T(8,128)(2,1)} %pad_maximum_fusion.7.refs_3_), channel_id=1, source_target_pairs={{0,8},{2,10},{4,12},{6,14},{8,16},{10,18},{12,20},{14,22},{16,24},... | collective-permute-start | bytes 1658888 | tf_op jit(solution)/shard_map/ppermute | solution.py:47
  130.9 42.4 %collective-permute-start.7 = (bf16[2,15,8,1152]{3,2,1,0:T(8,128)(2,1)}, bf16[2,15,8,1152]{3,2,1,0:T(8,128)(2,1)}, u32[]{:S(2)}, u32[]{:S(2)}) collective-permute-start(bf16[2,15,8,1152]{3,2,1,0:T(8,128)(2,1)} %pad_maximum_fusion.7.refs_3_), channel_id=1, source_target_pairs={{0,24},{2,26},{4,28},{6,30},{8,0},{10,2},{12,4},{14,6},{16,8},{18,... | collective-permute-start | bytes 1658888 | tf_op jit(solution)/shard_map/ppermute | solution.py:47
  144.8 29.7 %collective-permute-start.5 = (bf16[4,12,8,1152]{3,2,1,0:T(8,128)(2,1)S(1)}, bf16[4,12,8,1152]{3,2,1,0:T(8,128)(2,1)S(1)}, u32[]{:S(2)}, u32[]{:S(2)}) collective-permute-start(bf16[4,12,8,1152]{3,2,1,0:T(8,128)(2,1)S(1)} %pad_maximum_fusion.5.refs_1_), channel_id=1, source_target_pairs={{0,4},{2,6},{4,0},{6,2},{8,12},{10,14},{12,8},{14,10},{16,20},{18,... | collective-permute-start | bytes 2654216 | tf_op jit(solution)/shard_map/ppermute | solution.py:47
  146.0 70.5 %collective-permute-start.10 = (bf16[4,12,8,1152]{3,2,1,0:T(8,128)(2,1)S(1)}, bf16[4,12,8,1152]{3,2,1,0:T(8,128)(2,1)S(1)}, u32[]{:S(2)}, u32[]{:S(2)}) collective-permute-start(bf16[4,12,8,1152]{3,2,1,0:T(8,128)(2,1)S(1)} %pad_maximum_fusion.5.refs_1_), channel_id=1, source_target_pairs={{0,2},{2,0},{4,6},{6,4},{8,10},{10,8},{12,14},{14,12},{16,18},{18,... | collective-permute-start | bytes 2654216 | tf_op jit(solution)/shard_map/ppermute | solution.py:47
  173.3 38.1 %collective-permute-start.8 = (bf16[2,15,8,1152]{3,2,1,0:T(8,128)(2,1)}, bf16[2,15,8,1152]{3,2,1,0:T(8,128)(2,1)S(1)}, u32[]{:S(2)}, u32[]{:S(2)}) collective-permute-start(bf16[2,15,8,1152]{3,2,1,0:T(8,128)(2,1)} %collective-permute-done.7.refs_4_), channel_id=1, source_target_pairs={{0,24},{2,26},{4,28},{6,30},{8,0},{10,2},{12,4},{14,6},{16,8},{18,... | collective-permute-start | bytes 1658888 | tf_op jit(solution)/shard_map/ppermute | solution.py:47
  174.5 44.8 %collective-permute-start.11 = (bf16[4,12,8,1152]{3,2,1,0:T(8,128)(2,1)S(1)}, bf16[4,12,8,1152]{3,2,1,0:T(8,128)(2,1)}, u32[]{:S(2)}, u32[]{:S(2)}) collective-permute-start(bf16[4,12,8,1152]{3,2,1,0:T(8,128)(2,1)S(1)} %collective-permute-done.5.refs_2_), channel_id=1, source_target_pairs={{0,2},{2,0},{4,6},{6,4},{8,10},{10,8},{12,14},{14,12},{16,18},{18,... | collective-permute-start | bytes 2654216 | tf_op jit(solution)/shard_map/ppermute | solution.py:47
  175.3 42.2 %collective-permute-start.13 = (bf16[2,15,8,1152]{3,2,1,0:T(8,128)(2,1)}, bf16[2,15,8,1152]{3,2,1,0:T(8,128)(2,1)S(1)}, u32[]{:S(2)}, u32[]{:S(2)}) collective-permute-start(bf16[2,15,8,1152]{3,2,1,0:T(8,128)(2,1)} %collective-permute-done.7.refs_4_), channel_id=1, source_target_pairs={{0,2},{2,0},{4,6},{6,4},{8,10},{10,8},{12,14},{14,12},{16,18},{18,... | collective-permute-start | bytes 1658888 | tf_op jit(solution)/shard_map/ppermute | solution.py:47
  175.4 42.1 %collective-permute-start.15 = (bf16[2,15,8,1152]{3,2,1,0:T(8,128)(2,1)}, bf16[2,15,8,1152]{3,2,1,0:T(8,128)(2,1)S(1)}, u32[]{:S(2)}, u32[]{:S(2)}) collective-permute-start(bf16[2,15,8,1152]{3,2,1,0:T(8,128)(2,1)} %collective-permute-done.9.refs_6_), channel_id=1, source_target_pairs={{0,2},{2,0},{4,6},{6,4},{8,10},{10,8},{12,14},{14,12},{16,18},{18,... | collective-permute-start | bytes 1658888 | tf_op jit(solution)/shard_map/ppermute | solution.py:47
  463.4 186.6 %reduce-scatter.11.cloned.1.call-start = ((), (), s32[]{:S(2)}) async-start(), calls=%async_computation.12 | async-start | bytes 11280384 | tf_op jit(solution)/shard_map/reduce_scatter | solution.py:249
  483.2 291.3 %reduce-scatter.9.cloned.1.call-start = ((), (), s32[]{:S(2)}) async-start(), calls=%async_computation.11 | async-start | bytes 11280384 | tf_op jit(solution)/shard_map/reduce_scatter | solution.py:249
  483.8 572.7 %reduce-scatter.15.cloned.1.call-start = ((), (), s32[]{:S(2)}) async-start(), calls=%async_computation.14 | async-start | bytes 8460288
  876.5 80.2 %collective-permute-start.23 = (bf16[512,1152]{1,0:T(8,128)(2,1)}, bf16[512,1152]{1,0:T(8,128)(2,1)}, u32[]{:S(2)}, u32[]{:S(2)}) collective-permute-start(bf16[512,1152]{1,0:T(8,128)(2,1)} %fusion.38.refs_11_), channel_id=1, source_target_pairs={{0,1},{1,0},{2,3},{3,2},{4,5},{5,4},{6,7},{7,6},{8,9},{9,8},{10,11... | collective-permute-start | bytes 3538952 | tf_op jit(solution)/shard_map/ppermute | solution.py:47
  877.8 32.2 %collective-permute-start.19 = (bf16[72,576]{1,0:T(8,128)(2,1)}, bf16[72,576]{1,0:T(8,128)(2,1)}, u32[]{:S(2)}, u32[]{:S(2)}) collective-permute-start(bf16[72,576]{1,0:T(8,128)(2,1)} %bitcast.291.refs_8_), channel_id=1, source_target_pairs={{0,1},{1,0},{2,3},{3,2},{4,5},{5,4},{6,7},{7,6},{8,9},{9,8},{10,11... | collective-permute-start | bytes 248840 | tf_op jit(solution)/shard_map/ppermute | solution.py:47
  879.0 38.9 %collective-permute-start.20 = (bf16[288,576]{1,0:T(8,128)(2,1)}, bf16[288,576]{1,0:T(8,128)(2,1)}, u32[]{:S(2)}, u32[]{:S(2)}) collective-permute-start(bf16[288,576]{1,0:T(8,128)(2,1)} %bitcast.288.refs_9_), channel_id=1, source_target_pairs={{0,1},{1,0},{2,3},{3,2},{4,5},{5,4},{6,7},{7,6},{8,9},{9,8},{10,11... | collective-permute-start | bytes 995336 | tf_op jit(solution)/shard_map/ppermute | solution.py:47
  879.2 77.5 %collective-permute-start.24 = (bf16[512,1152]{1,0:T(8,128)(2,1)}, bf16[512,1152]{1,0:T(8,128)(2,1)}, u32[]{:S(2)}, u32[]{:S(2)}) collective-permute-start(bf16[512,1152]{1,0:T(8,128)(2,1)} %fusion.39.refs_10_), channel_id=1, source_target_pairs={{0,1},{1,0},{2,3},{3,2},{4,5},{5,4},{6,7},{7,6},{8,9},{9,8},{10,11... | collective-permute-start | bytes 3538952 | tf_op jit(solution)/shard_map/ppermute | solution.py:47
  963.3 66.9 %all-to-all-start.2 = ((f32[32,2,432]{2,1,0:T(2,128)}), f32[32,2,432]{2,1,0:T(2,128)S(1)}, u32[]{:S(2)}, u32[]{:S(2)}) async-start(f32[32,2,432]{2,1,0:T(2,128)} %bitcast.82), calls=%async_computation.4 | async-start | bytes 262144 | tf_op jit(solution)/shard_map/all_to_all | solution.py:318
  1088.4 37.7 %collective-permute-start.34 = (f32[4,1,144,144]{3,2,0,1:T(8,128)}, f32[4,1,144,144]{3,2,0,1:T(8,128)}, u32[]{:S(2)}, u32[]{:S(2)}) collective-permute-start(f32[4,1,144,144]{3,2,0,1:T(8,128)} %get-tuple-element.193), channel_id=1, source_target_pairs={{0,4},{2,6},{4,0},{6,2},{8,12},{10,14},{12,8},{14,10},{16,20},{18,... | collective-permute-start | bytes 995336 | tf_op jit(solution)/shard_map/ppermute | solution.py:47
  1090.4 49.9 %collective-permute-start.45 = (f32[4,2,144,144]{3,2,1,0:T(8,128)S(1)}, f32[4,2,144,144]{3,2,1,0:T(8,128)}, u32[]{:S(2)}, u32[]{:S(2)}) collective-permute-start(f32[4,2,144,144]{3,2,1,0:T(8,128)S(1)} %copy-done), channel_id=1, source_target_pairs={{0,2},{2,0},{4,6},{6,4},{8,10},{10,8},{12,14},{14,12},{16,18},{18,... | collective-permute-start | bytes 1990664 | tf_op jit(solution)/shard_map/ppermute | solution.py:47
  1115.7 32.8 %all-to-all-start.3 = ((f32[32,1,1656]{2,1,0:T(1,128)}), f32[32,1,1656]{2,1,0:T(1,128)}, u32[]{:S(2)}, u32[]{:S(2)}) async-start(f32[32,1,1656]{2,1,0:T(1,128)} %all_to_all.24), calls=%async_computation.5 | async-start | bytes 425984 | tf_op jit(solution)/shard_map/all_to_all | solution.py:318
  (142 other events, 2180.3 us)
Sparse Core Ops, SparseCore 0:
  57.0 46.5 all-gather.3
  106.4 124.0 all-gather.5
  233.4 87.4 all-gather.7
  463.5 60.8 reduce-scatter.12
  528.8 121.1 reduce-scatter.10
  654.4 119.9 reduce-scatter.8
  855.6 100.5 reduce-scatter.14

commit v5 on v4

--- a/solution.py
+++ b/solution.py
@@ -287,6 +287,49 @@
         full = place(self.spots(), sources, (zs, 2, 2, g, unit, depth), ga, parts, shapes)
         return [f.reshape(-1, f.shape[-1]) for f in full], lines[1:] + pairs[1:]
 
+    def scatter_steps(self, own, other, layout, part):
+        zs, _, g, unit, depth = own.shape
+        ga = max(1, int(part * g))
+        x, z = self.x.digit(), self.z.digit()
+        got = self.core.send(other, 1)
+        anchor = yield [other]
+        half = (own.astype(F32) + tie(got, anchor).astype(F32)).astype(BF)
+
+        def line_steps():
+            line = yield from self.x.scatter_steps(
+                lambda s: lax.dynamic_index_in_dim(half[:, :, :ga], (x + s) % 2, 1, keepdims=False)
+            )
+            line = line.astype(BF)
+            return (
+                yield from self.z.scatter_steps(
+                    lambda s: lax.dynamic_index_in_dim(line, (z + s) % zs, 0, keepdims=False), 1
+                )
+            )
+
+        def pair_steps():
+            pair = yield from self.z.scatter_steps(
+                lambda s: lax.dynamic_index_in_dim(half[:, :, ga:], (z + s) % zs, 0, keepdims=False), -1
+            )
+            pair = pair.astype(BF)
+            return (
+                yield from self.x.scatter_steps(
+                    lambda s: lax.dynamic_index_in_dim(pair, (x + s) % 2, 0, keepdims=False)
+                )
+            )
+
+        line, pair = yield from lockstep(line_steps(), pair_steps())
+        joined = jnp.concatenate([line, pair], axis=0).astype(BF)
+        count = layout[0][1]
+        if count > 1:
+            joined = jnp.transpose(joined.reshape(count, -1, unit, depth), (1, 2, 0, 3))
+        joined = joined.reshape(-1, self.seq, count * depth // self.seq)
+        y = self.y.digit()
+        return (
+            yield from self.y.scatter_steps(
+                lambda s: lax.dynamic_index_in_dim(joined, (y + s) % self.seq, 1, keepdims=False)
+            )
+        )
+
 
     def muon_steps(self, groups, masters, rates):
         momenta, own, other = muon_gram(self.spots(), self.z.size, groups)
@@ -353,73 +396,110 @@
     return jnp.einsum("srn,srk->nk", left, right, preferred_element_type=F32).astype(BF)
 
 
-def joined_outer_kernel(loads, parts, counts, tile, *refs):
-    inputs, out = refs[: counts[0]], refs[counts[1]]
-    buffers = refs[counts[1] + 1 : counts[1] + 1 + len(loads)]
-    acc, in_sems, out_sems = refs[counts[1] + 1 + len(loads) :]
-    arrivals = []
-    for n, (sources, start, size) in enumerate(loads):
+def shard_outer_kernel(plan, counts, tile, split, spots_ref, *refs):
+    outs = 2 if split else 1
+    inputs, where = refs[: counts[0]], refs[counts[1] : counts[1] + outs]
+    buffers = refs[counts[1] + outs : counts[1] + outs + len(plan["loads"])]
+    acc, in_sems, out_sems = refs[counts[1] + outs + len(plan["loads"]) :]
+    loads = []
+    for n, (sources, start, size) in enumerate(plan["loads"]):
         row, copies = 0, []
         for m, source in enumerate(sources):
             rows = inputs[source].shape[0]
             window = inputs[source].at[:, pl.ds(start, size)]
             copies.append(pltpu.make_async_copy(window, buffers[n].at[pl.ds(row, rows)], in_sems.at[n, m]))
+            copies[-1].start()
             row += rows
-        arrivals.append(copies)
-    order = [n for part in parts for n in part]
-    for n in sorted(range(len(loads)), key=order.index):
-        for copy in arrivals[n]:
-            copy.start()
-    ready, exits = set(), []
-    for n, (left, right) in enumerate(parts):
-        for m in (left, right):
-            if m not in ready:
-                for copy in arrivals[m]:
+        loads.append(copies)
+    ready = set()
+    shipped = []
+    unit = acc.shape[1]
+    for left, right, base, ships in plan["parts"]:
+        for n in (left, right):
+            if n not in ready:
+                for copy in loads[n]:
                     copy.wait()
-                ready.add(m)
+                ready.add(n)
         width = buffers[left].shape[1]
         step = tile if width % tile == 0 else width
 
         @pl.loop(0, width // step)
         def _(t):
-            spot = pl.multiple_of(t * step, step)
+            block = buffers[left][:, pl.ds(pl.multiple_of(t * step, step), step)]
             product = lax.dot_general(
-                buffers[left][:, pl.ds(spot, step)],
-                buffers[right][...],
-                (((0,), (0,)), ((), ())),
-                preferred_element_type=F32,
+                block, buffers[right][...], (((0,), (0,)), ((), ())), preferred_element_type=F32
             )
-            acc[n, pl.ds(spot, step)] = product.astype(BF)
-
-        exits.append(pltpu.make_async_copy(acc.at[n], out.at[pl.ds(n * width, width)], out_sems.at[n]))
-        exits[-1].start()
-    for copy in exits:
-        copy.wait()
-
-
-def joined_outer(inputs, loads, parts, deps=(), tile=384):
+            product = product.reshape(step // unit, unit, product.shape[1]).astype(BF)
+            acc[pl.ds(base + t * (step // unit), step // unit)] = product
+
+        for core, z, x, row, target, size in ships:
+            spot = (z, x) if split else (z, x, core)
+            places = [ref.at[(*spot, pl.ds(target, size))] for ref in where]
+            copies = [
+                pltpu.make_async_copy(acc.at[pl.ds(row, size)], each, out_sems.at[len(shipped)]) for each in places
+            ]
+            shipped.append((core, copies))
+            on_own_core(split, spots_ref, core, [copy.start for copy in copies])
+    for core, copies in shipped:
+        on_own_core(split, spots_ref, core, [copy.wait for copy in copies])
+
+
+def on_own_core(split, spots_ref, core, actions):
+    if not split:
+        actions[0]()
+        return
+
+    @pl.when(spots_ref[2] == core)
+    def _():
+        actions[0]()
+
+    @pl.when(spots_ref[2] != core)
+    def _():
+        actions[1]()
+
+
+def shard_outer(spots, inputs, loads, parts, zs, depth, unit, shard_units, deps=(), tile=384, split=True):
+    dp = zs * 4
+    plan_parts, base, row, placed = [], 0, 0, {}
+    begun = {}
+    for left, right, rows, first in parts:
+        if first not in begun:
+            begun[first] = (base, 0)
+        start, shipped = begun[first]
+        width = loads[left][2]
+        size = rows // unit
+        end = base + width // unit
+        ships = []
+        while shipped < dp and start + (shipped + 1) * size <= end:
+            core, x, z = shipped % 2, shipped // 2 % 2, shipped // 4
+            ships.append((core, z, x, start + shipped * size, first, size))
+            shipped += 1
+        begun[first] = (start, shipped)
+        plan_parts.append((left, right, base, ships))
+        base = end
+    total = sum(len(part[3]) for part in plan_parts)
+    shape = (zs, 2, shard_units, unit, depth) if split else (zs, 2, 2, shard_units, unit, depth)
+    outs = [jax.ShapeDtypeStruct(shape, BF)] * (2 if split else 1)
+    anywhere = pl.BlockSpec(memory_space=pl.ANY)
     heights = [sum(inputs[source].shape[0] for source in sources) for sources, _, _ in loads]
-    width, depth = loads[parts[0][0]][2], loads[parts[0][1]][2]
-    anywhere = pl.BlockSpec(memory_space=pl.ANY)
+    flops = sum(2 * heights[p[0]] * loads[p[0]][2] * loads[p[1]][2] for p in parts)
     return pl.pallas_call(
-        functools.partial(joined_outer_kernel, loads, parts, (len(inputs), len(inputs) + len(deps)), tile),
-        out_shape=jax.ShapeDtypeStruct((len(parts) * width, depth), BF),
-        in_specs=[anywhere] * (len(inputs) + len(deps)),
-        out_specs=anywhere,
+        functools.partial(
+            shard_outer_kernel, {"loads": loads, "parts": plan_parts}, (len(inputs), len(inputs) + len(deps)), tile, split
+        ),
+        out_shape=outs,
+        in_specs=[pl.BlockSpec(memory_space=pltpu.SMEM)] + [anywhere] * (len(inputs) + len(deps)),
+        out_specs=[anywhere] * len(outs),
         scratch_shapes=[pltpu.VMEM((height, load[2]), BF) for height, load in zip(heights, loads)]
         + [
-            pltpu.VMEM((len(parts), width, depth), BF),
+            pltpu.VMEM((base, unit, depth), BF),
             pltpu.SemaphoreType.DMA((len(loads), max(len(load[0]) for load in loads))),
-            pltpu.SemaphoreType.DMA((len(parts),)),
+            pltpu.SemaphoreType.DMA((total,)),
         ],
         compiler_params=pltpu.CompilerParams(vmem_limit_bytes=VMEM_LIMIT),
-        cost_estimate=pl.CostEstimate(
-            flops=sum(2 * heights[left] * width * depth for left, _ in parts),
-            bytes_accessed=2 * sum(heights) * width + 2 * len(parts) * width * depth,
-            transcendentals=0,
-        ),
-        name="joined_outer",
-    )(*inputs, *deps)
+        cost_estimate=pl.CostEstimate(flops=flops, bytes_accessed=2 * base * unit * depth, transcendentals=0),
+        name="shard_outer",
+    )(spots, *inputs, *deps)
 
 
 LANES = 128
@@ -764,19 +844,18 @@
     bounds = [0, 6 * width, 7 * width, 8 * width, 9 * width, 9 * width + hidden, 10 * width + hidden]
 
     n_qkv, n_proj, n_fc1, n_fc2 = [w.shape[1] for w in (w_qkv, w_proj, w_fc1, w_fc2)]
+    unit = math.gcd(math.gcd(n_qkv, n_proj), 8)
     unit_qkv, layout_qkv = math.gcd(n_qkv, 8), [(n_qkv, 1)]
     own_tokens = tokens.reshape(count, rows, width)
-    wires = net.y.gather(net.wire([w_qkv]))
-    units_qkv = net.joined(wires, unit_qkv, width)
+    wires = net.y.gather(net.wire([w_qkv, w_proj]))
+    first = Staged(net.gather_steps(net.joined(wires, unit, width), [(n_qkv, 1), (n_proj, 1)], 0.45))
+    sent = [first.advance(), first.advance(), first.advance()]
     token_pieces = [net.y.gather(tie(own_tokens[0], wires[-1]))]
-    wires = net.y.gather(tie(net.wire([w_proj, w_fc1]), token_pieces[0][-1]))
+    wires = net.y.gather(tie(net.wire([w_fc1]), token_pieces[0][-1], *sent[2]))
+    t_fc1 = lax.all_gather(net.rows(wires), "dp", axis=0, tiled=True)
     for i in range(1, count):
         token_pieces.append(net.y.gather(tie(own_tokens[i], wires[-1])))
-    rows_mid = net.rows(wires)
-    t_proj = lax.all_gather(rows_mid[:n_proj], "dp", axis=0, tiled=True)
-    t_fc1 = lax.all_gather(rows_mid[n_proj:], "dp", axis=0, tiled=True)
-    wires = net.y.gather(tie(net.wire([w_fc2]), token_pieces[-1][-1]))
-    t_fc2 = lax.all_gather(net.rows(wires), "dp", axis=0, tiled=True)
+    t_qkv, t_proj = first.finish()[0]
 
     ada_rows, ada_cols = w_ada.shape
     cond = conditioning.astype(F32).reshape(count, width)
@@ -792,7 +871,6 @@
     low_ada = w_ada.astype(BF)
     partial = jnp.dot(cond_all, low_ada, preferred_element_type=F32).reshape(dp, 1, count, ada_cols)
     received = jnp.sum(net.to_all(jnp.broadcast_to(partial, (dp, seq, count, ada_cols))), axis=1)
-    (t_qkv,), _ = Staged(net.gather_steps(units_qkv, layout_qkv, 0.45)).finish()
     modulation = jnp.transpose(received, (1, 0, 2)).reshape(count, dp * ada_cols) + b_ada
     shift_one, scale_one, gate_one, shift_two, scale_two, gate_two = jnp.split(
         modulation[:, None, :], 6, axis=-1
@@ -808,6 +886,11 @@
         keys.append(dot_t(attn[None], t_qkv[width : 2 * width]).astype(BF))
         values.append((dot_t(attn[None], t_qkv[2 * width :]) + b_v).astype(BF))
         mixed, lse = attend(lengths[i : i + 1], offsets, queries[i], keys[i], values[i], HEADS, 512)
+        if i == 0:
+            token_pieces[1:] = [each[:1] + [tie(a, mixed) for a in each[1:]] for each in token_pieces[1:]]
+            last_piece = token_pieces[-1][-1] if count > 1 else mixed
+            wires = net.y.gather(tie(net.wire([w_fc2]), last_piece))
+            t_fc2 = lax.all_gather(net.rows(wires), "dp", axis=0, tiled=True)
         normed_all.append(normed[:rows])
         inverse_all.append(inverse[:rows])
         attn_all.append(attn)
@@ -826,16 +909,15 @@
     grad_out = upstream.reshape(count, rows, width).astype(F32)
     grad_branch_two = (gate_two * grad_out).astype(BF)
     flat = lambda array: array.reshape(-1, array.shape[-1])
-    sum_fc2 = net.scatter(outer(grad_branch_two, activated_low))
-    branch_two = dot_t(activated_low, t_fc2) + b_fc2
+    term_fc2 = outer(grad_branch_two, activated_low)
+    sum_fc2 = net.scatter(term_fc2)
+    branch_two = dot_t(tie(activated_low, term_fc2), t_fc2) + b_fc2
+    grad_branch_two = tie(grad_branch_two, term_fc2)
     result = (mixed_one + gate_two * branch_two).astype(BF)
 
     grad_gate_two = jnp.sum(branch_two * grad_out, axis=1)
     bias_fc2 = jnp.sum(grad_branch_two.astype(F32), axis=(0, 1))
     grad_pre = gelu_back(dot(grad_branch_two, t_fc2))[0].astype(BF)
-    term_fc1 = outer(grad_pre, ffn_in)
-    sum_fc1 = net.scatter(term_fc1)
-    grad_pre = tie(grad_pre, term_fc1)
     bias_fc1 = jnp.sum(grad_pre.astype(F32), axis=(0, 1))
     grad_ffn_in = dot(grad_pre, t_fc1)
     grad_shift_two = jnp.sum(grad_ffn_in, axis=1)
@@ -843,9 +925,17 @@
     grad_mixed = grad_out + norm_back(normed_two, inverse_two, grad_ffn_in * (1.0 + scale_two))
     grad_gate_one = jnp.sum(branch_one * grad_mixed, axis=1)
     grad_branch_one = (gate_one * grad_mixed).astype(BF)
-    term_proj = outer(grad_branch_one, attended_low)
-    sum_proj = net.scatter(term_proj)
-    grad_branch_one = tie(grad_branch_one, term_proj)
+    unit_mid = math.gcd(math.gcd(n_proj, n_fc1), 8)
+    (term_mid,) = shard_outer(
+        net.spots(),
+        [flat(grad_pre), flat(ffn_in), flat(grad_branch_one), flat(attended_low)],
+        [([2], 0, width), ([3], 0, width), ([1], 0, width)] + [([0], j * width, width) for j in range(hidden // width)],
+        [(0, 1, n_proj, 0)] + [(3 + j, 2, n_fc1, n_proj // unit_mid) for j in range(hidden // width)],
+        net.z.size, width, unit_mid, (n_proj + n_fc1) // unit_mid, split=False,
+    )
+    term_mid = tie(term_mid, sum_fc2)
+    sum_mid = net.scatter(term_mid.reshape(dp * (n_proj + n_fc1), width))
+    grad_branch_one = tie(grad_branch_one, term_mid)
     bias_proj = jnp.sum(grad_branch_one.astype(F32), axis=(0, 1))
     grad_attended = dot(grad_branch_one, t_proj).astype(BF)
 
@@ -857,11 +947,7 @@
             lengths[i : i + 1], offsets, queries[i], keys[i], values[i], attended_low[i : i + 1],
             grad_attended[i : i + 1], log_total[i], HEADS, 512, sent,
         )
-        if i == 0:
-            early = Staged(lockstep(*[net.halves_steps(tie(each, dq)) for each in (sum_proj, sum_fc1, sum_fc2)]))
-            sent = early.advance()
-        else:
-            sent = early.advance(dq)
+        sent = []
         grad_q.append(dq)
         grad_k.append(dk)
         grad_v.append(dv)
@@ -877,22 +963,15 @@
         )
         sent = sent + far_steps.advance()
         far_parts.append(far_steps)
-    term_qkv = joined_outer(
+    own, other = shard_outer(
+        net.spots(),
         [flat(each) for each in grad_q + grad_k + grad_v] + [attn[:rows] for attn in attn_all] + attn_all,
         [([n * count + i for i in range(count)], 0, width) for n in range(5)],
-        [(0, 3), (1, 4), (2, 4)],
-        sent,
+        [(0, 3, n_qkv, 0), (1, 4, n_qkv, 0), (2, 4, n_qkv, 0)],
+        net.z.size, width, unit_qkv, n_qkv // unit_qkv, sent,
     )
-    sum_qkv = net.scatter(term_qkv)
-    sums = early.finish(term_qkv)
-    chain = Staged(
-        net.muon_steps(
-            [(sums[0], [turned[1]]), (sums[1], [turned[2]]), (sums[2], [turned[3]])],
-            [w_proj.T, w_fc1.T, w_fc2.T],
-            [1.0, math.sqrt(hidden / width), math.sqrt(width / hidden)],
-        )
-    )
-    sent = chain.advance()
+    back_qkv = Staged(net.scatter_steps(own, other, layout_qkv, 0.45))
+    sent = back_qkv.advance()
     grad_q[0] = tie(grad_q[0], *sent)
     bias_q = sum(jnp.sum(each.astype(F32), axis=(0, 1)) for each in grad_q)
     bias_v = sum(jnp.sum(each.astype(F32), axis=(0, 1)) for each in grad_v)
@@ -905,7 +984,11 @@
         ],
         axis=0,
     )
-    sent = chain.advance(own_part)
+    sent = back_qkv.advance(own_part)
+    early = Staged(
+        lockstep(*[net.halves_steps(tie(each, *sent)) for each in (sum_fc2, sum_mid)])
+    )
+    sent = early.advance()
     far_sum = jnp.stack([steps_of.finish() for steps_of in far_parts])
     grad_attn_in = tie(own_part, *sent) + far_sum
     normed_one, inverse_one = jnp.stack(normed_all), jnp.stack(inverse_all)
@@ -921,20 +1004,28 @@
     sent = jnp.transpose(grad_mod_local.reshape(count, dp, 1, ada_cols), (1, 2, 0, 3))
     sent = jnp.broadcast_to(sent, (dp, seq, count, ada_cols))
     mod_parts = net.to_all(sent)
-    anchor = grad_mod_local
-    while not chain.done:
-        anchor = (chain.advance(anchor) or [None])[0]
-        if anchor is not None:
-            mod_parts = tie(mod_parts, anchor)
-    halves = Staged(net.halves_steps(tie(sum_qkv, mod_parts)))
-    halves.advance()
+    sent = back_qkv.advance(sent)
+    sums = early.finish(sent[0])
+    chain = Staged(
+        net.muon_steps(
+            [(sums[1], [turned[1], turned[2]]), (sums[0], [turned[3]])],
+            [w_proj.T, w_fc1.T, w_fc2.T],
+            [1.0, math.sqrt(hidden / width), math.sqrt(width / hidden)],
+        )
+    )
+    anchor = chain.advance()[0]
+    while not back_qkv.done:
+        sent = back_qkv.advance(anchor)
+        if sent:
+            mod_parts = tie(mod_parts, *sent)
+            anchor = (chain.advance(sent[0]) or sent)[0]
     mod_cols = jnp.sum(mod_parts, axis=1).astype(BF).reshape(dp * count, ada_cols)
     shard_ada = jnp.einsum("sr,sc->cr", cond_all, mod_cols, preferred_element_type=F32)
 
     last = Staged(
         net.muon_steps(
             [
-                (halves.finish(), [turned[0]]),
+                (back_qkv.result, [turned[0]]),
                 (shard_ada, [turned[4]]),
             ],
             [w_qkv.T, w_ada.T],
@@ -951,6 +1042,8 @@
     while not last.done:
         anchor = sent[0] if sent else None
         sent = last.advance(anchor)
+        sent = sent + chain.advance(sent[0] if sent else None)
+    chain.finish()
     (next_qkv, next_ada), (new_qkv, new_ada) = last.result
     (next_proj, next_fc1, next_fc2), (new_proj, new_fc1, new_fc2) = chain.result
 

time: 1210 us -> 984 us (0.81)
  waiting for transfers between devices: 481 us -> 216 us
  matrix products: 228 us -> 189 us
  other arithmetic: 75.5 us -> 110 us
  Pallas kernels: 241 us -> 270 us
    reduce_scatter x2 -> x1, waiting for transfers between devices: 215 us -> 13.9 us  [scatter(): return lax.psum_scatter(term, 'dp', scatter_dimension=0, tiled=True)]
    ppermute x47 -> x55, waiting for transfers between devices: 260 us -> 194 us  [send(): return lax.ppermute(value, self.name, pairs)]
    pallas_call x1 -> x2, Pallas kernels: 21.6 us -> 49.1 us  [shard_outer(): pl.pallas_call(functools.partial(shard_outer_kernel, {'loads': loads, 'pa...]
    dot_general x3 -> x1, matrix products: 39.6 us -> 17.1 us  [outer(): jnp.einsum('srn,srk->nk', left, right, preferred_element_type=F32)]
    convert_element_type x0 -> x7, other arithmetic: none -> 16.2 us  [the longest x1 4.5 us: scatter_steps(): half = (own.astype(F32) + tie(got, anchor).astype(F32)).astype(BF)]
    unnamed x227 -> x224, local copies, waits for them, and re-layouts: 39.4 us -> 34 us
    ppermute x47 -> x55, starting transfers between devices: 46.7 us -> 51.9 us  [send(): return lax.ppermute(value, self.name, pairs)]
  transfers between devices with their start and end apart: 58 -> 63, of which waited for: 30 -> 22; matrix products, arithmetic and copies ran while one was open for 20% -> 37% of each run, Pallas kernels for 13% -> 26%
where the time goes in v5:
time: 984 us; the launch traced here: 976 us
  Pallas kernels  270 us (27%)
  waiting for transfers between devices  216 us (22%)
  matrix products  189 us (19%)
  other arithmetic  110 us (11%)
  local copies, waits for them, and re-layouts  96.9 us (10%)
  starting transfers between devices  77.6 us (8%)
  between operations  15.4 us (2%)
    ppermute x55, waiting for transfers between devices, send(): return lax.ppermute(value, self.name, pairs)  194 us
    pallas_call x2, Pallas kernels, attend_back(): pl.pallas_call(without(attend_back_kernel, 8, len(deps), heads, tile), gr...  91.4 us
    dot_general x13, matrix products, dot(): return jnp.einsum('srn,nk->srk', left, right, preferred_element_type=F32)  91 us
    dot_general x9, matrix products, dot_t(): return jnp.einsum('srk,nk->srn', left, right, preferred_element_type=F32)  77.1 us
    pallas_call x2, Pallas kernels, attend(): pl.pallas_call(without(attend_kernel, 5, len(deps), heads, tile), grid_sp...  64.6 us
    ppermute x55, starting transfers between devices, send(): return lax.ppermute(value, self.name, pairs)  51.9 us
    pallas_call x2, Pallas kernels, shard_outer(): pl.pallas_call(functools.partial(shard_outer_kernel, {'loads': loads, 'pa...  49.1 us
    unnamed x224, local copies, waits for them, and re-layouts  34 us
  transfers between devices with their start and end apart: 63, of which 22 were waited for; matrix products, arithmetic and copies ran while one was open for 37% of the time, Pallas kernels for 26%

profile of v5, /device:TPU:11, one launch (start us, length us, event | category | flops | bytes accessed | tf_op | source)
XLA Modules:
  0.0 975.8 jit_solution(8789553996738829091)
XLA Ops:
  34.3 17.6 %collective-permute-done.2 = bf16[16,8,1152]{2,1,0:T(8,128)(2,1)S(1)} collective-permute-done((bf16[16,8,1152]{2,1,0:T(8,128)(2,1)S(1)}, bf16[16,8,1152]{2,1,0:T(8,128)(2,1)S(1)}, u32[]{:S(2)}, u32[]{:S(2)}) %collective-permute-start.2) | collective-permute-done | bytes 294944 | tf_op jit(solution)/shard_map/ppermute | solution.py:47
  51.8 10.2 %collective-permute-done.4 = bf16[16,8,1152]{2,1,0:T(8,128)(2,1)S(1)} collective-permute-done((bf16[16,8,1152]{2,1,0:T(8,128)(2,1)S(1)}, bf16[16,8,1152]{2,1,0:T(8,128)(2,1)S(1)}, u32[]{:S(2)}, u32[]{:S(2)}) %collective-permute-start.4) | collective-permute-done | bytes 294944 | tf_op jit(solution)/shard_map/ppermute | solution.py:47
  128.6 45.7 %collective-permute-done.5.refs_2_ = bf16[4,16,8,1152]{3,2,1,0:T(8,128)(2,1)} collective-permute-done((bf16[4,16,8,1152]{3,2,1,0:T(8,128)(2,1)S(1)}, bf16[4,16,8,1152]{3,2,1,0:T(8,128)(2,1)}, u32[]{:S(2)}, u32[]{:S(2)}) %collective-permute-start.5) | collective-permute-done | bytes 1179680 | tf_op jit(solution)/shard_map/ppermute | solution.py:47
  176.4 16.8 %collective-permute-done.8.refs_5_ = bf16[2,20,8,1152]{3,2,1,0:T(8,128)(2,1)} collective-permute-done((bf16[2,20,8,1152]{3,2,1,0:T(8,128)(2,1)}, bf16[2,20,8,1152]{3,2,1,0:T(8,128)(2,1)}, u32[]{:S(2)}, u32[]{:S(2)}) %collective-permute-start.8) | collective-permute-done | bytes 737312 | tf_op jit(solution)/shard_map/ppermute | solution.py:47
  198.6 9.1 place.1
  222.1 32.4 %attend.2 = (bf16[1,512,1152]{2,1,0:T(8,128)(2,1)}, f32[1,16,1,512]{3,2,1,0:T(1,128)}) custom-call(s32[1]{0:T(128)} %bitcast.8.refs_0_, s32[2]{0:T(128)} %pad_add_fusion.refs_1_, bf16[1,512,1152]{2,1,0:T(8,128)(2,1)} %fusion.37.refs_2_, bf16[1,1024,1152]{2,1,0:T(8,128)(2,1)} %fusion.30.refs_3_, bf16[1,1024,1152]{2,1,0:T(8,128)(2,1)} %fusion.28.refs_4_), custom_call_target="tpu_custom_call" | custom-call | flops 4294967296 | bytes 7077888 | tf_op jit(solution)/shard_map/attend/pallas_call | solution.py:585
  256.3 8.6 collective-permute-done.18
  289.9 32.2 %attend.3 = (bf16[1,512,1152]{2,1,0:T(8,128)(2,1)}, f32[1,16,1,512]{3,2,1,0:T(1,128)}) custom-call(s32[1]{0:T(128)} %bitcast.29.refs_0_, s32[2]{0:T(128)} %pad_add_fusion.refs_1_, bf16[1,512,1152]{2,1,0:T(8,128)(2,1)} %fusion.36.refs_2_, bf16[1,1024,1152]{2,1,0:T(8,128)(2,1)} %fusion.31.refs_3_, bf16[1,1024,1152]{2,1,0:T(8,128)(2,1)} %fusion.29.refs_4_), custom_call_target="tpu_custom_call" | custom-call | flops 4294967296 | bytes 7077888 | tf_op jit(solution)/shard_map/attend/pallas_call | solution.py:585
  337.5 23.9 %multiply_convert_fusion = (bf16[2,512,4608]{2,1,0:T(8,128)(2,1)}, f32[2,512,4608]{2,1,0:T(8,128)}) fusion(f32[4608]{0:T(1024)S(1)} %slice.274, bf16[2,512,1152]{2,1,0:T(8,128)(2,1)} %add_convert_fusion.3, bf16[4608,1152]{1,0:T(8,128)(2,1)} %all-gather.3.cloned.1.call-done), kind=kOutput, calls=%fused_computation.12 | convolution fusion | flops 10918821888 | bytes 41306112 | tf_op jit(solution)/shard_map/srk,nk->srn/dot_general | solution.py:388
  361.4 17.1 %fusion.refs_1_ = bf16[1152,4608]{1,0:T(8,128)(2,1)} fusion(bf16[2,512,1152]{2,1,0:T(8,128)(2,1)S(1)} %fusion.24.refs_0_, bf16[2,512,4608]{2,1,0:T(8,128)(2,1)} %get-tuple-element.235.refs_0_), kind=kOutput, calls=%fused_computation.3 | convolution fusion | flops 10876944384 | bytes 22413312 | tf_op jit(solution)/shard_map/srn,srk->nk/dot_general | solution.py:396
  378.7 30.3 %convert_reduce_fusion = (f32[4608]{0:T(1024)}, bf16[2,512,4608]{2,1,0:T(8,128)(2,1)}) fusion(f32[2,512,4608]{2,1,0:T(8,128)} %get-tuple-element.236, f32[4608]{0:T(1024)S(1)} %slice.274, bf16[2,512,1152]{2,1,0:T(8,128)(2,1)} %tie.56, bf16[1152,4608]{1,0:T(8,128)(2,1)} %all-gather.5.cloned.1.call-done), kind=kOutput, calls=%fused_computation.11 | convolution fusion | flops 10980159488 | bytes 41324544 | tf_op jit(solution)/shard_map/srn,nk->srk/dot_general | solution.py:392
  409.0 21.6 %multiply_reduce_fusion = (f32[2,1152]{1,0:T(2,128)}, f32[2,512]{1,0:T(2,128)S(1)}, f32[2,512]{1,0:T(2,128)S(1)}, f32[2,1152]{1,0:T(2,128)}, f32[2,512,1152]{2,1,0:T(8,128)}) fusion(f32[2,512,1152]{2,1,0:T(8,128)S(1)} %bitcast.312, f32[2,512]{1,0:T(2,128)S(1)} %add_rsqrt_fusion, f32[2,512]{1,0:T(2,128)S(1)} %broadcast_multiply_fusion.4, ...), kind=kOutput, calls=%fused_computation.44 | convolution fusion | flops 10882246656 | bytes 29535232 | tf_op jit(solution)/shard_map/srn,nk->srk/dot_general | solution.py:392
  430.6 18.2 %fusion.19 = f32[2,512,1152]{2,1,0:T(8,128)} fusion(bf16[2,512,4608]{2,1,0:T(8,128)(2,1)S(1)} %copy-done.16, bf16[1152,4608]{1,0:T(8,128)(2,1)} %all-gather.5.cloned.1.call-done, f32[1152]{0:T(1024)S(1)} %copy-done.86), kind=kOutput, calls=%fused_computation.32 | convolution fusion | flops 10872815616 | bytes 24777216 | tf_op jit(solution)/shard_map/srk,nk->srn/dot_general | solution.py:388
  460.1 23.7 %shard_outer.2.refs_0_ = bf16[4,2,2,45,8,1152]{5,4,3,2,1,0:T(8,128)(2,1)} custom-call(s32[3]{0:T(128)} %pad_add_fusion.1.refs_0_.spots_ref, bf16[1024,4608]{1,0:T(8,128)(2,1)} %bitcast.380, bf16[1024,1152]{1,0:T(8,128)(2,1)} %bitcast.320, bf16[1024,1152]{1,0:T(8,128)(2,1)} %bitcast.313, bf16[1024,1152]{1,0:T(8,128)(2,1)} %bitcast.339), custom_call_target="tpu_custom_call" | custom-call | flops 13589544960 | bytes 13271040 | tf_op jit(solution)/shard_map/shard_outer/pallas_call | solution.py:486
  483.9 13.9 %reduce-scatter.5.cloned.1.call-done.refs_1_.refs_0_ = bf16[72,4608]{1,0:T(8,128)(2,1)} async-done(((bf16[1152,4608]{1,0:T(8,128)(2,1)}), bf16[72,4608]{1,0:T(8,128)(2,1)}) %reduce-scatter.5.cloned.1.call-update) | async-done | bytes 663568 | tf_op jit(solution)/shard_map/reduce_scatter | solution.py:249
  516.7 46.4 %attend_back.2 = (bf16[1,512,1152]{2,1,0:T(8,128)(2,1)}, bf16[1,1024,1152]{2,1,0:T(8,128)(2,1)}, bf16[1,1024,1152]{2,1,0:T(8,128)(2,1)}) custom-call(s32[1]{0:T(128)} %bitcast.8.refs_0_, s32[2]{0:T(128)} %pad_add_fusion.refs_1_, bf16[1,512,1152]{2,1,0:T(8,128)(2,1)} %fusion.37.refs_2_, bf16[1,1024,1152]{2,1,0:T(8,128)(2,1)} %fusion.30.refs_3_, ...), custom_call_target="tpu_custom_call" | custom-call | flops 10737418240 | bytes 14155776 | tf_op jit(solution)/shard_map/attend_back/pallas_call | solution.py:670
  571.8 45.1 %attend_back.3 = (bf16[1,512,1152]{2,1,0:T(8,128)(2,1)}, bf16[1,1024,1152]{2,1,0:T(8,128)(2,1)}, bf16[1,1024,1152]{2,1,0:T(8,128)(2,1)}) custom-call(s32[1]{0:T(128)} %bitcast.29.refs_0_, s32[2]{0:T(128)} %pad_add_fusion.refs_1_, bf16[1,512,1152]{2,1,0:T(8,128)(2,1)} %fusion.36.refs_2_, bf16[1,1024,1152]{2,1,0:T(8,128)(2,1)} %fusion.31.refs_3_, ...), custom_call_target="tpu_custom_call" | custom-call | flops 10737418240 | bytes 14155776 | tf_op jit(solution)/shard_map/attend_back/pallas_call | solution.py:670
  625.7 25.3 %shard_outer.3 = (bf16[4,2,27,8,1152]{4,3,2,1,0:T(8,128)(2,1)}, bf16[4,2,27,8,1152]{4,3,2,1,0:T(8,128)(2,1)}) custom-call(s32[3]{0:T(128)} %pad_add_fusion.1.refs_0_.spots_ref, bf16[512,1152]{1,0:T(8,128)(2,1)} %bitcast.316, bf16[512,1152]{1,0:T(8,128)(2,1)} %bitcast.328, bf16[1024,1152]{1,0:T(8,128)(2,1)} %bitcast.381, bf16[1024,1152]{1,0:T(8,128)(2,1)} %bitcast.382, ...), custom_call_target="tpu_custom_call" | custom-call | flops 13589544960 | bytes 7962624 | tf_op jit(solution)/shard_map/shard_outer/pallas_call | solution.py:486
  736.3 17.7 %muon_gram.2 = (f32[72,576]{1,0:T(8,128)}, f32[288,576]{1,0:T(8,128)}, f32[72,2304]{1,0:T(8,128)}, f32[2,4,2,144,144]{4,3,2,1,0:T(8,128)}, f32[2,4,2,144,144]{4,3,2,1,0:T(8,128)}) custom-call(s32[3]{0:T(128)} %pad_add_fusion.1.refs_0_.spots_ref, f32[360,576]{1,0:T(8,128)} %convert_add_fusion.6.refs_0_, f32[72,2304]{1,0:T(8,128)} %convert_add_fusion.7.refs_1_, ...), custom_call_target="tpu_custom_call" | custom-call | tf_op jit(solution)/shard_map/muon_gram/pallas_call | solution.py:756
  785.5 9.8 collective-permute-done.34.refs_0_
  800.2 9.1 muon_gram.3
  835.5 14.0 %collective-permute-done.47.refs_0_ = f32[2,144,144]{2,1,0:T(8,128)S(1)} collective-permute-done((f32[2,144,144]{2,1,0:T(8,128)}, f32[2,144,144]{2,1,0:T(8,128)S(1)}, u32[]{:S(2)}, u32[]{:S(2)}) %collective-permute-start.47) | collective-permute-done | bytes 165920 | tf_op jit(solution)/shard_map/ppermute | solution.py:47
  870.3 23.4 %collective-permute-done.50.refs_0_ = f32[2,144,144]{2,1,0:T(8,128)} collective-permute-done((f32[2,144,144]{2,1,0:T(8,128)}, f32[2,144,144]{2,1,0:T(8,128)}, u32[]{:S(2)}, u32[]{:S(2)}) %collective-permute-start.50) | collective-permute-done | bytes 165920 | tf_op jit(solution)/shard_map/ppermute | solution.py:47
  935.2 12.1 %collective-permute-done.43.refs_0_ = f32[4,1,144,144]{3,2,1,0:T(8,128)S(1)} collective-permute-done((f32[4,1,144,144]{3,2,1,0:T(8,128)S(1)}, f32[4,1,144,144]{3,2,1,0:T(8,128)S(1)}, u32[]{:S(2)}, u32[]{:S(2)}) %collective-permute-start.43) | collective-permute-done | bytes 331808 | tf_op jit(solution)/shard_map/ppermute | solution.py:47
  (561 shorter events, 436.3 us)
Async XLA Ops:
  7.2 330.4 %all-gather.3.cloned.1.call-start = ((), (), s32[]{:S(2)}) async-start(), calls=%async_computation.6 | async-start | bytes 11280384 | tf_op jit(solution)/shard_map/all_gather | solution.py:855
  20.3 43.0 %collective-permute-start.1 = (bf16[512,1152]{1,0:T(8,128)(2,1)}, bf16[512,1152]{1,0:T(8,128)(2,1)S(1)}, u32[]{:S(2)}, u32[]{:S(2)}) collective-permute-start(bf16[512,1152]{1,0:T(8,128)(2,1)} %tie.50), channel_id=1, source_target_pairs={{0,1},{1,0},{2,3},{3,2},{4,5},{5,4},{6,7},{7,6},{8,9},{9,8},{10,11... | collective-permute-start | bytes 3538952 | tf_op jit(solution)/shard_map/ppermute | solution.py:47
  114.3 264.4 %all-gather.5.cloned.1.call-start = ((), (), s32[]{:S(2)}) async-start(), calls=%async_computation.7 | async-start | bytes 11280384 | tf_op jit(solution)/shard_map/all_gather | solution.py:893
  123.8 50.6 %collective-permute-start.5 = (bf16[4,16,8,1152]{3,2,1,0:T(8,128)(2,1)S(1)}, bf16[4,16,8,1152]{3,2,1,0:T(8,128)(2,1)}, u32[]{:S(2)}, u32[]{:S(2)}) collective-permute-start(bf16[4,16,8,1152]{3,2,1,0:T(8,128)(2,1)S(1)} %copy-done.14), channel_id=1, source_target_pairs={{0,4},{2,6},{4,0},{6,2},{8,12},{10,14},{12,8},{14,10},{16,20},{18,... | collective-permute-start | bytes 3538952 | tf_op jit(solution)/shard_map/ppermute | solution.py:47
  125.7 50.1 %collective-permute-start.9 = (bf16[2,20,8,1152]{3,2,1,0:T(8,128)(2,1)}, bf16[2,20,8,1152]{3,2,1,0:T(8,128)(2,1)}, u32[]{:S(2)}, u32[]{:S(2)}) collective-permute-start(bf16[2,20,8,1152]{3,2,1,0:T(8,128)(2,1)} %copy-done.36), channel_id=1, source_target_pairs={{0,8},{2,10},{4,12},{6,14},{8,16},{10,18},{12,20},{14,22},{16,24},... | collective-permute-start | bytes 2211848 | tf_op jit(solution)/shard_map/ppermute | solution.py:47
  126.2 49.7 %collective-permute-start.12 = (bf16[2,20,8,1152]{3,2,1,0:T(8,128)(2,1)}, bf16[2,20,8,1152]{3,2,1,0:T(8,128)(2,1)}, u32[]{:S(2)}, u32[]{:S(2)}) collective-permute-start(bf16[2,20,8,1152]{3,2,1,0:T(8,128)(2,1)} %copy-done.36), channel_id=1, source_target_pairs={{0,2},{2,0},{4,6},{6,4},{8,10},{10,8},{12,14},{14,12},{16,18},{18,... | collective-permute-start | bytes 2211848 | tf_op jit(solution)/shard_map/ppermute | solution.py:47
  127.2 70.6 %collective-permute-start.10 = (bf16[4,16,8,1152]{3,2,1,0:T(8,128)(2,1)S(1)}, bf16[4,16,8,1152]{3,2,1,0:T(8,128)(2,1)}, u32[]{:S(2)}, u32[]{:S(2)}) collective-permute-start(bf16[4,16,8,1152]{3,2,1,0:T(8,128)(2,1)S(1)} %copy-done.14), channel_id=1, source_target_pairs={{0,2},{2,0},{4,6},{6,4},{8,10},{10,8},{12,14},{14,12},{16,18},{18,... | collective-permute-start | bytes 3538952 | tf_op jit(solution)/shard_map/ppermute | solution.py:47
  127.2 66.1 %collective-permute-start.8 = (bf16[2,20,8,1152]{3,2,1,0:T(8,128)(2,1)}, bf16[2,20,8,1152]{3,2,1,0:T(8,128)(2,1)}, u32[]{:S(2)}, u32[]{:S(2)}) collective-permute-start(bf16[2,20,8,1152]{3,2,1,0:T(8,128)(2,1)} %collective-permute-done.7.refs_4_.refs_3_), channel_id=1, source_target_pairs={{0,24},{2,26},{4,28},{6,30},{8,0},{10,2},{12,4},{14,6},{16,8},{18,... | collective-permute-start | bytes 2211848 | tf_op jit(solution)/shard_map/ppermute | solution.py:47
  197.8 56.7 %collective-permute-start.17 = (bf16[512,1152]{1,0:T(8,128)(2,1)}, bf16[512,1152]{1,0:T(8,128)(2,1)S(1)}, u32[]{:S(2)}, u32[]{:S(2)}) collective-permute-start(bf16[512,1152]{1,0:T(8,128)(2,1)} %tie.52), channel_id=1, source_target_pairs={{0,1},{1,0},{2,3},{3,2},{4,5},{5,4},{6,7},{7,6},{8,9},{9,8},{10,11... | collective-permute-start | bytes 3538952 | tf_op jit(solution)/shard_map/ppermute | solution.py:47
  267.0 230.8 %reduce-scatter.5.cloned.1.call-start = ((), (), s32[]{:S(2)}) async-start(), calls=%async_computation.8 | async-start | bytes 11280384 | tf_op jit(solution)/shard_map/reduce_scatter | solution.py:249
  378.6 315.2 %reduce-scatter.7.cloned.1.call-start = ((), (), s32[]{:S(2)}) async-start(), calls=%async_computation.9 | async-start | bytes 14100480
  652.0 48.0 %collective-permute-start.21 = (bf16[512,1152]{1,0:T(8,128)(2,1)}, bf16[512,1152]{1,0:T(8,128)(2,1)}, u32[]{:S(2)}, u32[]{:S(2)}) collective-permute-start(bf16[512,1152]{1,0:T(8,128)(2,1)} %fusion.35.refs_10_), channel_id=1, source_target_pairs={{0,1},{1,0},{2,3},{3,2},{4,5},{5,4},{6,7},{7,6},{8,9},{9,8},{10,11... | collective-permute-start | bytes 3538952 | tf_op jit(solution)/shard_map/ppermute | solution.py:47
  653.3 51.9 %collective-permute-start.20 = (bf16[512,1152]{1,0:T(8,128)(2,1)}, bf16[512,1152]{1,0:T(8,128)(2,1)}, u32[]{:S(2)}, u32[]{:S(2)}) collective-permute-start(bf16[512,1152]{1,0:T(8,128)(2,1)} %fusion.34.refs_8_), channel_id=1, source_target_pairs={{0,1},{1,0},{2,3},{3,2},{4,5},{5,4},{6,7},{7,6},{8,9},{9,8},{10,11... | collective-permute-start | bytes 3538952 | tf_op jit(solution)/shard_map/ppermute | solution.py:47
  685.1 38.3 %collective-permute-start.27 = (bf16[2,15,8,1152]{3,2,1,0:T(8,128)(2,1)}, bf16[2,15,8,1152]{3,2,1,0:T(8,128)(2,1)}, u32[]{:S(2)}, u32[]{:S(2)}) collective-permute-start(bf16[2,15,8,1152]{3,2,1,0:T(8,128)(2,1)} %get-tuple-element.200.refs_2_), channel_id=1, source_target_pairs={{0,24},{2,26},{4,28},{6,30},{8,0},{10,2},{12,4},{14,6},{16,8},{18,... | collective-permute-start | bytes 1658888 | tf_op jit(solution)/shard_map/ppermute | solution.py:47
  700.1 58.2 %collective-permute-start.26 = (bf16[2,15,8,1152]{3,2,1,0:T(8,128)(2,1)}, bf16[2,15,8,1152]{3,2,1,0:T(8,128)(2,1)}, u32[]{:S(2)}, u32[]{:S(2)}) collective-permute-start(bf16[2,15,8,1152]{3,2,1,0:T(8,128)(2,1)} %get-tuple-element.199), channel_id=1, source_target_pairs={{0,8},{2,10},{4,12},{6,14},{8,16},{10,18},{12,20},{14,22},{16,24},... | collective-permute-start | bytes 1658888 | tf_op jit(solution)/shard_map/ppermute | solution.py:47
  712.6 48.8 %all-to-all-start.2 = ((f32[32,2,432]{2,1,0:T(2,128)}), f32[32,2,432]{2,1,0:T(2,128)S(1)}, u32[]{:S(2)}, u32[]{:S(2)}) async-start(f32[32,2,432]{2,1,0:T(2,128)} %bitcast.89), calls=%async_computation.3 | async-start | bytes 262144 | tf_op jit(solution)/shard_map/all_to_all | solution.py:361
  720.2 36.4 %collective-permute-start.23 = (bf16[12,8,1152]{2,1,0:T(8,128)(2,1)}, bf16[12,8,1152]{2,1,0:T(8,128)(2,1)}, u32[]{:S(2)}, u32[]{:S(2)}) collective-permute-start(bf16[12,8,1152]{2,1,0:T(8,128)(2,1)} %get-tuple-element.208.refs_1_), channel_id=1, source_target_pairs={{0,8},{2,10},{4,12},{6,14},{8,16},{10,18},{12,20},{14,22},{16,24},... | collective-permute-start | bytes 663560 | tf_op jit(solution)/shard_map/ppermute | solution.py:47
  725.9 41.9 %collective-permute-start.31 = (bf16[12,8,1152]{2,1,0:T(8,128)(2,1)}, bf16[12,8,1152]{2,1,0:T(8,128)(2,1)}, u32[]{:S(2)}, u32[]{:S(2)}) collective-permute-start(bf16[12,8,1152]{2,1,0:T(8,128)(2,1)} %get-tuple-element.207.refs_2_), channel_id=1, source_target_pairs={{0,24},{2,26},{4,28},{6,30},{8,0},{10,2},{12,4},{14,6},{16,8},{18,... | collective-permute-start | bytes 663560 | tf_op jit(solution)/shard_map/ppermute | solution.py:47
  820.6 42.8 %collective-permute-start.36 = (f32[4,1,144,144]{3,2,0,1:T(8,128)}, f32[4,1,144,144]{3,2,0,1:T(8,128)}, u32[]{:S(2)}, u32[]{:S(2)}) collective-permute-start(f32[4,1,144,144]{3,2,0,1:T(8,128)} %get-tuple-element.206), channel_id=1, source_target_pairs={{0,4},{2,6},{4,0},{6,2},{8,12},{10,14},{12,8},{14,10},{16,20},{18,... | collective-permute-start | bytes 995336 | tf_op jit(solution)/shard_map/ppermute | solution.py:47
  829.8 74.6 %all-to-all-start.3 = ((f32[32,1,1656]{2,1,0:T(1,128)}), f32[32,1,1656]{2,1,0:T(1,128)}, u32[]{:S(2)}, u32[]{:S(2)}) async-start(f32[32,1,1656]{2,1,0:T(1,128)} %all_to_all.24), calls=%async_computation.4 | async-start | bytes 425984 | tf_op jit(solution)/shard_map/all_to_all | solution.py:361
  865.3 40.7 %collective-permute-start.37 = (f32[1,144,144]{2,1,0:T(8,128)S(1)}, f32[1,144,144]{2,1,0:T(8,128)S(1)}, u32[]{:S(2)}, u32[]{:S(2)}) collective-permute-start(f32[1,144,144]{2,1,0:T(8,128)S(1)} %get-tuple-element.219.refs_1_), channel_id=1, source_target_pairs={{0,8},{2,10},{4,12},{6,14},{8,16},{10,18},{12,20},{14,22},{16,24},... | collective-permute-start | bytes 248840 | tf_op jit(solution)/shard_map/ppermute | solution.py:47
  866.5 40.2 %collective-permute-start.38 = (f32[1,144,144]{2,1,0:T(8,128)S(1)}, f32[1,144,144]{2,1,0:T(8,128)S(1)}, u32[]{:S(2)}, u32[]{:S(2)}) collective-permute-start(f32[1,144,144]{2,1,0:T(8,128)S(1)} %get-tuple-element.218), channel_id=1, source_target_pairs={{0,16},{2,18},{4,20},{6,22},{8,24},{10,26},{12,28},{14,30},{16,0},... | collective-permute-start | bytes 248840 | tf_op jit(solution)/shard_map/ppermute | solution.py:47
  870.3 37.0 %collective-permute-start.39 = (f32[1,144,144]{2,1,0:T(8,128)S(1)}, f32[1,144,144]{2,1,0:T(8,128)S(1)}, u32[]{:S(2)}, u32[]{:S(2)}) collective-permute-start(f32[1,144,144]{2,1,0:T(8,128)S(1)} %get-tuple-element.217), channel_id=1, source_target_pairs={{0,24},{2,26},{4,28},{6,30},{8,0},{10,2},{12,4},{14,6},{16,8},{18,... | collective-permute-start | bytes 248840 | tf_op jit(solution)/shard_map/ppermute | solution.py:47
  897.0 36.1 %collective-permute-start.52 = (f32[4,2,144,144]{3,2,1,0:T(8,128)}, f32[4,2,144,144]{3,2,1,0:T(8,128)}, u32[]{:S(2)}, u32[]{:S(2)}) collective-permute-start(f32[4,2,144,144]{3,2,1,0:T(8,128)} %pad_maximum_fusion.5.refs_0_), channel_id=1, source_target_pairs={{0,4},{2,6},{4,0},{6,2},{8,12},{10,14},{12,8},{14,10},{16,20},{18,... | collective-permute-start | bytes 1990664 | tf_op jit(solution)/shard_map/ppermute | solution.py:47
  (146 other events, 1817.3 us)
Sparse Core Ops, SparseCore 0:
  76.2 121.7 all-gather.2
  267.1 86.3 all-gather.4
  378.7 118.9 reduce-scatter.4
  501.8 139.2 reduce-scatter.6

commit v6 on v5

--- a/solution.py
+++ b/solution.py
@@ -287,52 +287,9 @@
         full = place(self.spots(), sources, (zs, 2, 2, g, unit, depth), ga, parts, shapes)
         return [f.reshape(-1, f.shape[-1]) for f in full], lines[1:] + pairs[1:]
 
-    def scatter_steps(self, own, other, layout, part):
-        zs, _, g, unit, depth = own.shape
-        ga = max(1, int(part * g))
-        x, z = self.x.digit(), self.z.digit()
-        got = self.core.send(other, 1)
-        anchor = yield [other]
-        half = (own.astype(F32) + tie(got, anchor).astype(F32)).astype(BF)
-
-        def line_steps():
-            line = yield from self.x.scatter_steps(
-                lambda s: lax.dynamic_index_in_dim(half[:, :, :ga], (x + s) % 2, 1, keepdims=False)
-            )
-            line = line.astype(BF)
-            return (
-                yield from self.z.scatter_steps(
-                    lambda s: lax.dynamic_index_in_dim(line, (z + s) % zs, 0, keepdims=False), 1
-                )
-            )
-
-        def pair_steps():
-            pair = yield from self.z.scatter_steps(
-                lambda s: lax.dynamic_index_in_dim(half[:, :, ga:], (z + s) % zs, 0, keepdims=False), -1
-            )
-            pair = pair.astype(BF)
-            return (
-                yield from self.x.scatter_steps(
-                    lambda s: lax.dynamic_index_in_dim(pair, (x + s) % 2, 0, keepdims=False)
-                )
-            )
-
-        line, pair = yield from lockstep(line_steps(), pair_steps())
-        joined = jnp.concatenate([line, pair], axis=0).astype(BF)
-        count = layout[0][1]
-        if count > 1:
-            joined = jnp.transpose(joined.reshape(count, -1, unit, depth), (1, 2, 0, 3))
-        joined = joined.reshape(-1, self.seq, count * depth // self.seq)
-        y = self.y.digit()
-        return (
-            yield from self.y.scatter_steps(
-                lambda s: lax.dynamic_index_in_dim(joined, (y + s) % self.seq, 1, keepdims=False)
-            )
-        )
-
-
-    def muon_steps(self, groups, masters, rates):
-        momenta, own, other = muon_gram(self.spots(), self.z.size, groups)
+
+    def muon_scatter_steps(self, groups, spread):
+        momenta, own, other = muon_gram(self.spots(), self.z.size, groups, spread)
         got = self.core.send(other, 1)
         anchor = yield [other]
         half = own + tie(got, anchor)
@@ -343,7 +300,10 @@
         blocks = [kept[shift] for shift in range(self.z.size)]
         got = [self.z.send(blocks[shift], shift) for shift in range(1, self.z.size)]
         anchor = yield blocks[1:]
-        factor = polynomial([blocks[0]] + [tie(each, anchor) for each in got])
+        return momenta, [blocks[0]] + [tie(each, anchor) for each in got]
+
+    def muon_gather_steps(self, parts):
+        factor = polynomial(parts)
         got = [self.z.send(factor, -shift) for shift in range(1, self.z.size)]
         anchor = yield [factor]
         line = jnp.stack([factor] + [tie(each, anchor) for each in got])
@@ -352,8 +312,7 @@
         pair = [line, tie(got, anchor)]
         others = [self.core.send(each, 1) for each in pair]
         anchor = yield pair
-        factors = pair + [tie(each, anchor) for each in others]
-        return momenta, muon_apply(self.spots(), factors, momenta, masters, rates)
+        return pair + [tie(each, anchor) for each in others]
 
 
     def to_all(self, value):
@@ -702,21 +661,22 @@
     )(lengths, offsets, queries, keys, values, mixed, grads, lse, *deps)
 
 
-def block_spots(counts, zs):
-    per = -(-sum(counts) // (4 * zs))
+def block_spots(counts, spread):
+    per, first = spread
     spots = []
     for matrix, count in enumerate(counts):
         for block in range(count):
             device, place_in = divmod(len(spots), per)
+            device += first
             spots.append((matrix, block, device // 4, device // 2 % 2, device % 2, place_in))
-    return spots, per
+    return spots
 
 
 def precise(left, right, dims):
     return lax.dot_general(left, right, (dims, ((), ())), precision=PRECISE, preferred_element_type=F32)
 
 
-def muon_gram_kernel(groups, spots_ref, *refs):
+def muon_gram_kernel(groups, spread, spots_ref, *refs):
     count = sum(groups)
     sums, momenta = refs[: len(groups)], refs[len(groups) : len(groups) + count]
     outs = refs[len(groups) + count : len(groups) + 2 * count]
@@ -730,10 +690,9 @@
             start += size
             n += 1
     zs = own_ref.shape[1]
-    spots, per = block_spots([out.shape[1] // ROW_BLOCK for out in outs], zs)
-    if len(spots) < 4 * zs * per:
-        own_ref[...] = jnp.zeros_like(own_ref)
-        other_ref[...] = jnp.zeros_like(other_ref)
+    spots = block_spots([out.shape[1] // ROW_BLOCK for out in outs], spread)
+    own_ref[...] = jnp.zeros_like(own_ref)
+    other_ref[...] = jnp.zeros_like(other_ref)
     for matrix, block, z, x, core, place_in in spots:
         turned = outs[matrix][:, block * ROW_BLOCK : (block + 1) * ROW_BLOCK]
         gram = precise(turned, turned, ((0,), (0,)))
@@ -748,13 +707,12 @@
             other_ref[away] = gram
 
 
-def muon_gram(spots, zs, groups):
+def muon_gram(spots, zs, groups, spread):
     momenta = [momentum for _, each in groups for momentum in each]
-    _, per = block_spots([momentum.shape[1] // ROW_BLOCK for momentum in momenta], zs)
-    grams = jax.ShapeDtypeStruct((2, zs, per, ROW_BLOCK, ROW_BLOCK), F32)
+    grams = jax.ShapeDtypeStruct((2, zs, spread[0], ROW_BLOCK, ROW_BLOCK), F32)
     vmem = pl.BlockSpec(memory_space=pltpu.VMEM)
     outs = pl.pallas_call(
-        functools.partial(muon_gram_kernel, [len(each) for _, each in groups]),
+        functools.partial(muon_gram_kernel, [len(each) for _, each in groups], spread),
         out_shape=[jax.ShapeDtypeStruct(momentum.shape, F32) for momentum in momenta] + [grams, grams],
         in_specs=[pl.BlockSpec(memory_space=pltpu.SMEM)] + [vmem] * (len(groups) + len(momenta)),
         out_specs=[vmem] * (len(momenta) + 2),
@@ -801,14 +759,14 @@
     )(*parts)
 
 
-def muon_apply_kernel(rates, spots_ref, *refs):
+def muon_apply_kernel(rates, spread, spots_ref, *refs):
     count = len(rates)
     parts, momenta, masters = refs[:4], refs[4 : 4 + count], refs[4 + count : 4 + 2 * count]
     outs, factors = refs[4 + 2 * count : 4 + 3 * count], refs[4 + 3 * count]
     for n in range(4):
         factors[n] = parts[n][...]
     zs = factors.shape[1]
-    spots, _ = block_spots([momentum.shape[1] // ROW_BLOCK for momentum in momenta], zs)
+    spots = block_spots([momentum.shape[1] // ROW_BLOCK for momentum in momenta], spread)
     for matrix, block, z, x, core, place_in in spots:
         part = slice(block * ROW_BLOCK, (block + 1) * ROW_BLOCK)
         away = 2 * lax.rem(spots_ref[2] + core, 2) + lax.rem(spots_ref[1] + x, 2)
@@ -817,10 +775,10 @@
         outs[matrix][:, part] = masters[matrix][:, part] * (1.0 - WEIGHT_SHRINK) - rates[matrix] * direction
 
 
-def muon_apply(spots, factors, momenta, masters, rates):
+def muon_apply(spots, factors, momenta, masters, rates, spread):
     vmem = pl.BlockSpec(memory_space=pltpu.VMEM)
     return pl.pallas_call(
-        functools.partial(muon_apply_kernel, rates),
+        functools.partial(muon_apply_kernel, rates, spread),
         out_shape=[jax.ShapeDtypeStruct(master.shape, F32) for master in masters],
         in_specs=[pl.BlockSpec(memory_space=pltpu.SMEM)] + [vmem] * (4 + 2 * len(masters)),
         out_specs=[vmem] * len(masters),
@@ -848,14 +806,6 @@
     unit_qkv, layout_qkv = math.gcd(n_qkv, 8), [(n_qkv, 1)]
     own_tokens = tokens.reshape(count, rows, width)
     wires = net.y.gather(net.wire([w_qkv, w_proj]))
-    first = Staged(net.gather_steps(net.joined(wires, unit, width), [(n_qkv, 1), (n_proj, 1)], 0.45))
-    sent = [first.advance(), first.advance(), first.advance()]
-    token_pieces = [net.y.gather(tie(own_tokens[0], wires[-1]))]
-    wires = net.y.gather(tie(net.wire([w_fc1]), token_pieces[0][-1], *sent[2]))
-    t_fc1 = lax.all_gather(net.rows(wires), "dp", axis=0, tiled=True)
-    for i in range(1, count):
-        token_pieces.append(net.y.gather(tie(own_tokens[i], wires[-1])))
-    t_qkv, t_proj = first.finish()[0]
 
     ada_rows, ada_cols = w_ada.shape
     cond = conditioning.astype(F32).reshape(count, width)
@@ -863,18 +813,31 @@
     cond_low = cond_act.astype(BF).astype(F32)
     cond_parts = jnp.transpose(cond_low.reshape(count, seq, ada_rows), (1, 0, 2)).reshape(seq, -1)
     parcel = jnp.concatenate([jnp.broadcast_to(biases, (seq,) + biases.shape), cond_parts], axis=1)
-    parcel = net.to_all(jnp.broadcast_to(parcel[None], (dp,) + parcel.shape))
+    parcel = net.to_all(tie(jnp.broadcast_to(parcel[None], (dp,) + parcel.shape), wires[0]))
+    cond_all = parcel[:, 0, biases.shape[0] :].reshape(dp * count, ada_rows).astype(BF)
+    first = Staged(net.gather_steps(net.joined(wires, unit, width), [(n_qkv, 1), (n_proj, 1)], 0.45))
+    sent = first.advance()
+    token_pieces = [net.y.gather(tie(own_tokens[0], *sent))]
+
+    low_ada = w_ada.astype(BF)
+    partial = jnp.dot(tie(cond_all, *sent), low_ada, preferred_element_type=F32).reshape(dp, 1, count, ada_cols)
+    partial = jnp.broadcast_to(partial, (dp, seq, count, ada_cols))
+    received = net.to_all(partial)
+    sent = first.advance(partial)
+    sent = first.advance()
+    received, parcel = tie(received, *sent), tie(parcel, *sent)
+    received = jnp.sum(received, axis=1)
     bias_full = parcel[:, :, : biases.shape[0]].reshape(-1)
-    cond_all = parcel[:, 0, biases.shape[0] :].reshape(dp * count, ada_rows).astype(BF)
     b_ada, b_q, b_v, b_proj, b_fc1, b_fc2 = [bias_full[bounds[i] : bounds[i + 1]] for i in range(6)]
-
-    low_ada = w_ada.astype(BF)
-    partial = jnp.dot(cond_all, low_ada, preferred_element_type=F32).reshape(dp, 1, count, ada_cols)
-    received = jnp.sum(net.to_all(jnp.broadcast_to(partial, (dp, seq, count, ada_cols))), axis=1)
     modulation = jnp.transpose(received, (1, 0, 2)).reshape(count, dp * ada_cols) + b_ada
     shift_one, scale_one, gate_one, shift_two, scale_two, gate_two = jnp.split(
         modulation[:, None, :], 6, axis=-1
     )
+    (t_qkv, t_proj), arrived = first.finish(modulation)
+    wires = net.y.gather(tie(net.wire([w_fc1]), token_pieces[0][-1], *arrived))
+    t_fc1 = lax.all_gather(net.rows(wires), "dp", axis=0, tiled=True)
+    for i in range(1, count):
+        token_pieces.append(net.y.gather(tie(own_tokens[i], wires[-1])))
 
     lengths = (heights * widths).reshape(count).astype(jnp.int32)
     offsets = jnp.stack([((y + s) % seq) * rows for s in range(seq)]).astype(jnp.int32)
@@ -918,6 +881,8 @@
     grad_gate_two = jnp.sum(branch_two * grad_out, axis=1)
     bias_fc2 = jnp.sum(grad_branch_two.astype(F32), axis=(0, 1))
     grad_pre = gelu_back(dot(grad_branch_two, t_fc2))[0].astype(BF)
+    term_fc1 = outer(grad_pre, ffn_in)
+    grad_pre = tie(grad_pre, term_fc1)
     bias_fc1 = jnp.sum(grad_pre.astype(F32), axis=(0, 1))
     grad_ffn_in = dot(grad_pre, t_fc1)
     grad_shift_two = jnp.sum(grad_ffn_in, axis=1)
@@ -925,19 +890,11 @@
     grad_mixed = grad_out + norm_back(normed_two, inverse_two, grad_ffn_in * (1.0 + scale_two))
     grad_gate_one = jnp.sum(branch_one * grad_mixed, axis=1)
     grad_branch_one = (gate_one * grad_mixed).astype(BF)
-    unit_mid = math.gcd(math.gcd(n_proj, n_fc1), 8)
-    (term_mid,) = shard_outer(
-        net.spots(),
-        [flat(grad_pre), flat(ffn_in), flat(grad_branch_one), flat(attended_low)],
-        [([2], 0, width), ([3], 0, width), ([1], 0, width)] + [([0], j * width, width) for j in range(hidden // width)],
-        [(0, 1, n_proj, 0)] + [(3 + j, 2, n_fc1, n_proj // unit_mid) for j in range(hidden // width)],
-        net.z.size, width, unit_mid, (n_proj + n_fc1) // unit_mid, split=False,
-    )
-    term_mid = tie(term_mid, sum_fc2)
-    sum_mid = net.scatter(term_mid.reshape(dp * (n_proj + n_fc1), width))
-    grad_branch_one = tie(grad_branch_one, term_mid)
     bias_proj = jnp.sum(grad_branch_one.astype(F32), axis=(0, 1))
     grad_attended = dot(grad_branch_one, t_proj).astype(BF)
+    term_fc1 = tie(term_fc1, sum_fc2, grad_attended)
+    sum_fc1 = net.scatter(term_fc1)
+    grad_attended = tie(grad_attended, term_fc1)
 
     grad_q, grad_k, grad_v, far_parts = [], [], [], []
     turned = [momentum.T for momentum in momenta]
@@ -963,15 +920,21 @@
         )
         sent = sent + far_steps.advance()
         far_parts.append(far_steps)
-    own, other = shard_outer(
+    unit_last = math.gcd(math.gcd(n_qkv, n_proj), 8)
+    (term_last,) = shard_outer(
         net.spots(),
-        [flat(each) for each in grad_q + grad_k + grad_v] + [attn[:rows] for attn in attn_all] + attn_all,
-        [([n * count + i for i in range(count)], 0, width) for n in range(5)],
-        [(0, 3, n_qkv, 0), (1, 4, n_qkv, 0), (2, 4, n_qkv, 0)],
-        net.z.size, width, unit_qkv, n_qkv // unit_qkv, sent,
+        [flat(each) for each in grad_q + grad_k + grad_v]
+        + [attn[:rows] for attn in attn_all]
+        + attn_all
+        + [flat(grad_branch_one), flat(attended_low)],
+        [([n * count + i for i in range(count)], 0, width) for n in range(5)]
+        + [([5 * count], 0, width), ([5 * count + 1], 0, width)],
+        [(0, 3, n_qkv, 0), (1, 4, n_qkv, 0), (2, 4, n_qkv, 0), (5, 6, n_proj, n_qkv // unit_last)],
+        net.z.size, width, unit_last, (n_qkv + n_proj) // unit_last, sent, split=False,
     )
-    back_qkv = Staged(net.scatter_steps(own, other, layout_qkv, 0.45))
-    sent = back_qkv.advance()
+    sum_last = net.scatter(term_last.reshape(dp * (n_qkv + n_proj), width))
+    halves = Staged(lockstep(*[net.halves_steps(tie(each, term_last)) for each in (sum_fc2, sum_fc1)]))
+    sent = halves.advance()
     grad_q[0] = tie(grad_q[0], *sent)
     bias_q = sum(jnp.sum(each.astype(F32), axis=(0, 1)) for each in grad_q)
     bias_v = sum(jnp.sum(each.astype(F32), axis=(0, 1)) for each in grad_v)
@@ -984,9 +947,14 @@
         ],
         axis=0,
     )
-    sent = back_qkv.advance(own_part)
+    matrices = (w_qkv, w_proj, w_fc1, w_fc2, w_ada)
+    per = -(-sum(matrix.shape[0] // ROW_BLOCK for matrix in matrices) // dp)
+    spread_early = (per, 0)
+    early_blocks = (w_fc2.shape[0] + w_fc1.shape[0]) // ROW_BLOCK
+    spread_last = (per, -(-early_blocks // per))
+    sums = halves.finish(own_part)
     early = Staged(
-        lockstep(*[net.halves_steps(tie(each, *sent)) for each in (sum_fc2, sum_mid)])
+        net.muon_scatter_steps([(sums[0], [turned[3]]), (sums[1], [turned[2]])], spread_early)
     )
     sent = early.advance()
     far_sum = jnp.stack([steps_of.finish() for steps_of in far_parts])
@@ -1004,33 +972,16 @@
     sent = jnp.transpose(grad_mod_local.reshape(count, dp, 1, ada_cols), (1, 2, 0, 3))
     sent = jnp.broadcast_to(sent, (dp, seq, count, ada_cols))
     mod_parts = net.to_all(sent)
-    sent = back_qkv.advance(sent)
-    sums = early.finish(sent[0])
-    chain = Staged(
-        net.muon_steps(
-            [(sums[1], [turned[1], turned[2]]), (sums[0], [turned[3]])],
-            [w_proj.T, w_fc1.T, w_fc2.T],
-            [1.0, math.sqrt(hidden / width), math.sqrt(width / hidden)],
-        )
-    )
-    anchor = chain.advance()[0]
-    while not back_qkv.done:
-        sent = back_qkv.advance(anchor)
-        if sent:
-            mod_parts = tie(mod_parts, *sent)
-            anchor = (chain.advance(sent[0]) or sent)[0]
+    while not early.done:
+        sent = early.advance(sent if not isinstance(sent, list) else sent[0])
+    halves = Staged(net.halves_steps(tie(sum_last, *early.result[1])))
+    halves.advance()
     mod_cols = jnp.sum(mod_parts, axis=1).astype(BF).reshape(dp * count, ada_cols)
     shard_ada = jnp.einsum("sr,sc->cr", cond_all, mod_cols, preferred_element_type=F32)
 
+    total = halves.finish(shard_ada)
     last = Staged(
-        net.muon_steps(
-            [
-                (back_qkv.result, [turned[0]]),
-                (shard_ada, [turned[4]]),
-            ],
-            [w_qkv.T, w_ada.T],
-            [math.sqrt(3.0), math.sqrt(6.0)],
-        )
+        net.muon_scatter_steps([(total, [turned[0], turned[1]]), (shard_ada, [turned[4]])], spread_last)
     )
     sent = last.advance()
 
@@ -1040,12 +991,21 @@
     parcel = jnp.concatenate([term_bias.reshape(dp, seq, -1), cond_part], axis=-1)
     parcel = net.to_all(tie(parcel, *sent))
     while not last.done:
-        anchor = sent[0] if sent else None
-        sent = last.advance(anchor)
-        sent = sent + chain.advance(sent[0] if sent else None)
-    chain.finish()
-    (next_qkv, next_ada), (new_qkv, new_ada) = last.result
-    (next_proj, next_fc1, next_fc2), (new_proj, new_fc1, new_fc2) = chain.result
+        sent = last.advance(sent[0])
+    gathered = Staged(net.muon_gather_steps(early.result[1] + last.result[1]))
+    sent = gathered.advance()
+    while not gathered.done:
+        sent = gathered.advance(sent[0])
+    next_fc2, next_fc1 = early.result[0]
+    next_qkv, next_proj, next_ada = last.result[0]
+    new_fc2, new_fc1 = muon_apply(
+        net.spots(), gathered.result, [next_fc2, next_fc1], [w_fc2.T, w_fc1.T],
+        [math.sqrt(width / hidden), math.sqrt(hidden / width)], spread_early,
+    )
+    new_qkv, new_proj, new_ada = muon_apply(
+        net.spots(), gathered.result, [next_qkv, next_proj, next_ada], [w_qkv.T, w_proj.T, w_ada.T],
+        [math.sqrt(3.0), 1.0, math.sqrt(6.0)], spread_last,
+    )
 
     size = biases.shape[0]
     grad_bias = jnp.sum(parcel[..., :size], axis=(0, 1))

time: 984 us -> 963 us (0.979)
  other arithmetic: 110 us -> 77.7 us
  matrix products: 189 us -> 220 us
  blocking collectives: 0 us -> 28.6 us
  Pallas kernels: 270 us -> 245 us
  starting transfers between devices: 77.6 us -> 52.9 us
  waiting for transfers between devices: 216 us -> 227 us
  local copies, waits for them, and re-layouts: 96.9 us -> 87 us
    all_to_all x0 -> x1, blocking collectives: none -> 28.6 us  [to_all(): lax.all_to_all(flat, ('dp', 'seq'), 0, 0, tiled=True).reshape(value.shape)]
    pallas_call x2 -> x1, Pallas kernels: 49.1 us -> 28.8 us  [shard_outer(): pl.pallas_call(functools.partial(shard_outer_kernel, {'loads': loads, 'pa...]
    all_to_all x4 -> x3, waiting for transfers between devices: 8.19 us -> 27 us  [to_all(): lax.all_to_all(flat, ('dp', 'seq'), 0, 0, tiled=True).reshape(value.shape)]
    dot_general x1 -> x2, matrix products: 17.1 us -> 35.3 us  [outer(): jnp.einsum('srn,srk->nk', left, right, preferred_element_type=F32)]
    convert_element_type x7 -> x0, other arithmetic: 15.9 us -> none  [the longest x1 4.5 us: scatter_steps(): half = (own.astype(F32) + tie(got, anchor).astype(F32)).astype(BF)]
    ppermute x55 -> x40, starting transfers between devices: 51.9 us -> 37 us  [send(): return lax.ppermute(value, self.name, pairs)]
    ppermute x55 -> x40, waiting for transfers between devices: 194 us -> 183 us  [send(): return lax.ppermute(value, self.name, pairs)]
    all_to_all x4 -> x3, starting transfers between devices: 25.5 us -> 15.7 us  [to_all(): lax.all_to_all(flat, ('dp', 'seq'), 0, 0, tiled=True).reshape(value.shape)]
  transfers between devices with their start and end apart: 63 -> 48, of which waited for: 22 -> 22; matrix products, arithmetic and copies ran while one was open for 37% -> 35% of each run, Pallas kernels for 26% -> 22%
where the time goes in v6:
time: 963 us; the launch traced here: 955 us
  Pallas kernels  245 us (25%)
  waiting for transfers between devices  227 us (24%)
  matrix products  220 us (23%)
  local copies, waits for them, and re-layouts  87 us (9%)
  other arithmetic  77.7 us (8%)
  starting transfers between devices  52.9 us (5%)
  blocking collectives  28.6 us (3%)
  between operations  15.7 us (2%)
    ppermute x40, waiting for transfers between devices, send(): return lax.ppermute(value, self.name, pairs)  183 us
    dot_general x13, matrix products, dot(): return jnp.einsum('srn,nk->srk', left, right, preferred_element_type=F32)  96.6 us
    pallas_call x2, Pallas kernels, attend_back(): pl.pallas_call(without(attend_back_kernel, 8, len(deps), heads, tile), gr...  90.8 us
    dot_general x9, matrix products, dot_t(): return jnp.einsum('srk,nk->srn', left, right, preferred_element_type=F32)  85.7 us
    pallas_call x2, Pallas kernels, attend(): pl.pallas_call(without(attend_kernel, 5, len(deps), heads, tile), grid_sp...  64.7 us
    unnamed x246, local copies, waits for them, and re-layouts  39.4 us
    ppermute x40, starting transfers between devices, send(): return lax.ppermute(value, self.name, pairs)  37 us
    dot_general x2, matrix products, outer(): jnp.einsum('srn,srk->nk', left, right, preferred_element_type=F32)  35.3 us
  transfers between devices with their start and end apart: 48, of which 22 were waited for; matrix products, arithmetic and copies ran while one was open for 35% of the time, Pallas kernels for 22%

profile of v6, /device:TPU:11, one launch (start us, length us, event | category | flops | bytes accessed | tf_op | source)
XLA Modules:
  0.0 955.0 jit_solution(7865205048367519829)
XLA Ops:
  23.7 10.4 %all-to-all-done = f32[32,1,1656]{2,1,0:T(1,128)S(1)} async-done(((f32[32,1,1656]{2,1,0:T(1,128)}), f32[32,1,1656]{2,1,0:T(1,128)S(1)}, u32[]{:S(2)}, u32[]{:S(2)}) %all-to-all-start) | async-done | bytes 212000 | tf_op jit(solution)/shard_map/all_to_all | solution.py:320
  67.3 16.6 %all-to-all-done.1 = f32[32,2,432]{2,1,0:T(2,128)} async-done(((f32[32,2,432]{2,1,0:T(2,128)}), f32[32,2,432]{2,1,0:T(2,128)}, u32[]{:S(2)}, u32[]{:S(2)}) %all-to-all-start.1) | async-done | bytes 110624 | tf_op jit(solution)/shard_map/all_to_all | solution.py:320
  87.0 15.7 %collective-permute-done.8.refs_0_ = bf16[2,20,8,1152]{3,2,1,0:T(8,128)(2,1)} collective-permute-done((bf16[2,20,8,1152]{3,2,1,0:T(8,128)(2,1)S(1)}, bf16[2,20,8,1152]{3,2,1,0:T(8,128)(2,1)}, u32[]{:S(2)}, u32[]{:S(2)}) %collective-permute-start.8) | collective-permute-done | bytes 737312 | tf_op jit(solution)/shard_map/ppermute | solution.py:47
  158.5 32.4 %attend.2 = (bf16[1,512,1152]{2,1,0:T(8,128)(2,1)}, f32[1,16,1,512]{3,2,1,0:T(1,128)}) custom-call(s32[1]{0:T(128)} %bitcast.17.refs_0_, s32[2]{0:T(128)} %pad_add_fusion.refs_1_, bf16[1,512,1152]{2,1,0:T(8,128)(2,1)} %fusion.38.refs_2_, bf16[1,1024,1152]{2,1,0:T(8,128)(2,1)} %fusion.31.refs_3_, bf16[1,1024,1152]{2,1,0:T(8,128)(2,1)} %fusion.29.refs_4_), custom_call_target="tpu_custom_call" | custom-call | flops 4294967296 | bytes 7077888 | tf_op jit(solution)/shard_map/attend/pallas_call | solution.py:544
  225.4 32.2 %attend.3 = (bf16[1,512,1152]{2,1,0:T(8,128)(2,1)}, f32[1,16,1,512]{3,2,1,0:T(1,128)}) custom-call(s32[1]{0:T(128)} %bitcast.28.refs_0_, s32[2]{0:T(128)} %pad_add_fusion.refs_1_, bf16[1,512,1152]{2,1,0:T(8,128)(2,1)} %fusion.37.refs_2_, bf16[1,1024,1152]{2,1,0:T(8,128)(2,1)} %fusion.32.refs_3_, bf16[1,1024,1152]{2,1,0:T(8,128)(2,1)} %fusion.30.refs_4_), custom_call_target="tpu_custom_call" | custom-call | flops 4294967296 | bytes 7077888 | tf_op jit(solution)/shard_map/attend/pallas_call | solution.py:544
  272.0 25.1 %multiply_convert_fusion = (bf16[2,512,4608]{2,1,0:T(8,128)(2,1)}, f32[2,512,4608]{2,1,0:T(8,128)}) fusion(f32[4608]{0:T(1024)S(1)} %copy-done.88, bf16[4608,1152]{1,0:T(8,128)(2,1)} %all-gather.3.cloned.1.call-done, f32[2,512,1152]{2,1,0:T(8,128)} %copy-done.34, f32[2,1152]{1,0:T(2,128)S(1)} %copy-done.92, f32[2,1152]{1,0:T(2,128)S(1)} %copy-done.89, ...), kind=kOutput, calls=%fused_computation.14 | convolution fusion | flops 10924720128 | bytes 43692032 | tf_op jit(solution)/shard_map/srk,nk->srn/dot_general | solution.py:347
  297.1 17.3 %fusion.refs_1_ = bf16[1152,4608]{1,0:T(8,128)(2,1)} fusion(bf16[2,512,1152]{2,1,0:T(8,128)(2,1)S(1)} %fusion.25.refs_0_, bf16[2,512,4608]{2,1,0:T(8,128)(2,1)} %get-tuple-element.213.refs_0_), kind=kOutput, calls=%fused_computation.4 | convolution fusion | flops 10876944384 | bytes 22413312 | tf_op jit(solution)/shard_map/srn,srk->nk/dot_general | solution.py:355
  316.1 26.1 %fusion.8.refs_0_ = bf16[2,512,4608]{2,1,0:T(8,128)(2,1)S(1)} fusion(f32[2,512,4608]{2,1,0:T(8,128)} %get-tuple-element.214, bf16[2,512,1152]{2,1,0:T(8,128)(2,1)S(1)} %copy-done.8, bf16[1152,4608]{1,0:T(8,128)(2,1)} %all-gather.5.cloned.1.call-done, f32[4608]{0:T(1024)S(1)} %copy-done.88), kind=kOutput, calls=%fused_computation.12 | convolution fusion | flops 10970726400 | bytes 41306112 | tf_op jit(solution)/shard_map/srn,nk->srk/dot_general | solution.py:351
  346.0 18.1 %fusion.1.refs_1_.refs_0_ = bf16[4608,1152]{1,0:T(8,128)(2,1)} fusion(bf16[2,512,4608]{2,1,0:T(8,128)(2,1)S(1)} %fusion.8.refs_0_, f32[2,512,1152]{2,1,0:T(8,128)} %copy-done.34, f32[2,1152]{1,0:T(2,128)S(1)} %copy-done.92, f32[2,1152]{1,0:T(2,128)S(1)} %copy-done.89, f32[2,512]{1,0:T(2,128)S(1)} %add_rsqrt_fusion, f32[2,512]{1,0:T(2,128)S(1)} %broadcast_multiply_fusion.4), kind=kOutput, calls=%fused_computation.5 | convolution fusion | flops 10882842624 | bytes 24799232 | tf_op jit(solution)/shard_map/srn,srk->nk/dot_general | solution.py:355
  364.0 22.0 %multiply_reduce_fusion = (f32[2,1152]{1,0:T(2,128)}, f32[2,512]{1,0:T(2,128)S(1)}, f32[2,512]{1,0:T(2,128)S(1)}, f32[2,1152]{1,0:T(2,128)}, f32[2,512,1152]{2,1,0:T(8,128)}) fusion(f32[2,512,1152]{2,1,0:T(8,128)} %copy-done.34, f32[2,512]{1,0:T(2,128)S(1)} %add_rsqrt_fusion, f32[2,512]{1,0:T(2,128)S(1)} %broadcast_multiply_fusion.4, ...), kind=kOutput, calls=%fused_computation.45 | convolution fusion | flops 10882246656 | bytes 29535232 | tf_op jit(solution)/shard_map/srn,nk->srk/dot_general | solution.py:351
  386.0 24.6 %fusion.26 = (f32[2,1152]{1,0:T(2,128)S(1)}, bf16[2,1,512,1152]{3,2,1,0:T(8,128)(2,1)}, f32[1152]{0:T(1024)}, bf16[2,512,1152]{2,1,0:T(8,128)(2,1)}, f32[2,512,1152]{2,1,0:T(8,128)}) fusion(bf16[2,1,512,1152]{3,2,1,0:T(8,128)(2,1)S(1)} %copy-done.47, f32[2,512,1152]{2,1,0:T(8,128)} %copy-done.34, f32[2,1152]{1,0:T(2,128)S(1)} %copy-done.82, ...), kind=kOutput, calls=%fused_computation.37 | convolution fusion | flops 10894046208 | bytes 41350144 | tf_op jit(solution)/shard_map/srk,nk->srn/dot_general | solution.py:347
  418.3 17.0 %reduce-scatter.4.cloned.1.call-done.refs_1_.refs_0_ = bf16[72,4608]{1,0:T(8,128)(2,1)} async-done(((bf16[1152,4608]{1,0:T(8,128)(2,1)}), bf16[72,4608]{1,0:T(8,128)(2,1)}) %reduce-scatter.4.cloned.1.call-update) | async-done | bytes 663568 | tf_op jit(solution)/shard_map/reduce_scatter | solution.py:249
  443.4 45.5 %attend_back.2 = (bf16[1,512,1152]{2,1,0:T(8,128)(2,1)}, bf16[1,1024,1152]{2,1,0:T(8,128)(2,1)}, bf16[1,1024,1152]{2,1,0:T(8,128)(2,1)}) custom-call(s32[1]{0:T(128)} %bitcast.17.refs_0_, s32[2]{0:T(128)} %pad_add_fusion.refs_1_, bf16[1,512,1152]{2,1,0:T(8,128)(2,1)} %fusion.38.refs_2_, bf16[1,1024,1152]{2,1,0:T(8,128)(2,1)} %fusion.31.refs_3_, ...), custom_call_target="tpu_custom_call" | custom-call | flops 10737418240 | bytes 14155776 | tf_op jit(solution)/shard_map/attend_back/pallas_call | solution.py:629
  497.7 45.2 %attend_back.3 = (bf16[1,512,1152]{2,1,0:T(8,128)(2,1)}, bf16[1,1024,1152]{2,1,0:T(8,128)(2,1)}, bf16[1,1024,1152]{2,1,0:T(8,128)(2,1)}) custom-call(s32[1]{0:T(128)} %bitcast.28.refs_0_, s32[2]{0:T(128)} %pad_add_fusion.refs_1_, bf16[1,512,1152]{2,1,0:T(8,128)(2,1)} %fusion.37.refs_2_, bf16[1,1024,1152]{2,1,0:T(8,128)(2,1)} %fusion.32.refs_3_, ...), custom_call_target="tpu_custom_call" | custom-call | flops 10737418240 | bytes 14155776 | tf_op jit(solution)/shard_map/attend_back/pallas_call | solution.py:629
  551.7 28.8 %shard_outer.1.refs_1_ = bf16[4,2,2,36,8,1152]{5,4,3,2,1,0:T(8,128)(2,1)} custom-call(s32[3]{0:T(128)} %pad_add_fusion.1.refs_0_.spots_ref, bf16[512,1152]{1,0:T(8,128)(2,1)} %bitcast.270, bf16[512,1152]{1,0:T(8,128)(2,1)} %bitcast.284, bf16[1024,1152]{1,0:T(8,128)(2,1)} %bitcast.330, bf16[1024,1152]{1,0:T(8,128)(2,1)} %bitcast.331, ...), custom_call_target="tpu_custom_call" | custom-call | flops 16307453952 | bytes 10616832 | tf_op jit(solution)/shard_map/shard_outer/pallas_call | solution.py:445
  626.8 17.6 %collective-permute-done.19.refs_0_ = bf16[72,2304]{1,0:T(8,128)(2,1)} collective-permute-done((bf16[72,2304]{1,0:T(8,128)(2,1)}, bf16[72,2304]{1,0:T(8,128)(2,1)}, u32[]{:S(2)}, u32[]{:S(2)}) %collective-permute-start.19) | collective-permute-done | bytes 331808 | tf_op jit(solution)/shard_map/ppermute | solution.py:47
  654.2 15.5 %muon_gram.2 = (f32[72,2304]{1,0:T(8,128)}, f32[288,576]{1,0:T(8,128)}, f32[2,4,2,144,144]{4,3,2,1,0:T(8,128)}, f32[2,4,2,144,144]{4,3,2,1,0:T(8,128)}) custom-call(s32[3]{0:T(128)} %pad_add_fusion.1.refs_0_.spots_ref, f32[72,2304]{1,0:T(8,128)} %convert_add_fusion.5.refs_0_, f32[288,576]{1,0:T(8,128)} %convert_add_fusion.4.refs_1_, f32[72,2304]{1,0:T(8,128)} %bitcast.290, ...), custom_call_target="tpu_custom_call" | custom-call | tf_op jit(solution)/shard_map/muon_gram/pallas_call | solution.py:714
  694.7 23.8 %collective-permute-done.24.refs_0_ = f32[4,2,144,144]{3,2,1,0:T(8,128)S(1)} collective-permute-done((f32[4,2,144,144]{3,2,1,0:T(8,128)}, f32[4,2,144,144]{3,2,1,0:T(8,128)S(1)}, u32[]{:S(2)}, u32[]{:S(2)}) %collective-permute-start.24) | collective-permute-done | bytes 663584 | tf_op jit(solution)/shard_map/ppermute | solution.py:47
  730.2 12.7 %collective-permute-done.26.refs_0_ = f32[2,144,144]{2,1,0:T(8,128)S(1)} collective-permute-done((f32[2,144,144]{2,1,0:T(8,128)S(1)}, f32[2,144,144]{2,1,0:T(8,128)S(1)}, u32[]{:S(2)}, u32[]{:S(2)}) %collective-permute-start.26) | collective-permute-done | bytes 165920 | tf_op jit(solution)/shard_map/ppermute | solution.py:47
  766.3 12.4 %muon_gram.3 = (f32[216,576]{1,0:T(8,128)}, f32[72,576]{1,0:T(8,128)}, f32[432,576]{1,0:T(8,128)}, f32[2,4,2,144,144]{4,3,2,1,0:T(8,128)}, f32[2,4,2,144,144]{4,3,2,1,0:T(8,128)}) custom-call(s32[3]{0:T(128)} %pad_add_fusion.1.refs_0_.spots_ref, f32[288,576]{1,0:T(8,128)} %convert_add_fusion.3.refs_0_, f32[432,576]{1,0:T(8,128)} %fusion.104.refs_1_, ...), custom_call_target="tpu_custom_call" | custom-call | tf_op jit(solution)/shard_map/muon_gram/pallas_call | solution.py:714
  799.3 22.2 %collective-permute-done.30.refs_0_ = f32[4,2,144,144]{3,2,1,0:T(8,128)S(1)} collective-permute-done((f32[4,2,144,144]{3,2,1,0:T(8,128)S(1)}, f32[4,2,144,144]{3,2,1,0:T(8,128)S(1)}, u32[]{:S(2)}, u32[]{:S(2)}) %collective-permute-start.30) | collective-permute-done | bytes 663584 | tf_op jit(solution)/shard_map/ppermute | solution.py:47
  834.3 10.7 %collective-permute-done.32.refs_0_ = f32[2,144,144]{2,1,0:T(8,128)S(1)} collective-permute-done((f32[2,144,144]{2,1,0:T(8,128)S(1)}, f32[2,144,144]{2,1,0:T(8,128)S(1)}, u32[]{:S(2)}, u32[]{:S(2)}) %collective-permute-start.32) | collective-permute-done | bytes 165920 | tf_op jit(solution)/shard_map/ppermute | solution.py:47
  870.5 17.3 %collective-permute-done.35.refs_0_ = f32[2,144,144]{2,1,0:T(8,128)S(1)} collective-permute-done((f32[2,144,144]{2,1,0:T(8,128)}, f32[2,144,144]{2,1,0:T(8,128)S(1)}, u32[]{:S(2)}, u32[]{:S(2)}) %collective-permute-start.35) | collective-permute-done | bytes 165920 | tf_op jit(solution)/shard_map/ppermute | solution.py:47
  894.9 28.6 %all_to_all.30 = f32[32,1,1656]{2,1,0:T(1,128)S(1)} all-to-all(f32[32,1,1656]{2,1,0:T(1,128)S(1)} %all_to_all.25), channel_id=1, replica_groups=mesh['dp'=16,'seq'=2] {'dp','seq'}, dimensions={0} | all-to-all | bytes 423936 | tf_op jit(solution)/shard_map/all_to_all | solution.py:320
  (538 shorter events, 401.3 us)
Async XLA Ops:
  23.0 31.7 %collective-permute-start.1 = (bf16[16,8,1152]{2,1,0:T(8,128)(2,1)S(1)}, bf16[16,8,1152]{2,1,0:T(8,128)(2,1)}, u32[]{:S(2)}, u32[]{:S(2)}) collective-permute-start(bf16[16,8,1152]{2,1,0:T(8,128)(2,1)S(1)} %get-tuple-element.200.refs_1_.refs_2_), channel_id=1, source_target_pairs={{0,24},{2,26},{4,28},{6,30},{8,0},{10,2},{12,4},{14,6},{16,8},{18,... | collective-permute-start | bytes 884744 | tf_op jit(solution)/shard_map/ppermute | solution.py:47
  43.9 21.4 %collective-permute-start.5 = (bf16[2,20,8,1152]{3,2,1,0:T(8,128)(2,1)}, bf16[2,20,8,1152]{3,2,1,0:T(8,128)(2,1)S(1)}, u32[]{:S(2)}, u32[]{:S(2)}) collective-permute-start(bf16[2,20,8,1152]{3,2,1,0:T(8,128)(2,1)} %pad_maximum_fusion.6.refs_3_), channel_id=1, source_target_pairs={{0,24},{2,26},{4,28},{6,30},{8,0},{10,2},{12,4},{14,6},{16,8},{18,... | collective-permute-start | bytes 2211848 | tf_op jit(solution)/shard_map/ppermute | solution.py:47
  48.1 54.8 %collective-permute-start.6 = (bf16[512,1152]{1,0:T(8,128)(2,1)}, bf16[512,1152]{1,0:T(8,128)(2,1)S(1)}, u32[]{:S(2)}, u32[]{:S(2)}) collective-permute-start(bf16[512,1152]{1,0:T(8,128)(2,1)} %tie.57), channel_id=1, source_target_pairs={{0,1},{1,0},{2,3},{3,2},{4,5},{5,4},{6,7},{7,6},{8,9},{9,8},{10,11... | collective-permute-start | bytes 3538952 | tf_op jit(solution)/shard_map/ppermute | solution.py:47
  49.3 34.7 %all-to-all-start.1 = ((f32[32,2,432]{2,1,0:T(2,128)}), f32[32,2,432]{2,1,0:T(2,128)}, u32[]{:S(2)}, u32[]{:S(2)}) async-start(f32[32,2,432]{2,1,0:T(2,128)} %bitcast.7), calls=%async_computation.1 | async-start | bytes 262144 | tf_op jit(solution)/shard_map/all_to_all | solution.py:320
  54.6 217.3 %all-gather.3.cloned.1.call-start = ((), (), s32[]{:S(2)}) async-start(), calls=%async_computation.7 | async-start | bytes 11280384 | tf_op jit(solution)/shard_map/all_gather | solution.py:838
  54.7 48.1 %collective-permute-start.9 = (bf16[2,20,8,1152]{3,2,1,0:T(8,128)(2,1)}, bf16[2,20,8,1152]{3,2,1,0:T(8,128)(2,1)}, u32[]{:S(2)}, u32[]{:S(2)}) collective-permute-start(bf16[2,20,8,1152]{3,2,1,0:T(8,128)(2,1)} %pad_maximum_fusion.6.refs_3_), channel_id=1, source_target_pairs={{0,8},{2,10},{4,12},{6,14},{8,16},{10,18},{12,20},{14,22},{16,24},... | collective-permute-start | bytes 2211848 | tf_op jit(solution)/shard_map/ppermute | solution.py:47
  57.3 29.7 %collective-permute-start.7 = (bf16[4,16,8,1152]{3,2,1,0:T(8,128)(2,1)S(1)}, bf16[4,16,8,1152]{3,2,1,0:T(8,128)(2,1)}, u32[]{:S(2)}, u32[]{:S(2)}) collective-permute-start(bf16[4,16,8,1152]{3,2,1,0:T(8,128)(2,1)S(1)} %pad_maximum_fusion.4.refs_1_), channel_id=1, source_target_pairs={{0,4},{2,6},{4,0},{6,2},{8,12},{10,14},{12,8},{14,10},{16,20},{18,... | collective-permute-start | bytes 3538952 | tf_op jit(solution)/shard_map/ppermute | solution.py:47
  116.1 198.4 %all-gather.5.cloned.1.call-start = ((), (), s32[]{:S(2)}) async-start(), calls=%async_computation.8 | async-start | bytes 11280384 | tf_op jit(solution)/shard_map/all_gather | solution.py:856
  133.2 57.7 %collective-permute-start.17 = (bf16[512,1152]{1,0:T(8,128)(2,1)}, bf16[512,1152]{1,0:T(8,128)(2,1)S(1)}, u32[]{:S(2)}, u32[]{:S(2)}) collective-permute-start(bf16[512,1152]{1,0:T(8,128)(2,1)} %tie.67), channel_id=1, source_target_pairs={{0,1},{1,0},{2,3},{3,2},{4,5},{5,4},{6,7},{7,6},{8,9},{9,8},{10,11... | collective-permute-start | bytes 3538952 | tf_op jit(solution)/shard_map/ppermute | solution.py:47
  202.8 232.5 %reduce-scatter.4.cloned.1.call-start = ((), (), s32[]{:S(2)}) async-start(), calls=%async_computation.9 | async-start | bytes 11280384 | tf_op jit(solution)/shard_map/reduce_scatter | solution.py:249
  314.4 293.7 %reduce-scatter.6.cloned.1.call-start = ((), (), s32[]{:S(2)}) async-start(), calls=%async_computation.10 | async-start | bytes 11280384 | tf_op jit(solution)/shard_map/reduce_scatter | solution.py:249
  435.3 314.6 %reduce-scatter.8.cloned.1.call-start = ((), (), s32[]{:S(2)}) async-start(), calls=%async_computation.11 | async-start | bytes 11280384 | tf_op jit(solution)/shard_map/reduce_scatter | solution.py:249
  585.3 86.5 %collective-permute-start.21 = (bf16[512,1152]{1,0:T(8,128)(2,1)}, bf16[512,1152]{1,0:T(8,128)(2,1)}, u32[]{:S(2)}, u32[]{:S(2)}) collective-permute-start(bf16[512,1152]{1,0:T(8,128)(2,1)} %fusion.35.refs_8_), channel_id=1, source_target_pairs={{0,1},{1,0},{2,3},{3,2},{4,5},{5,4},{6,7},{7,6},{8,9},{9,8},{10,11... | collective-permute-start | bytes 3538952 | tf_op jit(solution)/shard_map/ppermute | solution.py:47
  586.5 85.3 %collective-permute-start.22 = (bf16[512,1152]{1,0:T(8,128)(2,1)}, bf16[512,1152]{1,0:T(8,128)(2,1)}, u32[]{:S(2)}, u32[]{:S(2)}) collective-permute-start(bf16[512,1152]{1,0:T(8,128)(2,1)} %fusion.36.refs_12_), channel_id=1, source_target_pairs={{0,1},{1,0},{2,3},{3,2},{4,5},{5,4},{6,7},{7,6},{8,9},{9,8},{10,11... | collective-permute-start | bytes 3538952 | tf_op jit(solution)/shard_map/ppermute | solution.py:47
  592.1 52.3 %collective-permute-start.19 = (bf16[72,2304]{1,0:T(8,128)(2,1)}, bf16[72,2304]{1,0:T(8,128)(2,1)}, u32[]{:S(2)}, u32[]{:S(2)}) collective-permute-start(bf16[72,2304]{1,0:T(8,128)(2,1)} %bitcast.264.refs_1_), channel_id=1, source_target_pairs={{0,1},{1,0},{2,3},{3,2},{4,5},{5,4},{6,7},{7,6},{8,9},{9,8},{10,11... | collective-permute-start | bytes 995336 | tf_op jit(solution)/shard_map/ppermute | solution.py:47
  615.1 37.2 %collective-permute-start.20 = (bf16[288,576]{1,0:T(8,128)(2,1)S(1)}, bf16[288,576]{1,0:T(8,128)(2,1)}, u32[]{:S(2)}, u32[]{:S(2)}) collective-permute-start(bf16[288,576]{1,0:T(8,128)(2,1)S(1)} %bitcast.277), channel_id=1, source_target_pairs={{0,1},{1,0},{2,3},{3,2},{4,5},{5,4},{6,7},{7,6},{8,9},{9,8},{10,11... | collective-permute-start | bytes 995336 | tf_op jit(solution)/shard_map/ppermute | solution.py:47
  689.5 28.9 %collective-permute-start.24 = (f32[4,2,144,144]{3,2,1,0:T(8,128)}, f32[4,2,144,144]{3,2,1,0:T(8,128)S(1)}, u32[]{:S(2)}, u32[]{:S(2)}) collective-permute-start(f32[4,2,144,144]{3,2,1,0:T(8,128)} %slice_bitcast_fusion.4.refs_1_), channel_id=1, source_target_pairs={{0,4},{2,6},{4,0},{6,2},{8,12},{10,14},{12,8},{14,10},{16,20},{18,... | collective-permute-start | bytes 1990664 | tf_op jit(solution)/shard_map/ppermute | solution.py:47
  689.9 65.3 %all-to-all-start.2 = ((f32[32,2,432]{2,1,0:T(2,128)}), f32[32,2,432]{2,1,0:T(2,128)}, u32[]{:S(2)}, u32[]{:S(2)}) async-start(f32[32,2,432]{2,1,0:T(2,128)} %bitcast.283), calls=%async_computation.4 | async-start | bytes 262144 | tf_op jit(solution)/shard_map/all_to_all | solution.py:320
  724.3 25.0 %collective-permute-start.25 = (f32[2,144,144]{2,1,0:T(8,128)S(1)}, f32[2,144,144]{2,1,0:T(8,128)S(1)}, u32[]{:S(2)}, u32[]{:S(2)}) collective-permute-start(f32[2,144,144]{2,1,0:T(8,128)S(1)} %get-tuple-element.189.refs_1_), channel_id=1, source_target_pairs={{0,8},{2,10},{4,12},{6,14},{8,16},{10,18},{12,20},{14,22},{16,24},... | collective-permute-start | bytes 497672 | tf_op jit(solution)/shard_map/ppermute | solution.py:47
  793.8 27.6 %collective-permute-start.30 = (f32[4,2,144,144]{3,2,1,0:T(8,128)S(1)}, f32[4,2,144,144]{3,2,1,0:T(8,128)S(1)}, u32[]{:S(2)}, u32[]{:S(2)}) collective-permute-start(f32[4,2,144,144]{3,2,1,0:T(8,128)S(1)} %slice_bitcast_fusion.2.refs_1_), channel_id=1, source_target_pairs={{0,4},{2,6},{4,0},{6,2},{8,12},{10,14},{12,8},{14,10},{16,20},{18,... | collective-permute-start | bytes 1990664 | tf_op jit(solution)/shard_map/ppermute | solution.py:47
  828.1 23.2 %collective-permute-start.31 = (f32[2,144,144]{2,1,0:T(8,128)S(1)}, f32[2,144,144]{2,1,0:T(8,128)S(1)}, u32[]{:S(2)}, u32[]{:S(2)}) collective-permute-start(f32[2,144,144]{2,1,0:T(8,128)S(1)} %get-tuple-element.185.refs_1_), channel_id=1, source_target_pairs={{0,8},{2,10},{4,12},{6,14},{8,16},{10,18},{12,20},{14,22},{16,24},... | collective-permute-start | bytes 497672 | tf_op jit(solution)/shard_map/ppermute | solution.py:47
  862.7 25.2 %collective-permute-start.35 = (f32[2,144,144]{2,1,0:T(8,128)}, f32[2,144,144]{2,1,0:T(8,128)S(1)}, u32[]{:S(2)}, u32[]{:S(2)}) collective-permute-start(f32[2,144,144]{2,1,0:T(8,128)} %polynomial.1.refs_1_), channel_id=1, source_target_pairs={{0,16},{2,18},{4,20},{6,22},{8,24},{10,26},{12,28},{14,30},{16,0},... | collective-permute-start | bytes 497672 | tf_op jit(solution)/shard_map/ppermute | solution.py:47
  865.7 24.9 %collective-permute-start.34 = (f32[2,144,144]{2,1,0:T(8,128)}, f32[2,144,144]{2,1,0:T(8,128)S(1)}, u32[]{:S(2)}, u32[]{:S(2)}) collective-permute-start(f32[2,144,144]{2,1,0:T(8,128)} %polynomial.1.refs_1_), channel_id=1, source_target_pairs={{0,24},{2,26},{4,28},{6,30},{8,0},{10,2},{12,4},{14,6},{16,8},{18,... | collective-permute-start | bytes 497672 | tf_op jit(solution)/shard_map/ppermute | solution.py:47
  892.6 33.2 %collective-permute-start.37 = (f32[4,2,144,144]{3,2,1,0:T(8,128)S(1)}, f32[4,2,144,144]{3,2,1,0:T(8,128)S(1)}, u32[]{:S(2)}, u32[]{:S(2)}) collective-permute-start(f32[4,2,144,144]{3,2,1,0:T(8,128)S(1)} %pad_maximum_fusion.5.refs_1_.refs_0_), channel_id=1, source_target_pairs={{0,4},{2,6},{4,0},{6,2},{8,12},{10,14},{12,8},{14,10},{16,20},{18,... | collective-permute-start | bytes 1990664 | tf_op jit(solution)/shard_map/ppermute | solution.py:47
  (142 other events, 1323.9 us)
Sparse Core Ops, SparseCore 0:
  116.2 89.2 all-gather.2
  208.3 86.8 all-gather.4
  314.5 120.7 reduce-scatter.3
  439.2 120.0 reduce-scatter.5
  580.7 121.7 reduce-scatter.7

commit v7 on v6

--- a/solution.py
+++ b/solution.py
@@ -288,19 +288,18 @@
         return [f.reshape(-1, f.shape[-1]) for f in full], lines[1:] + pairs[1:]
 
 
-    def muon_scatter_steps(self, groups, spread):
-        momenta, own, other = muon_gram(self.spots(), self.z.size, groups, spread)
+    def gram_steps(self, own, other):
         got = self.core.send(other, 1)
         anchor = yield [other]
         half = own + tie(got, anchor)
-        sent = half[1]
+        sent = half[1].astype(BF)
         got = self.x.send(sent, 1)
         anchor = yield [sent]
-        kept = half[0] + tie(got, anchor)
-        blocks = [kept[shift] for shift in range(self.z.size)]
-        got = [self.z.send(blocks[shift], shift) for shift in range(1, self.z.size)]
-        anchor = yield blocks[1:]
-        return momenta, [blocks[0]] + [tie(each, anchor) for each in got]
+        kept = half[0] + tie(got, anchor).astype(F32)
+        sent = [kept[shift].astype(BF) for shift in range(1, self.z.size)]
+        got = [self.z.send(each, shift) for shift, each in enumerate(sent, 1)]
+        anchor = yield sent
+        return [kept[0]] + [tie(each, anchor) for each in got]
 
     def muon_gather_steps(self, parts):
         factor = polynomial(parts)
@@ -676,7 +675,7 @@
     return lax.dot_general(left, right, (dims, ((), ())), precision=PRECISE, preferred_element_type=F32)
 
 
-def muon_gram_kernel(groups, spread, spots_ref, *refs):
+def muon_gram_kernel(groups, spread, spots_ref, base_own, base_other, *refs):
     count = sum(groups)
     sums, momenta = refs[: len(groups)], refs[len(groups) : len(groups) + count]
     outs = refs[len(groups) + count : len(groups) + 2 * count]
@@ -691,8 +690,8 @@
             n += 1
     zs = own_ref.shape[1]
     spots = block_spots([out.shape[1] // ROW_BLOCK for out in outs], spread)
-    own_ref[...] = jnp.zeros_like(own_ref)
-    other_ref[...] = jnp.zeros_like(other_ref)
+    own_ref[...] = base_own[...]
+    other_ref[...] = base_other[...]
     for matrix, block, z, x, core, place_in in spots:
         turned = outs[matrix][:, block * ROW_BLOCK : (block + 1) * ROW_BLOCK]
         gram = precise(turned, turned, ((0,), (0,)))
@@ -707,18 +706,18 @@
             other_ref[away] = gram
 
 
-def muon_gram(spots, zs, groups, spread):
+def muon_gram(spots, groups, spread, base):
     momenta = [momentum for _, each in groups for momentum in each]
-    grams = jax.ShapeDtypeStruct((2, zs, spread[0], ROW_BLOCK, ROW_BLOCK), F32)
+    grams = jax.ShapeDtypeStruct(base[0].shape, F32)
     vmem = pl.BlockSpec(memory_space=pltpu.VMEM)
     outs = pl.pallas_call(
         functools.partial(muon_gram_kernel, [len(each) for _, each in groups], spread),
         out_shape=[jax.ShapeDtypeStruct(momentum.shape, F32) for momentum in momenta] + [grams, grams],
-        in_specs=[pl.BlockSpec(memory_space=pltpu.SMEM)] + [vmem] * (len(groups) + len(momenta)),
+        in_specs=[pl.BlockSpec(memory_space=pltpu.SMEM)] + [vmem] * (2 + len(groups) + len(momenta)),
         out_specs=[vmem] * (len(momenta) + 2),
         compiler_params=pltpu.CompilerParams(vmem_limit_bytes=VMEM_LIMIT),
         name="muon_gram",
-    )(spots, *[group[0] for group in groups], *momenta)
+    )(spots, *base, *[group[0] for group in groups], *momenta)
     return outs[:-2], outs[-2], outs[-1]
 
 
@@ -732,7 +731,7 @@
     for n in blocks:
         gram = refs[0][n]
         for ref in refs[1:count]:
-            gram = gram + ref[n]
+            gram = gram + ref[n].astype(F32)
         square = jnp.sum(jnp.sum(gram * eye, axis=1, keepdims=True), axis=0, keepdims=True)
         scale = 1.0 / (jnp.sqrt(square) + NORM_EPS)
         scales.append(scale)
@@ -825,7 +824,9 @@
     received = net.to_all(partial)
     sent = first.advance(partial)
     sent = first.advance()
-    received, parcel = tie(received, *sent), tie(parcel, *sent)
+    sent = first.advance()
+    arrived = sent[-1]
+    received, parcel = tie(received, arrived), tie(parcel, arrived)
     received = jnp.sum(received, axis=1)
     bias_full = parcel[:, :, : biases.shape[0]].reshape(-1)
     b_ada, b_q, b_v, b_proj, b_fc1, b_fc2 = [bias_full[bounds[i] : bounds[i + 1]] for i in range(6)]
@@ -833,8 +834,9 @@
     shift_one, scale_one, gate_one, shift_two, scale_two, gate_two = jnp.split(
         modulation[:, None, :], 6, axis=-1
     )
-    (t_qkv, t_proj), arrived = first.finish(modulation)
-    wires = net.y.gather(tie(net.wire([w_fc1]), token_pieces[0][-1], *arrived))
+    t_qkv, t_proj = first.finish(modulation)[0]
+    wires = net.y.gather(tie(net.wire([w_fc1]), token_pieces[0][-1], arrived))
+    wires = wires[:1] + [tie(wire, t_qkv) for wire in wires[1:]]
     t_fc1 = lax.all_gather(net.rows(wires), "dp", axis=0, tiled=True)
     for i in range(1, count):
         token_pieces.append(net.y.gather(tie(own_tokens[i], wires[-1])))
@@ -952,13 +954,8 @@
     spread_early = (per, 0)
     early_blocks = (w_fc2.shape[0] + w_fc1.shape[0]) // ROW_BLOCK
     spread_last = (per, -(-early_blocks // per))
-    sums = halves.finish(own_part)
-    early = Staged(
-        net.muon_scatter_steps([(sums[0], [turned[3]]), (sums[1], [turned[2]])], spread_early)
-    )
-    sent = early.advance()
     far_sum = jnp.stack([steps_of.finish() for steps_of in far_parts])
-    grad_attn_in = tie(own_part, *sent) + far_sum
+    grad_attn_in = own_part + far_sum
     normed_one, inverse_one = jnp.stack(normed_all), jnp.stack(inverse_all)
     grad_shift_one = jnp.sum(grad_attn_in, axis=1)
     grad_scale_one = jnp.sum(grad_attn_in * normed_one, axis=1)
@@ -972,32 +969,36 @@
     sent = jnp.transpose(grad_mod_local.reshape(count, dp, 1, ada_cols), (1, 2, 0, 3))
     sent = jnp.broadcast_to(sent, (dp, seq, count, ada_cols))
     mod_parts = net.to_all(sent)
-    while not early.done:
-        sent = early.advance(sent if not isinstance(sent, list) else sent[0])
-    halves = Staged(net.halves_steps(tie(sum_last, *early.result[1])))
-    halves.advance()
+    sums = halves.finish(sent)
+    blank = jnp.zeros((2, net.z.size, per, ROW_BLOCK, ROW_BLOCK), F32)
+    (next_fc2, next_fc1), *early = muon_gram(
+        net.spots(), [(sums[0], [turned[3]]), (sums[1], [turned[2]])], spread_early, (blank, blank)
+    )
+    mod_parts = tie(mod_parts, early[0])
     mod_cols = jnp.sum(mod_parts, axis=1).astype(BF).reshape(dp * count, ada_cols)
     shard_ada = jnp.einsum("sr,sc->cr", cond_all, mod_cols, preferred_element_type=F32)
-
-    total = halves.finish(shard_ada)
-    last = Staged(
-        net.muon_scatter_steps([(total, [turned[0], turned[1]]), (shard_ada, [turned[4]])], spread_last)
-    )
-    sent = last.advance()
 
     cond_part = jnp.einsum("sc,rc->sr", mod_cols, low_ada, preferred_element_type=F32)
     cond_part = jnp.broadcast_to(cond_part.reshape(dp, 1, -1), (dp, seq, count * ada_rows))
     term_bias = jnp.concatenate([bias_ada, bias_q, bias_v, bias_proj, bias_fc1, bias_fc2])
     parcel = jnp.concatenate([term_bias.reshape(dp, seq, -1), cond_part], axis=-1)
-    parcel = net.to_all(tie(parcel, *sent))
-    while not last.done:
-        sent = last.advance(sent[0])
-    gathered = Staged(net.muon_gather_steps(early.result[1] + last.result[1]))
+    got_parcel = net.to_all(parcel)
+
+    halves = Staged(net.halves_steps(tie(sum_last, parcel)))
+    sent = halves.advance()
+    total = halves.finish(shard_ada)
+    (next_qkv, next_proj, next_ada), *grams = muon_gram(
+        net.spots(), [(total, [turned[0], turned[1]]), (shard_ada, [turned[4]])], spread_last, early
+    )
+    grams = Staged(net.gram_steps(*grams))
+    sent = grams.advance()
+    parcel = tie(got_parcel, *sent)
+    while not grams.done:
+        sent = grams.advance(sent[0])
+    gathered = Staged(net.muon_gather_steps(grams.result))
     sent = gathered.advance()
     while not gathered.done:
         sent = gathered.advance(sent[0])
-    next_fc2, next_fc1 = early.result[0]
-    next_qkv, next_proj, next_ada = last.result[0]
     new_fc2, new_fc1 = muon_apply(
         net.spots(), gathered.result, [next_fc2, next_fc1], [w_fc2.T, w_fc1.T],
         [math.sqrt(width / hidden), math.sqrt(hidden / width)], spread_early,

time: 963 us -> 884 us (0.918)
  waiting for transfers between devices: 227 us -> 137 us
  starting transfers between devices: 52.9 us -> 65.4 us
    ppermute x40 -> x35, waiting for transfers between devices: 183 us -> 94.9 us  [send(): return lax.ppermute(value, self.name, pairs)]
    ppermute x40 -> x35, starting transfers between devices: 37 us -> 46.3 us  [send(): return lax.ppermute(value, self.name, pairs)]
    unnamed x246 -> x232, local copies, waits for them, and re-layouts: 39.4 us -> 37.7 us
  transfers between devices with their start and end apart: 48 -> 43, of which waited for: 22 -> 17; matrix products, arithmetic and copies ran while one was open for 35% -> 38% of each run, Pallas kernels for 22% -> 24%
where the time goes in v7:
time: 884 us; the launch traced here: 876 us
  Pallas kernels  248 us (28%)
  matrix products  223 us (25%)
  waiting for transfers between devices  137 us (15%)
  local copies, waits for them, and re-layouts  86 us (10%)
  other arithmetic  70 us (8%)
  starting transfers between devices  65.4 us (7%)
  blocking collectives  30.6 us (3%)
  between operations  15.4 us (2%)
    dot_general x13, matrix products, dot(): return jnp.einsum('srn,nk->srk', left, right, preferred_element_type=F32)  95.5 us
    ppermute x35, waiting for transfers between devices, send(): return lax.ppermute(value, self.name, pairs)  94.9 us
    pallas_call x2, Pallas kernels, attend_back(): pl.pallas_call(without(attend_back_kernel, 8, len(deps), heads, tile), gr...  90.6 us
    dot_general x9, matrix products, dot_t(): return jnp.einsum('srk,nk->srn', left, right, preferred_element_type=F32)  89.5 us
    pallas_call x2, Pallas kernels, attend(): pl.pallas_call(without(attend_kernel, 5, len(deps), heads, tile), grid_sp...  65.1 us
    ppermute x35, starting transfers between devices, send(): return lax.ppermute(value, self.name, pairs)  46.3 us
    unnamed x232, local copies, waits for them, and re-layouts  37.7 us
    dot_general x2, matrix products, outer(): jnp.einsum('srn,srk->nk', left, right, preferred_element_type=F32)  35.4 us
  transfers between devices with their start and end apart: 43, of which 17 were waited for; matrix products, arithmetic and copies ran while one was open for 38% of the time, Pallas kernels for 24%

profile of v7, /device:TPU:11, one launch (start us, length us, event | category | flops | bytes accessed | tf_op | source)
XLA Modules:
  0.0 875.7 jit_solution(4236352241419399900)
XLA Ops:
  23.7 10.4 %all-to-all-done = f32[32,1,1656]{2,1,0:T(1,128)S(1)} async-done(((f32[32,1,1656]{2,1,0:T(1,128)}), f32[32,1,1656]{2,1,0:T(1,128)S(1)}, u32[]{:S(2)}, u32[]{:S(2)}) %all-to-all-start) | async-done | bytes 212000 | tf_op jit(solution)/shard_map/all_to_all | solution.py:319
  51.9 15.1 %collective-permute-start.10 = (bf16[4,16,8,1152]{3,2,1,0:T(8,128)(2,1)S(1)}, bf16[4,16,8,1152]{3,2,1,0:T(8,128)(2,1)}, u32[]{:S(2)}, u32[]{:S(2)}) collective-permute-start(bf16[4,16,8,1152]{3,2,1,0:T(8,128)(2,1)S(1)} %pad_maximum_fusion.3.refs_1_), channel_id=1, source_target_pairs={{0,2},{2,0},{4,6},{6,4},{8,10},{10,8},{12,14},{14,12},{16,18},{18,... | collective-permute-start | bytes 3538952 | tf_op jit(solution)/shard_map/ppermute | solution.py:47
  67.5 11.4 %collective-permute-done.2.refs_1_.refs_6_.refs_2_ = bf16[2,20,8,1152]{3,2,1,0:T(8,128)(2,1)S(1)} collective-permute-done((bf16[2,20,8,1152]{3,2,1,0:T(8,128)(2,1)}, bf16[2,20,8,1152]{3,2,1,0:T(8,128)(2,1)S(1)}, u32[]{:S(2)}, u32[]{:S(2)}) %collective-permute-start.2) | collective-permute-done | bytes 737312 | tf_op jit(solution)/shard_map/ppermute | solution.py:47
  90.9 11.3 %all-to-all-done.1 = f32[32,2,432]{2,1,0:T(2,128)S(1)} async-done(((f32[32,2,432]{2,1,0:T(2,128)}), f32[32,2,432]{2,1,0:T(2,128)S(1)}, u32[]{:S(2)}, u32[]{:S(2)}) %all-to-all-start.1) | async-done | bytes 110624 | tf_op jit(solution)/shard_map/all_to_all | solution.py:319
  112.9 9.1 %place.1 = (bf16[4,2,2,27,8,1152]{5,4,3,2,1,0:T(8,128)(2,1)}, bf16[4,2,2,9,8,1152]{5,4,3,2,1,0:T(8,128)(2,1)}) custom-call(s32[3]{0:T(128)} %pad_add_fusion.1.refs_0_.spots_ref, bf16[4,16,8,1152]{3,2,1,0:T(8,128)(2,1)} %copy-done.30, bf16[4,16,8,1152]{3,2,1,0:T(8,128)(2,1)} %collective-permute-done.7.refs_2_, ...), custom_call_target="tpu_custom_call" | custom-call | bytes 21233664 | tf_op jit(solution)/shard_map/place/pallas_call | solution.py:198
  155.6 32.2 %attend.2 = (bf16[1,512,1152]{2,1,0:T(8,128)(2,1)}, f32[1,16,1,512]{3,2,1,0:T(1,128)}) custom-call(s32[1]{0:T(128)} %bitcast.13.refs_0_, s32[2]{0:T(128)} %pad_add_fusion.refs_1_, bf16[1,512,1152]{2,1,0:T(8,128)(2,1)} %fusion.38.refs_2_, bf16[1,1024,1152]{2,1,0:T(8,128)(2,1)} %fusion.31.refs_3_, bf16[1,1024,1152]{2,1,0:T(8,128)(2,1)} %fusion.29.refs_4_), custom_call_target="tpu_custom_call" | custom-call | flops 4294967296 | bytes 7077888 | tf_op jit(solution)/shard_map/attend/pallas_call | solution.py:543
  222.8 32.9 %attend.3 = (bf16[1,512,1152]{2,1,0:T(8,128)(2,1)}, f32[1,16,1,512]{3,2,1,0:T(1,128)}) custom-call(s32[1]{0:T(128)} %bitcast.28.refs_0_, s32[2]{0:T(128)} %pad_add_fusion.refs_1_, bf16[1,512,1152]{2,1,0:T(8,128)(2,1)} %fusion.37.refs_2_, bf16[1,1024,1152]{2,1,0:T(8,128)(2,1)} %fusion.32.refs_3_, bf16[1,1024,1152]{2,1,0:T(8,128)(2,1)} %fusion.30.refs_4_), custom_call_target="tpu_custom_call" | custom-call | flops 4294967296 | bytes 7077888 | tf_op jit(solution)/shard_map/attend/pallas_call | solution.py:543
  258.5 9.0 %fusion.100 = (f32[2,512]{1,0:T(2,128)S(1)}, f32[2,512,1152]{2,1,0:T(8,128)S(1)}, f32[2,512,1152]{2,1,0:T(8,128)}) fusion(f32[2,1152]{1,0:T(2,128)S(1)} %get-tuple-element.206, bf16[2,1,512,1152]{3,2,1,0:T(8,128)(2,1)} %param.18, f32[1152]{0:T(1024)S(1)} %copy-done.92, bf16[2,512,1152]{2,1,0:T(8,128)(2,1)} %constant_dynamic-update-slice_fusion, ...), kind=kOutput, calls=%fused_computation.239 | convolution fusion | flops 2723806208 | bytes 16827904 | tf_op jit(solution)/shard_map/srk,nk->srn/dot_general | solution.py:346
  270.3 25.3 %multiply_convert_fusion = (bf16[2,512,4608]{2,1,0:T(8,128)(2,1)}, f32[2,512,4608]{2,1,0:T(8,128)}) fusion(f32[4608]{0:T(1024)S(1)} %copy-done.80, bf16[4608,1152]{1,0:T(8,128)(2,1)} %all-gather.3.cloned.1.call-done, f32[2,512,1152]{2,1,0:T(8,128)} %copy-done.28, f32[2,1152]{1,0:T(2,128)S(1)} %copy-done.85, f32[2,1152]{1,0:T(2,128)S(1)} %copy-done.82, ...), kind=kOutput, calls=%fused_computation.14 | convolution fusion | flops 10924720128 | bytes 43692032 | tf_op jit(solution)/shard_map/srk,nk->srn/dot_general | solution.py:346
  295.6 17.4 %fusion.refs_1_ = bf16[1152,4608]{1,0:T(8,128)(2,1)} fusion(bf16[2,512,1152]{2,1,0:T(8,128)(2,1)S(1)} %fusion.25.refs_0_, bf16[2,512,4608]{2,1,0:T(8,128)(2,1)} %get-tuple-element.210.refs_0_), kind=kOutput, calls=%fused_computation.4 | convolution fusion | flops 10876944384 | bytes 22413312 | tf_op jit(solution)/shard_map/srn,srk->nk/dot_general | solution.py:354
  314.8 26.1 %fusion.8.refs_0_ = bf16[2,512,4608]{2,1,0:T(8,128)(2,1)S(1)} fusion(f32[2,512,4608]{2,1,0:T(8,128)} %get-tuple-element.211, bf16[2,512,1152]{2,1,0:T(8,128)(2,1)S(1)} %copy-done.8, bf16[1152,4608]{1,0:T(8,128)(2,1)} %all-gather.5.cloned.1.call-done, f32[4608]{0:T(1024)S(1)} %copy-done.80), kind=kOutput, calls=%fused_computation.12 | convolution fusion | flops 10970726400 | bytes 41306112 | tf_op jit(solution)/shard_map/srn,nk->srk/dot_general | solution.py:350
  344.6 18.0 %fusion.1.refs_1_.refs_0_ = bf16[4608,1152]{1,0:T(8,128)(2,1)} fusion(bf16[2,512,4608]{2,1,0:T(8,128)(2,1)S(1)} %fusion.8.refs_0_, f32[2,512,1152]{2,1,0:T(8,128)} %copy-done.28, f32[2,1152]{1,0:T(2,128)S(1)} %copy-done.85, f32[2,1152]{1,0:T(2,128)S(1)} %copy-done.82, f32[2,512]{1,0:T(2,128)S(1)} %add_rsqrt_fusion, f32[2,512]{1,0:T(2,128)S(1)} %broadcast_multiply_fusion.4), kind=kOutput, calls=%fused_computation.5 | convolution fusion | flops 10882842624 | bytes 24799232 | tf_op jit(solution)/shard_map/srn,srk->nk/dot_general | solution.py:354
  362.7 21.7 %multiply_reduce_fusion = (f32[2,1152]{1,0:T(2,128)}, f32[2,512]{1,0:T(2,128)S(1)}, f32[2,512]{1,0:T(2,128)S(1)}, f32[2,1152]{1,0:T(2,128)}, f32[2,512,1152]{2,1,0:T(8,128)}) fusion(f32[2,512,1152]{2,1,0:T(8,128)} %copy-done.28, f32[2,512]{1,0:T(2,128)S(1)} %add_rsqrt_fusion, f32[2,512]{1,0:T(2,128)S(1)} %broadcast_multiply_fusion.4, ...), kind=kOutput, calls=%fused_computation.45 | convolution fusion | flops 10882246656 | bytes 29535232 | tf_op jit(solution)/shard_map/srn,nk->srk/dot_general | solution.py:350
  384.4 24.9 %fusion.26 = (f32[2,1152]{1,0:T(2,128)}, bf16[2,1,512,1152]{3,2,1,0:T(8,128)(2,1)}, f32[1152]{0:T(1024)}, bf16[2,512,1152]{2,1,0:T(8,128)(2,1)}, f32[2,512,1152]{2,1,0:T(8,128)}) fusion(bf16[2,1,512,1152]{3,2,1,0:T(8,128)(2,1)S(1)} %copy-done.44, f32[2,512,1152]{2,1,0:T(8,128)} %copy-done.28, f32[2,1152]{1,0:T(2,128)S(1)} %copy-done.75, ...), kind=kOutput, calls=%fused_computation.37 | convolution fusion | flops 10894046208 | bytes 41350144 | tf_op jit(solution)/shard_map/srk,nk->srn/dot_general | solution.py:346
  417.1 17.6 %reduce-scatter.4.cloned.1.call-done.refs_1_.refs_0_ = bf16[72,4608]{1,0:T(8,128)(2,1)} async-done(((bf16[1152,4608]{1,0:T(8,128)(2,1)}), bf16[72,4608]{1,0:T(8,128)(2,1)}) %reduce-scatter.4.cloned.1.call-update) | async-done | bytes 663568 | tf_op jit(solution)/shard_map/reduce_scatter | solution.py:249
  442.9 45.6 %attend_back.2 = (bf16[1,512,1152]{2,1,0:T(8,128)(2,1)}, bf16[1,1024,1152]{2,1,0:T(8,128)(2,1)}, bf16[1,1024,1152]{2,1,0:T(8,128)(2,1)}) custom-call(s32[1]{0:T(128)} %bitcast.13.refs_0_, s32[2]{0:T(128)} %pad_add_fusion.refs_1_, bf16[1,512,1152]{2,1,0:T(8,128)(2,1)} %fusion.38.refs_2_, bf16[1,1024,1152]{2,1,0:T(8,128)(2,1)} %fusion.31.refs_3_, ...), custom_call_target="tpu_custom_call" | custom-call | flops 10737418240 | bytes 14155776 | tf_op jit(solution)/shard_map/attend_back/pallas_call | solution.py:628
  497.2 45.1 %attend_back.3 = (bf16[1,512,1152]{2,1,0:T(8,128)(2,1)}, bf16[1,1024,1152]{2,1,0:T(8,128)(2,1)}, bf16[1,1024,1152]{2,1,0:T(8,128)(2,1)}) custom-call(s32[1]{0:T(128)} %bitcast.28.refs_0_, s32[2]{0:T(128)} %pad_add_fusion.refs_1_, bf16[1,512,1152]{2,1,0:T(8,128)(2,1)} %fusion.37.refs_2_, bf16[1,1024,1152]{2,1,0:T(8,128)(2,1)} %fusion.32.refs_3_, ...), custom_call_target="tpu_custom_call" | custom-call | flops 10737418240 | bytes 14155776 | tf_op jit(solution)/shard_map/attend_back/pallas_call | solution.py:628
  551.1 29.0 %shard_outer.1.refs_1_ = bf16[4,2,2,36,8,1152]{5,4,3,2,1,0:T(8,128)(2,1)} custom-call(s32[3]{0:T(128)} %pad_add_fusion.1.refs_0_.spots_ref, bf16[512,1152]{1,0:T(8,128)(2,1)} %bitcast.275, bf16[512,1152]{1,0:T(8,128)(2,1)} %bitcast.292, bf16[1024,1152]{1,0:T(8,128)(2,1)} %bitcast.318, bf16[1024,1152]{1,0:T(8,128)(2,1)} %bitcast.319, ...), custom_call_target="tpu_custom_call" | custom-call | flops 16307453952 | bytes 10616832 | tf_op jit(solution)/shard_map/shard_outer/pallas_call | solution.py:444
  631.9 12.9 %collective-permute-done.20 = bf16[512,1152]{1,0:T(8,128)(2,1)} collective-permute-done((bf16[512,1152]{1,0:T(8,128)(2,1)}, bf16[512,1152]{1,0:T(8,128)(2,1)}, u32[]{:S(2)}, u32[]{:S(2)}) %collective-permute-start.20) | collective-permute-done | bytes 1179680 | tf_op jit(solution)/shard_map/ppermute | solution.py:47
  677.3 17.1 %muon_gram.2 = (f32[72,2304]{1,0:T(8,128)}, f32[288,576]{1,0:T(8,128)}, f32[2,4,2,144,144]{4,3,2,1,0:T(8,128)}, f32[2,4,2,144,144]{4,3,2,1,0:T(8,128)}) custom-call(s32[3]{0:T(128)} %pad_add_fusion.1.refs_0_.spots_ref, f32[2,4,2,144,144]{4,3,2,1,0:T(8,128)} %broadcast_in_dim.24.base_own.base_other, ...), custom_call_target="tpu_custom_call" | custom-call | tf_op jit(solution)/shard_map/muon_gram/pallas_call | solution.py:713
  716.9 13.5 %muon_gram.3 = (f32[216,576]{1,0:T(8,128)}, f32[72,576]{1,0:T(8,128)}, f32[432,576]{1,0:T(8,128)}, f32[2,4,2,144,144]{4,3,2,1,0:T(8,128)}, f32[2,4,2,144,144]{4,3,2,1,0:T(8,128)}) custom-call(s32[3]{0:T(128)} %pad_add_fusion.1.refs_0_.spots_ref, f32[2,4,2,144,144]{4,3,2,1,0:T(8,128)} %get-tuple-element.54.refs_1_.base_own, ...), custom_call_target="tpu_custom_call" | custom-call | tf_op jit(solution)/shard_map/muon_gram/pallas_call | solution.py:713
  741.1 14.3 %collective-permute-done.25.refs_0_ = bf16[4,2,144,144]{3,2,1,0:T(8,128)(2,1)S(1)} collective-permute-done((bf16[4,2,144,144]{3,2,1,0:T(8,128)(2,1)S(1)}, bf16[4,2,144,144]{3,2,1,0:T(8,128)(2,1)S(1)}, u32[]{:S(2)}, u32[]{:S(2)}) %collective-permute-start.25) | collective-permute-done | bytes 331808 | tf_op jit(solution)/shard_map/ppermute | solution.py:47
  791.4 17.5 %collective-permute-done.30.refs_0_ = f32[2,144,144]{2,1,0:T(8,128)S(1)} collective-permute-done((f32[2,144,144]{2,1,0:T(8,128)}, f32[2,144,144]{2,1,0:T(8,128)S(1)}, u32[]{:S(2)}, u32[]{:S(2)}) %collective-permute-start.30) | collective-permute-done | bytes 165920 | tf_op jit(solution)/shard_map/ppermute | solution.py:47
  812.8 30.6 %all_to_all.29 = f32[32,1,1656]{2,1,0:T(1,128)S(1)} all-to-all(f32[32,1,1656]{2,1,0:T(1,128)S(1)} %all_to_all.22), channel_id=1, replica_groups=mesh['dp'=16,'seq'=2] {'dp','seq'}, dimensions={0} | all-to-all | bytes 423936 | tf_op jit(solution)/shard_map/all_to_all | solution.py:319
  (509 shorter events, 352.5 us)
Async XLA Ops:
  14.9 19.1 %all-to-all-start = ((f32[32,1,1656]{2,1,0:T(1,128)}), f32[32,1,1656]{2,1,0:T(1,128)S(1)}, u32[]{:S(2)}, u32[]{:S(2)}) async-start(f32[32,1,1656]{2,1,0:T(1,128)} %all_to_all.24), calls=%async_computation | async-start | bytes 425984 | tf_op jit(solution)/shard_map/all_to_all | solution.py:319
  23.0 26.9 %collective-permute-start.4 = (bf16[16,8,1152]{2,1,0:T(8,128)(2,1)S(1)}, bf16[16,8,1152]{2,1,0:T(8,128)(2,1)S(1)}, u32[]{:S(2)}, u32[]{:S(2)}) collective-permute-start(bf16[16,8,1152]{2,1,0:T(8,128)(2,1)S(1)} %get-tuple-element.194.refs_1_.refs_2_), channel_id=1, source_target_pairs={{0,24},{2,26},{4,28},{6,30},{8,0},{10,2},{12,4},{14,6},{16,8},{18,... | collective-permute-start | bytes 884744 | tf_op jit(solution)/shard_map/ppermute | solution.py:47
  43.9 23.3 %collective-permute-start.8 = (bf16[2,20,8,1152]{3,2,1,0:T(8,128)(2,1)}, bf16[2,20,8,1152]{3,2,1,0:T(8,128)(2,1)}, u32[]{:S(2)}, u32[]{:S(2)}) collective-permute-start(bf16[2,20,8,1152]{3,2,1,0:T(8,128)(2,1)} %pad_maximum_fusion.5.refs_3_), channel_id=1, source_target_pairs={{0,24},{2,26},{4,28},{6,30},{8,0},{10,2},{12,4},{14,6},{16,8},{18,... | collective-permute-start | bytes 2211848 | tf_op jit(solution)/shard_map/ppermute | solution.py:47
  43.9 35.0 %collective-permute-start.2 = (bf16[2,20,8,1152]{3,2,1,0:T(8,128)(2,1)}, bf16[2,20,8,1152]{3,2,1,0:T(8,128)(2,1)S(1)}, u32[]{:S(2)}, u32[]{:S(2)}) collective-permute-start(bf16[2,20,8,1152]{3,2,1,0:T(8,128)(2,1)} %pad_maximum_fusion.5.refs_3_), channel_id=1, source_target_pairs={{0,8},{2,10},{4,12},{6,14},{8,16},{10,18},{12,20},{14,22},{16,24},... | collective-permute-start | bytes 2211848 | tf_op jit(solution)/shard_map/ppermute | solution.py:47
  48.6 56.6 %collective-permute-start.3 = (bf16[512,1152]{1,0:T(8,128)(2,1)}, bf16[512,1152]{1,0:T(8,128)(2,1)S(1)}, u32[]{:S(2)}, u32[]{:S(2)}) collective-permute-start(bf16[512,1152]{1,0:T(8,128)(2,1)} %tie.49), channel_id=1, source_target_pairs={{0,1},{1,0},{2,3},{3,2},{4,5},{5,4},{6,7},{7,6},{8,9},{9,8},{10,11... | collective-permute-start | bytes 3538952 | tf_op jit(solution)/shard_map/ppermute | solution.py:47
  51.9 55.0 %collective-permute-start.10 = (bf16[4,16,8,1152]{3,2,1,0:T(8,128)(2,1)S(1)}, bf16[4,16,8,1152]{3,2,1,0:T(8,128)(2,1)}, u32[]{:S(2)}, u32[]{:S(2)}) collective-permute-start(bf16[4,16,8,1152]{3,2,1,0:T(8,128)(2,1)S(1)} %pad_maximum_fusion.3.refs_1_), channel_id=1, source_target_pairs={{0,2},{2,0},{4,6},{6,4},{8,10},{10,8},{12,14},{14,12},{16,18},{18,... | collective-permute-start | bytes 3538952 | tf_op jit(solution)/shard_map/ppermute | solution.py:47
  67.0 40.6 %collective-permute-start.7 = (bf16[4,16,8,1152]{3,2,1,0:T(8,128)(2,1)S(1)}, bf16[4,16,8,1152]{3,2,1,0:T(8,128)(2,1)}, u32[]{:S(2)}, u32[]{:S(2)}) collective-permute-start(bf16[4,16,8,1152]{3,2,1,0:T(8,128)(2,1)S(1)} %pad_maximum_fusion.3.refs_1_), channel_id=1, source_target_pairs={{0,4},{2,6},{4,0},{6,2},{8,12},{10,14},{12,8},{14,10},{16,20},{18,... | collective-permute-start | bytes 3538952 | tf_op jit(solution)/shard_map/ppermute | solution.py:47
  67.1 39.1 %collective-permute-start.12 = (bf16[2,20,8,1152]{3,2,1,0:T(8,128)(2,1)}, bf16[2,20,8,1152]{3,2,1,0:T(8,128)(2,1)}, u32[]{:S(2)}, u32[]{:S(2)}) collective-permute-start(bf16[2,20,8,1152]{3,2,1,0:T(8,128)(2,1)} %pad_maximum_fusion.5.refs_3_), channel_id=1, source_target_pairs={{0,2},{2,0},{4,6},{6,4},{8,10},{10,8},{12,14},{14,12},{16,18},{18,... | collective-permute-start | bytes 2211848 | tf_op jit(solution)/shard_map/ppermute | solution.py:47
  78.9 29.1 %collective-permute-start.9 = (bf16[2,20,8,1152]{3,2,1,0:T(8,128)(2,1)}, bf16[2,20,8,1152]{3,2,1,0:T(8,128)(2,1)}, u32[]{:S(2)}, u32[]{:S(2)}) collective-permute-start(bf16[2,20,8,1152]{3,2,1,0:T(8,128)(2,1)} %collective-permute-done.8.refs_4_), channel_id=1, source_target_pairs={{0,24},{2,26},{4,28},{6,30},{8,0},{10,2},{12,4},{14,6},{16,8},{18,... | collective-permute-start | bytes 2211848 | tf_op jit(solution)/shard_map/ppermute | solution.py:47
  82.7 19.5 %all-to-all-start.1 = ((f32[32,2,432]{2,1,0:T(2,128)}), f32[32,2,432]{2,1,0:T(2,128)S(1)}, u32[]{:S(2)}, u32[]{:S(2)}) async-start(f32[32,2,432]{2,1,0:T(2,128)} %bitcast.7), calls=%async_computation.1 | async-start | bytes 262144 | tf_op jit(solution)/shard_map/all_to_all | solution.py:319
  87.9 182.4 %all-gather.3.cloned.1.call-start = ((), (), s32[]{:S(2)}) async-start(), calls=%async_computation.7 | async-start | bytes 11280384 | tf_op jit(solution)/shard_map/all_gather | solution.py:840
  126.3 186.9 %all-gather.5.cloned.1.call-start = ((), (), s32[]{:S(2)}) async-start(), calls=%async_computation.8 | async-start | bytes 11280384 | tf_op jit(solution)/shard_map/all_gather | solution.py:858
  136.0 51.8 %collective-permute-start.17 = (bf16[512,1152]{1,0:T(8,128)(2,1)}, bf16[512,1152]{1,0:T(8,128)(2,1)S(1)}, u32[]{:S(2)}, u32[]{:S(2)}) collective-permute-start(bf16[512,1152]{1,0:T(8,128)(2,1)} %tie.60), channel_id=1, source_target_pairs={{0,1},{1,0},{2,3},{3,2},{4,5},{5,4},{6,7},{7,6},{8,9},{9,8},{10,11... | collective-permute-start | bytes 3538952 | tf_op jit(solution)/shard_map/ppermute | solution.py:47
  200.1 234.6 %reduce-scatter.4.cloned.1.call-start = ((), (), s32[]{:S(2)}) async-start(), calls=%async_computation.9 | async-start | bytes 11280384 | tf_op jit(solution)/shard_map/reduce_scatter | solution.py:249
  313.1 303.3 %reduce-scatter.6.cloned.1.call-start = ((), (), s32[]{:S(2)}) async-start(), calls=%async_computation.10 | async-start | bytes 11280384 | tf_op jit(solution)/shard_map/reduce_scatter | solution.py:249
  434.8 266.2 %reduce-scatter.8.cloned.1.call-start = ((), (), s32[]{:S(2)}) async-start(), calls=%async_computation.11 | async-start | bytes 11280384 | tf_op jit(solution)/shard_map/reduce_scatter | solution.py:249
  593.0 38.9 %collective-permute-start.19 = (bf16[512,1152]{1,0:T(8,128)(2,1)}, bf16[512,1152]{1,0:T(8,128)(2,1)}, u32[]{:S(2)}, u32[]{:S(2)}) collective-permute-start(bf16[512,1152]{1,0:T(8,128)(2,1)} %fusion.35.refs_8_), channel_id=1, source_target_pairs={{0,1},{1,0},{2,3},{3,2},{4,5},{5,4},{6,7},{7,6},{8,9},{9,8},{10,11... | collective-permute-start | bytes 3538952 | tf_op jit(solution)/shard_map/ppermute | solution.py:47
  594.2 50.6 %collective-permute-start.20 = (bf16[512,1152]{1,0:T(8,128)(2,1)}, bf16[512,1152]{1,0:T(8,128)(2,1)}, u32[]{:S(2)}, u32[]{:S(2)}) collective-permute-start(bf16[512,1152]{1,0:T(8,128)(2,1)} %fusion.36.refs_12_), channel_id=1, source_target_pairs={{0,1},{1,0},{2,3},{3,2},{4,5},{5,4},{6,7},{7,6},{8,9},{9,8},{10,11... | collective-permute-start | bytes 3538952 | tf_op jit(solution)/shard_map/ppermute | solution.py:47
  599.8 62.9 %collective-permute-start.21 = (bf16[72,2304]{1,0:T(8,128)(2,1)}, bf16[72,2304]{1,0:T(8,128)(2,1)}, u32[]{:S(2)}, u32[]{:S(2)}) collective-permute-start(bf16[72,2304]{1,0:T(8,128)(2,1)} %bitcast.250.refs_1_), channel_id=1, source_target_pairs={{0,1},{1,0},{2,3},{3,2},{4,5},{5,4},{6,7},{7,6},{8,9},{9,8},{10,11... | collective-permute-start | bytes 995336 | tf_op jit(solution)/shard_map/ppermute | solution.py:47
  622.1 51.7 %collective-permute-start.22 = (bf16[288,576]{1,0:T(8,128)(2,1)}, bf16[288,576]{1,0:T(8,128)(2,1)}, u32[]{:S(2)}, u32[]{:S(2)}) collective-permute-start(bf16[288,576]{1,0:T(8,128)(2,1)} %bitcast.249.refs_2_), channel_id=1, source_target_pairs={{0,1},{1,0},{2,3},{3,2},{4,5},{5,4},{6,7},{7,6},{8,9},{9,8},{10,11... | collective-permute-start | bytes 995336 | tf_op jit(solution)/shard_map/ppermute | solution.py:47
  654.7 39.7 %all-to-all-start.2 = ((f32[32,2,432]{2,1,0:T(2,128)}), f32[32,2,432]{2,1,0:T(2,128)S(1)}, u32[]{:S(2)}, u32[]{:S(2)}) async-start(f32[32,2,432]{2,1,0:T(2,128)} %bitcast.82), calls=%async_computation.4 | async-start | bytes 262144 | tf_op jit(solution)/shard_map/all_to_all | solution.py:319
  783.8 25.2 %collective-permute-start.30 = (f32[2,144,144]{2,1,0:T(8,128)}, f32[2,144,144]{2,1,0:T(8,128)S(1)}, u32[]{:S(2)}, u32[]{:S(2)}) collective-permute-start(f32[2,144,144]{2,1,0:T(8,128)} %polynomial.1.refs_1_), channel_id=1, source_target_pairs={{0,16},{2,18},{4,20},{6,22},{8,24},{10,26},{12,28},{14,30},{16,0},... | collective-permute-start | bytes 497672 | tf_op jit(solution)/shard_map/ppermute | solution.py:47
  784.6 25.9 %collective-permute-start.29 = (f32[2,144,144]{2,1,0:T(8,128)}, f32[2,144,144]{2,1,0:T(8,128)S(1)}, u32[]{:S(2)}, u32[]{:S(2)}) collective-permute-start(f32[2,144,144]{2,1,0:T(8,128)} %polynomial.1.refs_1_), channel_id=1, source_target_pairs={{0,24},{2,26},{4,28},{6,30},{8,0},{10,2},{12,4},{14,6},{16,8},{18,... | collective-permute-start | bytes 497672 | tf_op jit(solution)/shard_map/ppermute | solution.py:47
  812.5 34.3 %collective-permute-start.32 = (f32[4,2,144,144]{3,2,1,0:T(8,128)S(1)}, f32[4,2,144,144]{3,2,1,0:T(8,128)S(1)}, u32[]{:S(2)}, u32[]{:S(2)}) collective-permute-start(f32[4,2,144,144]{3,2,1,0:T(8,128)S(1)} %pad_maximum_fusion.4.refs_1_.refs_0_), channel_id=1, source_target_pairs={{0,4},{2,6},{4,0},{6,2},{8,12},{10,14},{12,8},{14,10},{16,20},{18,... | collective-permute-start | bytes 1990664 | tf_op jit(solution)/shard_map/ppermute | solution.py:47
  (130 other events, 1196.2 us)
Sparse Core Ops, SparseCore 0:
  126.4 87.9 all-gather.2
  217.3 86.8 all-gather.4
  313.2 121.5 reduce-scatter.3
  438.7 119.9 reduce-scatter.5
  580.3 120.7 reduce-scatter.7

commit v8 on v7

--- a/solution.py
+++ b/solution.py
@@ -679,7 +679,7 @@
     count = sum(groups)
     sums, momenta = refs[: len(groups)], refs[len(groups) : len(groups) + count]
     outs = refs[len(groups) + count : len(groups) + 2 * count]
-    own_ref, other_ref = refs[len(groups) + 2 * count :]
+    own_ref, other_ref, grams, sems = refs[len(groups) + 2 * count :]
     n = 0
     for matrices, sum_ref in zip(groups, sums):
         start = 0
@@ -690,31 +690,34 @@
             n += 1
     zs = own_ref.shape[1]
     spots = block_spots([out.shape[1] // ROW_BLOCK for out in outs], spread)
-    own_ref[...] = base_own[...]
-    other_ref[...] = base_other[...]
-    for matrix, block, z, x, core, place_in in spots:
+    copies = []
+    for n, (matrix, block, z, x, core, place_in) in enumerate(spots):
         turned = outs[matrix][:, block * ROW_BLOCK : (block + 1) * ROW_BLOCK]
-        gram = precise(turned, turned, ((0,), (0,)))
+        grams[n] = precise(turned, turned, ((0,), (0,)))
         away = (lax.rem(spots_ref[1] + x, 2), lax.rem(zs + z - spots_ref[0], zs), place_in)
-
-        @pl.when(spots_ref[2] == core)
-        def _():
-            own_ref[away] = gram
-
-        @pl.when(spots_ref[2] != core)
-        def _():
-            other_ref[away] = gram
+        pair = [pltpu.make_async_copy(grams.at[n], ref.at[away], sems.at[n]) for ref in (own_ref, other_ref)]
+        on_own_core(True, spots_ref, core, [copy.start for copy in pair])
+        copies.append((core, pair))
+    for core, pair in copies:
+        on_own_core(True, spots_ref, core, [copy.wait for copy in pair])
 
 
 def muon_gram(spots, groups, spread, base):
     momenta = [momentum for _, each in groups for momentum in each]
-    grams = jax.ShapeDtypeStruct(base[0].shape, F32)
-    vmem = pl.BlockSpec(memory_space=pltpu.VMEM)
+    terms = jax.ShapeDtypeStruct(base[0].shape, F32)
+    vmem, anywhere = pl.BlockSpec(memory_space=pltpu.VMEM), pl.BlockSpec(memory_space=pl.ANY)
+    blocks = len(block_spots([momentum.shape[1] // ROW_BLOCK for momentum in momenta], spread))
     outs = pl.pallas_call(
         functools.partial(muon_gram_kernel, [len(each) for _, each in groups], spread),
-        out_shape=[jax.ShapeDtypeStruct(momentum.shape, F32) for momentum in momenta] + [grams, grams],
-        in_specs=[pl.BlockSpec(memory_space=pltpu.SMEM)] + [vmem] * (2 + len(groups) + len(momenta)),
-        out_specs=[vmem] * (len(momenta) + 2),
+        out_shape=[jax.ShapeDtypeStruct(momentum.shape, F32) for momentum in momenta] + [terms, terms],
+        in_specs=[pl.BlockSpec(memory_space=pltpu.SMEM), anywhere, anywhere]
+        + [vmem] * (len(groups) + len(momenta)),
+        out_specs=[vmem] * len(momenta) + [anywhere, anywhere],
+        input_output_aliases={1: len(momenta), 2: len(momenta) + 1},
+        scratch_shapes=[
+            pltpu.VMEM((blocks, ROW_BLOCK, ROW_BLOCK), F32),
+            pltpu.SemaphoreType.DMA((blocks,)),
+        ],
         compiler_params=pltpu.CompilerParams(vmem_limit_bytes=VMEM_LIMIT),
         name="muon_gram",
     )(spots, *base, *[group[0] for group in groups], *momenta)
@@ -758,15 +761,14 @@
     )(*parts)
 
 
-def muon_apply_kernel(rates, spread, spots_ref, *refs):
+def muon_apply_kernel(rates, placed, spots_ref, *refs):
     count = len(rates)
     parts, momenta, masters = refs[:4], refs[4 : 4 + count], refs[4 + count : 4 + 2 * count]
     outs, factors = refs[4 + 2 * count : 4 + 3 * count], refs[4 + 3 * count]
     for n in range(4):
         factors[n] = parts[n][...]
     zs = factors.shape[1]
-    spots = block_spots([momentum.shape[1] // ROW_BLOCK for momentum in momenta], spread)
-    for matrix, block, z, x, core, place_in in spots:
+    for matrix, block, z, x, core, place_in in placed:
         part = slice(block * ROW_BLOCK, (block + 1) * ROW_BLOCK)
         away = 2 * lax.rem(spots_ref[2] + core, 2) + lax.rem(spots_ref[1] + x, 2)
         factor = factors[away, lax.rem(zs + z - spots_ref[0], zs), place_in]
@@ -774,10 +776,10 @@
         outs[matrix][:, part] = masters[matrix][:, part] * (1.0 - WEIGHT_SHRINK) - rates[matrix] * direction
 
 
-def muon_apply(spots, factors, momenta, masters, rates, spread):
+def muon_apply(spots, factors, momenta, masters, rates, placed):
     vmem = pl.BlockSpec(memory_space=pltpu.VMEM)
     return pl.pallas_call(
-        functools.partial(muon_apply_kernel, rates, spread),
+        functools.partial(muon_apply_kernel, rates, placed),
         out_shape=[jax.ShapeDtypeStruct(master.shape, F32) for master in masters],
         in_specs=[pl.BlockSpec(memory_space=pltpu.SMEM)] + [vmem] * (4 + 2 * len(masters)),
         out_specs=[vmem] * len(masters),
@@ -822,11 +824,9 @@
     partial = jnp.dot(tie(cond_all, *sent), low_ada, preferred_element_type=F32).reshape(dp, 1, count, ada_cols)
     partial = jnp.broadcast_to(partial, (dp, seq, count, ada_cols))
     received = net.to_all(partial)
-    sent = first.advance(partial)
-    sent = first.advance()
-    sent = first.advance()
-    arrived = sent[-1]
-    received, parcel = tie(received, arrived), tie(parcel, arrived)
+    first.advance(partial)
+    sent = first.advance(received)
+    received, parcel = tie(received, *sent), tie(parcel, *sent)
     received = jnp.sum(received, axis=1)
     bias_full = parcel[:, :, : biases.shape[0]].reshape(-1)
     b_ada, b_q, b_v, b_proj, b_fc1, b_fc2 = [bias_full[bounds[i] : bounds[i + 1]] for i in range(6)]
@@ -835,7 +835,7 @@
         modulation[:, None, :], 6, axis=-1
     )
     t_qkv, t_proj = first.finish(modulation)[0]
-    wires = net.y.gather(tie(net.wire([w_fc1]), token_pieces[0][-1], arrived))
+    wires = net.y.gather(tie(net.wire([w_fc1]), token_pieces[0][-1], *sent))
     wires = wires[:1] + [tie(wire, t_qkv) for wire in wires[1:]]
     t_fc1 = lax.all_gather(net.rows(wires), "dp", axis=0, tiled=True)
     for i in range(1, count):
@@ -855,12 +855,13 @@
             token_pieces[1:] = [each[:1] + [tie(a, mixed) for a in each[1:]] for each in token_pieces[1:]]
             last_piece = token_pieces[-1][-1] if count > 1 else mixed
             wires = net.y.gather(tie(net.wire([w_fc2]), last_piece))
-            t_fc2 = lax.all_gather(net.rows(wires), "dp", axis=0, tiled=True)
         normed_all.append(normed[:rows])
         inverse_all.append(inverse[:rows])
         attn_all.append(attn)
         attended_low.append(mixed[0])
         log_total.append(lse)
+    wires = wires[:1] + [tie(wire, keys[-1]) for wire in wires[1:]]
+    t_fc2 = lax.all_gather(net.rows(wires), "dp", axis=0, tiled=True)
     attended_low = jnp.stack(attended_low)
 
     inputs = own_tokens.astype(F32)
@@ -896,7 +897,15 @@
     grad_attended = dot(grad_branch_one, t_proj).astype(BF)
     term_fc1 = tie(term_fc1, sum_fc2, grad_attended)
     sum_fc1 = net.scatter(term_fc1)
-    grad_attended = tie(grad_attended, term_fc1)
+    term_proj = tie(outer(grad_branch_one, attended_low), term_fc1)
+    sum_proj = net.scatter(term_proj)
+    grad_attended = tie(grad_attended, term_proj)
+
+    def far_steps(dk, dv):
+        part = dot(dk[:, rows:], t_qkv[width : 2 * width]) + dot(dv[:, rows:], t_qkv[2 * width :])
+        part = part.astype(BF)[0]
+        blank = jnp.zeros((rows, width), BF)
+        return Staged(net.y.scatter_steps(lambda s: blank if s == 0 else part[(s - 1) * rows : s * rows]))
 
     grad_q, grad_k, grad_v, far_parts = [], [], [], []
     turned = [momentum.T for momentum in momenta]
@@ -910,33 +919,25 @@
         grad_q.append(dq)
         grad_k.append(dk)
         grad_v.append(dv)
-        far_part = (
-            dot(dk[:, rows:], t_qkv[width : 2 * width]) + dot(dv[:, rows:], t_qkv[2 * width :])
-        ).astype(BF)[0]
-        far_steps = Staged(
-            net.y.scatter_steps(
-                lambda s, p=far_part: (
-                    jnp.zeros((rows, width), BF) if s == 0 else p[(s - 1) * rows : s * rows]
-                )
-            )
-        )
-        sent = sent + far_steps.advance()
-        far_parts.append(far_steps)
-    unit_last = math.gcd(math.gcd(n_qkv, n_proj), 8)
+        if i + 1 < count:
+            far_parts.append(far_steps(dk, dv))
+            sent = sent + far_parts[-1].advance()
+    unit_last = math.gcd(n_qkv, 8)
     (term_last,) = shard_outer(
         net.spots(),
         [flat(each) for each in grad_q + grad_k + grad_v]
         + [attn[:rows] for attn in attn_all]
-        + attn_all
-        + [flat(grad_branch_one), flat(attended_low)],
-        [([n * count + i for i in range(count)], 0, width) for n in range(5)]
-        + [([5 * count], 0, width), ([5 * count + 1], 0, width)],
-        [(0, 3, n_qkv, 0), (1, 4, n_qkv, 0), (2, 4, n_qkv, 0), (5, 6, n_proj, n_qkv // unit_last)],
-        net.z.size, width, unit_last, (n_qkv + n_proj) // unit_last, sent, split=False,
+        + attn_all,
+        [([n * count + i for i in range(count)], 0, width) for n in range(5)],
+        [(0, 3, n_qkv, 0), (1, 4, n_qkv, 0), (2, 4, n_qkv, 0)],
+        net.z.size, width, unit_last, n_qkv // unit_last, sent, split=False,
     )
-    sum_last = net.scatter(term_last.reshape(dp * (n_qkv + n_proj), width))
-    halves = Staged(lockstep(*[net.halves_steps(tie(each, term_last)) for each in (sum_fc2, sum_fc1)]))
-    sent = halves.advance()
+    sum_last = net.scatter(term_last.reshape(dp * n_qkv, width))
+    grad_k[-1] = tie(grad_k[-1], term_last)
+    far_parts.append(far_steps(grad_k[-1], grad_v[-1]))
+    sent = far_parts[-1].advance()
+    halves = Staged(lockstep(*[net.halves_steps(tie(each, *sent)) for each in (sum_fc2, sum_fc1, sum_proj)]))
+    sent = sent + halves.advance()
     grad_q[0] = tie(grad_q[0], *sent)
     bias_q = sum(jnp.sum(each.astype(F32), axis=(0, 1)) for each in grad_q)
     bias_v = sum(jnp.sum(each.astype(F32), axis=(0, 1)) for each in grad_v)
@@ -952,7 +953,7 @@
     matrices = (w_qkv, w_proj, w_fc1, w_fc2, w_ada)
     per = -(-sum(matrix.shape[0] // ROW_BLOCK for matrix in matrices) // dp)
     spread_early = (per, 0)
-    early_blocks = (w_fc2.shape[0] + w_fc1.shape[0]) // ROW_BLOCK
+    early_blocks = (w_fc2.shape[0] + w_fc1.shape[0] + w_proj.shape[0]) // ROW_BLOCK
     spread_last = (per, -(-early_blocks // per))
     far_sum = jnp.stack([steps_of.finish() for steps_of in far_parts])
     grad_attn_in = own_part + far_sum
@@ -969,12 +970,7 @@
     sent = jnp.transpose(grad_mod_local.reshape(count, dp, 1, ada_cols), (1, 2, 0, 3))
     sent = jnp.broadcast_to(sent, (dp, seq, count, ada_cols))
     mod_parts = net.to_all(sent)
-    sums = halves.finish(sent)
-    blank = jnp.zeros((2, net.z.size, per, ROW_BLOCK, ROW_BLOCK), F32)
-    (next_fc2, next_fc1), *early = muon_gram(
-        net.spots(), [(sums[0], [turned[3]]), (sums[1], [turned[2]])], spread_early, (blank, blank)
-    )
-    mod_parts = tie(mod_parts, early[0])
+    mod_parts = tie(mod_parts, sent)
     mod_cols = jnp.sum(mod_parts, axis=1).astype(BF).reshape(dp * count, ada_cols)
     shard_ada = jnp.einsum("sr,sc->cr", cond_all, mod_cols, preferred_element_type=F32)
 
@@ -984,11 +980,19 @@
     parcel = jnp.concatenate([term_bias.reshape(dp, seq, -1), cond_part], axis=-1)
     got_parcel = net.to_all(parcel)
 
-    halves = Staged(net.halves_steps(tie(sum_last, parcel)))
+    sums = halves.finish(parcel)
+    blank = jnp.zeros((2, net.z.size, per, ROW_BLOCK, ROW_BLOCK), F32)
+    (next_fc2, next_fc1, next_proj), *early = muon_gram(
+        net.spots(),
+        [(sums[0], [turned[3]]), (sums[1], [turned[2]]), (sums[2], [turned[1]])],
+        spread_early, (blank, blank),
+    )
+    got_parcel = tie(got_parcel, early[0])
+    halves = Staged(net.halves_steps(tie(sum_last, got_parcel)))
     sent = halves.advance()
     total = halves.finish(shard_ada)
-    (next_qkv, next_proj, next_ada), *grams = muon_gram(
-        net.spots(), [(total, [turned[0], turned[1]]), (shard_ada, [turned[4]])], spread_last, early
+    (next_qkv, next_ada), *grams = muon_gram(
+        net.spots(), [(total, [turned[0]]), (shard_ada, [turned[4]])], spread_last, early
     )
     grams = Staged(net.gram_steps(*grams))
     sent = grams.advance()
@@ -999,13 +1003,13 @@
     sent = gathered.advance()
     while not gathered.done:
         sent = gathered.advance(sent[0])
-    new_fc2, new_fc1 = muon_apply(
-        net.spots(), gathered.result, [next_fc2, next_fc1], [w_fc2.T, w_fc1.T],
-        [math.sqrt(width / hidden), math.sqrt(hidden / width)], spread_early,
-    )
-    new_qkv, new_proj, new_ada = muon_apply(
-        net.spots(), gathered.result, [next_qkv, next_proj, next_ada], [w_qkv.T, w_proj.T, w_ada.T],
-        [math.sqrt(3.0), 1.0, math.sqrt(6.0)], spread_last,
+    momenta_in = [next_fc2, next_fc1, next_proj, next_qkv, next_ada]
+    heights_of = [momentum.shape[1] // ROW_BLOCK for momentum in momenta_in]
+    placed = block_spots(heights_of[:3], spread_early)
+    placed += [(3 + spot[0],) + spot[1:] for spot in block_spots(heights_of[3:], spread_last)]
+    new_fc2, new_fc1, new_proj, new_qkv, new_ada = muon_apply(
+        net.spots(), gathered.result, momenta_in, [w.T for w in (w_fc2, w_fc1, w_proj, w_qkv, w_ada)],
+        [math.sqrt(width / hidden), math.sqrt(hidden / width), 1.0, math.sqrt(3.0), math.sqrt(6.0)], placed,
     )
 
     size = biases.shape[0]

time: 884 us -> 902 us (1.020)
  waiting for transfers between devices: 137 us -> 196 us
  blocking collectives: 30.6 us -> 0 us
  Pallas kernels: 248 us -> 223 us
    unnamed x5 -> x8, waiting for transfers between devices: 0.08 us -> 41.8 us
    all_to_all x1 -> x0, blocking collectives: 30.6 us -> none  [to_all(): lax.all_to_all(flat, ('dp', 'seq'), 0, 0, tiled=True).reshape(value.shape)]
    pallas_call x2, Pallas kernels: 30.6 us -> 13.5 us  [muon_gram(): pl.pallas_call(functools.partial(muon_gram_kernel, [len(each) for _, each...]
    ppermute x35 -> x36, waiting for transfers between devices: 94.9 us -> 110 us  [send(): return lax.ppermute(value, self.name, pairs)]
    ppermute x35 -> x36, starting transfers between devices: 46.3 us -> 36.7 us  [send(): return lax.ppermute(value, self.name, pairs)]
    reduce_scatter x3 -> x2, waiting for transfers between devices: 20.5 us -> 28.9 us  [scatter(): return lax.psum_scatter(term, 'dp', scatter_dimension=0, tiled=True)]
    all_to_all x3 -> x4, waiting for transfers between devices: 21.7 us -> 14.5 us  [to_all(): lax.all_to_all(flat, ('dp', 'seq'), 0, 0, tiled=True).reshape(value.shape)]
    unnamed x232 -> x223, local copies, waits for them, and re-layouts: 37.7 us -> 32.4 us
  transfers between devices with their start and end apart: 43 -> 46, of which waited for: 17 -> 19; matrix products, arithmetic and copies ran while one was open for 38% -> 40% of each run, Pallas kernels for 24% -> 22%
where the time goes in v8:
time: 902 us; the launch traced here: 890 us
  matrix products  230 us (25%)
  Pallas kernels  223 us (25%)
  waiting for transfers between devices  196 us (22%)
  local copies, waits for them, and re-layouts  93.3 us (10%)
  other arithmetic  73.1 us (8%)
  starting transfers between devices  58.7 us (7%)
  between operations  15.8 us (2%)
    ppermute x36, waiting for transfers between devices, send(): return lax.ppermute(value, self.name, pairs)  110 us
    dot_general x9, matrix products, dot_t(): return jnp.einsum('srk,nk->srn', left, right, preferred_element_type=F32)  96.1 us
    dot_general x13, matrix products, dot(): return jnp.einsum('srn,nk->srk', left, right, preferred_element_type=F32)  91.1 us
    pallas_call x2, Pallas kernels, attend_back(): pl.pallas_call(without(attend_back_kernel, 8, len(deps), heads, tile), gr...  90.3 us
    pallas_call x2, Pallas kernels, attend(): pl.pallas_call(without(attend_kernel, 5, len(deps), heads, tile), grid_sp...  64.6 us
    unnamed x8, waiting for transfers between devices  41.8 us
    dot_general x3, matrix products, outer(): jnp.einsum('srn,srk->nk', left, right, preferred_element_type=F32)  40.7 us
    ppermute x36, starting transfers between devices, send(): return lax.ppermute(value, self.name, pairs)  36.7 us
  transfers between devices with their start and end apart: 46, of which 19 were waited for; matrix products, arithmetic and copies ran while one was open for 40% of the time, Pallas kernels for 22%

profile of v8, /device:TPU:11, one launch (start us, length us, event | category | flops | bytes accessed | tf_op | source)
XLA Modules:
  0.0 889.7 jit_solution(2480043650104595771)
XLA Ops:
  23.0 11.0 %all-to-all-done = f32[32,1,1656]{2,1,0:T(1,128)S(1)} async-done(((f32[32,1,1656]{2,1,0:T(1,128)}), f32[32,1,1656]{2,1,0:T(1,128)S(1)}, u32[]{:S(2)}, u32[]{:S(2)}) %all-to-all-start) | async-done | bytes 212000 | tf_op jit(solution)/shard_map/all_to_all | solution.py:319
  55.1 13.5 %collective-permute-done.3.refs_0_ = bf16[16,8,1152]{2,1,0:T(8,128)(2,1)S(1)} collective-permute-done((bf16[16,8,1152]{2,1,0:T(8,128)(2,1)}, bf16[16,8,1152]{2,1,0:T(8,128)(2,1)S(1)}, u32[]{:S(2)}, u32[]{:S(2)}) %collective-permute-start.3) | collective-permute-done | bytes 294944 | tf_op jit(solution)/shard_map/ppermute | solution.py:47
  76.7 8.2 collective-permute-done.9.refs_0_
  109.3 9.1 %place.1 = (bf16[4,2,2,27,8,1152]{5,4,3,2,1,0:T(8,128)(2,1)}, bf16[4,2,2,9,8,1152]{5,4,3,2,1,0:T(8,128)(2,1)}) custom-call(s32[3]{0:T(128)} %pad_add_fusion.1.refs_0_.spots_ref, bf16[4,16,8,1152]{3,2,1,0:T(8,128)(2,1)} %copy-done.3, bf16[4,16,8,1152]{3,2,1,0:T(8,128)(2,1)} %tie.65.refs_2_, bf16[2,20,8,1152]{3,2,1,0:T(8,128)(2,1)} %pad_maximum_fusion.5.refs_3_, ...), custom_call_target="tpu_custom_call" | custom-call | bytes 21233664 | tf_op jit(solution)/shard_map/place/pallas_call | solution.py:198
  151.9 32.2 %attend.2 = (bf16[1,512,1152]{2,1,0:T(8,128)(2,1)}, f32[1,16,1,512]{3,2,1,0:T(1,128)}) custom-call(s32[1]{0:T(128)} %bitcast.17.refs_0_, s32[2]{0:T(128)} %pad_add_fusion.refs_1_, bf16[1,512,1152]{2,1,0:T(8,128)(2,1)} %fusion.39.refs_2_, bf16[1,1024,1152]{2,1,0:T(8,128)(2,1)} %fusion.32.refs_3_, bf16[1,1024,1152]{2,1,0:T(8,128)(2,1)} %fusion.30.refs_4_), custom_call_target="tpu_custom_call" | custom-call | flops 4294967296 | bytes 7077888 | tf_op jit(solution)/shard_map/attend/pallas_call | solution.py:543
  219.7 32.5 %attend.3 = (bf16[1,512,1152]{2,1,0:T(8,128)(2,1)}, f32[1,16,1,512]{3,2,1,0:T(1,128)}) custom-call(s32[1]{0:T(128)} %bitcast.28.refs_0_, s32[2]{0:T(128)} %pad_add_fusion.refs_1_, bf16[1,512,1152]{2,1,0:T(8,128)(2,1)} %fusion.38.refs_2_, bf16[1,1024,1152]{2,1,0:T(8,128)(2,1)} %fusion.33.refs_3_.refs_1_, bf16[1,1024,1152]{2,1,0:T(8,128)(2,1)} %fusion.31.refs_4_), custom_call_target="tpu_custom_call" | custom-call | flops 4294967296 | bytes 7077888 | tf_op jit(solution)/shard_map/attend/pallas_call | solution.py:543
  254.7 8.9 %fusion.97 = (f32[2,512]{1,0:T(2,128)S(1)}, f32[2,512,1152]{2,1,0:T(8,128)S(1)}, f32[2,512,1152]{2,1,0:T(8,128)}) fusion(f32[2,1152]{1,0:T(2,128)S(1)} %get-tuple-element.208, bf16[2,1,512,1152]{3,2,1,0:T(8,128)(2,1)} %param.18, f32[1152]{0:T(1024)S(1)} %copy-done.87, bf16[2,512,1152]{2,1,0:T(8,128)(2,1)} %constant_dynamic-update-slice_fusion, ...), kind=kOutput, calls=%fused_computation.244 | convolution fusion | flops 2723806208 | bytes 16827904 | tf_op jit(solution)/shard_map/srk,nk->srn/dot_general | solution.py:346
  266.7 25.8 %multiply_convert_fusion = (bf16[2,512,4608]{2,1,0:T(8,128)(2,1)}, f32[2,512,4608]{2,1,0:T(8,128)}) fusion(f32[4608]{0:T(1024)S(1)} %copy-done.78, bf16[4608,1152]{1,0:T(8,128)(2,1)} %all-gather.3.cloned.1.call-done, f32[2,512,1152]{2,1,0:T(8,128)} %copy-done.27, f32[2,1152]{1,0:T(2,128)S(1)} %copy-done.81, f32[2,1152]{1,0:T(2,128)S(1)} %get-tuple-element.207, ...), kind=kOutput, calls=%fused_computation.14 | convolution fusion | flops 10924720128 | bytes 43692032 | tf_op jit(solution)/shard_map/srk,nk->srn/dot_general | solution.py:346
  292.4 17.2 %fusion.refs_1_ = bf16[1152,4608]{1,0:T(8,128)(2,1)} fusion(bf16[2,512,1152]{2,1,0:T(8,128)(2,1)S(1)} %fusion.26.refs_0_, bf16[2,512,4608]{2,1,0:T(8,128)(2,1)} %get-tuple-element.212.refs_0_), kind=kOutput, calls=%fused_computation.4 | convolution fusion | flops 10876944384 | bytes 22413312 | tf_op jit(solution)/shard_map/srn,srk->nk/dot_general | solution.py:354
  309.8 27.1 %fusion.8.refs_0_ = bf16[2,512,4608]{2,1,0:T(8,128)(2,1)S(1)} fusion(f32[2,512,4608]{2,1,0:T(8,128)} %get-tuple-element.213, bf16[2,512,1152]{2,1,0:T(8,128)(2,1)} %tie.81, bf16[1152,4608]{1,0:T(8,128)(2,1)} %all-gather.5.cloned.1.call-done, f32[4608]{0:T(1024)S(1)} %copy-done.78), kind=kOutput, calls=%fused_computation.12 | convolution fusion | flops 10970726400 | bytes 41306112 | tf_op jit(solution)/shard_map/srn,nk->srk/dot_general | solution.py:350
  340.5 16.1 %fusion.1.refs_1_.refs_0_ = bf16[4608,1152]{1,0:T(8,128)(2,1)} fusion(bf16[2,512,4608]{2,1,0:T(8,128)(2,1)S(1)} %fusion.8.refs_0_, f32[2,512,1152]{2,1,0:T(8,128)S(1)} %bitcast.292, f32[2,1152]{1,0:T(2,128)S(1)} %copy-done.81, f32[2,1152]{1,0:T(2,128)S(1)} %get-tuple-element.207, f32[2,512]{1,0:T(2,128)S(1)} %add_rsqrt_fusion, ...), kind=kOutput, calls=%fused_computation.5 | convolution fusion | flops 10882842624 | bytes 24799232 | tf_op jit(solution)/shard_map/srn,srk->nk/dot_general | solution.py:354
  356.7 21.6 %multiply_reduce_fusion = (f32[2,1152]{1,0:T(2,128)}, f32[2,512]{1,0:T(2,128)S(1)}, f32[2,512]{1,0:T(2,128)S(1)}, f32[2,1152]{1,0:T(2,128)}, f32[2,512,1152]{2,1,0:T(8,128)}) fusion(f32[2,512,1152]{2,1,0:T(8,128)} %copy-done.27, f32[2,512]{1,0:T(2,128)S(1)} %add_rsqrt_fusion, f32[2,512]{1,0:T(2,128)S(1)} %broadcast_multiply_fusion.4, ...), kind=kOutput, calls=%fused_computation.47 | convolution fusion | flops 10882246656 | bytes 29535232 | tf_op jit(solution)/shard_map/srn,nk->srk/dot_general | solution.py:350
  378.3 24.5 %fusion.27 = (f32[2,1152]{1,0:T(2,128)}, bf16[2,1,512,1152]{3,2,1,0:T(8,128)(2,1)}, f32[1152]{0:T(1024)}, bf16[2,512,1152]{2,1,0:T(8,128)(2,1)}, f32[2,512,1152]{2,1,0:T(8,128)}) fusion(bf16[2,1,512,1152]{3,2,1,0:T(8,128)(2,1)S(1)} %copy-done.47, f32[2,512,1152]{2,1,0:T(8,128)} %copy-done.27, f32[2,1152]{1,0:T(2,128)S(1)} %copy-done.75, ...), kind=kOutput, calls=%fused_computation.39 | convolution fusion | flops 10894046208 | bytes 41350144 | tf_op jit(solution)/shard_map/srk,nk->srn/dot_general | solution.py:346
  414.8 16.9 %reduce-scatter.9.cloned.1.call-done.refs_1_.refs_0_ = bf16[72,4608]{1,0:T(8,128)(2,1)} async-done(((bf16[1152,4608]{1,0:T(8,128)(2,1)}), bf16[72,4608]{1,0:T(8,128)(2,1)}) %reduce-scatter.9.cloned.1.call-update) | async-done | bytes 663568 | tf_op jit(solution)/shard_map/reduce_scatter | solution.py:249
  445.2 45.2 %attend_back.2 = (bf16[1,512,1152]{2,1,0:T(8,128)(2,1)}, bf16[1,1024,1152]{2,1,0:T(8,128)(2,1)}, bf16[1,1024,1152]{2,1,0:T(8,128)(2,1)}) custom-call(s32[1]{0:T(128)} %bitcast.17.refs_0_, s32[2]{0:T(128)} %pad_add_fusion.refs_1_, bf16[1,512,1152]{2,1,0:T(8,128)(2,1)} %fusion.39.refs_2_, bf16[1,1024,1152]{2,1,0:T(8,128)(2,1)} %fusion.32.refs_3_, ...), custom_call_target="tpu_custom_call" | custom-call | flops 10737418240 | bytes 14155776 | tf_op jit(solution)/shard_map/attend_back/pallas_call | solution.py:628
  499.3 45.0 %attend_back.3 = (bf16[1,512,1152]{2,1,0:T(8,128)(2,1)}, bf16[1,1024,1152]{2,1,0:T(8,128)(2,1)}, bf16[1,1024,1152]{2,1,0:T(8,128)(2,1)}) custom-call(s32[1]{0:T(128)} %bitcast.28.refs_0_, s32[2]{0:T(128)} %pad_add_fusion.refs_1_, bf16[1,512,1152]{2,1,0:T(8,128)(2,1)} %fusion.38.refs_2_, bf16[1,1024,1152]{2,1,0:T(8,128)(2,1)} %fusion.33.refs_3_.refs_1_, ...), custom_call_target="tpu_custom_call" | custom-call | flops 10737418240 | bytes 14155776 | tf_op jit(solution)/shard_map/attend_back/pallas_call | solution.py:628
  544.3 25.2 %shard_outer.1.refs_1_ = bf16[4,2,2,27,8,1152]{5,4,3,2,1,0:T(8,128)(2,1)} custom-call(s32[3]{0:T(128)} %pad_add_fusion.1.refs_0_.spots_ref, bf16[512,1152]{1,0:T(8,128)(2,1)} %bitcast.286, bf16[512,1152]{1,0:T(8,128)(2,1)} %bitcast.311, bf16[1024,1152]{1,0:T(8,128)(2,1)} %bitcast.336, bf16[1024,1152]{1,0:T(8,128)(2,1)} %bitcast.301, ...), custom_call_target="tpu_custom_call" | custom-call | flops 13589544960 | bytes 7962624 | tf_op jit(solution)/shard_map/shard_outer/pallas_call | solution.py:444
  610.6 12.1 %reduce-scatter.11.cloned.1.call-done.refs_0_ = bf16[288,1152]{1,0:T(8,128)(2,1)} async-done(((bf16[4608,1152]{1,0:T(8,128)(2,1)}), bf16[288,1152]{1,0:T(8,128)(2,1)}) %reduce-scatter.11.cloned.1.call-update) | async-done | bytes 663568 | tf_op jit(solution)/shard_map/reduce_scatter | solution.py:249
  695.4 41.1 %reduce-scatter.15.cloned.1.call-done.refs_0_ = bf16[216,1152]{1,0:T(8,128)(2,1)} async-done(((bf16[3456,1152]{1,0:T(8,128)(2,1)}), bf16[216,1152]{1,0:T(8,128)(2,1)}) %reduce-scatter.15.cloned.1.call-update) | async-done | bytes 497680
  765.4 14.3 %collective-permute-done.26.refs_0_ = bf16[4,2,144,144]{3,2,1,0:T(8,128)(2,1)S(1)} collective-permute-done((bf16[4,2,144,144]{3,2,1,0:T(8,128)(2,1)S(1)}, bf16[4,2,144,144]{3,2,1,0:T(8,128)(2,1)S(1)}, u32[]{:S(2)}, u32[]{:S(2)}) %collective-permute-start.26) | collective-permute-done | bytes 331808 | tf_op jit(solution)/shard_map/ppermute | solution.py:47
  798.1 8.0 polynomial.1.refs_1_
  816.2 11.1 %collective-permute-done.31.refs_0_ = f32[2,144,144]{2,1,0:T(8,128)S(1)} collective-permute-done((f32[2,144,144]{2,1,0:T(8,128)}, f32[2,144,144]{2,1,0:T(8,128)S(1)}, u32[]{:S(2)}, u32[]{:S(2)}) %collective-permute-start.31) | collective-permute-done | bytes 165920 | tf_op jit(solution)/shard_map/ppermute | solution.py:47
  837.9 24.9 %collective-permute-done.33.refs_0_ = f32[4,2,144,144]{3,2,1,0:T(8,128)S(1)} collective-permute-done((f32[4,2,144,144]{3,2,1,0:T(8,128)S(1)}, f32[4,2,144,144]{3,2,1,0:T(8,128)S(1)}, u32[]{:S(2)}, u32[]{:S(2)}) %collective-permute-start.33) | collective-permute-done | bytes 663584 | tf_op jit(solution)/shard_map/ppermute | solution.py:47
  870.7 11.9 %muon_apply.1 = (f32[72,2304]{1,0:T(8,128)}, f32[288,576]{1,0:T(8,128)}, f32[72,576]{1,0:T(8,128)}, f32[216,576]{1,0:T(8,128)}, f32[432,576]{1,0:T(8,128)}) custom-call(s32[3]{0:T(128)} %pad_add_fusion.1.refs_0_.spots_ref, f32[4,2,144,144]{3,2,1,0:T(8,128)} %copy-done.2, f32[4,2,144,144]{3,2,1,0:T(8,128)} %tie.107.refs_1_, f32[4,2,144,144]{3,2,1,0:T(8,128)} %tie.108.refs_2_, ...), custom_call_target="tpu_custom_call" | custom-call | tf_op jit(solution)/shard_map/muon_apply/pallas_call | solution.py:781
  (521 shorter events, 370.6 us)
Async XLA Ops:
  22.3 31.2 %collective-permute-start.1 = (bf16[16,8,1152]{2,1,0:T(8,128)(2,1)S(1)}, bf16[16,8,1152]{2,1,0:T(8,128)(2,1)}, u32[]{:S(2)}, u32[]{:S(2)}) collective-permute-start(bf16[16,8,1152]{2,1,0:T(8,128)(2,1)S(1)} %get-tuple-element.192.refs_1_.refs_2_), channel_id=1, source_target_pairs={{0,24},{2,26},{4,28},{6,30},{8,0},{10,2},{12,4},{14,6},{16,8},{18,... | collective-permute-start | bytes 884744 | tf_op jit(solution)/shard_map/ppermute | solution.py:47
  43.6 223.0 %all-gather.3.cloned.1.call-start = ((), (), s32[]{:S(2)}) async-start(), calls=%async_computation.8 | async-start | bytes 11280384 | tf_op jit(solution)/shard_map/all_gather | solution.py:840
  43.7 24.9 %collective-permute-start.3 = (bf16[16,8,1152]{2,1,0:T(8,128)(2,1)}, bf16[16,8,1152]{2,1,0:T(8,128)(2,1)S(1)}, u32[]{:S(2)}, u32[]{:S(2)}) collective-permute-start(bf16[16,8,1152]{2,1,0:T(8,128)(2,1)} %tie.58), channel_id=1, source_target_pairs={{0,8},{2,10},{4,12},{6,14},{8,16},{10,18},{12,20},{14,22},{16,24},... | collective-permute-start | bytes 884744 | tf_op jit(solution)/shard_map/ppermute | solution.py:47
  47.6 24.2 %collective-permute-start.5 = (bf16[2,20,8,1152]{3,2,1,0:T(8,128)(2,1)}, bf16[2,20,8,1152]{3,2,1,0:T(8,128)(2,1)}, u32[]{:S(2)}, u32[]{:S(2)}) collective-permute-start(bf16[2,20,8,1152]{3,2,1,0:T(8,128)(2,1)} %pad_maximum_fusion.5.refs_3_), channel_id=1, source_target_pairs={{0,24},{2,26},{4,28},{6,30},{8,0},{10,2},{12,4},{14,6},{16,8},{18,... | collective-permute-start | bytes 2211848 | tf_op jit(solution)/shard_map/ppermute | solution.py:47
  47.8 37.1 %collective-permute-start.9 = (bf16[2,20,8,1152]{3,2,1,0:T(8,128)(2,1)}, bf16[2,20,8,1152]{3,2,1,0:T(8,128)(2,1)}, u32[]{:S(2)}, u32[]{:S(2)}) collective-permute-start(bf16[2,20,8,1152]{3,2,1,0:T(8,128)(2,1)} %pad_maximum_fusion.5.refs_3_), channel_id=1, source_target_pairs={{0,8},{2,10},{4,12},{6,14},{8,16},{10,18},{12,20},{14,22},{16,24},... | collective-permute-start | bytes 2211848 | tf_op jit(solution)/shard_map/ppermute | solution.py:47
  52.4 52.6 %collective-permute-start.6 = (bf16[512,1152]{1,0:T(8,128)(2,1)}, bf16[512,1152]{1,0:T(8,128)(2,1)S(1)}, u32[]{:S(2)}, u32[]{:S(2)}) collective-permute-start(bf16[512,1152]{1,0:T(8,128)(2,1)} %tie.64), channel_id=1, source_target_pairs={{0,1},{1,0},{2,3},{3,2},{4,5},{5,4},{6,7},{7,6},{8,9},{9,8},{10,11... | collective-permute-start | bytes 3538952 | tf_op jit(solution)/shard_map/ppermute | solution.py:47
  53.6 51.4 %collective-permute-start.12 = (bf16[2,20,8,1152]{3,2,1,0:T(8,128)(2,1)}, bf16[2,20,8,1152]{3,2,1,0:T(8,128)(2,1)}, u32[]{:S(2)}, u32[]{:S(2)}) collective-permute-start(bf16[2,20,8,1152]{3,2,1,0:T(8,128)(2,1)} %pad_maximum_fusion.5.refs_3_), channel_id=1, source_target_pairs={{0,2},{2,0},{4,6},{6,4},{8,10},{10,8},{12,14},{14,12},{16,18},{18,... | collective-permute-start | bytes 2211848 | tf_op jit(solution)/shard_map/ppermute | solution.py:47
  70.6 26.5 %collective-permute-start.7 = (bf16[4,16,8,1152]{3,2,1,0:T(8,128)(2,1)S(1)}, bf16[4,16,8,1152]{3,2,1,0:T(8,128)(2,1)}, u32[]{:S(2)}, u32[]{:S(2)}) collective-permute-start(bf16[4,16,8,1152]{3,2,1,0:T(8,128)(2,1)S(1)} %pad_maximum_fusion.3.refs_1_.refs_2_), channel_id=1, source_target_pairs={{0,4},{2,6},{4,0},{6,2},{8,12},{10,14},{12,8},{14,10},{16,20},{18,... | collective-permute-start | bytes 3538952 | tf_op jit(solution)/shard_map/ppermute | solution.py:47
  71.8 35.6 %collective-permute-start.10 = (bf16[4,16,8,1152]{3,2,1,0:T(8,128)(2,1)S(1)}, bf16[4,16,8,1152]{3,2,1,0:T(8,128)(2,1)S(1)}, u32[]{:S(2)}, u32[]{:S(2)}) collective-permute-start(bf16[4,16,8,1152]{3,2,1,0:T(8,128)(2,1)S(1)} %pad_maximum_fusion.3.refs_1_.refs_2_), channel_id=1, source_target_pairs={{0,2},{2,0},{4,6},{6,4},{8,10},{10,8},{12,14},{14,12},{16,18},{18,... | collective-permute-start | bytes 3538952 | tf_op jit(solution)/shard_map/ppermute | solution.py:47
  122.7 187.1 %all-gather.5.cloned.1.call-start = ((), (), s32[]{:S(2)}) async-start(), calls=%async_computation.9 | async-start | bytes 11280384 | tf_op jit(solution)/shard_map/all_gather | solution.py:864
  132.4 51.7 %collective-permute-start.17 = (bf16[512,1152]{1,0:T(8,128)(2,1)}, bf16[512,1152]{1,0:T(8,128)(2,1)S(1)}, u32[]{:S(2)}, u32[]{:S(2)}) collective-permute-start(bf16[512,1152]{1,0:T(8,128)(2,1)} %tie.76), channel_id=1, source_target_pairs={{0,1},{1,0},{2,3},{3,2},{4,5},{5,4},{6,7},{7,6},{8,9},{9,8},{10,11... | collective-permute-start | bytes 3538952 | tf_op jit(solution)/shard_map/ppermute | solution.py:47
  202.2 229.4 %reduce-scatter.9.cloned.1.call-start = ((), (), s32[]{:S(2)}) async-start(), calls=%async_computation.10 | async-start | bytes 11280384 | tf_op jit(solution)/shard_map/reduce_scatter | solution.py:249
  309.7 295.5 %reduce-scatter.13.cloned.1.call-start = ((), (), s32[]{:S(2)}) async-start(), calls=%async_computation.12 | async-start | bytes 2820096
  431.7 191.0 %reduce-scatter.11.cloned.1.call-start = ((), (), s32[]{:S(2)}) async-start(), calls=%async_computation.11 | async-start | bytes 11280384 | tf_op jit(solution)/shard_map/reduce_scatter | solution.py:249
  432.3 304.3 %reduce-scatter.15.cloned.1.call-start = ((), (), s32[]{:S(2)}) async-start(), calls=%async_computation.13 | async-start | bytes 8460288
  575.3 68.8 %collective-permute-start.19 = (bf16[512,1152]{1,0:T(8,128)(2,1)}, bf16[512,1152]{1,0:T(8,128)(2,1)}, u32[]{:S(2)}, u32[]{:S(2)}) collective-permute-start(bf16[512,1152]{1,0:T(8,128)(2,1)} %fusion.36.refs_8_), channel_id=1, source_target_pairs={{0,1},{1,0},{2,3},{3,2},{4,5},{5,4},{6,7},{7,6},{8,9},{9,8},{10,11... | collective-permute-start | bytes 3538952 | tf_op jit(solution)/shard_map/ppermute | solution.py:47
  584.3 59.8 %collective-permute-start.20 = (bf16[512,1152]{1,0:T(8,128)(2,1)S(1)}, bf16[512,1152]{1,0:T(8,128)(2,1)}, u32[]{:S(2)}, u32[]{:S(2)}) collective-permute-start(bf16[512,1152]{1,0:T(8,128)(2,1)S(1)} %fusion.37.refs_1_), channel_id=1, source_target_pairs={{0,1},{1,0},{2,3},{3,2},{4,5},{5,4},{6,7},{7,6},{8,9},{9,8},{10,11... | collective-permute-start | bytes 3538952 | tf_op jit(solution)/shard_map/ppermute | solution.py:47
  592.7 85.2 %collective-permute-start.21 = (bf16[72,2304]{1,0:T(8,128)(2,1)}, bf16[72,2304]{1,0:T(8,128)(2,1)}, u32[]{:S(2)}, u32[]{:S(2)}) collective-permute-start(bf16[72,2304]{1,0:T(8,128)(2,1)} %bitcast.261.refs_2_), channel_id=1, source_target_pairs={{0,1},{1,0},{2,3},{3,2},{4,5},{5,4},{6,7},{7,6},{8,9},{9,8},{10,11... | collective-permute-start | bytes 995336 | tf_op jit(solution)/shard_map/ppermute | solution.py:47
  609.7 70.1 %collective-permute-start.23 = (bf16[72,576]{1,0:T(8,128)(2,1)}, bf16[72,576]{1,0:T(8,128)(2,1)}, u32[]{:S(2)}, u32[]{:S(2)}) collective-permute-start(bf16[72,576]{1,0:T(8,128)(2,1)} %bitcast.263.refs_4_), channel_id=1, source_target_pairs={{0,1},{1,0},{2,3},{3,2},{4,5},{5,4},{6,7},{7,6},{8,9},{9,8},{10,11... | collective-permute-start | bytes 248840 | tf_op jit(solution)/shard_map/ppermute | solution.py:47
  630.5 50.9 %collective-permute-start.22 = (bf16[288,576]{1,0:T(8,128)(2,1)}, bf16[288,576]{1,0:T(8,128)(2,1)}, u32[]{:S(2)}, u32[]{:S(2)}) collective-permute-start(bf16[288,576]{1,0:T(8,128)(2,1)} %bitcast.304), channel_id=1, source_target_pairs={{0,1},{1,0},{2,3},{3,2},{4,5},{5,4},{6,7},{7,6},{8,9},{9,8},{10,11... | collective-permute-start | bytes 995336 | tf_op jit(solution)/shard_map/ppermute | solution.py:47
  670.4 23.7 %all-to-all-start.3 = ((f32[32,1,1656]{2,1,0:T(1,128)}), f32[32,1,1656]{2,1,0:T(1,128)S(1)}, u32[]{:S(2)}, u32[]{:S(2)}) async-start(f32[32,1,1656]{2,1,0:T(1,128)} %all_to_all.22), calls=%async_computation.5 | async-start | bytes 425984 | tf_op jit(solution)/shard_map/all_to_all | solution.py:319
  809.5 24.2 %collective-permute-start.32 = (f32[2,144,144]{2,1,0:T(8,128)}, f32[2,144,144]{2,1,0:T(8,128)S(1)}, u32[]{:S(2)}, u32[]{:S(2)}) collective-permute-start(f32[2,144,144]{2,1,0:T(8,128)} %polynomial.1.refs_1_), channel_id=1, source_target_pairs={{0,8},{2,10},{4,12},{6,14},{8,16},{10,18},{12,20},{14,22},{16,24},... | collective-permute-start | bytes 497672 | tf_op jit(solution)/shard_map/ppermute | solution.py:47
  835.6 27.1 %collective-permute-start.33 = (f32[4,2,144,144]{3,2,1,0:T(8,128)S(1)}, f32[4,2,144,144]{3,2,1,0:T(8,128)S(1)}, u32[]{:S(2)}, u32[]{:S(2)}) collective-permute-start(f32[4,2,144,144]{3,2,1,0:T(8,128)S(1)} %pad_maximum_fusion.4.refs_1_.refs_0_), channel_id=1, source_target_pairs={{0,4},{2,6},{4,0},{6,2},{8,12},{10,14},{12,8},{14,10},{16,20},{18,... | collective-permute-start | bytes 1990664 | tf_op jit(solution)/shard_map/ppermute | solution.py:47
  837.3 31.4 %collective-permute-start.34 = (f32[4,2,144,144]{3,2,1,0:T(8,128)S(1)}, f32[4,2,144,144]{3,2,1,0:T(8,128)S(1)}, u32[]{:S(2)}, u32[]{:S(2)}) collective-permute-start(f32[4,2,144,144]{3,2,1,0:T(8,128)S(1)} %pad_maximum_fusion.4.refs_1_.refs_0_), channel_id=1, source_target_pairs={{0,2},{2,0},{4,6},{6,4},{8,10},{10,8},{12,14},{14,12},{16,18},{18,... | collective-permute-start | bytes 1990664 | tf_op jit(solution)/shard_map/ppermute | solution.py:47
  (128 other events, 1161.3 us)
Sparse Core Ops, SparseCore 0:
  122.8 88.7 all-gather.2
  214.4 86.8 all-gather.4
  309.8 121.7 reduce-scatter.8
  435.4 61.6 reduce-scatter.12
  501.5 121.1 reduce-scatter.10
  627.2 109.2 reduce-scatter.14

commit v9 on v8

--- a/solution.py
+++ b/solution.py
@@ -338,16 +338,79 @@
     return values * jax.nn.sigmoid(values)
 
 
-def gelu_tanh(values):
-    return jax.nn.gelu(values, approximate=True)
-
-
 def dot_t(left, right):
     return jnp.einsum("srk,nk->srn", left, right, preferred_element_type=F32)
 
 
 def dot(left, right):
     return jnp.einsum("srn,nk->srk", left, right, preferred_element_type=F32)
+
+
+GELU_SCALE = math.sqrt(2.0 / math.pi)
+GELU_CUBE = 0.044715
+
+
+def hidden_kernel(x_ref, w_ref, b_ref, act_ref, slope_ref):
+    value = nt(x_ref[...], w_ref[...]) + b_ref[...]
+    square = value * value
+    bend = jnp.tanh(value * (GELU_SCALE + (GELU_SCALE * GELU_CUBE) * square))
+    half = 0.5 + 0.5 * bend
+    act_ref[...] = (value * half).astype(BF)
+    steep = (0.5 * value) * (GELU_SCALE + (3.0 * GELU_SCALE * GELU_CUBE) * square)
+    slope_ref[...] = (half + steep * (1.0 - bend * bend)).astype(BF)
+
+
+def hidden_forward(x, w, bias):
+    rows, depth = x.shape
+    n = w.shape[0]
+    tile = math.gcd(n, 512)
+    out = pl.BlockSpec((rows, tile), lambda i: (0, i))
+    return pl.pallas_call(
+        hidden_kernel,
+        grid=(n // tile,),
+        in_specs=[
+            pl.BlockSpec((rows, depth), lambda i: (0, 0)),
+            pl.BlockSpec((tile, depth), lambda i: (i, 0)),
+            pl.BlockSpec((1, tile), lambda i: (0, i)),
+        ],
+        out_specs=[out, out],
+        out_shape=[jax.ShapeDtypeStruct((rows, n), BF)] * 2,
+        compiler_params=pltpu.CompilerParams(vmem_limit_bytes=VMEM_LIMIT),
+        cost_estimate=pl.CostEstimate(
+            flops=2 * rows * n * depth, bytes_accessed=2 * (rows + n) * depth + 4 * rows * n, transcendentals=rows * n
+        ),
+        name="hidden_forward",
+    )(x, w, bias.reshape(1, n))
+
+
+def hidden_back_kernel(g_ref, w_ref, slope_ref, out_ref, bias_ref):
+    grad = (nn(g_ref[...], w_ref[...]) * slope_ref[...].astype(F32)).astype(BF)
+    out_ref[...] = grad
+    bias_ref[...] = jnp.sum(grad.astype(F32), axis=0, keepdims=True)
+
+
+def hidden_backward(grad, w, slope):
+    rows, depth = grad.shape
+    n = w.shape[1]
+    tile = math.gcd(n, 512)
+    out = pl.BlockSpec((rows, tile), lambda i: (0, i))
+    result, bias = pl.pallas_call(
+        hidden_back_kernel,
+        grid=(n // tile,),
+        in_specs=[
+            pl.BlockSpec((rows, depth), lambda i: (0, 0)),
+            pl.BlockSpec((depth, tile), lambda i: (0, i)),
+            out,
+        ],
+        out_specs=[out, pl.BlockSpec((1, tile), lambda i: (0, i))],
+        out_shape=[jax.ShapeDtypeStruct((rows, n), BF), jax.ShapeDtypeStruct((1, n), F32)],
+        compiler_params=pltpu.CompilerParams(vmem_limit_bytes=VMEM_LIMIT),
+        cost_estimate=pl.CostEstimate(
+            flops=2 * rows * n * depth, bytes_accessed=2 * (rows + n) * depth + 4 * rows * n, transcendentals=0
+        ),
+        name="hidden_backward",
+    )(grad, w, slope)
+    return result, bias[0]
 
 
 def outer(left, right):
@@ -529,7 +592,7 @@
         lse_ref[0, h] = peak * factor + jnp.log2(sums)
         return carry
 
-    lax.fori_loop(0, heads, one_head, 0)
+    lax.fori_loop(0, heads, one_head, 0, unroll=4)
     for h in range(heads):
         o_ref[0, :, h * depth : (h + 1) * depth] = o_s[h].astype(BF)
 
@@ -609,7 +672,7 @@
         dq_s[h] = jnp.transpose(dq * scale)
         return carry
 
-    lax.fori_loop(0, heads, one_head, 0)
+    lax.fori_loop(0, heads, one_head, 0, unroll=4)
     for h in range(heads):
         span = slice(h * depth, (h + 1) * depth)
         dq_ref[0, :, span] = dq_s[h].astype(BF)
@@ -671,6 +734,22 @@
     return spots
 
 
+EXTRA = ROW_BLOCK - 128
+PACKED = (ROW_BLOCK + EXTRA, 128)
+
+
+def packed(block):
+    corner = block[128:, 128:]
+    corner = jnp.concatenate([corner, jnp.zeros((EXTRA, 128 - EXTRA), block.dtype)], axis=1)
+    return jnp.concatenate([block[:, :128], corner], axis=0)
+
+
+def unpacked(block):
+    side = jnp.transpose(block[128:ROW_BLOCK])
+    right = jnp.concatenate([side, block[ROW_BLOCK:, :EXTRA]], axis=0)
+    return jnp.concatenate([block[:ROW_BLOCK], right], axis=1)
+
+
 def precise(left, right, dims):
     return lax.dot_general(left, right, (dims, ((), ())), precision=PRECISE, preferred_element_type=F32)
 
@@ -693,7 +772,7 @@
     copies = []
     for n, (matrix, block, z, x, core, place_in) in enumerate(spots):
         turned = outs[matrix][:, block * ROW_BLOCK : (block + 1) * ROW_BLOCK]
-        grams[n] = precise(turned, turned, ((0,), (0,)))
+        grams[n] = packed(precise(turned, turned, ((0,), (0,))))
         away = (lax.rem(spots_ref[1] + x, 2), lax.rem(zs + z - spots_ref[0], zs), place_in)
         pair = [pltpu.make_async_copy(grams.at[n], ref.at[away], sems.at[n]) for ref in (own_ref, other_ref)]
         on_own_core(True, spots_ref, core, [copy.start for copy in pair])
@@ -715,7 +794,7 @@
         out_specs=[vmem] * len(momenta) + [anywhere, anywhere],
         input_output_aliases={1: len(momenta), 2: len(momenta) + 1},
         scratch_shapes=[
-            pltpu.VMEM((blocks, ROW_BLOCK, ROW_BLOCK), F32),
+            pltpu.VMEM((blocks,) + PACKED, F32),
             pltpu.SemaphoreType.DMA((blocks,)),
         ],
         compiler_params=pltpu.CompilerParams(vmem_limit_bytes=VMEM_LIMIT),
@@ -735,6 +814,7 @@
         gram = refs[0][n]
         for ref in refs[1:count]:
             gram = gram + ref[n].astype(F32)
+        gram = unpacked(gram)
         square = jnp.sum(jnp.sum(gram * eye, axis=1, keepdims=True), axis=0, keepdims=True)
         scale = 1.0 / (jnp.sqrt(square) + NORM_EPS)
         scales.append(scale)
@@ -746,7 +826,7 @@
             currents = [mul(f, a) for f, a in zip(factors, currents)]
             currents = [mul(a, f) for f, a in zip(factors, currents)]
     for n in blocks:
-        out[n] = totals[n] * scales[n]
+        out[n] = packed(totals[n] * scales[n])
 
 
 def polynomial(parts):
@@ -771,7 +851,7 @@
     for matrix, block, z, x, core, place_in in placed:
         part = slice(block * ROW_BLOCK, (block + 1) * ROW_BLOCK)
         away = 2 * lax.rem(spots_ref[2] + core, 2) + lax.rem(spots_ref[1] + x, 2)
-        factor = factors[away, lax.rem(zs + z - spots_ref[0], zs), place_in]
+        factor = unpacked(factors[away, lax.rem(zs + z - spots_ref[0], zs), place_in])
         direction = precise(momenta[matrix][:, part], factor, ((1,), (1,)))
         outs[matrix][:, part] = masters[matrix][:, part] * (1.0 - WEIGHT_SHRINK) - rates[matrix] * direction
 
@@ -869,12 +949,11 @@
     mixed_one = inputs + gate_one * branch_one
     normed_two, inverse_two = layer_norm(mixed_one)
     ffn_in = (normed_two * (1.0 + scale_two) + shift_two).astype(BF)
-    pre_act = dot_t(ffn_in, t_fc1) + b_fc1
-    activated, gelu_back = jax.vjp(gelu_tanh, pre_act)
-    activated_low = activated.astype(BF)
+    flat = lambda array: array.reshape(-1, array.shape[-1])
+    activated_low, slope = hidden_forward(flat(ffn_in), t_fc1, b_fc1)
+    activated_low = activated_low.reshape(count, rows, hidden)
     grad_out = upstream.reshape(count, rows, width).astype(F32)
     grad_branch_two = (gate_two * grad_out).astype(BF)
-    flat = lambda array: array.reshape(-1, array.shape[-1])
     term_fc2 = outer(grad_branch_two, activated_low)
     sum_fc2 = net.scatter(term_fc2)
     branch_two = dot_t(tie(activated_low, term_fc2), t_fc2) + b_fc2
@@ -883,10 +962,8 @@
 
     grad_gate_two = jnp.sum(branch_two * grad_out, axis=1)
     bias_fc2 = jnp.sum(grad_branch_two.astype(F32), axis=(0, 1))
-    grad_pre = gelu_back(dot(grad_branch_two, t_fc2))[0].astype(BF)
-    term_fc1 = outer(grad_pre, ffn_in)
-    grad_pre = tie(grad_pre, term_fc1)
-    bias_fc1 = jnp.sum(grad_pre.astype(F32), axis=(0, 1))
+    grad_pre, bias_fc1 = hidden_backward(flat(grad_branch_two), t_fc2, slope)
+    grad_pre = grad_pre.reshape(count, rows, hidden)
     grad_ffn_in = dot(grad_pre, t_fc1)
     grad_shift_two = jnp.sum(grad_ffn_in, axis=1)
     grad_scale_two = jnp.sum(grad_ffn_in * normed_two, axis=1)
@@ -895,11 +972,18 @@
     grad_branch_one = (gate_one * grad_mixed).astype(BF)
     bias_proj = jnp.sum(grad_branch_one.astype(F32), axis=(0, 1))
     grad_attended = dot(grad_branch_one, t_proj).astype(BF)
-    term_fc1 = tie(term_fc1, sum_fc2, grad_attended)
-    sum_fc1 = net.scatter(term_fc1)
-    term_proj = tie(outer(grad_branch_one, attended_low), term_fc1)
-    sum_proj = net.scatter(term_proj)
-    grad_attended = tie(grad_attended, term_proj)
+    unit_mid = math.gcd(math.gcd(n_proj, n_fc1), 8)
+    (term_mid,) = shard_outer(
+        net.spots(),
+        [flat(grad_pre), flat(ffn_in), flat(grad_branch_one), flat(attended_low)],
+        [([2], 0, width), ([3], 0, width), ([1], 0, width)]
+        + [([0], j * width, width) for j in range(hidden // width)],
+        [(0, 1, n_proj, 0)] + [(3 + j, 2, n_fc1, n_proj // unit_mid) for j in range(hidden // width)],
+        net.z.size, width, unit_mid, (n_proj + n_fc1) // unit_mid, split=False,
+    )
+    term_mid = tie(term_mid, sum_fc2, grad_attended)
+    sum_mid = net.scatter(term_mid.reshape(dp * (n_proj + n_fc1), width))
+    grad_attended = tie(grad_attended, term_mid)
 
     def far_steps(dk, dv):
         part = dot(dk[:, rows:], t_qkv[width : 2 * width]) + dot(dv[:, rows:], t_qkv[2 * width :])
@@ -936,7 +1020,7 @@
     grad_k[-1] = tie(grad_k[-1], term_last)
     far_parts.append(far_steps(grad_k[-1], grad_v[-1]))
     sent = far_parts[-1].advance()
-    halves = Staged(lockstep(*[net.halves_steps(tie(each, *sent)) for each in (sum_fc2, sum_fc1, sum_proj)]))
+    halves = Staged(lockstep(*[net.halves_steps(tie(each, *sent)) for each in (sum_fc2, sum_mid)]))
     sent = sent + halves.advance()
     grad_q[0] = tie(grad_q[0], *sent)
     bias_q = sum(jnp.sum(each.astype(F32), axis=(0, 1)) for each in grad_q)
@@ -981,11 +1065,9 @@
     got_parcel = net.to_all(parcel)
 
     sums = halves.finish(parcel)
-    blank = jnp.zeros((2, net.z.size, per, ROW_BLOCK, ROW_BLOCK), F32)
-    (next_fc2, next_fc1, next_proj), *early = muon_gram(
-        net.spots(),
-        [(sums[0], [turned[3]]), (sums[1], [turned[2]]), (sums[2], [turned[1]])],
-        spread_early, (blank, blank),
+    blank = jnp.zeros((2, net.z.size, per) + PACKED, F32)
+    (next_fc2, next_proj, next_fc1), *early = muon_gram(
+        net.spots(), [(sums[0], [turned[3]]), (sums[1], [turned[1], turned[2]])], spread_early, (blank, blank)
     )
     got_parcel = tie(got_parcel, early[0])
     halves = Staged(net.halves_steps(tie(sum_last, got_parcel)))
@@ -1003,13 +1085,13 @@
     sent = gathered.advance()
     while not gathered.done:
         sent = gathered.advance(sent[0])
-    momenta_in = [next_fc2, next_fc1, next_proj, next_qkv, next_ada]
+    momenta_in = [next_fc2, next_proj, next_fc1, next_qkv, next_ada]
     heights_of = [momentum.shape[1] // ROW_BLOCK for momentum in momenta_in]
     placed = block_spots(heights_of[:3], spread_early)
     placed += [(3 + spot[0],) + spot[1:] for spot in block_spots(heights_of[3:], spread_last)]
-    new_fc2, new_fc1, new_proj, new_qkv, new_ada = muon_apply(
-        net.spots(), gathered.result, momenta_in, [w.T for w in (w_fc2, w_fc1, w_proj, w_qkv, w_ada)],
-        [math.sqrt(width / hidden), math.sqrt(hidden / width), 1.0, math.sqrt(3.0), math.sqrt(6.0)], placed,
+    new_fc2, new_proj, new_fc1, new_qkv, new_ada = muon_apply(
+        net.spots(), gathered.result, momenta_in, [w.T for w in (w_fc2, w_proj, w_fc1, w_qkv, w_ada)],
+        [math.sqrt(width / hidden), 1.0, math.sqrt(hidden / width), math.sqrt(3.0), math.sqrt(6.0)], placed,
     )
 
     size = biases.shape[0]

time: 902 us -> 804 us (0.89)
  matrix products: 230 us -> 157 us
  waiting for transfers between devices: 196 us -> 132 us
  Pallas kernels: 223 us -> 281 us
  local copies, waits for them, and re-layouts: 93.3 us -> 81.3 us
    pallas_call x0 -> x2, Pallas kernels: none -> 46.7 us  [the longest x1 26.2 us: hidden_forward(): pl.pallas_call(hidden_kernel, grid=(n // tile,), in_specs=[pl.BlockSpec((...]
    ppermute x36 -> x35, waiting for transfers between devices: 110 us -> 76.6 us  [send(): return lax.ppermute(value, self.name, pairs)]
    unnamed x8 -> x7, waiting for transfers between devices: 41.8 us -> 14.5 us
    dot_general x9 -> x8, matrix products: 96.1 us -> 69.3 us  [dot_t(): return jnp.einsum('srk,nk->srn', left, right, preferred_element_type=F32)]
    dot_general x13 -> x12, matrix products: 91.1 us -> 67.4 us  [dot(): return jnp.einsum('srn,nk->srk', left, right, preferred_element_type=F32)]
    pallas_call x1 -> x2, Pallas kernels: 25.2 us -> 48.7 us  [shard_outer(): pl.pallas_call(functools.partial(shard_outer_kernel, {'loads': loads, 'pa...]
    dot_general x3 -> x1, matrix products: 40.7 us -> 17.3 us  [outer(): jnp.einsum('srn,srk->nk', left, right, preferred_element_type=F32)]
    unnamed x223 -> x214, local copies, waits for them, and re-layouts: 32.4 us -> 26.5 us
  transfers between devices with their start and end apart: 46 -> 44, of which waited for: 19 -> 19; matrix products, arithmetic and copies ran while one was open for 40% -> 33% of each run, Pallas kernels for 22% -> 32%
where the time goes in v9:
time: 804 us; the launch traced here: 795 us
  Pallas kernels  281 us (35%)
  matrix products  157 us (20%)
  waiting for transfers between devices  132 us (16%)
  local copies, waits for them, and re-layouts  81.3 us (10%)
  other arithmetic  66.3 us (8%)
  starting transfers between devices  62.1 us (8%)
  between operations  15.8 us (2%)
    pallas_call x2, Pallas kernels, attend_back(): pl.pallas_call(without(attend_back_kernel, 8, len(deps), heads, tile), gr...  85.3 us
    ppermute x35, waiting for transfers between devices, send(): return lax.ppermute(value, self.name, pairs)  76.6 us
    dot_general x8, matrix products, dot_t(): return jnp.einsum('srk,nk->srn', left, right, preferred_element_type=F32)  69.3 us
    dot_general x12, matrix products, dot(): return jnp.einsum('srn,nk->srk', left, right, preferred_element_type=F32)  67.4 us
    pallas_call x2, Pallas kernels, attend(): pl.pallas_call(without(attend_kernel, 5, len(deps), heads, tile), grid_sp...  59 us
    pallas_call x2, Pallas kernels, shard_outer(): pl.pallas_call(functools.partial(shard_outer_kernel, {'loads': loads, 'pa...  48.7 us
    ppermute x35, starting transfers between devices, send(): return lax.ppermute(value, self.name, pairs)  36.9 us
    unnamed x214, local copies, waits for them, and re-layouts  26.5 us
  transfers between devices with their start and end apart: 44, of which 19 were waited for; matrix products, arithmetic and copies ran while one was open for 33% of the time, Pallas kernels for 32%

profile of v9, /device:TPU:11, one launch (start us, length us, event | category | flops | bytes accessed | tf_op | source)
XLA Modules:
  0.0 795.0 jit_solution(14124882528721277186)
XLA Ops:
  23.0 11.0 %all-to-all-done = f32[32,1,1656]{2,1,0:T(1,128)S(1)} async-done(((f32[32,1,1656]{2,1,0:T(1,128)}), f32[32,1,1656]{2,1,0:T(1,128)S(1)}, u32[]{:S(2)}, u32[]{:S(2)}) %all-to-all-start) | async-done | bytes 212000 | tf_op jit(solution)/shard_map/all_to_all | solution.py:319
  54.9 13.6 %collective-permute-done.3.refs_0_ = bf16[16,8,1152]{2,1,0:T(8,128)(2,1)S(1)} collective-permute-done((bf16[16,8,1152]{2,1,0:T(8,128)(2,1)}, bf16[16,8,1152]{2,1,0:T(8,128)(2,1)S(1)}, u32[]{:S(2)}, u32[]{:S(2)}) %collective-permute-start.3) | collective-permute-done | bytes 294944 | tf_op jit(solution)/shard_map/ppermute | solution.py:47
  76.7 8.2 %collective-permute-done.9.refs_0_ = bf16[2,20,8,1152]{3,2,1,0:T(8,128)(2,1)} collective-permute-done((bf16[2,20,8,1152]{3,2,1,0:T(8,128)(2,1)}, bf16[2,20,8,1152]{3,2,1,0:T(8,128)(2,1)}, u32[]{:S(2)}, u32[]{:S(2)}) %collective-permute-start.9) | collective-permute-done | bytes 737312 | tf_op jit(solution)/shard_map/ppermute | solution.py:47
  109.3 9.1 %place.1 = (bf16[4,2,2,27,8,1152]{5,4,3,2,1,0:T(8,128)(2,1)}, bf16[4,2,2,9,8,1152]{5,4,3,2,1,0:T(8,128)(2,1)}) custom-call(s32[3]{0:T(128)} %pad_add_fusion.1.refs_0_.spots_ref, bf16[4,16,8,1152]{3,2,1,0:T(8,128)(2,1)} %copy-done.1, bf16[4,16,8,1152]{3,2,1,0:T(8,128)(2,1)} %tie.61.refs_2_, bf16[2,20,8,1152]{3,2,1,0:T(8,128)(2,1)} %pad_maximum_fusion.4.refs_3_, ...), custom_call_target="tpu_custom_call" | custom-call | bytes 21233664 | tf_op jit(solution)/shard_map/place/pallas_call | solution.py:198
  151.8 29.6 %attend.2 = (bf16[1,512,1152]{2,1,0:T(8,128)(2,1)}, f32[1,16,1,512]{3,2,1,0:T(1,128)}) custom-call(s32[1]{0:T(128)} %bitcast.17.refs_0_, s32[2]{0:T(128)} %pad_add_fusion.refs_1_, bf16[1,512,1152]{2,1,0:T(8,128)(2,1)} %fusion.27.refs_2_, bf16[1,1024,1152]{2,1,0:T(8,128)(2,1)} %fusion.20.refs_3_, bf16[1,1024,1152]{2,1,0:T(8,128)(2,1)} %fusion.18.refs_4_), custom_call_target="tpu_custom_call" | custom-call | flops 4294967296 | bytes 7077888 | tf_op jit(solution)/shard_map/attend/pallas_call | solution.py:606
  217.8 29.4 %attend.3 = (bf16[1,512,1152]{2,1,0:T(8,128)(2,1)}, f32[1,16,1,512]{3,2,1,0:T(1,128)}) custom-call(s32[1]{0:T(128)} %bitcast.28.refs_0_, s32[2]{0:T(128)} %pad_add_fusion.refs_1_, bf16[1,512,1152]{2,1,0:T(8,128)(2,1)} %fusion.26.refs_2_, bf16[1,1024,1152]{2,1,0:T(8,128)(2,1)} %fusion.21.refs_3_.refs_1_, bf16[1,1024,1152]{2,1,0:T(8,128)(2,1)} %fusion.19.refs_4_), custom_call_target="tpu_custom_call" | custom-call | flops 4294967296 | bytes 7077888 | tf_op jit(solution)/shard_map/attend/pallas_call | solution.py:606
  249.8 8.4 %fusion.85 = (f32[2,512]{1,0:T(2,128)S(1)}, f32[2,512,1152]{2,1,0:T(8,128)S(1)}, f32[2,512,1152]{2,1,0:T(8,128)}) fusion(f32[2,1152]{1,0:T(2,128)S(1)} %get-tuple-element.214, bf16[2,1,512,1152]{3,2,1,0:T(8,128)(2,1)S(1)} %copy-done.36, f32[1152]{0:T(1024)S(1)} %copy-done.85, bf16[2,512,1152]{2,1,0:T(8,128)(2,1)} %constant_dynamic-update-slice_fusion, ...), kind=kOutput, calls=%fused_computation.219 | convolution fusion | flops 2723806208 | bytes 16827904 | tf_op jit(solution)/shard_map/srk,nk->srn/dot_general | solution.py:342
  262.6 26.2 %hidden_forward.1 = (bf16[1024,4608]{1,0:T(8,128)(2,1)}, bf16[1024,4608]{1,0:T(8,128)(2,1)}) custom-call(bf16[1024,1152]{1,0:T(8,128)(2,1)} %bitcast.280, bf16[4608,1152]{1,0:T(8,128)(2,1)} %all-gather.3.cloned.1.call-done.w_ref, f32[1,4608]{1,0:T(1,128)} %reshape.549.b_ref), custom_call_target="tpu_custom_call" | custom-call | flops 10871635968 | bytes 31850496 | tf_op jit(solution)/shard_map/hidden_forward/pallas_call | solution.py:368
  288.8 17.3 %fusion.refs_1_ = bf16[1152,4608]{1,0:T(8,128)(2,1)} fusion(bf16[2,512,1152]{2,1,0:T(8,128)(2,1)S(1)} %fusion.14.refs_0_, bf16[2,512,4608]{2,1,0:T(8,128)(2,1)} %bitcast.246), kind=kOutput, calls=%fused_computation.1 | convolution fusion | flops 10876944384 | bytes 22413312 | tf_op jit(solution)/shard_map/srn,srk->nk/dot_general | solution.py:417
  306.2 20.5 %hidden_backward.1 = (bf16[1024,4608]{1,0:T(8,128)(2,1)}, f32[1,4608]{1,0:T(1,128)}) custom-call(bf16[1024,1152]{1,0:T(8,128)(2,1)} %bitcast.244, bf16[1152,4608]{1,0:T(8,128)(2,1)} %all-gather.5.cloned.1.call-done.w_ref, bf16[1024,4608]{1,0:T(8,128)(2,1)} %get-tuple-element.51.slope_ref), custom_call_target="tpu_custom_call" | custom-call | flops 10871635968 | bytes 31850496 | tf_op jit(solution)/shard_map/hidden_backward/pallas_call | solution.py:397
  326.7 22.8 %multiply_reduce_fusion = (f32[2,1152]{1,0:T(2,128)}, f32[2,512]{1,0:T(2,128)S(1)}, f32[2,512]{1,0:T(2,128)S(1)}, f32[2,1152]{1,0:T(2,128)}, f32[2,512,1152]{2,1,0:T(8,128)}) fusion(f32[2,512,1152]{2,1,0:T(8,128)} %copy-done.9, f32[2,512]{1,0:T(2,128)S(1)} %add_rsqrt_fusion, f32[2,512]{1,0:T(2,128)S(1)} %broadcast_multiply_fusion.4, ...), kind=kOutput, calls=%fused_computation.29 | convolution fusion | flops 10882246656 | bytes 29535232 | tf_op jit(solution)/shard_map/srn,nk->srk/dot_general | solution.py:346
  349.6 24.4 %fusion.15 = (f32[2,1152]{1,0:T(2,128)}, bf16[2,1,512,1152]{3,2,1,0:T(8,128)(2,1)}, f32[1152]{0:T(1024)}, bf16[2,512,1152]{2,1,0:T(8,128)(2,1)}, f32[2,512,1152]{2,1,0:T(8,128)}) fusion(bf16[2,1,512,1152]{3,2,1,0:T(8,128)(2,1)S(1)} %copy-done.42, f32[2,512,1152]{2,1,0:T(8,128)} %copy-done.9, f32[2,1152]{1,0:T(2,128)S(1)} %get-tuple-element.211, ...), kind=kOutput, calls=%fused_computation.21 | convolution fusion | flops 10894046208 | bytes 41350144 | tf_op jit(solution)/shard_map/srk,nk->srn/dot_general | solution.py:342
  381.3 23.6 %shard_outer.2.refs_0_ = bf16[4,2,2,45,8,1152]{5,4,3,2,1,0:T(8,128)(2,1)} custom-call(s32[3]{0:T(128)} %pad_add_fusion.1.refs_0_.spots_ref, bf16[1024,4608]{1,0:T(8,128)(2,1)} %get-tuple-element.52.refs_0_, bf16[1024,1152]{1,0:T(8,128)(2,1)} %bitcast.281, bf16[1024,1152]{1,0:T(8,128)(2,1)} %bitcast.322, bf16[1024,1152]{1,0:T(8,128)(2,1)} %bitcast.302), custom_call_target="tpu_custom_call" | custom-call | flops 13589544960 | bytes 13271040 | tf_op jit(solution)/shard_map/shard_outer/pallas_call | solution.py:507
  404.9 23.2 %reduce-scatter.8.cloned.1.call-done.refs_1_.refs_0_ = bf16[72,4608]{1,0:T(8,128)(2,1)} async-done(((bf16[1152,4608]{1,0:T(8,128)(2,1)}), bf16[72,4608]{1,0:T(8,128)(2,1)}) %reduce-scatter.8.cloned.1.call-update) | async-done | bytes 663568 | tf_op jit(solution)/shard_map/reduce_scatter | solution.py:249
  436.9 43.1 %attend_back.2 = (bf16[1,512,1152]{2,1,0:T(8,128)(2,1)}, bf16[1,1024,1152]{2,1,0:T(8,128)(2,1)}, bf16[1,1024,1152]{2,1,0:T(8,128)(2,1)}) custom-call(s32[1]{0:T(128)} %bitcast.17.refs_0_, s32[2]{0:T(128)} %pad_add_fusion.refs_1_, bf16[1,512,1152]{2,1,0:T(8,128)(2,1)} %fusion.27.refs_2_, bf16[1,1024,1152]{2,1,0:T(8,128)(2,1)} %fusion.20.refs_3_, ...), custom_call_target="tpu_custom_call" | custom-call | flops 10737418240 | bytes 14155776 | tf_op jit(solution)/shard_map/attend_back/pallas_call | solution.py:691
  488.8 42.2 %attend_back.3 = (bf16[1,512,1152]{2,1,0:T(8,128)(2,1)}, bf16[1,1024,1152]{2,1,0:T(8,128)(2,1)}, bf16[1,1024,1152]{2,1,0:T(8,128)(2,1)}) custom-call(s32[1]{0:T(128)} %bitcast.28.refs_0_, s32[2]{0:T(128)} %pad_add_fusion.refs_1_, bf16[1,512,1152]{2,1,0:T(8,128)(2,1)} %fusion.26.refs_2_, bf16[1,1024,1152]{2,1,0:T(8,128)(2,1)} %fusion.21.refs_3_.refs_1_, ...), custom_call_target="tpu_custom_call" | custom-call | flops 10737418240 | bytes 14155776 | tf_op jit(solution)/shard_map/attend_back/pallas_call | solution.py:691
  531.0 25.1 %shard_outer.3.refs_1_ = bf16[4,2,2,27,8,1152]{5,4,3,2,1,0:T(8,128)(2,1)} custom-call(s32[3]{0:T(128)} %pad_add_fusion.1.refs_0_.spots_ref, bf16[512,1152]{1,0:T(8,128)(2,1)} %bitcast.267, bf16[512,1152]{1,0:T(8,128)(2,1)} %bitcast.291, bf16[1024,1152]{1,0:T(8,128)(2,1)} %bitcast.321, bf16[1024,1152]{1,0:T(8,128)(2,1)} %bitcast.284, ...), custom_call_target="tpu_custom_call" | custom-call | flops 13589544960 | bytes 7962624 | tf_op jit(solution)/shard_map/shard_outer/pallas_call | solution.py:507
  624.1 7.5 all-to-all-start.2
  666.5 14.4 %reduce-scatter.12.cloned.1.call-done.refs_0_ = bf16[216,1152]{1,0:T(8,128)(2,1)} async-done(((bf16[3456,1152]{1,0:T(8,128)(2,1)}), bf16[216,1152]{1,0:T(8,128)(2,1)}) %reduce-scatter.12.cloned.1.call-update) | async-done | bytes 497680
  707.1 8.7 %collective-permute-done.25.refs_0_ = bf16[4,2,160,128]{3,2,1,0:T(8,128)(2,1)S(1)} collective-permute-done((bf16[4,2,160,128]{3,2,1,0:T(8,128)(2,1)S(1)}, bf16[4,2,160,128]{3,2,1,0:T(8,128)(2,1)S(1)}, u32[]{:S(2)}, u32[]{:S(2)}) %collective-permute-start.25) | collective-permute-done | bytes 327712 | tf_op jit(solution)/shard_map/ppermute | solution.py:47
  727.8 7.8 polynomial.1.refs_1_
  742.0 7.7 collective-permute-done.30.refs_0_
  757.4 13.7 %collective-permute-done.32.refs_0_ = f32[4,2,160,128]{3,2,1,0:T(8,128)S(1)} collective-permute-done((f32[4,2,160,128]{3,2,1,0:T(8,128)S(1)}, f32[4,2,160,128]{3,2,1,0:T(8,128)S(1)}, u32[]{:S(2)}, u32[]{:S(2)}) %collective-permute-start.32) | collective-permute-done | bytes 655392 | tf_op jit(solution)/shard_map/ppermute | solution.py:47
  777.1 10.9 %muon_apply.1 = (f32[72,2304]{1,0:T(8,128)}, f32[72,576]{1,0:T(8,128)}, f32[288,576]{1,0:T(8,128)}, f32[216,576]{1,0:T(8,128)}, f32[432,576]{1,0:T(8,128)}) custom-call(s32[3]{0:T(128)} %pad_add_fusion.1.refs_0_.spots_ref, f32[4,2,160,128]{3,2,1,0:T(8,128)} %copy-done.12, f32[4,2,160,128]{3,2,1,0:T(8,128)} %tie.99.refs_1_, f32[4,2,160,128]{3,2,1,0:T(8,128)} %tie.100.refs_2_, ...), custom_call_target="tpu_custom_call" | custom-call | tf_op jit(solution)/shard_map/muon_apply/pallas_call | solution.py:861
  (501 shorter events, 330.8 us)
Async XLA Ops:
  14.9 19.1 %all-to-all-start = ((f32[32,1,1656]{2,1,0:T(1,128)}), f32[32,1,1656]{2,1,0:T(1,128)S(1)}, u32[]{:S(2)}, u32[]{:S(2)}) async-start(f32[32,1,1656]{2,1,0:T(1,128)} %all_to_all.24), calls=%async_computation | async-start | bytes 425984 | tf_op jit(solution)/shard_map/all_to_all | solution.py:319
  21.1 22.5 %collective-permute-start.2 = (bf16[16,8,1152]{2,1,0:T(8,128)(2,1)S(1)}, bf16[16,8,1152]{2,1,0:T(8,128)(2,1)}, u32[]{:S(2)}, u32[]{:S(2)}) collective-permute-start(bf16[16,8,1152]{2,1,0:T(8,128)(2,1)S(1)} %get-tuple-element.200.refs_1_.refs_2_), channel_id=1, source_target_pairs={{0,8},{2,10},{4,12},{6,14},{8,16},{10,18},{12,20},{14,22},{16,24},... | collective-permute-start | bytes 884744 | tf_op jit(solution)/shard_map/ppermute | solution.py:47
  22.3 31.1 %collective-permute-start.1 = (bf16[16,8,1152]{2,1,0:T(8,128)(2,1)S(1)}, bf16[16,8,1152]{2,1,0:T(8,128)(2,1)}, u32[]{:S(2)}, u32[]{:S(2)}) collective-permute-start(bf16[16,8,1152]{2,1,0:T(8,128)(2,1)S(1)} %get-tuple-element.200.refs_1_.refs_2_), channel_id=1, source_target_pairs={{0,24},{2,26},{4,28},{6,30},{8,0},{10,2},{12,4},{14,6},{16,8},{18,... | collective-permute-start | bytes 884744 | tf_op jit(solution)/shard_map/ppermute | solution.py:47
  22.7 22.2 %collective-permute-start.4 = (bf16[20,8,1152]{2,1,0:T(8,128)(2,1)S(1)}, bf16[20,8,1152]{2,1,0:T(8,128)(2,1)S(1)}, u32[]{:S(2)}, u32[]{:S(2)}) collective-permute-start(bf16[20,8,1152]{2,1,0:T(8,128)(2,1)S(1)} %get-tuple-element.198.refs_3_), channel_id=1, source_target_pairs={{0,4},{2,6},{4,0},{6,2},{8,12},{10,14},{12,8},{14,10},{16,20},{18,... | collective-permute-start | bytes 1105928 | tf_op jit(solution)/shard_map/ppermute | solution.py:47
  43.6 219.0 %all-gather.3.cloned.1.call-start = ((), (), s32[]{:S(2)}) async-start(), calls=%async_computation.7 | async-start | bytes 11280384 | tf_op jit(solution)/shard_map/all_gather | solution.py:920
  43.7 24.9 %collective-permute-start.3 = (bf16[16,8,1152]{2,1,0:T(8,128)(2,1)}, bf16[16,8,1152]{2,1,0:T(8,128)(2,1)S(1)}, u32[]{:S(2)}, u32[]{:S(2)}) collective-permute-start(bf16[16,8,1152]{2,1,0:T(8,128)(2,1)} %tie.54), channel_id=1, source_target_pairs={{0,8},{2,10},{4,12},{6,14},{8,16},{10,18},{12,20},{14,22},{16,24},... | collective-permute-start | bytes 884744 | tf_op jit(solution)/shard_map/ppermute | solution.py:47
  47.6 24.2 %collective-permute-start.5 = (bf16[2,20,8,1152]{3,2,1,0:T(8,128)(2,1)}, bf16[2,20,8,1152]{3,2,1,0:T(8,128)(2,1)}, u32[]{:S(2)}, u32[]{:S(2)}) collective-permute-start(bf16[2,20,8,1152]{3,2,1,0:T(8,128)(2,1)} %pad_maximum_fusion.4.refs_3_), channel_id=1, source_target_pairs={{0,24},{2,26},{4,28},{6,30},{8,0},{10,2},{12,4},{14,6},{16,8},{18,... | collective-permute-start | bytes 2211848 | tf_op jit(solution)/shard_map/ppermute | solution.py:47
  47.8 37.1 %collective-permute-start.9 = (bf16[2,20,8,1152]{3,2,1,0:T(8,128)(2,1)}, bf16[2,20,8,1152]{3,2,1,0:T(8,128)(2,1)}, u32[]{:S(2)}, u32[]{:S(2)}) collective-permute-start(bf16[2,20,8,1152]{3,2,1,0:T(8,128)(2,1)} %pad_maximum_fusion.4.refs_3_), channel_id=1, source_target_pairs={{0,8},{2,10},{4,12},{6,14},{8,16},{10,18},{12,20},{14,22},{16,24},... | collective-permute-start | bytes 2211848 | tf_op jit(solution)/shard_map/ppermute | solution.py:47
  52.2 52.7 %collective-permute-start.6 = (bf16[512,1152]{1,0:T(8,128)(2,1)}, bf16[512,1152]{1,0:T(8,128)(2,1)S(1)}, u32[]{:S(2)}, u32[]{:S(2)}) collective-permute-start(bf16[512,1152]{1,0:T(8,128)(2,1)} %tie.60), channel_id=1, source_target_pairs={{0,1},{1,0},{2,3},{3,2},{4,5},{5,4},{6,7},{7,6},{8,9},{9,8},{10,11... | collective-permute-start | bytes 3538952 | tf_op jit(solution)/shard_map/ppermute | solution.py:47
  53.4 51.5 %collective-permute-start.12 = (bf16[2,20,8,1152]{3,2,1,0:T(8,128)(2,1)}, bf16[2,20,8,1152]{3,2,1,0:T(8,128)(2,1)}, u32[]{:S(2)}, u32[]{:S(2)}) collective-permute-start(bf16[2,20,8,1152]{3,2,1,0:T(8,128)(2,1)} %pad_maximum_fusion.4.refs_3_), channel_id=1, source_target_pairs={{0,2},{2,0},{4,6},{6,4},{8,10},{10,8},{12,14},{14,12},{16,18},{18,... | collective-permute-start | bytes 2211848 | tf_op jit(solution)/shard_map/ppermute | solution.py:47
  70.6 26.5 %collective-permute-start.7 = (bf16[4,16,8,1152]{3,2,1,0:T(8,128)(2,1)S(1)}, bf16[4,16,8,1152]{3,2,1,0:T(8,128)(2,1)}, u32[]{:S(2)}, u32[]{:S(2)}) collective-permute-start(bf16[4,16,8,1152]{3,2,1,0:T(8,128)(2,1)S(1)} %pad_maximum_fusion.3.refs_1_.refs_2_), channel_id=1, source_target_pairs={{0,4},{2,6},{4,0},{6,2},{8,12},{10,14},{12,8},{14,10},{16,20},{18,... | collective-permute-start | bytes 3538952 | tf_op jit(solution)/shard_map/ppermute | solution.py:47
  71.8 35.6 %collective-permute-start.10 = (bf16[4,16,8,1152]{3,2,1,0:T(8,128)(2,1)S(1)}, bf16[4,16,8,1152]{3,2,1,0:T(8,128)(2,1)S(1)}, u32[]{:S(2)}, u32[]{:S(2)}) collective-permute-start(bf16[4,16,8,1152]{3,2,1,0:T(8,128)(2,1)S(1)} %pad_maximum_fusion.3.refs_1_.refs_2_), channel_id=1, source_target_pairs={{0,2},{2,0},{4,6},{6,4},{8,10},{10,8},{12,14},{14,12},{16,18},{18,... | collective-permute-start | bytes 3538952 | tf_op jit(solution)/shard_map/ppermute | solution.py:47
  84.9 18.8 %collective-permute-start.8 = (bf16[2,20,8,1152]{3,2,1,0:T(8,128)(2,1)}, bf16[2,20,8,1152]{3,2,1,0:T(8,128)(2,1)}, u32[]{:S(2)}, u32[]{:S(2)}) collective-permute-start(bf16[2,20,8,1152]{3,2,1,0:T(8,128)(2,1)} %tie.57.refs_2_.refs_4_.refs_3_), channel_id=1, source_target_pairs={{0,24},{2,26},{4,28},{6,30},{8,0},{10,2},{12,4},{14,6},{16,8},{18,... | collective-permute-start | bytes 2211848 | tf_op jit(solution)/shard_map/ppermute | solution.py:47
  122.7 183.5 %all-gather.5.cloned.1.call-start = ((), (), s32[]{:S(2)}) async-start(), calls=%async_computation.8 | async-start | bytes 11280384 | tf_op jit(solution)/shard_map/all_gather | solution.py:944
  132.1 49.3 %collective-permute-start.17 = (bf16[512,1152]{1,0:T(8,128)(2,1)}, bf16[512,1152]{1,0:T(8,128)(2,1)S(1)}, u32[]{:S(2)}, u32[]{:S(2)}) collective-permute-start(bf16[512,1152]{1,0:T(8,128)(2,1)} %tie.72), channel_id=1, source_target_pairs={{0,1},{1,0},{2,3},{3,2},{4,5},{5,4},{6,7},{7,6},{8,9},{9,8},{10,11... | collective-permute-start | bytes 3538952 | tf_op jit(solution)/shard_map/ppermute | solution.py:47
  199.1 229.0 %reduce-scatter.8.cloned.1.call-start = ((), (), s32[]{:S(2)}) async-start(), calls=%async_computation.9 | async-start | bytes 11280384 | tf_op jit(solution)/shard_map/reduce_scatter | solution.py:249
  306.1 288.0 %reduce-scatter.10.cloned.1.call-start = ((), (), s32[]{:S(2)}) async-start(), calls=%async_computation.10 | async-start | bytes 14100480
  428.2 252.7 %reduce-scatter.12.cloned.1.call-start = ((), (), s32[]{:S(2)}) async-start(), calls=%async_computation.11 | async-start | bytes 8460288
  562.1 52.2 %collective-permute-start.19 = (bf16[512,1152]{1,0:T(8,128)(2,1)}, bf16[512,1152]{1,0:T(8,128)(2,1)}, u32[]{:S(2)}, u32[]{:S(2)}) collective-permute-start(bf16[512,1152]{1,0:T(8,128)(2,1)} %fusion.24.refs_8_), channel_id=1, source_target_pairs={{0,1},{1,0},{2,3},{3,2},{4,5},{5,4},{6,7},{7,6},{8,9},{9,8},{10,11... | collective-permute-start | bytes 3538952 | tf_op jit(solution)/shard_map/ppermute | solution.py:47
  570.9 43.4 %collective-permute-start.20 = (bf16[512,1152]{1,0:T(8,128)(2,1)S(1)}, bf16[512,1152]{1,0:T(8,128)(2,1)}, u32[]{:S(2)}, u32[]{:S(2)}) collective-permute-start(bf16[512,1152]{1,0:T(8,128)(2,1)S(1)} %fusion.25.refs_1_), channel_id=1, source_target_pairs={{0,1},{1,0},{2,3},{3,2},{4,5},{5,4},{6,7},{7,6},{8,9},{9,8},{10,11... | collective-permute-start | bytes 3538952 | tf_op jit(solution)/shard_map/ppermute | solution.py:47
  579.5 72.0 %collective-permute-start.21 = (bf16[72,2304]{1,0:T(8,128)(2,1)}, bf16[72,2304]{1,0:T(8,128)(2,1)}, u32[]{:S(2)}, u32[]{:S(2)}) collective-permute-start(bf16[72,2304]{1,0:T(8,128)(2,1)} %bitcast.240.refs_2_), channel_id=1, source_target_pairs={{0,1},{1,0},{2,3},{3,2},{4,5},{5,4},{6,7},{7,6},{8,9},{9,8},{10,11... | collective-permute-start | bytes 995336 | tf_op jit(solution)/shard_map/ppermute | solution.py:47
  600.7 52.6 %collective-permute-start.22 = (bf16[360,576]{1,0:T(8,128)(2,1)}, bf16[360,576]{1,0:T(8,128)(2,1)}, u32[]{:S(2)}, u32[]{:S(2)}) collective-permute-start(bf16[360,576]{1,0:T(8,128)(2,1)} %bitcast.287), channel_id=1, source_target_pairs={{0,1},{1,0},{2,3},{3,2},{4,5},{5,4},{6,7},{7,6},{8,9},{9,8},{10,11... | collective-permute-start | bytes 1244168 | tf_op jit(solution)/shard_map/ppermute | solution.py:47
  643.5 21.7 %all-to-all-start.3 = ((f32[32,1,1656]{2,1,0:T(1,128)}), f32[32,1,1656]{2,1,0:T(1,128)S(1)}, u32[]{:S(2)}, u32[]{:S(2)}) async-start(f32[32,1,1656]{2,1,0:T(1,128)} %all_to_all.22), calls=%async_computation.4 | async-start | bytes 425984 | tf_op jit(solution)/shard_map/all_to_all | solution.py:319
  756.8 18.6 %collective-permute-start.33 = (f32[4,2,160,128]{3,2,1,0:T(8,128)S(1)}, f32[4,2,160,128]{3,2,1,0:T(8,128)S(1)}, u32[]{:S(2)}, u32[]{:S(2)}) collective-permute-start(f32[4,2,160,128]{3,2,1,0:T(8,128)S(1)} %pad_maximum_fusion.5.refs_1_.refs_0_), channel_id=1, source_target_pairs={{0,2},{2,0},{4,6},{6,4},{8,10},{10,8},{12,14},{14,12},{16,18},{18,... | collective-permute-start | bytes 1966088 | tf_op jit(solution)/shard_map/ppermute | solution.py:47
  (122 other events, 890.1 us)
Sparse Core Ops, SparseCore 0:
  122.8 88.7 all-gather.2
  214.4 86.8 all-gather.4
  306.2 121.9 reduce-scatter.7
  432.2 139.2 reduce-scatter.9
  575.4 105.4 reduce-scatter.11

commit v10 on v9

--- a/solution.py
+++ b/solution.py
@@ -350,14 +350,20 @@
 GELU_CUBE = 0.044715
 
 
+def row_parts(rows):
+    step = rows // 4 if rows % 64 == 0 else rows
+    return [slice(start, start + step) for start in range(0, rows, step)]
+
+
 def hidden_kernel(x_ref, w_ref, b_ref, act_ref, slope_ref):
-    value = nt(x_ref[...], w_ref[...]) + b_ref[...]
-    square = value * value
-    bend = jnp.tanh(value * (GELU_SCALE + (GELU_SCALE * GELU_CUBE) * square))
-    half = 0.5 + 0.5 * bend
-    act_ref[...] = (value * half).astype(BF)
-    steep = (0.5 * value) * (GELU_SCALE + (3.0 * GELU_SCALE * GELU_CUBE) * square)
-    slope_ref[...] = (half + steep * (1.0 - bend * bend)).astype(BF)
+    for part in row_parts(x_ref.shape[0]):
+        value = nt(x_ref[part], w_ref[...]) + b_ref[...]
+        square = value * value
+        bend = jnp.tanh(value * (GELU_SCALE + (GELU_SCALE * GELU_CUBE) * square))
+        half = 0.5 + 0.5 * bend
+        act_ref[part] = (value * half).astype(BF)
+        steep = (0.5 * value) * (GELU_SCALE + (3.0 * GELU_SCALE * GELU_CUBE) * square)
+        slope_ref[part] = (half + steep * (1.0 - bend * bend)).astype(BF)
 
 
 def hidden_forward(x, w, bias):
@@ -384,9 +390,12 @@
 
 
 def hidden_back_kernel(g_ref, w_ref, slope_ref, out_ref, bias_ref):
-    grad = (nn(g_ref[...], w_ref[...]) * slope_ref[...].astype(F32)).astype(BF)
-    out_ref[...] = grad
-    bias_ref[...] = jnp.sum(grad.astype(F32), axis=0, keepdims=True)
+    total = 0.0
+    for part in row_parts(g_ref.shape[0]):
+        grad = (nn(g_ref[part], w_ref[...]) * slope_ref[part].astype(F32)).astype(BF)
+        out_ref[part] = grad
+        total = total + jnp.sum(grad.astype(F32), axis=0, keepdims=True)
+    bias_ref[...] = total
 
 
 def hidden_backward(grad, w, slope):
@@ -564,12 +573,16 @@
     depth = width // heads
     factor = depth**-0.5 * LOG2E
     mask = mask_column(lengths_ref, offsets_ref, pl.program_id(0), total, rows)
-    ones = jnp.ones((rows, 1), F32)
+    q_blank = padded(jnp.zeros((rows, depth), BF), jnp.ones((rows, 1), F32))
+    k_blank = padded(jnp.zeros((total, depth), BF), mask)
+    turned = jnp.transpose(v_ref[0].astype(F32))
     for h in range(heads):
         span = slice(h * depth, (h + 1) * depth)
-        q_s[h] = padded(q_ref[0, :, span], ones)
-        k_s[h] = padded(k_ref[0, :, span], mask)
-        vt_s[h] = jnp.transpose(v_ref[0, :, span])
+        q_s[h] = q_blank
+        k_s[h] = k_blank
+        q_s[h, :, :depth] = q_ref[0, :, span]
+        k_s[h, :, :depth] = k_ref[0, :, span]
+        vt_s[h] = turned[span].astype(BF)
 
     def one_head(h, carry):
         peak = jnp.full((1, rows), MASKED, F32)
@@ -680,20 +693,21 @@
         dv_ref[0, :, span] = dv_s[h][:, :depth]
 
 
-def attend_back(lengths, offsets, queries, keys, values, mixed, grads, lse, heads, tile, deps=()):
+def attend_back(lengths, offsets, queries, keys, values, mixed, grads, sample, lse, heads, tile, deps=()):
     count, rows, width = queries.shape
     total = keys.shape[1]
     depth = width // heads
     tile = min(tile, total)
     pick = lambda i, *_: (i, 0, 0)
     near = pl.BlockSpec((1, rows, width), pick)
+    picked = pl.BlockSpec((1, rows, width), lambda i, *_: (sample + i, 0, 0))
     far = pl.BlockSpec((1, total, width), pick)
     return pl.pallas_call(
         without(attend_back_kernel, 8, len(deps), heads, tile),
         grid_spec=pltpu.PrefetchScalarGridSpec(
             num_scalar_prefetch=2,
             grid=(count,),
-            in_specs=[near, far, far, near, near, pl.BlockSpec((1, heads, 1, rows), lambda i, *_: (i, 0, 0, 0))]
+            in_specs=[near, far, far, near, picked, pl.BlockSpec((1, heads, 1, rows), lambda i, *_: (i, 0, 0, 0))]
             + [pl.BlockSpec(memory_space=pl.ANY)] * len(deps),
             out_specs=[near, far, far],
             scratch_shapes=[
@@ -914,7 +928,16 @@
     shift_one, scale_one, gate_one, shift_two, scale_two, gate_two = jnp.split(
         modulation[:, None, :], 6, axis=-1
     )
-    t_qkv, t_proj = first.finish(modulation)[0]
+    first.advance(modulation)
+    norms, attn_all = [], []
+
+    def norm_one(i):
+        normed, inverse = layer_norm(jnp.concatenate(token_pieces[i], axis=0).astype(F32))
+        norms.append((normed[:rows], inverse[:rows]))
+        attn_all.append((normed * (1.0 + scale_one[i]) + shift_one[i]).astype(BF))
+
+    norm_one(0)
+    t_qkv, t_proj = first.finish(attn_all[0])[0]
     wires = net.y.gather(tie(net.wire([w_fc1]), token_pieces[0][-1], *sent))
     wires = wires[:1] + [tie(wire, t_qkv) for wire in wires[1:]]
     t_fc1 = lax.all_gather(net.rows(wires), "dp", axis=0, tiled=True)
@@ -923,10 +946,11 @@
 
     lengths = (heights * widths).reshape(count).astype(jnp.int32)
     offsets = jnp.stack([((y + s) % seq) * rows for s in range(seq)]).astype(jnp.int32)
-    normed_all, inverse_all, attn_all, queries, keys, values, attended_low, log_total = [[] for _ in range(8)]
+    queries, keys, values, attended, log_total = [[] for _ in range(5)]
     for i in range(count):
-        normed, inverse = layer_norm(jnp.concatenate(token_pieces[i], axis=0).astype(F32))
-        attn = (normed * (1.0 + scale_one[i]) + shift_one[i]).astype(BF)
+        if i > 0:
+            norm_one(i)
+        attn = attn_all[i]
         queries.append((dot_t(attn[None, :rows], t_qkv[:width]) + b_q).astype(BF))
         keys.append(dot_t(attn[None], t_qkv[width : 2 * width]).astype(BF))
         values.append((dot_t(attn[None], t_qkv[2 * width :]) + b_v).astype(BF))
@@ -935,14 +959,11 @@
             token_pieces[1:] = [each[:1] + [tie(a, mixed) for a in each[1:]] for each in token_pieces[1:]]
             last_piece = token_pieces[-1][-1] if count > 1 else mixed
             wires = net.y.gather(tie(net.wire([w_fc2]), last_piece))
-        normed_all.append(normed[:rows])
-        inverse_all.append(inverse[:rows])
-        attn_all.append(attn)
-        attended_low.append(mixed[0])
+        attended.append(mixed)
         log_total.append(lse)
     wires = wires[:1] + [tie(wire, keys[-1]) for wire in wires[1:]]
     t_fc2 = lax.all_gather(net.rows(wires), "dp", axis=0, tiled=True)
-    attended_low = jnp.stack(attended_low)
+    attended_low = jnp.concatenate(attended, axis=0)
 
     inputs = own_tokens.astype(F32)
     branch_one = dot_t(attended_low, t_proj) + b_proj
@@ -996,8 +1017,8 @@
     sent = []
     for i in range(count):
         dq, dk, dv = attend_back(
-            lengths[i : i + 1], offsets, queries[i], keys[i], values[i], attended_low[i : i + 1],
-            grad_attended[i : i + 1], log_total[i], HEADS, 512, sent,
+            lengths[i : i + 1], offsets, queries[i], keys[i], values[i], attended[i],
+            grad_attended, i, log_total[i], HEADS, 512, sent,
         )
         sent = []
         grad_q.append(dq)
@@ -1025,27 +1046,27 @@
     grad_q[0] = tie(grad_q[0], *sent)
     bias_q = sum(jnp.sum(each.astype(F32), axis=(0, 1)) for each in grad_q)
     bias_v = sum(jnp.sum(each.astype(F32), axis=(0, 1)) for each in grad_v)
-    own_part = jnp.concatenate(
-        [
-            dot(grad_q[i], t_qkv[:width])
-            + dot(grad_k[i][:, :rows], t_qkv[width : 2 * width])
-            + dot(grad_v[i][:, :rows], t_qkv[2 * width :])
-            for i in range(count)
-        ],
-        axis=0,
-    )
+    own_part = [
+        dot(grad_q[i], t_qkv[:width])
+        + dot(grad_k[i][:, :rows], t_qkv[width : 2 * width])
+        + dot(grad_v[i][:, :rows], t_qkv[2 * width :])
+        for i in range(count)
+    ]
+    grad_shift_one, grad_scale_one, grad_inputs = [], [], []
+    for i, (normed, inverse) in enumerate(norms):
+        grad_attn_in = own_part[i][0] + far_parts[i].finish()
+        grad_shift_one.append(jnp.sum(grad_attn_in, axis=0))
+        grad_scale_one.append(jnp.sum(grad_attn_in * normed, axis=0))
+        grad_in = grad_mixed[i] + norm_back(normed, inverse, grad_attn_in * (1.0 + scale_one[i]))
+        grad_inputs.append(grad_in.astype(BF))
+    grad_shift_one, grad_scale_one = jnp.stack(grad_shift_one), jnp.stack(grad_scale_one)
+    grad_inputs = jnp.stack(grad_inputs).reshape(tokens.shape)
+
     matrices = (w_qkv, w_proj, w_fc1, w_fc2, w_ada)
     per = -(-sum(matrix.shape[0] // ROW_BLOCK for matrix in matrices) // dp)
     spread_early = (per, 0)
     early_blocks = (w_fc2.shape[0] + w_fc1.shape[0] + w_proj.shape[0]) // ROW_BLOCK
     spread_last = (per, -(-early_blocks // per))
-    far_sum = jnp.stack([steps_of.finish() for steps_of in far_parts])
-    grad_attn_in = own_part + far_sum
-    normed_one, inverse_one = jnp.stack(normed_all), jnp.stack(inverse_all)
-    grad_shift_one = jnp.sum(grad_attn_in, axis=1)
-    grad_scale_one = jnp.sum(grad_attn_in * normed_one, axis=1)
-    grad_inputs = grad_mixed + norm_back(normed_one, inverse_one, grad_attn_in * (1.0 + scale_one))
-    grad_inputs = grad_inputs.astype(BF).reshape(tokens.shape)
 
     grad_mod_local = jnp.concatenate(
         [grad_shift_one, grad_scale_one, grad_gate_one, grad_shift_two, grad_scale_two, grad_gate_two], axis=-1

time: 804 us -> 828 us (1.030)
  waiting for transfers between devices: 132 us -> 142 us
  other arithmetic: 66.3 us -> 74.7 us
    ppermute x35, waiting for transfers between devices: 76.6 us -> 105 us  [send(): return lax.ppermute(value, self.name, pairs)]
    unnamed x7, waiting for transfers between devices: 14.5 us -> 0.09 us
    all_to_all x4, waiting for transfers between devices: 17.6 us -> 5.34 us  [to_all(): lax.all_to_all(flat, ('dp', 'seq'), 0, 0, tiled=True).reshape(value.shape)]
    unnamed x214 -> x220, local copies, waits for them, and re-layouts: 26.5 us -> 30.8 us
  transfers between devices with their start and end apart: 44 -> 44, of which waited for: 19 -> 17; matrix products, arithmetic and copies ran while one was open for 33% -> 34% of each run, Pallas kernels for 32% -> 31%
where the time goes in v10:
time: 828 us; the launch traced here: 817 us
  Pallas kernels  278 us (34%)
  matrix products  162 us (20%)
  waiting for transfers between devices  142 us (17%)
  local copies, waits for them, and re-layouts  77.3 us (9%)
  other arithmetic  74.7 us (9%)
  starting transfers between devices  67.4 us (8%)
  between operations  15.7 us (2%)
    ppermute x35, waiting for transfers between devices, send(): return lax.ppermute(value, self.name, pairs)  105 us
    pallas_call x2, Pallas kernels, attend_back(): pl.pallas_call(without(attend_back_kernel, 8, len(deps), heads, tile), gr...  84.4 us
    dot_general x12, matrix products, dot(): return jnp.einsum('srn,nk->srk', left, right, preferred_element_type=F32)  72.4 us
    dot_general x8, matrix products, dot_t(): return jnp.einsum('srk,nk->srn', left, right, preferred_element_type=F32)  69.6 us
    pallas_call x2, Pallas kernels, attend(): pl.pallas_call(without(attend_kernel, 5, len(deps), heads, tile), grid_sp...  58.1 us
    pallas_call x2, Pallas kernels, shard_outer(): pl.pallas_call(functools.partial(shard_outer_kernel, {'loads': loads, 'pa...  48.4 us
    ppermute x35, starting transfers between devices, send(): return lax.ppermute(value, self.name, pairs)  40.2 us
    unnamed x220, local copies, waits for them, and re-layouts  30.8 us
  transfers between devices with their start and end apart: 44, of which 17 were waited for; matrix products, arithmetic and copies ran while one was open for 34% of the time, Pallas kernels for 31%

profile of v10, /device:TPU:11, one launch (start us, length us, event | category | flops | bytes accessed | tf_op | source)
XLA Modules:
  0.0 817.2 jit_solution(12129488372366283524)
XLA Ops:
  47.2 8.0 all-to-all-start.1
  57.2 30.1 %collective-permute-done.1.refs_0_ = bf16[16,8,1152]{2,1,0:T(8,128)(2,1)} collective-permute-done((bf16[16,8,1152]{2,1,0:T(8,128)(2,1)S(1)}, bf16[16,8,1152]{2,1,0:T(8,128)(2,1)}, u32[]{:S(2)}, u32[]{:S(2)}) %collective-permute-start.1) | collective-permute-done | bytes 294944 | tf_op jit(solution)/shard_map/ppermute | solution.py:47
  110.1 7.3 collective-permute-done.7.refs_0_
  133.0 9.1 %place.1 = (bf16[4,2,2,27,8,1152]{5,4,3,2,1,0:T(8,128)(2,1)}, bf16[4,2,2,9,8,1152]{5,4,3,2,1,0:T(8,128)(2,1)}) custom-call(s32[3]{0:T(128)} %pad_add_fusion.1.refs_0_.spots_ref, bf16[4,16,8,1152]{3,2,1,0:T(8,128)(2,1)} %copy-done.4, bf16[4,16,8,1152]{3,2,1,0:T(8,128)(2,1)} %tie.61.refs_2_, bf16[2,20,8,1152]{3,2,1,0:T(8,128)(2,1)} %pad_maximum_fusion.3.refs_3_, ...), custom_call_target="tpu_custom_call" | custom-call | bytes 21233664 | tf_op jit(solution)/shard_map/place/pallas_call | solution.py:198
  166.5 29.2 %attend.2 = (bf16[1,512,1152]{2,1,0:T(8,128)(2,1)}, f32[1,16,1,512]{3,2,1,0:T(1,128)}) custom-call(s32[1]{0:T(128)} %bitcast.17.refs_0_, s32[2]{0:T(128)} %pad_add_fusion.refs_1_, bf16[1,512,1152]{2,1,0:T(8,128)(2,1)} %fusion.25.refs_2_, bf16[1,1024,1152]{2,1,0:T(8,128)(2,1)} %fusion.18.refs_3_, bf16[1,1024,1152]{2,1,0:T(8,128)(2,1)} %fusion.16.refs_4_), custom_call_target="tpu_custom_call" | custom-call | flops 4294967296 | bytes 7077888 | tf_op jit(solution)/shard_map/attend/pallas_call | solution.py:619
  202.8 7.4 fusion.19.refs_3_.refs_1_
  230.0 29.0 %attend.3 = (bf16[1,512,1152]{2,1,0:T(8,128)(2,1)}, f32[1,16,1,512]{3,2,1,0:T(1,128)}) custom-call(s32[1]{0:T(128)} %bitcast.28.refs_0_, s32[2]{0:T(128)} %pad_add_fusion.refs_1_, bf16[1,512,1152]{2,1,0:T(8,128)(2,1)} %fusion.24.refs_2_, bf16[1,1024,1152]{2,1,0:T(8,128)(2,1)} %fusion.19.refs_3_.refs_1_, bf16[1,1024,1152]{2,1,0:T(8,128)(2,1)} %fusion.17.refs_4_), custom_call_target="tpu_custom_call" | custom-call | flops 4294967296 | bytes 7077888 | tf_op jit(solution)/shard_map/attend/pallas_call | solution.py:619
  261.6 8.4 %fusion.90 = (f32[2,512]{1,0:T(2,128)S(1)}, f32[2,512,1152]{2,1,0:T(8,128)S(1)}, f32[2,512,1152]{2,1,0:T(8,128)}) fusion(f32[2,1152]{1,0:T(2,128)S(1)} %get-tuple-element.215, bf16[2,1,512,1152]{3,2,1,0:T(8,128)(2,1)S(1)} %copy-done.35, f32[1152]{0:T(1024)S(1)} %copy-done.85, bf16[2,512,1152]{2,1,0:T(8,128)(2,1)} %constant_dynamic-update-slice_fusion, ...), kind=kOutput, calls=%fused_computation.223 | convolution fusion | flops 2723806208 | bytes 16827904 | tf_op jit(solution)/shard_map/srk,nk->srn/dot_general | solution.py:342
  274.3 25.3 %hidden_forward.1 = (bf16[1024,4608]{1,0:T(8,128)(2,1)}, bf16[1024,4608]{1,0:T(8,128)(2,1)}) custom-call(bf16[1024,1152]{1,0:T(8,128)(2,1)} %bitcast.292, bf16[4608,1152]{1,0:T(8,128)(2,1)} %all-gather.3.cloned.1.call-done.w_ref, f32[1,4608]{1,0:T(1,128)} %reshape.559.b_ref), custom_call_target="tpu_custom_call" | custom-call | flops 10871635968 | bytes 31850496 | tf_op jit(solution)/shard_map/hidden_forward/pallas_call | solution.py:374
  299.7 17.1 %fusion.refs_1_ = bf16[1152,4608]{1,0:T(8,128)(2,1)} fusion(bf16[2,512,1152]{2,1,0:T(8,128)(2,1)S(1)} %fusion.14.refs_0_, bf16[2,512,4608]{2,1,0:T(8,128)(2,1)} %bitcast.262), kind=kOutput, calls=%fused_computation.1 | convolution fusion | flops 10876944384 | bytes 22413312 | tf_op jit(solution)/shard_map/srn,srk->nk/dot_general | solution.py:426
  324.1 20.4 %hidden_backward.1 = (bf16[1024,4608]{1,0:T(8,128)(2,1)}, f32[1,4608]{1,0:T(1,128)}) custom-call(bf16[1024,1152]{1,0:T(8,128)(2,1)} %bitcast.256, bf16[1152,4608]{1,0:T(8,128)(2,1)} %all-gather.5.cloned.1.call-done.w_ref, bf16[1024,4608]{1,0:T(8,128)(2,1)} %get-tuple-element.51.slope_ref), custom_call_target="tpu_custom_call" | custom-call | flops 10871635968 | bytes 31850496 | tf_op jit(solution)/shard_map/hidden_backward/pallas_call | solution.py:406
  344.5 23.3 %multiply_reduce_fusion = (f32[2,1152]{1,0:T(2,128)}, f32[2,512]{1,0:T(2,128)S(1)}, f32[2,512]{1,0:T(2,128)S(1)}, f32[2,1152]{1,0:T(2,128)}, f32[2,512,1152]{2,1,0:T(8,128)}) fusion(f32[2,512,1152]{2,1,0:T(8,128)} %copy-done.10, f32[2,512]{1,0:T(2,128)S(1)} %add_rsqrt_fusion, f32[2,512]{1,0:T(2,128)S(1)} %broadcast_multiply_fusion.2, ...), kind=kOutput, calls=%fused_computation.27 | convolution fusion | flops 10882246656 | bytes 29535232 | tf_op jit(solution)/shard_map/srn,nk->srk/dot_general | solution.py:346
  367.8 24.4 %fusion.15 = (f32[2,1152]{1,0:T(2,128)}, bf16[2,1,512,1152]{3,2,1,0:T(8,128)(2,1)}, f32[1152]{0:T(1024)}, bf16[2,512,1152]{2,1,0:T(8,128)(2,1)}, f32[2,512,1152]{2,1,0:T(8,128)}) fusion(bf16[2,1,512,1152]{3,2,1,0:T(8,128)(2,1)S(1)} %copy-done.41, f32[2,512,1152]{2,1,0:T(8,128)} %copy-done.10, f32[2,1152]{1,0:T(2,128)S(1)} %get-tuple-element.212, ...), kind=kOutput, calls=%fused_computation.21 | convolution fusion | flops 10894046208 | bytes 41350144 | tf_op jit(solution)/shard_map/srk,nk->srn/dot_general | solution.py:342
  392.2 7.3 convolution_convert_fusion.refs_2_.refs_0_
  399.5 23.4 %shard_outer.2.refs_0_ = bf16[4,2,2,45,8,1152]{5,4,3,2,1,0:T(8,128)(2,1)} custom-call(s32[3]{0:T(128)} %pad_add_fusion.1.refs_0_.spots_ref, bf16[1024,4608]{1,0:T(8,128)(2,1)} %get-tuple-element.52.refs_0_, bf16[1024,1152]{1,0:T(8,128)(2,1)} %bitcast.293, bf16[1024,1152]{1,0:T(8,128)(2,1)} %bitcast.331, bf16[1024,1152]{1,0:T(8,128)(2,1)} %bitcast.313), custom_call_target="tpu_custom_call" | custom-call | flops 13589544960 | bytes 13271040 | tf_op jit(solution)/shard_map/shard_outer/pallas_call | solution.py:516
  423.0 25.1 %reduce-scatter.8.cloned.1.call-done.refs_1_.refs_0_ = bf16[72,4608]{1,0:T(8,128)(2,1)} async-done(((bf16[1152,4608]{1,0:T(8,128)(2,1)}), bf16[72,4608]{1,0:T(8,128)(2,1)}) %reduce-scatter.8.cloned.1.call-update) | async-done | bytes 663568 | tf_op jit(solution)/shard_map/reduce_scatter | solution.py:249
  452.9 42.3 %attend_back.2 = (bf16[1,512,1152]{2,1,0:T(8,128)(2,1)}, bf16[1,1024,1152]{2,1,0:T(8,128)(2,1)}, bf16[1,1024,1152]{2,1,0:T(8,128)(2,1)}) custom-call(s32[1]{0:T(128)} %bitcast.17.refs_0_, s32[2]{0:T(128)} %pad_add_fusion.refs_1_, bf16[1,512,1152]{2,1,0:T(8,128)(2,1)} %fusion.25.refs_2_, bf16[1,1024,1152]{2,1,0:T(8,128)(2,1)} %fusion.18.refs_3_, ...), custom_call_target="tpu_custom_call" | custom-call | flops 10737418240 | bytes 14155776 | tf_op jit(solution)/shard_map/attend_back/pallas_call | solution.py:705
  504.1 42.1 %attend_back.3 = (bf16[1,512,1152]{2,1,0:T(8,128)(2,1)}, bf16[1,1024,1152]{2,1,0:T(8,128)(2,1)}, bf16[1,1024,1152]{2,1,0:T(8,128)(2,1)}) custom-call(s32[1]{0:T(128)} %bitcast.28.refs_0_, s32[2]{0:T(128)} %pad_add_fusion.refs_1_, bf16[1,512,1152]{2,1,0:T(8,128)(2,1)} %fusion.24.refs_2_, bf16[1,1024,1152]{2,1,0:T(8,128)(2,1)} %fusion.19.refs_3_.refs_1_, ...), custom_call_target="tpu_custom_call" | custom-call | flops 10737418240 | bytes 14155776 | tf_op jit(solution)/shard_map/attend_back/pallas_call | solution.py:705
  546.1 25.0 %shard_outer.3.refs_1_ = bf16[4,2,2,27,8,1152]{5,4,3,2,1,0:T(8,128)(2,1)} custom-call(s32[3]{0:T(128)} %pad_add_fusion.1.refs_0_.spots_ref, bf16[512,1152]{1,0:T(8,128)(2,1)} %bitcast.283, bf16[512,1152]{1,0:T(8,128)(2,1)} %bitcast.302, bf16[1024,1152]{1,0:T(8,128)(2,1)} %bitcast.330, bf16[1024,1152]{1,0:T(8,128)(2,1)} %bitcast.296, ...), custom_call_target="tpu_custom_call" | custom-call | flops 13589544960 | bytes 7962624 | tf_op jit(solution)/shard_map/shard_outer/pallas_call | solution.py:516
  606.2 25.3 %collective-permute-done.20 = bf16[512,1152]{1,0:T(8,128)(2,1)} collective-permute-done((bf16[512,1152]{1,0:T(8,128)(2,1)S(1)}, bf16[512,1152]{1,0:T(8,128)(2,1)}, u32[]{:S(2)}, u32[]{:S(2)}) %collective-permute-start.20) | collective-permute-done | bytes 1179680 | tf_op jit(solution)/shard_map/ppermute | solution.py:47
  694.8 7.4 muon_gram.2
  730.0 8.6 %collective-permute-done.25.refs_0_ = bf16[4,2,160,128]{3,2,1,0:T(8,128)(2,1)S(1)} collective-permute-done((bf16[4,2,160,128]{3,2,1,0:T(8,128)(2,1)S(1)}, bf16[4,2,160,128]{3,2,1,0:T(8,128)(2,1)S(1)}, u32[]{:S(2)}, u32[]{:S(2)}) %collective-permute-start.25) | collective-permute-done | bytes 327712 | tf_op jit(solution)/shard_map/ppermute | solution.py:47
  750.2 7.8 polynomial.1.refs_1_
  799.3 10.9 %muon_apply.1 = (f32[72,2304]{1,0:T(8,128)}, f32[72,576]{1,0:T(8,128)}, f32[288,576]{1,0:T(8,128)}, f32[216,576]{1,0:T(8,128)}, f32[432,576]{1,0:T(8,128)}) custom-call(s32[3]{0:T(128)} %pad_add_fusion.1.refs_0_.spots_ref, f32[4,2,160,128]{3,2,1,0:T(8,128)} %copy-done.13, f32[4,2,160,128]{3,2,1,0:T(8,128)} %tie.99.refs_1_, f32[4,2,160,128]{3,2,1,0:T(8,128)} %tie.100.refs_2_, ...), custom_call_target="tpu_custom_call" | custom-call | tf_op jit(solution)/shard_map/muon_apply/pallas_call | solution.py:875
  (513 shorter events, 337.4 us)
Async XLA Ops:
  22.2 23.8 %collective-permute-start.2 = (bf16[16,8,1152]{2,1,0:T(8,128)(2,1)S(1)}, bf16[16,8,1152]{2,1,0:T(8,128)(2,1)S(1)}, u32[]{:S(2)}, u32[]{:S(2)}) collective-permute-start(bf16[16,8,1152]{2,1,0:T(8,128)(2,1)S(1)} %get-tuple-element.202.refs_1_.refs_2_), channel_id=1, source_target_pairs={{0,8},{2,10},{4,12},{6,14},{8,16},{10,18},{12,20},{14,22},{16,24},... | collective-permute-start | bytes 884744 | tf_op jit(solution)/shard_map/ppermute | solution.py:47
  35.3 55.4 %collective-permute-start.5 = (bf16[2,20,8,1152]{3,2,1,0:T(8,128)(2,1)}, bf16[2,20,8,1152]{3,2,1,0:T(8,128)(2,1)}, u32[]{:S(2)}, u32[]{:S(2)}) collective-permute-start(bf16[2,20,8,1152]{3,2,1,0:T(8,128)(2,1)} %pad_maximum_fusion.3.refs_3_), channel_id=1, source_target_pairs={{0,24},{2,26},{4,28},{6,30},{8,0},{10,2},{12,4},{14,6},{16,8},{18,... | collective-permute-start | bytes 2211848 | tf_op jit(solution)/shard_map/ppermute | solution.py:47
  41.3 50.9 %collective-permute-start.9 = (bf16[2,20,8,1152]{3,2,1,0:T(8,128)(2,1)}, bf16[2,20,8,1152]{3,2,1,0:T(8,128)(2,1)}, u32[]{:S(2)}, u32[]{:S(2)}) collective-permute-start(bf16[2,20,8,1152]{3,2,1,0:T(8,128)(2,1)} %pad_maximum_fusion.3.refs_3_), channel_id=1, source_target_pairs={{0,8},{2,10},{4,12},{6,14},{8,16},{10,18},{12,20},{14,22},{16,24},... | collective-permute-start | bytes 2211848 | tf_op jit(solution)/shard_map/ppermute | solution.py:47
  44.5 42.8 %collective-permute-start.1 = (bf16[16,8,1152]{2,1,0:T(8,128)(2,1)S(1)}, bf16[16,8,1152]{2,1,0:T(8,128)(2,1)}, u32[]{:S(2)}, u32[]{:S(2)}) collective-permute-start(bf16[16,8,1152]{2,1,0:T(8,128)(2,1)S(1)} %copy-done.18), channel_id=1, source_target_pairs={{0,24},{2,26},{4,28},{6,30},{8,0},{10,2},{12,4},{14,6},{16,8},{18,... | collective-permute-start | bytes 884744 | tf_op jit(solution)/shard_map/ppermute | solution.py:47
  46.7 41.9 %collective-permute-start.3 = (bf16[16,8,1152]{2,1,0:T(8,128)(2,1)}, bf16[16,8,1152]{2,1,0:T(8,128)(2,1)S(1)}, u32[]{:S(2)}, u32[]{:S(2)}) collective-permute-start(bf16[16,8,1152]{2,1,0:T(8,128)(2,1)} %tie.54), channel_id=1, source_target_pairs={{0,8},{2,10},{4,12},{6,14},{8,16},{10,18},{12,20},{14,22},{16,24},... | collective-permute-start | bytes 884744 | tf_op jit(solution)/shard_map/ppermute | solution.py:47
  47.2 41.4 %all-to-all-start.1 = ((f32[32,2,432]{2,1,0:T(2,128)}), f32[32,2,432]{2,1,0:T(2,128)S(1)}, u32[]{:S(2)}, u32[]{:S(2)}) async-start(f32[32,2,432]{2,1,0:T(2,128)} %bitcast.7), calls=%async_computation.1 | async-start | bytes 262144 | tf_op jit(solution)/shard_map/all_to_all | solution.py:319
  55.2 219.1 %all-gather.3.cloned.1.call-start = ((), (), s32[]{:S(2)}) async-start(), calls=%async_computation.7 | async-start | bytes 11280384 | tf_op jit(solution)/shard_map/all_gather | solution.py:943
  56.1 49.6 %collective-permute-start.6 = (bf16[512,1152]{1,0:T(8,128)(2,1)}, bf16[512,1152]{1,0:T(8,128)(2,1)S(1)}, u32[]{:S(2)}, u32[]{:S(2)}) collective-permute-start(bf16[512,1152]{1,0:T(8,128)(2,1)} %tie.60), channel_id=1, source_target_pairs={{0,1},{1,0},{2,3},{3,2},{4,5},{5,4},{6,7},{7,6},{8,9},{9,8},{10,11... | collective-permute-start | bytes 3538952 | tf_op jit(solution)/shard_map/ppermute | solution.py:47
  87.3 38.1 %collective-permute-start.12 = (bf16[2,20,8,1152]{3,2,1,0:T(8,128)(2,1)}, bf16[2,20,8,1152]{3,2,1,0:T(8,128)(2,1)}, u32[]{:S(2)}, u32[]{:S(2)}) collective-permute-start(bf16[2,20,8,1152]{3,2,1,0:T(8,128)(2,1)} %pad_maximum_fusion.3.refs_3_), channel_id=1, source_target_pairs={{0,2},{2,0},{4,6},{6,4},{8,10},{10,8},{12,14},{14,12},{16,18},{18,... | collective-permute-start | bytes 2211848 | tf_op jit(solution)/shard_map/ppermute | solution.py:47
  90.6 26.8 %collective-permute-start.7 = (bf16[4,16,8,1152]{3,2,1,0:T(8,128)(2,1)S(1)}, bf16[4,16,8,1152]{3,2,1,0:T(8,128)(2,1)}, u32[]{:S(2)}, u32[]{:S(2)}) collective-permute-start(bf16[4,16,8,1152]{3,2,1,0:T(8,128)(2,1)S(1)} %pad_maximum_fusion.2.refs_1_.refs_2_), channel_id=1, source_target_pairs={{0,4},{2,6},{4,0},{6,2},{8,12},{10,14},{12,8},{14,10},{16,20},{18,... | collective-permute-start | bytes 3538952 | tf_op jit(solution)/shard_map/ppermute | solution.py:47
  90.7 36.4 %collective-permute-start.10 = (bf16[4,16,8,1152]{3,2,1,0:T(8,128)(2,1)S(1)}, bf16[4,16,8,1152]{3,2,1,0:T(8,128)(2,1)}, u32[]{:S(2)}, u32[]{:S(2)}) collective-permute-start(bf16[4,16,8,1152]{3,2,1,0:T(8,128)(2,1)S(1)} %pad_maximum_fusion.2.refs_1_.refs_2_), channel_id=1, source_target_pairs={{0,2},{2,0},{4,6},{6,4},{8,10},{10,8},{12,14},{14,12},{16,18},{18,... | collective-permute-start | bytes 3538952 | tf_op jit(solution)/shard_map/ppermute | solution.py:47
  92.2 39.9 %collective-permute-start.15 = (bf16[2,20,8,1152]{3,2,1,0:T(8,128)(2,1)}, bf16[2,20,8,1152]{3,2,1,0:T(8,128)(2,1)}, u32[]{:S(2)}, u32[]{:S(2)}) collective-permute-start(bf16[2,20,8,1152]{3,2,1,0:T(8,128)(2,1)} %tie.63.refs_6_), channel_id=1, source_target_pairs={{0,2},{2,0},{4,6},{6,4},{8,10},{10,8},{12,14},{14,12},{16,18},{18,... | collective-permute-start | bytes 2211848 | tf_op jit(solution)/shard_map/ppermute | solution.py:47
  105.7 19.0 %collective-permute-start.8 = (bf16[2,20,8,1152]{3,2,1,0:T(8,128)(2,1)}, bf16[2,20,8,1152]{3,2,1,0:T(8,128)(2,1)}, u32[]{:S(2)}, u32[]{:S(2)}) collective-permute-start(bf16[2,20,8,1152]{3,2,1,0:T(8,128)(2,1)} %tie.57.refs_2_.refs_4_.refs_3_), channel_id=1, source_target_pairs={{0,24},{2,26},{4,28},{6,30},{8,0},{10,2},{12,4},{14,6},{16,8},{18,... | collective-permute-start | bytes 2211848 | tf_op jit(solution)/shard_map/ppermute | solution.py:47
  145.6 178.5 %all-gather.5.cloned.1.call-start = ((), (), s32[]{:S(2)}) async-start(), calls=%async_computation.8 | async-start | bytes 11280384 | tf_op jit(solution)/shard_map/all_gather | solution.py:965
  148.5 47.2 %collective-permute-start.17 = (bf16[512,1152]{1,0:T(8,128)(2,1)}, bf16[512,1152]{1,0:T(8,128)(2,1)S(1)}, u32[]{:S(2)}, u32[]{:S(2)}) collective-permute-start(bf16[512,1152]{1,0:T(8,128)(2,1)} %tie.72), channel_id=1, source_target_pairs={{0,1},{1,0},{2,3},{3,2},{4,5},{5,4},{6,7},{7,6},{8,9},{9,8},{10,11... | collective-permute-start | bytes 3538952 | tf_op jit(solution)/shard_map/ppermute | solution.py:47
  213.4 234.6 %reduce-scatter.8.cloned.1.call-start = ((), (), s32[]{:S(2)}) async-start(), calls=%async_computation.9 | async-start | bytes 11280384 | tf_op jit(solution)/shard_map/reduce_scatter | solution.py:249
  316.8 321.2 %reduce-scatter.10.cloned.1.call-start = ((), (), s32[]{:S(2)}) async-start(), calls=%async_computation.10 | async-start | bytes 14100480
  448.0 255.5 %reduce-scatter.12.cloned.1.call-start = ((), (), s32[]{:S(2)}) async-start(), calls=%async_computation.11 | async-start | bytes 8460288
  579.3 71.7 %collective-permute-start.19 = (bf16[512,1152]{1,0:T(8,128)(2,1)}, bf16[512,1152]{1,0:T(8,128)(2,1)}, u32[]{:S(2)}, u32[]{:S(2)}) collective-permute-start(bf16[512,1152]{1,0:T(8,128)(2,1)} %fusion.22.refs_8_), channel_id=1, source_target_pairs={{0,1},{1,0},{2,3},{3,2},{4,5},{5,4},{6,7},{7,6},{8,9},{9,8},{10,11... | collective-permute-start | bytes 3538952 | tf_op jit(solution)/shard_map/ppermute | solution.py:47
  588.3 43.3 %collective-permute-start.20 = (bf16[512,1152]{1,0:T(8,128)(2,1)S(1)}, bf16[512,1152]{1,0:T(8,128)(2,1)}, u32[]{:S(2)}, u32[]{:S(2)}) collective-permute-start(bf16[512,1152]{1,0:T(8,128)(2,1)S(1)} %fusion.23.refs_1_), channel_id=1, source_target_pairs={{0,1},{1,0},{2,3},{3,2},{4,5},{5,4},{6,7},{7,6},{8,9},{9,8},{10,11... | collective-permute-start | bytes 3538952 | tf_op jit(solution)/shard_map/ppermute | solution.py:47
  593.9 93.7 %collective-permute-start.21 = (bf16[72,2304]{1,0:T(8,128)(2,1)}, bf16[72,2304]{1,0:T(8,128)(2,1)}, u32[]{:S(2)}, u32[]{:S(2)}) collective-permute-start(bf16[72,2304]{1,0:T(8,128)(2,1)} %bitcast.252.refs_2_), channel_id=1, source_target_pairs={{0,1},{1,0},{2,3},{3,2},{4,5},{5,4},{6,7},{7,6},{8,9},{9,8},{10,11... | collective-permute-start | bytes 995336 | tf_op jit(solution)/shard_map/ppermute | solution.py:47
  641.8 47.8 %collective-permute-start.22 = (bf16[360,576]{1,0:T(8,128)(2,1)}, bf16[360,576]{1,0:T(8,128)(2,1)S(1)}, u32[]{:S(2)}, u32[]{:S(2)}) collective-permute-start(bf16[360,576]{1,0:T(8,128)(2,1)} %bitcast.68.refs_3_), channel_id=1, source_target_pairs={{0,1},{1,0},{2,3},{3,2},{4,5},{5,4},{6,7},{7,6},{8,9},{9,8},{10,11... | collective-permute-start | bytes 1244168 | tf_op jit(solution)/shard_map/ppermute | solution.py:47
  659.2 18.2 %all-to-all-start.2 = ((f32[32,2,432]{2,1,0:T(2,128)}), f32[32,2,432]{2,1,0:T(2,128)S(1)}, u32[]{:S(2)}, u32[]{:S(2)}) async-start(f32[32,2,432]{2,1,0:T(2,128)} %bitcast.82), calls=%async_computation.3 | async-start | bytes 262144 | tf_op jit(solution)/shard_map/all_to_all | solution.py:319
  680.6 21.7 %all-to-all-start.3 = ((f32[32,1,1656]{2,1,0:T(1,128)}), f32[32,1,1656]{2,1,0:T(1,128)S(1)}, u32[]{:S(2)}, u32[]{:S(2)}) async-start(f32[32,1,1656]{2,1,0:T(1,128)} %all_to_all.22), calls=%async_computation.4 | async-start | bytes 425984 | tf_op jit(solution)/shard_map/all_to_all | solution.py:319
  (126 other events, 1146.2 us)
Sparse Core Ops, SparseCore 0:
  145.7 88.6 all-gather.2
  237.2 86.8 all-gather.4
  328.2 119.7 reduce-scatter.7
  452.0 139.2 reduce-scatter.9
  595.3 104.5 reduce-scatter.11

commit v11 on v10

--- a/solution.py
+++ b/solution.py
@@ -248,6 +248,10 @@
     def scatter(self, term):
         return lax.psum_scatter(term, "dp", scatter_dimension=0, tiled=True)
 
+    def scatter_chips(self, term):
+        groups = [list(range(core, self.dp, 2)) for core in range(2)]
+        return lax.psum_scatter(term, "dp", scatter_dimension=0, tiled=True, axis_index_groups=groups)
+
     def halves_steps(self, term):
         y = self.y.digit()
         blocks = term.reshape(term.shape[0], self.seq, -1)
@@ -292,11 +296,11 @@
         got = self.core.send(other, 1)
         anchor = yield [other]
         half = own + tie(got, anchor)
-        sent = half[1].astype(BF)
+        sent = half[1]
         got = self.x.send(sent, 1)
         anchor = yield [sent]
-        kept = half[0] + tie(got, anchor).astype(F32)
-        sent = [kept[shift].astype(BF) for shift in range(1, self.z.size)]
+        kept = half[0] + tie(got, anchor)
+        sent = [kept[shift] for shift in range(1, self.z.size)]
         got = [self.z.send(each, shift) for shift, each in enumerate(sent, 1)]
         anchor = yield sent
         return [kept[0]] + [tie(each, anchor) for each in got]
@@ -610,9 +614,9 @@
         o_ref[0, :, h * depth : (h + 1) * depth] = o_s[h].astype(BF)
 
 
-def attend(lengths, offsets, queries, keys, values, heads, tile, deps=()):
+def attend(lengths, offsets, queries, keys_values, heads, tile, deps=()):
     count, rows, width = queries.shape
-    total = keys.shape[1]
+    total = keys_values.shape[1]
     depth = width // heads
     tile = min(tile, total)
     pick = lambda i, *_: (i, 0, 0)
@@ -624,7 +628,7 @@
             in_specs=[
                 pl.BlockSpec((1, rows, width), pick),
                 pl.BlockSpec((1, total, width), pick),
-                pl.BlockSpec((1, total, width), pick),
+                pl.BlockSpec((1, total, width), lambda i, *_: (i, 0, 1)),
             ]
             + [pl.BlockSpec(memory_space=pl.ANY)] * len(deps),
             out_specs=[
@@ -649,7 +653,7 @@
             transcendentals=count * heads * rows * total,
         ),
         name="attend",
-    )(lengths, offsets, queries, keys, values, *deps)
+    )(lengths, offsets, queries, keys_values, keys_values, *deps)
 
 
 def attend_back_kernel(
@@ -693,21 +697,22 @@
         dv_ref[0, :, span] = dv_s[h][:, :depth]
 
 
-def attend_back(lengths, offsets, queries, keys, values, mixed, grads, sample, lse, heads, tile, deps=()):
+def attend_back(lengths, offsets, queries, keys_values, mixed, grads, sample, lse, heads, tile, deps=()):
     count, rows, width = queries.shape
-    total = keys.shape[1]
+    total = keys_values.shape[1]
     depth = width // heads
     tile = min(tile, total)
     pick = lambda i, *_: (i, 0, 0)
     near = pl.BlockSpec((1, rows, width), pick)
     picked = pl.BlockSpec((1, rows, width), lambda i, *_: (sample + i, 0, 0))
     far = pl.BlockSpec((1, total, width), pick)
+    far_values = pl.BlockSpec((1, total, width), lambda i, *_: (i, 0, 1))
     return pl.pallas_call(
         without(attend_back_kernel, 8, len(deps), heads, tile),
         grid_spec=pltpu.PrefetchScalarGridSpec(
             num_scalar_prefetch=2,
             grid=(count,),
-            in_specs=[near, far, far, near, picked, pl.BlockSpec((1, heads, 1, rows), lambda i, *_: (i, 0, 0, 0))]
+            in_specs=[near, far, far_values, near, picked, pl.BlockSpec((1, heads, 1, rows), lambda i, *_: (i, 0, 0, 0))]
             + [pl.BlockSpec(memory_space=pl.ANY)] * len(deps),
             out_specs=[near, far, far],
             scratch_shapes=[
@@ -734,7 +739,7 @@
             transcendentals=count * heads * rows * total,
         ),
         name="attend_back",
-    )(lengths, offsets, queries, keys, values, mixed, grads, lse, *deps)
+    )(lengths, offsets, queries, keys_values, keys_values, mixed, grads, lse, *deps)
 
 
 def block_spots(counts, spread):
@@ -827,7 +832,7 @@
     for n in blocks:
         gram = refs[0][n]
         for ref in refs[1:count]:
-            gram = gram + ref[n].astype(F32)
+            gram = gram + ref[n]
         gram = unpacked(gram)
         square = jnp.sum(jnp.sum(gram * eye, axis=1, keepdims=True), axis=0, keepdims=True)
         scale = 1.0 / (jnp.sqrt(square) + NORM_EPS)
@@ -928,7 +933,8 @@
     shift_one, scale_one, gate_one, shift_two, scale_two, gate_two = jnp.split(
         modulation[:, None, :], 6, axis=-1
     )
-    first.advance(modulation)
+    pieces = first.advance(modulation)
+    token_pieces[0] = token_pieces[0][:1] + [tie(each, pieces[-1]) for each in token_pieces[0][1:]]
     norms, attn_all = [], []
 
     def norm_one(i):
@@ -946,22 +952,22 @@
 
     lengths = (heights * widths).reshape(count).astype(jnp.int32)
     offsets = jnp.stack([((y + s) % seq) * rows for s in range(seq)]).astype(jnp.int32)
-    queries, keys, values, attended, log_total = [[] for _ in range(5)]
+    queries, keys_values, attended, log_total = [[] for _ in range(4)]
+    b_kv = jnp.concatenate([jnp.zeros_like(b_v), b_v])
     for i in range(count):
         if i > 0:
             norm_one(i)
         attn = attn_all[i]
         queries.append((dot_t(attn[None, :rows], t_qkv[:width]) + b_q).astype(BF))
-        keys.append(dot_t(attn[None], t_qkv[width : 2 * width]).astype(BF))
-        values.append((dot_t(attn[None], t_qkv[2 * width :]) + b_v).astype(BF))
-        mixed, lse = attend(lengths[i : i + 1], offsets, queries[i], keys[i], values[i], HEADS, 512)
+        keys_values.append((dot_t(attn[None], t_qkv[width:]) + b_kv).astype(BF))
+        mixed, lse = attend(lengths[i : i + 1], offsets, queries[i], keys_values[i], HEADS, 512)
         if i == 0:
             token_pieces[1:] = [each[:1] + [tie(a, mixed) for a in each[1:]] for each in token_pieces[1:]]
             last_piece = token_pieces[-1][-1] if count > 1 else mixed
             wires = net.y.gather(tie(net.wire([w_fc2]), last_piece))
         attended.append(mixed)
         log_total.append(lse)
-    wires = wires[:1] + [tie(wire, keys[-1]) for wire in wires[1:]]
+    wires = wires[:1] + [tie(wire, keys_values[-1]) for wire in wires[1:]]
     t_fc2 = lax.all_gather(net.rows(wires), "dp", axis=0, tiled=True)
     attended_low = jnp.concatenate(attended, axis=0)
 
@@ -994,16 +1000,17 @@
     bias_proj = jnp.sum(grad_branch_one.astype(F32), axis=(0, 1))
     grad_attended = dot(grad_branch_one, t_proj).astype(BF)
     unit_mid = math.gcd(math.gcd(n_proj, n_fc1), 8)
-    (term_mid,) = shard_outer(
+    own, other = shard_outer(
         net.spots(),
         [flat(grad_pre), flat(ffn_in), flat(grad_branch_one), flat(attended_low)],
         [([2], 0, width), ([3], 0, width), ([1], 0, width)]
         + [([0], j * width, width) for j in range(hidden // width)],
         [(0, 1, n_proj, 0)] + [(3 + j, 2, n_fc1, n_proj // unit_mid) for j in range(hidden // width)],
-        net.z.size, width, unit_mid, (n_proj + n_fc1) // unit_mid, split=False,
+        net.z.size, width, unit_mid, (n_proj + n_fc1) // unit_mid,
     )
+    term_mid = (own.astype(F32) + net.core.send(other, 1).astype(F32)).astype(BF)
     term_mid = tie(term_mid, sum_fc2, grad_attended)
-    sum_mid = net.scatter(term_mid.reshape(dp * (n_proj + n_fc1), width))
+    sum_mid = net.scatter_chips(term_mid.reshape(dp // 2 * (n_proj + n_fc1), width))
     grad_attended = tie(grad_attended, term_mid)
 
     def far_steps(dk, dv):
@@ -1017,7 +1024,7 @@
     sent = []
     for i in range(count):
         dq, dk, dv = attend_back(
-            lengths[i : i + 1], offsets, queries[i], keys[i], values[i], attended[i],
+            lengths[i : i + 1], offsets, queries[i], keys_values[i], attended[i],
             grad_attended, i, log_total[i], HEADS, 512, sent,
         )
         sent = []

time: 828 us -> 845 us (1.021)
  other arithmetic: 74.7 us -> 86.5 us
    reduce_scatter x1, waiting for transfers between devices: 25.1 us -> 12 us  [scatter(): return lax.psum_scatter(term, 'dp', scatter_dimension=0, tiled=True)]
    convert_element_type x0 -> x1, other arithmetic: none -> 9.27 us  [body(): (own.astype(F32) + net.core.send(other, 1).astype(F32)).astype(BF)]
    all_to_all x4, waiting for transfers between devices: 5.34 us -> 14.4 us  [to_all(): lax.all_to_all(flat, ('dp', 'seq'), 0, 0, tiled=True).reshape(value.shape)]
    ppermute x35 -> x36, waiting for transfers between devices: 105 us -> 112 us  [send(): return lax.ppermute(value, self.name, pairs)]
    dot_general x8 -> x6, matrix products: 69.6 us -> 63.8 us  [dot_t(): return jnp.einsum('srk,nk->srn', left, right, preferred_element_type=F32)]
    ppermute x35 -> x36, starting transfers between devices: 40.2 us -> 43 us  [send(): return lax.ppermute(value, self.name, pairs)]
    unnamed x220 -> x216, local copies, waits for them, and re-layouts: 30.8 us -> 32.2 us
  transfers between devices with their start and end apart: 44 -> 45, of which waited for: 17 -> 18; matrix products, arithmetic and copies ran while one was open for 34% -> 34% of each run, Pallas kernels for 31% -> 30%
where the time goes in v11:
time: 845 us; the launch traced here: 833 us
  Pallas kernels  278 us (33%)
  matrix products  156 us (18%)
  waiting for transfers between devices  149 us (18%)
  other arithmetic  86.5 us (10%)
  local copies, waits for them, and re-layouts  80.1 us (9%)
  starting transfers between devices  68.3 us (8%)
  between operations  15.6 us (2%)
    ppermute x36, waiting for transfers between devices, send(): return lax.ppermute(value, self.name, pairs)  112 us
    pallas_call x2, Pallas kernels, attend_back(): pl.pallas_call(without(attend_back_kernel, 8, len(deps), heads, tile), gr...  84.4 us
    dot_general x12, matrix products, dot(): return jnp.einsum('srn,nk->srk', left, right, preferred_element_type=F32)  72.1 us
    dot_general x6, matrix products, dot_t(): return jnp.einsum('srk,nk->srn', left, right, preferred_element_type=F32)  63.8 us
    pallas_call x2, Pallas kernels, attend(): pl.pallas_call(without(attend_kernel, 5, len(deps), heads, tile), grid_sp...  58.1 us
    pallas_call x2, Pallas kernels, shard_outer(): pl.pallas_call(functools.partial(shard_outer_kernel, {'loads': loads, 'pa...  49 us
    ppermute x36, starting transfers between devices, send(): return lax.ppermute(value, self.name, pairs)  43 us
    unnamed x216, local copies, waits for them, and re-layouts  32.2 us
  transfers between devices with their start and end apart: 45, of which 18 were waited for; matrix products, arithmetic and copies ran while one was open for 34% of the time, Pallas kernels for 30%

profile of v11, /device:TPU:11, one launch (start us, length us, event | category | flops | bytes accessed | tf_op | source)
XLA Modules:
  0.0 832.9 jit_solution(8658169959926819484)
XLA Ops:
  58.9 23.1 %collective-permute-done.1.refs_0_ = bf16[16,8,1152]{2,1,0:T(8,128)(2,1)} collective-permute-done((bf16[16,8,1152]{2,1,0:T(8,128)(2,1)S(1)}, bf16[16,8,1152]{2,1,0:T(8,128)(2,1)}, u32[]{:S(2)}, u32[]{:S(2)}) %collective-permute-start.1) | collective-permute-done | bytes 294944 | tf_op jit(solution)/shard_map/ppermute | solution.py:47
  83.0 9.3 %all-to-all-done.1 = f32[32,2,432]{2,1,0:T(2,128)S(1)} async-done(((f32[32,2,432]{2,1,0:T(2,128)}), f32[32,2,432]{2,1,0:T(2,128)S(1)}, u32[]{:S(2)}, u32[]{:S(2)}) %all-to-all-start.1) | async-done | bytes 110624 | tf_op jit(solution)/shard_map/all_to_all | solution.py:323
  137.1 9.1 %place.1 = (bf16[4,2,2,27,8,1152]{5,4,3,2,1,0:T(8,128)(2,1)}, bf16[4,2,2,9,8,1152]{5,4,3,2,1,0:T(8,128)(2,1)}) custom-call(s32[3]{0:T(128)} %pad_add_fusion.1.refs_0_.spots_ref, bf16[4,16,8,1152]{3,2,1,0:T(8,128)(2,1)} %copy-done.4, bf16[4,16,8,1152]{3,2,1,0:T(8,128)(2,1)} %tie.64.refs_2_, bf16[2,20,8,1152]{3,2,1,0:T(8,128)(2,1)} %pad_maximum_fusion.3.refs_3_, ...), custom_call_target="tpu_custom_call" | custom-call | bytes 21233664 | tf_op jit(solution)/shard_map/place/pallas_call | solution.py:198
  153.2 10.5 %fusion.9.refs_3_.refs_4_ = bf16[1,1024,2304]{2,1,0:T(8,128)(2,1)} fusion(bf16[1024,1152]{1,0:T(8,128)(2,1)S(1)} %copy-done, f32[2304]{0:T(1024)} %concatenate.61, bf16[3456,1152]{1,0:T(8,128)(2,1)} %bitcast.255), kind=kOutput, calls=%fused_computation.20 | convolution fusion | flops 5440536576 | bytes 12398592 | tf_op jit(solution)/shard_map/srk,nk->srn/dot_general | solution.py:346
  168.4 29.2 %attend.2 = (bf16[1,512,1152]{2,1,0:T(8,128)(2,1)}, f32[1,16,1,512]{3,2,1,0:T(1,128)}) custom-call(s32[1]{0:T(128)} %bitcast.17.refs_0_, s32[2]{0:T(128)} %pad_add_fusion.refs_1_, bf16[1,512,1152]{2,1,0:T(8,128)(2,1)} %fusion.25.refs_2_, bf16[1,1024,2304]{2,1,0:T(8,128)(2,1)} %fusion.9.refs_3_.refs_4_, bf16[1,1024,2304]{2,1,0:T(8,128)(2,1)} %fusion.9.refs_3_.refs_4_), custom_call_target="tpu_custom_call" | custom-call | flops 4294967296 | bytes 7077888 | tf_op jit(solution)/shard_map/attend/pallas_call | solution.py:623
  204.7 11.4 %fusion.10.refs_3_.refs_4_.refs_1_ = bf16[1,1024,2304]{2,1,0:T(8,128)(2,1)} fusion(bf16[1024,1152]{1,0:T(8,128)(2,1)S(1)} %get-tuple-element.194.refs_9_, f32[2304]{0:T(1024)S(1)} %copy-done.79, bf16[3456,1152]{1,0:T(8,128)(2,1)} %bitcast.257), kind=kOutput, calls=%fused_computation.21 | convolution fusion | flops 5440536576 | bytes 12395520 | tf_op jit(solution)/shard_map/srk,nk->srn/dot_general | solution.py:346
  228.9 28.9 %attend.3 = (bf16[1,512,1152]{2,1,0:T(8,128)(2,1)}, f32[1,16,1,512]{3,2,1,0:T(1,128)}) custom-call(s32[1]{0:T(128)} %bitcast.27.refs_0_, s32[2]{0:T(128)} %pad_add_fusion.refs_1_, bf16[1,512,1152]{2,1,0:T(8,128)(2,1)} %fusion.24.refs_2_, bf16[1,1024,2304]{2,1,0:T(8,128)(2,1)} %fusion.10.refs_3_.refs_4_.refs_1_, ...), custom_call_target="tpu_custom_call" | custom-call | flops 4294967296 | bytes 7077888 | tf_op jit(solution)/shard_map/attend/pallas_call | solution.py:623
  260.4 8.4 %fusion.83 = (f32[2,512]{1,0:T(2,128)S(1)}, f32[2,512,1152]{2,1,0:T(8,128)S(1)}, f32[2,512,1152]{2,1,0:T(8,128)}) fusion(f32[2,1152]{1,0:T(2,128)S(1)} %get-tuple-element.218, bf16[2,1,512,1152]{3,2,1,0:T(8,128)(2,1)S(1)} %copy-done.39, f32[1152]{0:T(1024)S(1)} %copy-done.84, bf16[2,512,1152]{2,1,0:T(8,128)(2,1)} %constant_dynamic-update-slice_fusion, ...), kind=kOutput, calls=%fused_computation.216 | convolution fusion | flops 2723806208 | bytes 16827904 | tf_op jit(solution)/shard_map/srk,nk->srn/dot_general | solution.py:346
  273.3 25.0 %hidden_forward.1 = (bf16[1024,4608]{1,0:T(8,128)(2,1)}, bf16[1024,4608]{1,0:T(8,128)(2,1)}) custom-call(bf16[1024,1152]{1,0:T(8,128)(2,1)} %bitcast.280, bf16[4608,1152]{1,0:T(8,128)(2,1)} %all-gather.3.cloned.1.call-done.w_ref, f32[1,4608]{1,0:T(1,128)} %reshape.507.b_ref), custom_call_target="tpu_custom_call" | custom-call | flops 10871635968 | bytes 31850496 | tf_op jit(solution)/shard_map/hidden_forward/pallas_call | solution.py:378
  298.3 17.3 %fusion.refs_1_ = bf16[1152,4608]{1,0:T(8,128)(2,1)} fusion(bf16[2,512,1152]{2,1,0:T(8,128)(2,1)S(1)} %fusion.16.refs_0_, bf16[2,512,4608]{2,1,0:T(8,128)(2,1)} %bitcast.252), kind=kOutput, calls=%fused_computation.1 | convolution fusion | flops 10876944384 | bytes 22413312 | tf_op jit(solution)/shard_map/srn,srk->nk/dot_general | solution.py:430
  315.7 10.4 %all-gather.5.cloned.1.call-done.w_ref = bf16[1152,4608]{1,0:T(8,128)(2,1)} async-done(((bf16[72,4608]{1,0:T(8,128)(2,1)}), bf16[1152,4608]{1,0:T(8,128)(2,1)}) %all-gather.5.cloned.1.call-update) | async-done | bytes 10616848 | tf_op jit(solution)/shard_map/all_gather | solution.py:971
  326.1 20.1 %hidden_backward.1 = (bf16[1024,4608]{1,0:T(8,128)(2,1)}, f32[1,4608]{1,0:T(1,128)}) custom-call(bf16[1024,1152]{1,0:T(8,128)(2,1)} %bitcast.246, bf16[1152,4608]{1,0:T(8,128)(2,1)} %all-gather.5.cloned.1.call-done.w_ref, bf16[1024,4608]{1,0:T(8,128)(2,1)} %get-tuple-element.53.slope_ref), custom_call_target="tpu_custom_call" | custom-call | flops 10871635968 | bytes 31850496 | tf_op jit(solution)/shard_map/hidden_backward/pallas_call | solution.py:410
  346.2 23.3 %multiply_reduce_fusion = (f32[2,1152]{1,0:T(2,128)}, f32[2,512]{1,0:T(2,128)S(1)}, f32[2,512]{1,0:T(2,128)S(1)}, f32[2,1152]{1,0:T(2,128)}, f32[2,512,1152]{2,1,0:T(8,128)}) fusion(f32[2,512,1152]{2,1,0:T(8,128)} %copy-done.12, f32[2,512]{1,0:T(2,128)S(1)} %add_rsqrt_fusion, f32[2,512]{1,0:T(2,128)S(1)} %broadcast_multiply_fusion.2, ...), kind=kOutput, calls=%fused_computation.32 | convolution fusion | flops 10882246656 | bytes 29535232 | tf_op jit(solution)/shard_map/srn,nk->srk/dot_general | solution.py:350
  369.5 24.2 %fusion.17 = (f32[2,1152]{1,0:T(2,128)}, bf16[2,1,512,1152]{3,2,1,0:T(8,128)(2,1)}, f32[1152]{0:T(1024)}, bf16[2,512,1152]{2,1,0:T(8,128)(2,1)}, f32[2,512,1152]{2,1,0:T(8,128)}) fusion(bf16[2,1,512,1152]{3,2,1,0:T(8,128)(2,1)S(1)} %copy-done.45, f32[2,512,1152]{2,1,0:T(8,128)} %copy-done.12, f32[2,1152]{1,0:T(2,128)S(1)} %get-tuple-element.215, ...), kind=kOutput, calls=%fused_computation.26 | convolution fusion | flops 10894046208 | bytes 41350144 | tf_op jit(solution)/shard_map/srk,nk->srn/dot_general | solution.py:346
  393.7 24.0 %shard_outer.2 = (bf16[4,2,45,8,1152]{4,3,2,1,0:T(8,128)(2,1)}, bf16[4,2,45,8,1152]{4,3,2,1,0:T(8,128)(2,1)}) custom-call(s32[3]{0:T(128)} %pad_add_fusion.1.refs_0_.spots_ref, bf16[1024,4608]{1,0:T(8,128)(2,1)} %get-tuple-element.54.refs_0_, bf16[1024,1152]{1,0:T(8,128)(2,1)} %bitcast.281, bf16[1024,1152]{1,0:T(8,128)(2,1)} %bitcast.318, ...), custom_call_target="tpu_custom_call" | custom-call | flops 13589544960 | bytes 13271040 | tf_op jit(solution)/shard_map/shard_outer/pallas_call | solution.py:520
  428.7 9.3 %add_convert_fusion.refs_0_ = bf16[4,2,45,8,1152]{4,3,2,1,0:T(8,128)(2,1)} fusion(bf16[4,2,45,8,1152]{4,3,2,1,0:T(8,128)(2,1)} %collective-permute-done.19, bf16[4,2,45,8,1152]{4,3,2,1,0:T(8,128)(2,1)} %get-tuple-element.55), kind=kLoop, calls=%fused_computation.2 | loop fusion | flops 13271040 | bytes 19906560 | tf_op jit(solution)/shard_map/convert_element_type | solution.py:1011
  438.0 12.0 %reduce-scatter.8.cloned.1.call-done.refs_1_.refs_0_ = bf16[72,4608]{1,0:T(8,128)(2,1)} async-done(((bf16[1152,4608]{1,0:T(8,128)(2,1)}), bf16[72,4608]{1,0:T(8,128)(2,1)}) %reduce-scatter.8.cloned.1.call-update) | async-done | bytes 663568 | tf_op jit(solution)/shard_map/reduce_scatter | solution.py:249
  454.8 42.3 %attend_back.2 = (bf16[1,512,1152]{2,1,0:T(8,128)(2,1)}, bf16[1,1024,1152]{2,1,0:T(8,128)(2,1)}, bf16[1,1024,1152]{2,1,0:T(8,128)(2,1)}) custom-call(s32[1]{0:T(128)} %bitcast.17.refs_0_, s32[2]{0:T(128)} %pad_add_fusion.refs_1_, bf16[1,512,1152]{2,1,0:T(8,128)(2,1)} %fusion.25.refs_2_, bf16[1,1024,2304]{2,1,0:T(8,128)(2,1)} %fusion.9.refs_3_.refs_4_, ...), custom_call_target="tpu_custom_call" | custom-call | flops 10737418240 | bytes 14155776 | tf_op jit(solution)/shard_map/attend_back/pallas_call | solution.py:710
  505.9 42.1 %attend_back.3 = (bf16[1,512,1152]{2,1,0:T(8,128)(2,1)}, bf16[1,1024,1152]{2,1,0:T(8,128)(2,1)}, bf16[1,1024,1152]{2,1,0:T(8,128)(2,1)}) custom-call(s32[1]{0:T(128)} %bitcast.27.refs_0_, s32[2]{0:T(128)} %pad_add_fusion.refs_1_, bf16[1,512,1152]{2,1,0:T(8,128)(2,1)} %fusion.24.refs_2_, bf16[1,1024,2304]{2,1,0:T(8,128)(2,1)} %fusion.10.refs_3_.refs_4_.refs_1_, ...), custom_call_target="tpu_custom_call" | custom-call | flops 10737418240 | bytes 14155776 | tf_op jit(solution)/shard_map/attend_back/pallas_call | solution.py:710
  548.0 25.0 %shard_outer.3.refs_1_ = bf16[4,2,2,27,8,1152]{5,4,3,2,1,0:T(8,128)(2,1)} custom-call(s32[3]{0:T(128)} %pad_add_fusion.1.refs_0_.spots_ref, bf16[512,1152]{1,0:T(8,128)(2,1)} %bitcast.271, bf16[512,1152]{1,0:T(8,128)(2,1)} %bitcast.289, bf16[1024,1152]{1,0:T(8,128)(2,1)} %bitcast.317, bf16[1024,1152]{1,0:T(8,128)(2,1)} %bitcast.284, ...), custom_call_target="tpu_custom_call" | custom-call | flops 13589544960 | bytes 7962624 | tf_op jit(solution)/shard_map/shard_outer/pallas_call | solution.py:520
  608.9 24.6 %collective-permute-done.21 = bf16[512,1152]{1,0:T(8,128)(2,1)} collective-permute-done((bf16[512,1152]{1,0:T(8,128)(2,1)S(1)}, bf16[512,1152]{1,0:T(8,128)(2,1)}, u32[]{:S(2)}, u32[]{:S(2)}) %collective-permute-start.21) | collective-permute-done | bytes 1179680 | tf_op jit(solution)/shard_map/ppermute | solution.py:47
  731.8 15.7 %collective-permute-done.26.refs_0_ = f32[4,2,160,128]{3,2,1,0:T(8,128)S(1)} collective-permute-done((f32[4,2,160,128]{3,2,1,0:T(8,128)S(1)}, f32[4,2,160,128]{3,2,1,0:T(8,128)S(1)}, u32[]{:S(2)}, u32[]{:S(2)}) %collective-permute-start.26) | collective-permute-done | bytes 655392 | tf_op jit(solution)/shard_map/ppermute | solution.py:47
  766.9 7.9 polynomial.1.refs_1_
  815.1 10.9 %muon_apply.1 = (f32[72,2304]{1,0:T(8,128)}, f32[72,576]{1,0:T(8,128)}, f32[288,576]{1,0:T(8,128)}, f32[216,576]{1,0:T(8,128)}, f32[432,576]{1,0:T(8,128)}) custom-call(s32[3]{0:T(128)} %pad_add_fusion.1.refs_0_.spots_ref, f32[4,2,160,128]{3,2,1,0:T(8,128)} %copy-done.13, f32[4,2,160,128]{3,2,1,0:T(8,128)} %tie.101.refs_1_, ...), custom_call_target="tpu_custom_call" | custom-call | tf_op jit(solution)/shard_map/muon_apply/pallas_call | solution.py:880
  (511 shorter events, 353.4 us)
Async XLA Ops:
  22.2 27.2 %collective-permute-start.2 = (bf16[16,8,1152]{2,1,0:T(8,128)(2,1)S(1)}, bf16[16,8,1152]{2,1,0:T(8,128)(2,1)S(1)}, u32[]{:S(2)}, u32[]{:S(2)}) collective-permute-start(bf16[16,8,1152]{2,1,0:T(8,128)(2,1)S(1)} %get-tuple-element.204.refs_1_.refs_2_), channel_id=1, source_target_pairs={{0,8},{2,10},{4,12},{6,14},{8,16},{10,18},{12,20},{14,22},{16,24},... | collective-permute-start | bytes 884744 | tf_op jit(solution)/shard_map/ppermute | solution.py:47
  35.6 60.4 %collective-permute-start.7 = (bf16[2,20,8,1152]{3,2,1,0:T(8,128)(2,1)}, bf16[2,20,8,1152]{3,2,1,0:T(8,128)(2,1)S(1)}, u32[]{:S(2)}, u32[]{:S(2)}) collective-permute-start(bf16[2,20,8,1152]{3,2,1,0:T(8,128)(2,1)} %pad_maximum_fusion.3.refs_3_), channel_id=1, source_target_pairs={{0,8},{2,10},{4,12},{6,14},{8,16},{10,18},{12,20},{14,22},{16,24},... | collective-permute-start | bytes 2211848 | tf_op jit(solution)/shard_map/ppermute | solution.py:47
  36.4 58.1 %collective-permute-start.5 = (bf16[2,20,8,1152]{3,2,1,0:T(8,128)(2,1)}, bf16[2,20,8,1152]{3,2,1,0:T(8,128)(2,1)}, u32[]{:S(2)}, u32[]{:S(2)}) collective-permute-start(bf16[2,20,8,1152]{3,2,1,0:T(8,128)(2,1)} %pad_maximum_fusion.3.refs_3_), channel_id=1, source_target_pairs={{0,24},{2,26},{4,28},{6,30},{8,0},{10,2},{12,4},{14,6},{16,8},{18,... | collective-permute-start | bytes 2211848 | tf_op jit(solution)/shard_map/ppermute | solution.py:47
  46.2 35.8 %collective-permute-start.1 = (bf16[16,8,1152]{2,1,0:T(8,128)(2,1)S(1)}, bf16[16,8,1152]{2,1,0:T(8,128)(2,1)}, u32[]{:S(2)}, u32[]{:S(2)}) collective-permute-start(bf16[16,8,1152]{2,1,0:T(8,128)(2,1)S(1)} %copy-done.18), channel_id=1, source_target_pairs={{0,24},{2,26},{4,28},{6,30},{8,0},{10,2},{12,4},{14,6},{16,8},{18,... | collective-permute-start | bytes 884744 | tf_op jit(solution)/shard_map/ppermute | solution.py:47
  50.1 42.2 %collective-permute-start.3 = (bf16[16,8,1152]{2,1,0:T(8,128)(2,1)}, bf16[16,8,1152]{2,1,0:T(8,128)(2,1)}, u32[]{:S(2)}, u32[]{:S(2)}) collective-permute-start(bf16[16,8,1152]{2,1,0:T(8,128)(2,1)} %tie.55), channel_id=1, source_target_pairs={{0,8},{2,10},{4,12},{6,14},{8,16},{10,18},{12,20},{14,22},{16,24},... | collective-permute-start | bytes 884744 | tf_op jit(solution)/shard_map/ppermute | solution.py:47
  50.8 41.5 %all-to-all-start.1 = ((f32[32,2,432]{2,1,0:T(2,128)}), f32[32,2,432]{2,1,0:T(2,128)S(1)}, u32[]{:S(2)}, u32[]{:S(2)}) async-start(f32[32,2,432]{2,1,0:T(2,128)} %bitcast.7), calls=%async_computation.1 | async-start | bytes 262144 | tf_op jit(solution)/shard_map/all_to_all | solution.py:323
  56.9 216.4 %all-gather.3.cloned.1.call-start = ((), (), s32[]{:S(2)}) async-start(), calls=%async_computation.7 | async-start | bytes 11280384 | tf_op jit(solution)/shard_map/all_gather | solution.py:949
  57.7 52.6 %collective-permute-start.6 = (bf16[512,1152]{1,0:T(8,128)(2,1)}, bf16[512,1152]{1,0:T(8,128)(2,1)S(1)}, u32[]{:S(2)}, u32[]{:S(2)}) collective-permute-start(bf16[512,1152]{1,0:T(8,128)(2,1)} %tie.61), channel_id=1, source_target_pairs={{0,1},{1,0},{2,3},{3,2},{4,5},{5,4},{6,7},{7,6},{8,9},{9,8},{10,11... | collective-permute-start | bytes 3538952 | tf_op jit(solution)/shard_map/ppermute | solution.py:47
  82.0 47.6 %collective-permute-start.12 = (bf16[2,20,8,1152]{3,2,1,0:T(8,128)(2,1)}, bf16[2,20,8,1152]{3,2,1,0:T(8,128)(2,1)}, u32[]{:S(2)}, u32[]{:S(2)}) collective-permute-start(bf16[2,20,8,1152]{3,2,1,0:T(8,128)(2,1)} %pad_maximum_fusion.3.refs_3_), channel_id=1, source_target_pairs={{0,2},{2,0},{4,6},{6,4},{8,10},{10,8},{12,14},{14,12},{16,18},{18,... | collective-permute-start | bytes 2211848 | tf_op jit(solution)/shard_map/ppermute | solution.py:47
  94.4 26.7 %collective-permute-start.8 = (bf16[4,16,8,1152]{3,2,1,0:T(8,128)(2,1)S(1)}, bf16[4,16,8,1152]{3,2,1,0:T(8,128)(2,1)}, u32[]{:S(2)}, u32[]{:S(2)}) collective-permute-start(bf16[4,16,8,1152]{3,2,1,0:T(8,128)(2,1)S(1)} %pad_maximum_fusion.2.refs_1_.refs_2_), channel_id=1, source_target_pairs={{0,4},{2,6},{4,0},{6,2},{8,12},{10,14},{12,8},{14,10},{16,20},{18,... | collective-permute-start | bytes 3538952 | tf_op jit(solution)/shard_map/ppermute | solution.py:47
  94.5 36.7 %collective-permute-start.10 = (bf16[4,16,8,1152]{3,2,1,0:T(8,128)(2,1)S(1)}, bf16[4,16,8,1152]{3,2,1,0:T(8,128)(2,1)}, u32[]{:S(2)}, u32[]{:S(2)}) collective-permute-start(bf16[4,16,8,1152]{3,2,1,0:T(8,128)(2,1)S(1)} %pad_maximum_fusion.2.refs_1_.refs_2_), channel_id=1, source_target_pairs={{0,2},{2,0},{4,6},{6,4},{8,10},{10,8},{12,14},{14,12},{16,18},{18,... | collective-permute-start | bytes 3538952 | tf_op jit(solution)/shard_map/ppermute | solution.py:47
  96.9 39.3 %collective-permute-start.15 = (bf16[2,20,8,1152]{3,2,1,0:T(8,128)(2,1)}, bf16[2,20,8,1152]{3,2,1,0:T(8,128)(2,1)}, u32[]{:S(2)}, u32[]{:S(2)}) collective-permute-start(bf16[2,20,8,1152]{3,2,1,0:T(8,128)(2,1)} %tie.62.refs_1_.refs_6_), channel_id=1, source_target_pairs={{0,2},{2,0},{4,6},{6,4},{8,10},{10,8},{12,14},{14,12},{16,18},{18,... | collective-permute-start | bytes 2211848 | tf_op jit(solution)/shard_map/ppermute | solution.py:47
  110.4 18.2 %collective-permute-start.9 = (bf16[2,20,8,1152]{3,2,1,0:T(8,128)(2,1)}, bf16[2,20,8,1152]{3,2,1,0:T(8,128)(2,1)}, u32[]{:S(2)}, u32[]{:S(2)}) collective-permute-start(bf16[2,20,8,1152]{3,2,1,0:T(8,128)(2,1)} %tie.58.refs_2_.refs_4_.refs_3_), channel_id=1, source_target_pairs={{0,24},{2,26},{4,28},{6,30},{8,0},{10,2},{12,4},{14,6},{16,8},{18,... | collective-permute-start | bytes 2211848 | tf_op jit(solution)/shard_map/ppermute | solution.py:47
  149.7 176.4 %all-gather.5.cloned.1.call-start = ((), (), s32[]{:S(2)}) async-start(), calls=%async_computation.8 | async-start | bytes 11280384 | tf_op jit(solution)/shard_map/all_gather | solution.py:971
  153.1 44.4 %collective-permute-start.17 = (bf16[512,1152]{1,0:T(8,128)(2,1)}, bf16[512,1152]{1,0:T(8,128)(2,1)S(1)}, u32[]{:S(2)}, u32[]{:S(2)}) collective-permute-start(bf16[512,1152]{1,0:T(8,128)(2,1)} %tie.74), channel_id=1, source_target_pairs={{0,1},{1,0},{2,3},{3,2},{4,5},{5,4},{6,7},{7,6},{8,9},{9,8},{10,11... | collective-permute-start | bytes 3538952 | tf_op jit(solution)/shard_map/ppermute | solution.py:47
  219.3 230.7 %reduce-scatter.8.cloned.1.call-start = ((), (), s32[]{:S(2)}) async-start(), calls=%async_computation.9 | async-start | bytes 11280384 | tf_op jit(solution)/shard_map/reduce_scatter | solution.py:249
  315.6 324.3 %reduce-scatter.10.cloned.1.call-start = ((), (), s32[]{:S(2)}) async-start(), calls=%async_computation.10 | async-start | bytes 7464960
  450.0 255.5 %reduce-scatter.12.cloned.1.call-start = ((), (), s32[]{:S(2)}) async-start(), calls=%async_computation.11 | async-start | bytes 8460288
  581.2 71.7 %collective-permute-start.20 = (bf16[512,1152]{1,0:T(8,128)(2,1)}, bf16[512,1152]{1,0:T(8,128)(2,1)}, u32[]{:S(2)}, u32[]{:S(2)}) collective-permute-start(bf16[512,1152]{1,0:T(8,128)(2,1)} %fusion.22.refs_8_), channel_id=1, source_target_pairs={{0,1},{1,0},{2,3},{3,2},{4,5},{5,4},{6,7},{7,6},{8,9},{9,8},{10,11... | collective-permute-start | bytes 3538952 | tf_op jit(solution)/shard_map/ppermute | solution.py:47
  590.3 43.2 %collective-permute-start.21 = (bf16[512,1152]{1,0:T(8,128)(2,1)S(1)}, bf16[512,1152]{1,0:T(8,128)(2,1)}, u32[]{:S(2)}, u32[]{:S(2)}) collective-permute-start(bf16[512,1152]{1,0:T(8,128)(2,1)S(1)} %fusion.23.refs_1_), channel_id=1, source_target_pairs={{0,1},{1,0},{2,3},{3,2},{4,5},{5,4},{6,7},{7,6},{8,9},{9,8},{10,11... | collective-permute-start | bytes 3538952 | tf_op jit(solution)/shard_map/ppermute | solution.py:47
  596.1 93.5 %collective-permute-start.22 = (bf16[72,2304]{1,0:T(8,128)(2,1)}, bf16[72,2304]{1,0:T(8,128)(2,1)}, u32[]{:S(2)}, u32[]{:S(2)}) collective-permute-start(bf16[72,2304]{1,0:T(8,128)(2,1)} %bitcast.242.refs_2_), channel_id=1, source_target_pairs={{0,1},{1,0},{2,3},{3,2},{4,5},{5,4},{6,7},{7,6},{8,9},{9,8},{10,11... | collective-permute-start | bytes 995336 | tf_op jit(solution)/shard_map/ppermute | solution.py:47
  643.8 47.7 %collective-permute-start.23 = (bf16[360,576]{1,0:T(8,128)(2,1)}, bf16[360,576]{1,0:T(8,128)(2,1)S(1)}, u32[]{:S(2)}, u32[]{:S(2)}) collective-permute-start(bf16[360,576]{1,0:T(8,128)(2,1)} %bitcast.66.refs_3_), channel_id=1, source_target_pairs={{0,1},{1,0},{2,3},{3,2},{4,5},{5,4},{6,7},{7,6},{8,9},{9,8},{10,11... | collective-permute-start | bytes 1244168 | tf_op jit(solution)/shard_map/ppermute | solution.py:47
  661.1 18.3 %all-to-all-start.2 = ((f32[32,2,432]{2,1,0:T(2,128)}), f32[32,2,432]{2,1,0:T(2,128)S(1)}, u32[]{:S(2)}, u32[]{:S(2)}) async-start(f32[32,2,432]{2,1,0:T(2,128)} %bitcast.80), calls=%async_computation.3 | async-start | bytes 262144 | tf_op jit(solution)/shard_map/all_to_all | solution.py:323
  682.5 21.6 %all-to-all-start.3 = ((f32[32,1,1656]{2,1,0:T(1,128)}), f32[32,1,1656]{2,1,0:T(1,128)S(1)}, u32[]{:S(2)}, u32[]{:S(2)}) async-start(f32[32,1,1656]{2,1,0:T(1,128)} %all_to_all.22), calls=%async_computation.4 | async-start | bytes 425984 | tf_op jit(solution)/shard_map/all_to_all | solution.py:323
  (125 other events, 1152.7 us)
Sparse Core Ops, SparseCore 0:
  149.8 86.4 all-gather.2
  239.2 86.8 all-gather.4
  330.1 119.8 reduce-scatter.7
  453.5 122.7 reduce-scatter.9
  580.7 102.7 reduce-scatter.11

commit v12 on v11

--- a/solution.py
+++ b/solution.py
@@ -933,17 +933,7 @@
     shift_one, scale_one, gate_one, shift_two, scale_two, gate_two = jnp.split(
         modulation[:, None, :], 6, axis=-1
     )
-    pieces = first.advance(modulation)
-    token_pieces[0] = token_pieces[0][:1] + [tie(each, pieces[-1]) for each in token_pieces[0][1:]]
-    norms, attn_all = [], []
-
-    def norm_one(i):
-        normed, inverse = layer_norm(jnp.concatenate(token_pieces[i], axis=0).astype(F32))
-        norms.append((normed[:rows], inverse[:rows]))
-        attn_all.append((normed * (1.0 + scale_one[i]) + shift_one[i]).astype(BF))
-
-    norm_one(0)
-    t_qkv, t_proj = first.finish(attn_all[0])[0]
+    t_qkv, t_proj = first.finish(modulation)[0]
     wires = net.y.gather(tie(net.wire([w_fc1]), token_pieces[0][-1], *sent))
     wires = wires[:1] + [tie(wire, t_qkv) for wire in wires[1:]]
     t_fc1 = lax.all_gather(net.rows(wires), "dp", axis=0, tiled=True)
@@ -952,12 +942,11 @@
 
     lengths = (heights * widths).reshape(count).astype(jnp.int32)
     offsets = jnp.stack([((y + s) % seq) * rows for s in range(seq)]).astype(jnp.int32)
-    queries, keys_values, attended, log_total = [[] for _ in range(4)]
+    normed_all, inverse_all, attn_all, queries, keys_values, attended, log_total = [[] for _ in range(7)]
     b_kv = jnp.concatenate([jnp.zeros_like(b_v), b_v])
     for i in range(count):
-        if i > 0:
-            norm_one(i)
-        attn = attn_all[i]
+        normed, inverse = layer_norm(jnp.concatenate(token_pieces[i], axis=0).astype(F32))
+        attn = (normed * (1.0 + scale_one[i]) + shift_one[i]).astype(BF)
         queries.append((dot_t(attn[None, :rows], t_qkv[:width]) + b_q).astype(BF))
         keys_values.append((dot_t(attn[None], t_qkv[width:]) + b_kv).astype(BF))
         mixed, lse = attend(lengths[i : i + 1], offsets, queries[i], keys_values[i], HEADS, 512)
@@ -965,6 +954,9 @@
             token_pieces[1:] = [each[:1] + [tie(a, mixed) for a in each[1:]] for each in token_pieces[1:]]
             last_piece = token_pieces[-1][-1] if count > 1 else mixed
             wires = net.y.gather(tie(net.wire([w_fc2]), last_piece))
+        normed_all.append(normed[:rows])
+        inverse_all.append(inverse[:rows])
+        attn_all.append(attn)
         attended.append(mixed)
         log_total.append(lse)
     wires = wires[:1] + [tie(wire, keys_values[-1]) for wire in wires[1:]]
@@ -1048,32 +1040,32 @@
     grad_k[-1] = tie(grad_k[-1], term_last)
     far_parts.append(far_steps(grad_k[-1], grad_v[-1]))
     sent = far_parts[-1].advance()
-    halves = Staged(lockstep(*[net.halves_steps(tie(each, *sent)) for each in (sum_fc2, sum_mid)]))
-    sent = sent + halves.advance()
     grad_q[0] = tie(grad_q[0], *sent)
     bias_q = sum(jnp.sum(each.astype(F32), axis=(0, 1)) for each in grad_q)
     bias_v = sum(jnp.sum(each.astype(F32), axis=(0, 1)) for each in grad_v)
-    own_part = [
-        dot(grad_q[i], t_qkv[:width])
-        + dot(grad_k[i][:, :rows], t_qkv[width : 2 * width])
-        + dot(grad_v[i][:, :rows], t_qkv[2 * width :])
-        for i in range(count)
-    ]
-    grad_shift_one, grad_scale_one, grad_inputs = [], [], []
-    for i, (normed, inverse) in enumerate(norms):
-        grad_attn_in = own_part[i][0] + far_parts[i].finish()
-        grad_shift_one.append(jnp.sum(grad_attn_in, axis=0))
-        grad_scale_one.append(jnp.sum(grad_attn_in * normed, axis=0))
-        grad_in = grad_mixed[i] + norm_back(normed, inverse, grad_attn_in * (1.0 + scale_one[i]))
-        grad_inputs.append(grad_in.astype(BF))
-    grad_shift_one, grad_scale_one = jnp.stack(grad_shift_one), jnp.stack(grad_scale_one)
-    grad_inputs = jnp.stack(grad_inputs).reshape(tokens.shape)
-
+    own_part = jnp.concatenate(
+        [
+            dot(grad_q[i], t_qkv[:width])
+            + dot(grad_k[i][:, :rows], t_qkv[width : 2 * width])
+            + dot(grad_v[i][:, :rows], t_qkv[2 * width :])
+            for i in range(count)
+        ],
+        axis=0,
+    )
+    halves = Staged(lockstep(*[net.halves_steps(tie(each, own_part)) for each in (sum_fc2, sum_mid)]))
+    halves.advance()
     matrices = (w_qkv, w_proj, w_fc1, w_fc2, w_ada)
     per = -(-sum(matrix.shape[0] // ROW_BLOCK for matrix in matrices) // dp)
     spread_early = (per, 0)
     early_blocks = (w_fc2.shape[0] + w_fc1.shape[0] + w_proj.shape[0]) // ROW_BLOCK
     spread_last = (per, -(-early_blocks // per))
+    far_sum = jnp.stack([steps_of.finish() for steps_of in far_parts])
+    grad_attn_in = own_part + far_sum
+    normed_one, inverse_one = jnp.stack(normed_all), jnp.stack(inverse_all)
+    grad_shift_one = jnp.sum(grad_attn_in, axis=1)
+    grad_scale_one = jnp.sum(grad_attn_in * normed_one, axis=1)
+    grad_inputs = grad_mixed + norm_back(normed_one, inverse_one, grad_attn_in * (1.0 + scale_one))
+    grad_inputs = grad_inputs.astype(BF).reshape(tokens.shape)
 
     grad_mod_local = jnp.concatenate(
         [grad_shift_one, grad_scale_one, grad_gate_one, grad_shift_two, grad_scale_two, grad_gate_two], axis=-1

time: 845 us -> 814 us (0.963)
  other arithmetic: 86.5 us -> 72 us
  matrix products: 156 us -> 147 us
    ppermute x36, waiting for transfers between devices: 112 us -> 123 us  [send(): return lax.ppermute(value, self.name, pairs)]
    dot_general x12, matrix products: 72.1 us -> 63.2 us  [dot(): return jnp.einsum('srn,nk->srk', left, right, preferred_element_type=F32)]
    unnamed x216 -> x220, local copies, waits for them, and re-layouts: 32.2 us -> 28.5 us
  transfers between devices with their start and end apart: 45 -> 45, of which waited for: 18 -> 23; matrix products, arithmetic and copies ran while one was open for 34% -> 31% of each run, Pallas kernels for 30% -> 32%
where the time goes in v12:
time: 814 us; the launch traced here: 803 us
  Pallas kernels  278 us (34%)
  waiting for transfers between devices  156 us (19%)
  matrix products  147 us (18%)
  local copies, waits for them, and re-layouts  72.8 us (9%)
  other arithmetic  72 us (9%)
  starting transfers between devices  60.9 us (7%)
  between operations  15.5 us (2%)
    ppermute x36, waiting for transfers between devices, send(): return lax.ppermute(value, self.name, pairs)  123 us
    pallas_call x2, Pallas kernels, attend_back(): pl.pallas_call(without(attend_back_kernel, 8, len(deps), heads, tile), gr...  84.5 us
    dot_general x6, matrix products, dot_t(): return jnp.einsum('srk,nk->srn', left, right, preferred_element_type=F32)  63.7 us
    dot_general x12, matrix products, dot(): return jnp.einsum('srn,nk->srk', left, right, preferred_element_type=F32)  63.2 us
    pallas_call x2, Pallas kernels, attend(): pl.pallas_call(without(attend_kernel, 5, len(deps), heads, tile), grid_sp...  58.1 us
    pallas_call x2, Pallas kernels, shard_outer(): pl.pallas_call(functools.partial(shard_outer_kernel, {'loads': loads, 'pa...  49 us
    ppermute x36, starting transfers between devices, send(): return lax.ppermute(value, self.name, pairs)  38.9 us
    unnamed x220, local copies, waits for them, and re-layouts  28.5 us
  transfers between devices with their start and end apart: 45, of which 23 were waited for; matrix products, arithmetic and copies ran while one was open for 31% of the time, Pallas kernels for 32%

profile of v12, /device:TPU:11, one launch (start us, length us, event | category | flops | bytes accessed | tf_op | source)
XLA Modules:
  0.0 802.8 jit_solution(15073291211358559432)
XLA Ops:
  23.0 11.0 %all-to-all-done = f32[32,1,1656]{2,1,0:T(1,128)S(1)} async-done(((f32[32,1,1656]{2,1,0:T(1,128)}), f32[32,1,1656]{2,1,0:T(1,128)S(1)}, u32[]{:S(2)}, u32[]{:S(2)}) %all-to-all-start) | async-done | bytes 212000 | tf_op jit(solution)/shard_map/all_to_all | solution.py:323
  55.6 12.9 %collective-permute-done.3.refs_0_ = bf16[16,8,1152]{2,1,0:T(8,128)(2,1)} collective-permute-done((bf16[16,8,1152]{2,1,0:T(8,128)(2,1)}, bf16[16,8,1152]{2,1,0:T(8,128)(2,1)}, u32[]{:S(2)}, u32[]{:S(2)}) %collective-permute-start.3) | collective-permute-done | bytes 294944 | tf_op jit(solution)/shard_map/ppermute | solution.py:47
  76.7 8.2 %collective-permute-done.9.refs_0_ = bf16[2,20,8,1152]{3,2,1,0:T(8,128)(2,1)} collective-permute-done((bf16[2,20,8,1152]{3,2,1,0:T(8,128)(2,1)}, bf16[2,20,8,1152]{3,2,1,0:T(8,128)(2,1)}, u32[]{:S(2)}, u32[]{:S(2)}) %collective-permute-start.9) | collective-permute-done | bytes 737312 | tf_op jit(solution)/shard_map/ppermute | solution.py:47
  109.4 9.1 %place.1 = (bf16[4,2,2,27,8,1152]{5,4,3,2,1,0:T(8,128)(2,1)}, bf16[4,2,2,9,8,1152]{5,4,3,2,1,0:T(8,128)(2,1)}) custom-call(s32[3]{0:T(128)} %pad_add_fusion.1.refs_0_.spots_ref, bf16[4,16,8,1152]{3,2,1,0:T(8,128)(2,1)} %copy-done.1, bf16[4,16,8,1152]{3,2,1,0:T(8,128)(2,1)} %tie.61.refs_2_, bf16[2,20,8,1152]{3,2,1,0:T(8,128)(2,1)} %pad_maximum_fusion.5.refs_3_, ...), custom_call_target="tpu_custom_call" | custom-call | bytes 21233664 | tf_op jit(solution)/shard_map/place/pallas_call | solution.py:198
  135.2 10.5 %fusion.9.refs_3_.refs_4_ = bf16[1,1024,2304]{2,1,0:T(8,128)(2,1)} fusion(bf16[1024,1152]{1,0:T(8,128)(2,1)S(1)} %copy-done.16, f32[2304]{0:T(1024)} %concatenate.64, bf16[3456,1152]{1,0:T(8,128)(2,1)} %bitcast.243), kind=kOutput, calls=%fused_computation.20 | convolution fusion | flops 5440536576 | bytes 12398592 | tf_op jit(solution)/shard_map/srk,nk->srn/dot_general | solution.py:346
  150.4 29.2 %attend.2 = (bf16[1,512,1152]{2,1,0:T(8,128)(2,1)}, f32[1,16,1,512]{3,2,1,0:T(1,128)}) custom-call(s32[1]{0:T(128)} %bitcast.17.refs_0_, s32[2]{0:T(128)} %pad_add_fusion.refs_1_, bf16[1,512,1152]{2,1,0:T(8,128)(2,1)} %fusion.27.refs_2_, bf16[1,1024,2304]{2,1,0:T(8,128)(2,1)} %fusion.9.refs_3_.refs_4_, bf16[1,1024,2304]{2,1,0:T(8,128)(2,1)} %fusion.9.refs_3_.refs_4_), custom_call_target="tpu_custom_call" | custom-call | flops 4294967296 | bytes 7077888 | tf_op jit(solution)/shard_map/attend/pallas_call | solution.py:623
  186.7 11.4 %fusion.10.refs_3_.refs_4_.refs_1_ = bf16[1,1024,2304]{2,1,0:T(8,128)(2,1)} fusion(bf16[1024,1152]{1,0:T(8,128)(2,1)S(1)} %get-tuple-element.191.refs_9_, f32[2304]{0:T(1024)S(1)} %copy-done.82, bf16[3456,1152]{1,0:T(8,128)(2,1)} %bitcast.245), kind=kOutput, calls=%fused_computation.21 | convolution fusion | flops 5440536576 | bytes 12395520 | tf_op jit(solution)/shard_map/srk,nk->srn/dot_general | solution.py:346
  211.5 28.9 %attend.3 = (bf16[1,512,1152]{2,1,0:T(8,128)(2,1)}, f32[1,16,1,512]{3,2,1,0:T(1,128)}) custom-call(s32[1]{0:T(128)} %bitcast.27.refs_0_, s32[2]{0:T(128)} %pad_add_fusion.refs_1_, bf16[1,512,1152]{2,1,0:T(8,128)(2,1)} %fusion.26.refs_2_, bf16[1,1024,2304]{2,1,0:T(8,128)(2,1)} %fusion.10.refs_3_.refs_4_.refs_1_, ...), custom_call_target="tpu_custom_call" | custom-call | flops 4294967296 | bytes 7077888 | tf_op jit(solution)/shard_map/attend/pallas_call | solution.py:623
  243.0 8.3 %fusion.78 = (f32[2,512]{1,0:T(2,128)S(1)}, f32[2,512,1152]{2,1,0:T(8,128)S(1)}, f32[2,512,1152]{2,1,0:T(8,128)}) fusion(f32[2,1152]{1,0:T(2,128)S(1)} %get-tuple-element.216, bf16[2,1,512,1152]{3,2,1,0:T(8,128)(2,1)S(1)} %copy-done.37, f32[1152]{0:T(1024)S(1)} %copy-done.89, bf16[2,512,1152]{2,1,0:T(8,128)(2,1)} %constant_dynamic-update-slice_fusion, ...), kind=kOutput, calls=%fused_computation.213 | convolution fusion | flops 2723806208 | bytes 16827904 | tf_op jit(solution)/shard_map/srk,nk->srn/dot_general | solution.py:346
  255.8 25.0 %hidden_forward.1 = (bf16[1024,4608]{1,0:T(8,128)(2,1)}, bf16[1024,4608]{1,0:T(8,128)(2,1)}) custom-call(bf16[1024,1152]{1,0:T(8,128)(2,1)} %bitcast.276, bf16[4608,1152]{1,0:T(8,128)(2,1)} %all-gather.3.cloned.1.call-done.w_ref, f32[1,4608]{1,0:T(1,128)} %reshape.497.b_ref), custom_call_target="tpu_custom_call" | custom-call | flops 10871635968 | bytes 31850496 | tf_op jit(solution)/shard_map/hidden_forward/pallas_call | solution.py:378
  280.9 17.6 %fusion.refs_1_ = bf16[1152,4608]{1,0:T(8,128)(2,1)} fusion(bf16[2,512,1152]{2,1,0:T(8,128)(2,1)S(1)} %fusion.16.refs_0_, bf16[2,512,4608]{2,1,0:T(8,128)(2,1)} %bitcast.240), kind=kOutput, calls=%fused_computation.1 | convolution fusion | flops 10876944384 | bytes 22413312 | tf_op jit(solution)/shard_map/srn,srk->nk/dot_general | solution.py:430
  301.3 20.2 %hidden_backward.1 = (bf16[1024,4608]{1,0:T(8,128)(2,1)}, f32[1,4608]{1,0:T(1,128)}) custom-call(bf16[1024,1152]{1,0:T(8,128)(2,1)} %bitcast.238, bf16[1152,4608]{1,0:T(8,128)(2,1)} %all-gather.5.cloned.1.call-done.w_ref, bf16[1024,4608]{1,0:T(8,128)(2,1)} %get-tuple-element.53.slope_ref), custom_call_target="tpu_custom_call" | custom-call | flops 10871635968 | bytes 31850496 | tf_op jit(solution)/shard_map/hidden_backward/pallas_call | solution.py:410
  321.5 23.3 %multiply_reduce_fusion = (f32[2,1152]{1,0:T(2,128)}, f32[2,512]{1,0:T(2,128)S(1)}, f32[2,512]{1,0:T(2,128)S(1)}, f32[2,1152]{1,0:T(2,128)}, f32[2,512,1152]{2,1,0:T(8,128)}) fusion(f32[2,512,1152]{2,1,0:T(8,128)} %copy-done.9, f32[2,512]{1,0:T(2,128)S(1)} %add_rsqrt_fusion, f32[2,512]{1,0:T(2,128)S(1)} %broadcast_multiply_fusion.4, ...), kind=kOutput, calls=%fused_computation.34 | convolution fusion | flops 10882246656 | bytes 29535232 | tf_op jit(solution)/shard_map/srn,nk->srk/dot_general | solution.py:350
  344.8 24.2 %fusion.17 = (f32[2,1152]{1,0:T(2,128)}, bf16[2,1,512,1152]{3,2,1,0:T(8,128)(2,1)}, f32[1152]{0:T(1024)}, bf16[2,512,1152]{2,1,0:T(8,128)(2,1)}, f32[2,512,1152]{2,1,0:T(8,128)}) fusion(bf16[2,1,512,1152]{3,2,1,0:T(8,128)(2,1)S(1)} %copy-done.42, f32[2,512,1152]{2,1,0:T(8,128)} %copy-done.9, f32[2,1152]{1,0:T(2,128)S(1)} %get-tuple-element.213, ...), kind=kOutput, calls=%fused_computation.26 | convolution fusion | flops 10894046208 | bytes 41350144 | tf_op jit(solution)/shard_map/srk,nk->srn/dot_general | solution.py:346
  369.0 24.0 %shard_outer.2 = (bf16[4,2,45,8,1152]{4,3,2,1,0:T(8,128)(2,1)}, bf16[4,2,45,8,1152]{4,3,2,1,0:T(8,128)(2,1)}) custom-call(s32[3]{0:T(128)} %pad_add_fusion.1.refs_0_.spots_ref, bf16[1024,4608]{1,0:T(8,128)(2,1)} %get-tuple-element.54.refs_0_, bf16[1024,1152]{1,0:T(8,128)(2,1)} %bitcast.277, bf16[1024,1152]{1,0:T(8,128)(2,1)} %bitcast.318, ...), custom_call_target="tpu_custom_call" | custom-call | flops 13589544960 | bytes 13271040 | tf_op jit(solution)/shard_map/shard_outer/pallas_call | solution.py:520
  404.1 9.3 %add_convert_fusion.refs_0_ = bf16[4,2,45,8,1152]{4,3,2,1,0:T(8,128)(2,1)} fusion(bf16[4,2,45,8,1152]{4,3,2,1,0:T(8,128)(2,1)} %collective-permute-done.19, bf16[4,2,45,8,1152]{4,3,2,1,0:T(8,128)(2,1)} %get-tuple-element.55), kind=kLoop, calls=%fused_computation.2 | loop fusion | flops 13271040 | bytes 19906560 | tf_op jit(solution)/shard_map/convert_element_type | solution.py:1003
  413.4 11.8 %reduce-scatter.8.cloned.1.call-done.refs_1_.refs_0_ = bf16[72,4608]{1,0:T(8,128)(2,1)} async-done(((bf16[1152,4608]{1,0:T(8,128)(2,1)}), bf16[72,4608]{1,0:T(8,128)(2,1)}) %reduce-scatter.8.cloned.1.call-update) | async-done | bytes 663568 | tf_op jit(solution)/shard_map/reduce_scatter | solution.py:249
  430.6 42.4 %attend_back.2 = (bf16[1,512,1152]{2,1,0:T(8,128)(2,1)}, bf16[1,1024,1152]{2,1,0:T(8,128)(2,1)}, bf16[1,1024,1152]{2,1,0:T(8,128)(2,1)}) custom-call(s32[1]{0:T(128)} %bitcast.17.refs_0_, s32[2]{0:T(128)} %pad_add_fusion.refs_1_, bf16[1,512,1152]{2,1,0:T(8,128)(2,1)} %fusion.27.refs_2_, bf16[1,1024,2304]{2,1,0:T(8,128)(2,1)} %fusion.9.refs_3_.refs_4_, ...), custom_call_target="tpu_custom_call" | custom-call | flops 10737418240 | bytes 14155776 | tf_op jit(solution)/shard_map/attend_back/pallas_call | solution.py:710
  481.9 42.1 %attend_back.3 = (bf16[1,512,1152]{2,1,0:T(8,128)(2,1)}, bf16[1,1024,1152]{2,1,0:T(8,128)(2,1)}, bf16[1,1024,1152]{2,1,0:T(8,128)(2,1)}) custom-call(s32[1]{0:T(128)} %bitcast.27.refs_0_, s32[2]{0:T(128)} %pad_add_fusion.refs_1_, bf16[1,512,1152]{2,1,0:T(8,128)(2,1)} %fusion.26.refs_2_, bf16[1,1024,2304]{2,1,0:T(8,128)(2,1)} %fusion.10.refs_3_.refs_4_.refs_1_, ...), custom_call_target="tpu_custom_call" | custom-call | flops 10737418240 | bytes 14155776 | tf_op jit(solution)/shard_map/attend_back/pallas_call | solution.py:710
  524.0 25.0 %shard_outer.3.refs_1_ = bf16[4,2,2,27,8,1152]{5,4,3,2,1,0:T(8,128)(2,1)} custom-call(s32[3]{0:T(128)} %pad_add_fusion.1.refs_0_.spots_ref, bf16[512,1152]{1,0:T(8,128)(2,1)} %bitcast.259, bf16[512,1152]{1,0:T(8,128)(2,1)} %bitcast.285, bf16[1024,1152]{1,0:T(8,128)(2,1)} %bitcast.317, bf16[1024,1152]{1,0:T(8,128)(2,1)} %bitcast.280, ...), custom_call_target="tpu_custom_call" | custom-call | flops 13589544960 | bytes 7962624 | tf_op jit(solution)/shard_map/shard_outer/pallas_call | solution.py:520
  591.7 25.3 %collective-permute-done.20 = bf16[512,1152]{1,0:T(8,128)(2,1)S(1)} collective-permute-done((bf16[512,1152]{1,0:T(8,128)(2,1)}, bf16[512,1152]{1,0:T(8,128)(2,1)S(1)}, u32[]{:S(2)}, u32[]{:S(2)}) %collective-permute-start.20) | collective-permute-done | bytes 1179680 | tf_op jit(solution)/shard_map/ppermute | solution.py:47
  702.2 15.5 %collective-permute-done.26.refs_0_ = f32[4,2,160,128]{3,2,1,0:T(8,128)S(1)} collective-permute-done((f32[4,2,160,128]{3,2,1,0:T(8,128)S(1)}, f32[4,2,160,128]{3,2,1,0:T(8,128)S(1)}, u32[]{:S(2)}, u32[]{:S(2)}) %collective-permute-start.26) | collective-permute-done | bytes 655392 | tf_op jit(solution)/shard_map/ppermute | solution.py:47
  766.1 12.5 %collective-permute-done.33.refs_0_ = f32[4,2,160,128]{3,2,1,0:T(8,128)S(1)} collective-permute-done((f32[4,2,160,128]{3,2,1,0:T(8,128)S(1)}, f32[4,2,160,128]{3,2,1,0:T(8,128)S(1)}, u32[]{:S(2)}, u32[]{:S(2)}) %collective-permute-start.33) | collective-permute-done | bytes 655392 | tf_op jit(solution)/shard_map/ppermute | solution.py:47
  785.1 10.9 %muon_apply.1 = (f32[72,2304]{1,0:T(8,128)}, f32[72,576]{1,0:T(8,128)}, f32[288,576]{1,0:T(8,128)}, f32[216,576]{1,0:T(8,128)}, f32[432,576]{1,0:T(8,128)}) custom-call(s32[3]{0:T(128)} %pad_add_fusion.1.refs_0_.spots_ref, f32[4,2,160,128]{3,2,1,0:T(8,128)} %copy-done.12, f32[4,2,160,128]{3,2,1,0:T(8,128)} %tie.99.refs_1_, f32[4,2,160,128]{3,2,1,0:T(8,128)} %tie.100.refs_2_, ...), custom_call_target="tpu_custom_call" | custom-call | tf_op jit(solution)/shard_map/muon_apply/pallas_call | solution.py:880
  (507 shorter events, 328.8 us)
Async XLA Ops:
  14.9 19.1 %all-to-all-start = ((f32[32,1,1656]{2,1,0:T(1,128)}), f32[32,1,1656]{2,1,0:T(1,128)S(1)}, u32[]{:S(2)}, u32[]{:S(2)}) async-start(f32[32,1,1656]{2,1,0:T(1,128)} %all_to_all.24), calls=%async_computation | async-start | bytes 425984 | tf_op jit(solution)/shard_map/all_to_all | solution.py:323
  21.1 22.5 %collective-permute-start.2 = (bf16[16,8,1152]{2,1,0:T(8,128)(2,1)S(1)}, bf16[16,8,1152]{2,1,0:T(8,128)(2,1)}, u32[]{:S(2)}, u32[]{:S(2)}) collective-permute-start(bf16[16,8,1152]{2,1,0:T(8,128)(2,1)S(1)} %get-tuple-element.201.refs_1_.refs_2_), channel_id=1, source_target_pairs={{0,8},{2,10},{4,12},{6,14},{8,16},{10,18},{12,20},{14,22},{16,24},... | collective-permute-start | bytes 884744 | tf_op jit(solution)/shard_map/ppermute | solution.py:47
  22.3 31.1 %collective-permute-start.1 = (bf16[16,8,1152]{2,1,0:T(8,128)(2,1)S(1)}, bf16[16,8,1152]{2,1,0:T(8,128)(2,1)S(1)}, u32[]{:S(2)}, u32[]{:S(2)}) collective-permute-start(bf16[16,8,1152]{2,1,0:T(8,128)(2,1)S(1)} %get-tuple-element.201.refs_1_.refs_2_), channel_id=1, source_target_pairs={{0,24},{2,26},{4,28},{6,30},{8,0},{10,2},{12,4},{14,6},{16,8},{18,... | collective-permute-start | bytes 884744 | tf_op jit(solution)/shard_map/ppermute | solution.py:47
  22.7 22.2 %collective-permute-start.4 = (bf16[20,8,1152]{2,1,0:T(8,128)(2,1)S(1)}, bf16[20,8,1152]{2,1,0:T(8,128)(2,1)S(1)}, u32[]{:S(2)}, u32[]{:S(2)}) collective-permute-start(bf16[20,8,1152]{2,1,0:T(8,128)(2,1)S(1)} %get-tuple-element.199.refs_3_), channel_id=1, source_target_pairs={{0,4},{2,6},{4,0},{6,2},{8,12},{10,14},{12,8},{14,10},{16,20},{18,... | collective-permute-start | bytes 1105928 | tf_op jit(solution)/shard_map/ppermute | solution.py:47
  39.1 16.5 %all-to-all-start.1 = ((f32[32,2,432]{2,1,0:T(2,128)}), f32[32,2,432]{2,1,0:T(2,128)S(1)}, u32[]{:S(2)}, u32[]{:S(2)}) async-start(f32[32,2,432]{2,1,0:T(2,128)} %bitcast.7), calls=%async_computation.1 | async-start | bytes 262144 | tf_op jit(solution)/shard_map/all_to_all | solution.py:323
  43.6 212.3 %all-gather.3.cloned.1.call-start = ((), (), s32[]{:S(2)}) async-start(), calls=%async_computation.7 | async-start | bytes 11280384 | tf_op jit(solution)/shard_map/all_gather | solution.py:939
  43.7 24.9 %collective-permute-start.3 = (bf16[16,8,1152]{2,1,0:T(8,128)(2,1)}, bf16[16,8,1152]{2,1,0:T(8,128)(2,1)}, u32[]{:S(2)}, u32[]{:S(2)}) collective-permute-start(bf16[16,8,1152]{2,1,0:T(8,128)(2,1)} %tie.54), channel_id=1, source_target_pairs={{0,8},{2,10},{4,12},{6,14},{8,16},{10,18},{12,20},{14,22},{16,24},... | collective-permute-start | bytes 884744 | tf_op jit(solution)/shard_map/ppermute | solution.py:47
  47.6 24.2 %collective-permute-start.5 = (bf16[2,20,8,1152]{3,2,1,0:T(8,128)(2,1)}, bf16[2,20,8,1152]{3,2,1,0:T(8,128)(2,1)}, u32[]{:S(2)}, u32[]{:S(2)}) collective-permute-start(bf16[2,20,8,1152]{3,2,1,0:T(8,128)(2,1)} %pad_maximum_fusion.5.refs_3_), channel_id=1, source_target_pairs={{0,24},{2,26},{4,28},{6,30},{8,0},{10,2},{12,4},{14,6},{16,8},{18,... | collective-permute-start | bytes 2211848 | tf_op jit(solution)/shard_map/ppermute | solution.py:47
  47.8 37.1 %collective-permute-start.9 = (bf16[2,20,8,1152]{3,2,1,0:T(8,128)(2,1)}, bf16[2,20,8,1152]{3,2,1,0:T(8,128)(2,1)}, u32[]{:S(2)}, u32[]{:S(2)}) collective-permute-start(bf16[2,20,8,1152]{3,2,1,0:T(8,128)(2,1)} %pad_maximum_fusion.5.refs_3_), channel_id=1, source_target_pairs={{0,8},{2,10},{4,12},{6,14},{8,16},{10,18},{12,20},{14,22},{16,24},... | collective-permute-start | bytes 2211848 | tf_op jit(solution)/shard_map/ppermute | solution.py:47
  52.2 52.7 %collective-permute-start.6 = (bf16[512,1152]{1,0:T(8,128)(2,1)}, bf16[512,1152]{1,0:T(8,128)(2,1)S(1)}, u32[]{:S(2)}, u32[]{:S(2)}) collective-permute-start(bf16[512,1152]{1,0:T(8,128)(2,1)} %tie.60), channel_id=1, source_target_pairs={{0,1},{1,0},{2,3},{3,2},{4,5},{5,4},{6,7},{7,6},{8,9},{9,8},{10,11... | collective-permute-start | bytes 3538952 | tf_op jit(solution)/shard_map/ppermute | solution.py:47
  54.2 50.8 %collective-permute-start.12 = (bf16[2,20,8,1152]{3,2,1,0:T(8,128)(2,1)}, bf16[2,20,8,1152]{3,2,1,0:T(8,128)(2,1)}, u32[]{:S(2)}, u32[]{:S(2)}) collective-permute-start(bf16[2,20,8,1152]{3,2,1,0:T(8,128)(2,1)} %pad_maximum_fusion.5.refs_3_), channel_id=1, source_target_pairs={{0,2},{2,0},{4,6},{6,4},{8,10},{10,8},{12,14},{14,12},{16,18},{18,... | collective-permute-start | bytes 2211848 | tf_op jit(solution)/shard_map/ppermute | solution.py:47
  69.9 26.5 %collective-permute-start.7 = (bf16[4,16,8,1152]{3,2,1,0:T(8,128)(2,1)S(1)}, bf16[4,16,8,1152]{3,2,1,0:T(8,128)(2,1)}, u32[]{:S(2)}, u32[]{:S(2)}) collective-permute-start(bf16[4,16,8,1152]{3,2,1,0:T(8,128)(2,1)S(1)} %pad_maximum_fusion.4.refs_1_.refs_2_), channel_id=1, source_target_pairs={{0,4},{2,6},{4,0},{6,2},{8,12},{10,14},{12,8},{14,10},{16,20},{18,... | collective-permute-start | bytes 3538952 | tf_op jit(solution)/shard_map/ppermute | solution.py:47
  71.8 35.6 %collective-permute-start.10 = (bf16[4,16,8,1152]{3,2,1,0:T(8,128)(2,1)S(1)}, bf16[4,16,8,1152]{3,2,1,0:T(8,128)(2,1)S(1)}, u32[]{:S(2)}, u32[]{:S(2)}) collective-permute-start(bf16[4,16,8,1152]{3,2,1,0:T(8,128)(2,1)S(1)} %pad_maximum_fusion.4.refs_1_.refs_2_), channel_id=1, source_target_pairs={{0,2},{2,0},{4,6},{6,4},{8,10},{10,8},{12,14},{14,12},{16,18},{18,... | collective-permute-start | bytes 3538952 | tf_op jit(solution)/shard_map/ppermute | solution.py:47
  84.9 18.8 %collective-permute-start.8 = (bf16[2,20,8,1152]{3,2,1,0:T(8,128)(2,1)}, bf16[2,20,8,1152]{3,2,1,0:T(8,128)(2,1)}, u32[]{:S(2)}, u32[]{:S(2)}) collective-permute-start(bf16[2,20,8,1152]{3,2,1,0:T(8,128)(2,1)} %tie.57.refs_2_.refs_4_.refs_3_), channel_id=1, source_target_pairs={{0,24},{2,26},{4,28},{6,30},{8,0},{10,2},{12,4},{14,6},{16,8},{18,... | collective-permute-start | bytes 2211848 | tf_op jit(solution)/shard_map/ppermute | solution.py:47
  122.7 178.6 %all-gather.5.cloned.1.call-start = ((), (), s32[]{:S(2)}) async-start(), calls=%async_computation.8 | async-start | bytes 11280384 | tf_op jit(solution)/shard_map/all_gather | solution.py:963
  133.3 46.2 %collective-permute-start.17 = (bf16[512,1152]{1,0:T(8,128)(2,1)}, bf16[512,1152]{1,0:T(8,128)(2,1)S(1)}, u32[]{:S(2)}, u32[]{:S(2)}) collective-permute-start(bf16[512,1152]{1,0:T(8,128)(2,1)} %tie.72), channel_id=1, source_target_pairs={{0,1},{1,0},{2,3},{3,2},{4,5},{5,4},{6,7},{7,6},{8,9},{9,8},{10,11... | collective-permute-start | bytes 3538952 | tf_op jit(solution)/shard_map/ppermute | solution.py:47
  180.6 17.5 %collective-permute-start.18 = (bf16[72,2304]{1,0:T(8,128)(2,1)}, bf16[72,2304]{1,0:T(8,128)(2,1)S(1)}, u32[]{:S(2)}, u32[]{:S(2)}) collective-permute-start(bf16[72,2304]{1,0:T(8,128)(2,1)} %tie.75), channel_id=1, source_target_pairs={{0,1},{1,0},{2,3},{3,2},{4,5},{5,4},{6,7},{7,6},{8,9},{9,8},{10,11... | collective-permute-start | bytes 995336 | tf_op jit(solution)/shard_map/ppermute | solution.py:47
  201.3 223.9 %reduce-scatter.8.cloned.1.call-start = ((), (), s32[]{:S(2)}) async-start(), calls=%async_computation.9 | async-start | bytes 11280384 | tf_op jit(solution)/shard_map/reduce_scatter | solution.py:249
  298.5 349.3 %reduce-scatter.10.cloned.1.call-start = ((), (), s32[]{:S(2)}) async-start(), calls=%async_computation.10 | async-start | bytes 7464960
  425.2 250.5 %reduce-scatter.12.cloned.1.call-start = ((), (), s32[]{:S(2)}) async-start(), calls=%async_computation.11 | async-start | bytes 8460288
  565.0 26.7 %collective-permute-start.21 = (bf16[512,1152]{1,0:T(8,128)(2,1)S(1)}, bf16[512,1152]{1,0:T(8,128)(2,1)S(1)}, u32[]{:S(2)}, u32[]{:S(2)}) collective-permute-start(bf16[512,1152]{1,0:T(8,128)(2,1)S(1)} %copy-done.52), channel_id=1, source_target_pairs={{0,1},{1,0},{2,3},{3,2},{4,5},{5,4},{6,7},{7,6},{8,9},{9,8},{10,11... | collective-permute-start | bytes 3538952 | tf_op jit(solution)/shard_map/ppermute | solution.py:47
  566.2 50.8 %collective-permute-start.20 = (bf16[512,1152]{1,0:T(8,128)(2,1)}, bf16[512,1152]{1,0:T(8,128)(2,1)S(1)}, u32[]{:S(2)}, u32[]{:S(2)}) collective-permute-start(bf16[512,1152]{1,0:T(8,128)(2,1)} %fusion.24.refs_8_), channel_id=1, source_target_pairs={{0,1},{1,0},{2,3},{3,2},{4,5},{5,4},{6,7},{7,6},{8,9},{9,8},{10,11... | collective-permute-start | bytes 3538952 | tf_op jit(solution)/shard_map/ppermute | solution.py:47
  641.0 17.3 %all-to-all-start.3 = ((f32[32,1,1656]{2,1,0:T(1,128)}), f32[32,1,1656]{2,1,0:T(1,128)S(1)}, u32[]{:S(2)}, u32[]{:S(2)}) async-start(f32[32,1,1656]{2,1,0:T(1,128)} %all_to_all.22), calls=%async_computation.4 | async-start | bytes 425984 | tf_op jit(solution)/shard_map/all_to_all | solution.py:323
  765.3 18.1 %collective-permute-start.34 = (f32[4,2,160,128]{3,2,1,0:T(8,128)S(1)}, f32[4,2,160,128]{3,2,1,0:T(8,128)S(1)}, u32[]{:S(2)}, u32[]{:S(2)}) collective-permute-start(f32[4,2,160,128]{3,2,1,0:T(8,128)S(1)} %pad_maximum_fusion.6.refs_1_.refs_0_), channel_id=1, source_target_pairs={{0,2},{2,0},{4,6},{6,4},{8,10},{10,8},{12,14},{14,12},{16,18},{18,... | collective-permute-start | bytes 1966088 | tf_op jit(solution)/shard_map/ppermute | solution.py:47
  (126 other events, 944.5 us)
Sparse Core Ops, SparseCore 0:
  122.8 88.6 all-gather.2
  214.4 86.8 all-gather.4
  305.4 119.7 reduce-scatter.7
  428.7 122.7 reduce-scatter.9
  556.0 104.6 reduce-scatter.11

commit v13 on v12

--- a/solution.py
+++ b/solution.py
@@ -1026,6 +1026,8 @@
         if i + 1 < count:
             far_parts.append(far_steps(dk, dv))
             sent = sent + far_parts[-1].advance()
+    far_parts.append(far_steps(grad_k[-1], grad_v[-1]))
+    sent = sent + far_parts[-1].advance()
     unit_last = math.gcd(n_qkv, 8)
     (term_last,) = shard_outer(
         net.spots(),
@@ -1037,9 +1039,7 @@
         net.z.size, width, unit_last, n_qkv // unit_last, sent, split=False,
     )
     sum_last = net.scatter(term_last.reshape(dp * n_qkv, width))
-    grad_k[-1] = tie(grad_k[-1], term_last)
-    far_parts.append(far_steps(grad_k[-1], grad_v[-1]))
-    sent = far_parts[-1].advance()
+    sent = [term_last]
     grad_q[0] = tie(grad_q[0], *sent)
     bias_q = sum(jnp.sum(each.astype(F32), axis=(0, 1)) for each in grad_q)
     bias_v = sum(jnp.sum(each.astype(F32), axis=(0, 1)) for each in grad_v)

time: 814 us -> 814 us (level)
    unnamed x220 -> x202, local copies, waits for them, and re-layouts: 28.5 us -> 27.4 us
where the time goes in v13:
time: 814 us; the launch traced here: 802 us
  Pallas kernels  279 us (34%)
  waiting for transfers between devices  159 us (20%)
  matrix products  144 us (18%)
  local copies, waits for them, and re-layouts  72.2 us (9%)
  other arithmetic  71.6 us (9%)
  starting transfers between devices  60.4 us (7%)
  between operations  15.5 us (2%)
    ppermute x36, waiting for transfers between devices, send(): return lax.ppermute(value, self.name, pairs)  125 us
    pallas_call x2, Pallas kernels, attend_back(): pl.pallas_call(without(attend_back_kernel, 8, len(deps), heads, tile), gr...  84.7 us
    dot_general x6, matrix products, dot_t(): return jnp.einsum('srk,nk->srn', left, right, preferred_element_type=F32)  63.1 us
    dot_general x12, matrix products, dot(): return jnp.einsum('srn,nk->srk', left, right, preferred_element_type=F32)  60.8 us
    pallas_call x2, Pallas kernels, attend(): pl.pallas_call(without(attend_kernel, 5, len(deps), heads, tile), grid_sp...  58.1 us
    pallas_call x2, Pallas kernels, shard_outer(): pl.pallas_call(functools.partial(shard_outer_kernel, {'loads': loads, 'pa...  49.3 us
    ppermute x36, starting transfers between devices, send(): return lax.ppermute(value, self.name, pairs)  38.6 us
    unnamed x202, local copies, waits for them, and re-layouts  27.4 us
  transfers between devices with their start and end apart: 45, of which 23 were waited for; matrix products, arithmetic and copies ran while one was open for 31% of the time, Pallas kernels for 32%

profile of v13, /device:TPU:11, one launch (start us, length us, event | category | flops | bytes accessed | tf_op | source)
XLA Modules:
  0.0 801.7 jit_solution(15850372893708196534)
XLA Ops:
  23.0 11.0 %all-to-all-done = f32[32,1,1656]{2,1,0:T(1,128)S(1)} async-done(((f32[32,1,1656]{2,1,0:T(1,128)}), f32[32,1,1656]{2,1,0:T(1,128)S(1)}, u32[]{:S(2)}, u32[]{:S(2)}) %all-to-all-start) | async-done | bytes 212000 | tf_op jit(solution)/shard_map/all_to_all | solution.py:323
  55.6 12.9 %collective-permute-done.3.refs_0_ = bf16[16,8,1152]{2,1,0:T(8,128)(2,1)} collective-permute-done((bf16[16,8,1152]{2,1,0:T(8,128)(2,1)}, bf16[16,8,1152]{2,1,0:T(8,128)(2,1)}, u32[]{:S(2)}, u32[]{:S(2)}) %collective-permute-start.3) | collective-permute-done | bytes 294944 | tf_op jit(solution)/shard_map/ppermute | solution.py:47
  76.7 8.2 %collective-permute-done.9.refs_0_ = bf16[2,20,8,1152]{3,2,1,0:T(8,128)(2,1)} collective-permute-done((bf16[2,20,8,1152]{3,2,1,0:T(8,128)(2,1)}, bf16[2,20,8,1152]{3,2,1,0:T(8,128)(2,1)}, u32[]{:S(2)}, u32[]{:S(2)}) %collective-permute-start.9) | collective-permute-done | bytes 737312 | tf_op jit(solution)/shard_map/ppermute | solution.py:47
  109.4 9.1 %place.1 = (bf16[4,2,2,27,8,1152]{5,4,3,2,1,0:T(8,128)(2,1)}, bf16[4,2,2,9,8,1152]{5,4,3,2,1,0:T(8,128)(2,1)}) custom-call(s32[3]{0:T(128)} %pad_add_fusion.1.refs_0_.spots_ref, bf16[4,16,8,1152]{3,2,1,0:T(8,128)(2,1)} %copy-done.1, bf16[4,16,8,1152]{3,2,1,0:T(8,128)(2,1)} %tie.60.refs_2_, bf16[2,20,8,1152]{3,2,1,0:T(8,128)(2,1)} %pad_maximum_fusion.5.refs_3_, ...), custom_call_target="tpu_custom_call" | custom-call | bytes 21233664 | tf_op jit(solution)/shard_map/place/pallas_call | solution.py:198
  135.3 10.5 %fusion.9.refs_3_.refs_4_ = bf16[1,1024,2304]{2,1,0:T(8,128)(2,1)} fusion(bf16[1024,1152]{1,0:T(8,128)(2,1)S(1)} %copy-done.16, f32[2304]{0:T(1024)} %concatenate.64, bf16[3456,1152]{1,0:T(8,128)(2,1)} %bitcast.243), kind=kOutput, calls=%fused_computation.20 | convolution fusion | flops 5440536576 | bytes 12398592 | tf_op jit(solution)/shard_map/srk,nk->srn/dot_general | solution.py:346
  150.5 29.2 %attend.2 = (bf16[1,512,1152]{2,1,0:T(8,128)(2,1)}, f32[1,16,1,512]{3,2,1,0:T(1,128)}) custom-call(s32[1]{0:T(128)} %bitcast.17.refs_0_, s32[2]{0:T(128)} %pad_add_fusion.refs_1_, bf16[1,512,1152]{2,1,0:T(8,128)(2,1)} %fusion.27.refs_2_, bf16[1,1024,2304]{2,1,0:T(8,128)(2,1)} %fusion.9.refs_3_.refs_4_, bf16[1,1024,2304]{2,1,0:T(8,128)(2,1)} %fusion.9.refs_3_.refs_4_), custom_call_target="tpu_custom_call" | custom-call | flops 4294967296 | bytes 7077888 | tf_op jit(solution)/shard_map/attend/pallas_call | solution.py:623
  186.9 11.4 %fusion.10.refs_3_.refs_4_.refs_1_ = bf16[1,1024,2304]{2,1,0:T(8,128)(2,1)} fusion(bf16[1024,1152]{1,0:T(8,128)(2,1)S(1)} %get-tuple-element.191.refs_9_, f32[2304]{0:T(1024)S(1)} %copy-done.74, bf16[3456,1152]{1,0:T(8,128)(2,1)} %bitcast.245), kind=kOutput, calls=%fused_computation.21 | convolution fusion | flops 5440536576 | bytes 12395520 | tf_op jit(solution)/shard_map/srk,nk->srn/dot_general | solution.py:346
  211.6 28.9 %attend.3 = (bf16[1,512,1152]{2,1,0:T(8,128)(2,1)}, f32[1,16,1,512]{3,2,1,0:T(1,128)}) custom-call(s32[1]{0:T(128)} %bitcast.27.refs_0_, s32[2]{0:T(128)} %pad_add_fusion.refs_1_, bf16[1,512,1152]{2,1,0:T(8,128)(2,1)} %fusion.26.refs_2_, bf16[1,1024,2304]{2,1,0:T(8,128)(2,1)} %fusion.10.refs_3_.refs_4_.refs_1_, ...), custom_call_target="tpu_custom_call" | custom-call | flops 4294967296 | bytes 7077888 | tf_op jit(solution)/shard_map/attend/pallas_call | solution.py:623
  243.1 8.3 %fusion.82 = (f32[2,512]{1,0:T(2,128)S(1)}, f32[2,512,1152]{2,1,0:T(8,128)S(1)}, f32[2,512,1152]{2,1,0:T(8,128)}) fusion(f32[2,1152]{1,0:T(2,128)S(1)} %get-tuple-element.216, bf16[2,1,512,1152]{3,2,1,0:T(8,128)(2,1)S(1)} %copy-done.37, f32[1152]{0:T(1024)S(1)} %copy-done.79, bf16[2,512,1152]{2,1,0:T(8,128)(2,1)} %constant_dynamic-update-slice_fusion, ...), kind=kOutput, calls=%fused_computation.215 | convolution fusion | flops 2723806208 | bytes 16827904 | tf_op jit(solution)/shard_map/srk,nk->srn/dot_general | solution.py:346
  255.9 25.0 %hidden_forward.1 = (bf16[1024,4608]{1,0:T(8,128)(2,1)}, bf16[1024,4608]{1,0:T(8,128)(2,1)}) custom-call(bf16[1024,1152]{1,0:T(8,128)(2,1)} %bitcast.276, bf16[4608,1152]{1,0:T(8,128)(2,1)} %all-gather.3.cloned.1.call-done.w_ref, f32[1,4608]{1,0:T(1,128)} %reshape.497.b_ref), custom_call_target="tpu_custom_call" | custom-call | flops 10871635968 | bytes 31850496 | tf_op jit(solution)/shard_map/hidden_forward/pallas_call | solution.py:378
  281.0 17.6 %fusion.refs_1_ = bf16[1152,4608]{1,0:T(8,128)(2,1)} fusion(bf16[2,512,1152]{2,1,0:T(8,128)(2,1)S(1)} %fusion.16.refs_0_, bf16[2,512,4608]{2,1,0:T(8,128)(2,1)} %bitcast.240), kind=kOutput, calls=%fused_computation.1 | convolution fusion | flops 10876944384 | bytes 22413312 | tf_op jit(solution)/shard_map/srn,srk->nk/dot_general | solution.py:430
  301.3 20.2 %hidden_backward.1 = (bf16[1024,4608]{1,0:T(8,128)(2,1)}, f32[1,4608]{1,0:T(1,128)}) custom-call(bf16[1024,1152]{1,0:T(8,128)(2,1)} %bitcast.238, bf16[1152,4608]{1,0:T(8,128)(2,1)} %all-gather.5.cloned.1.call-done.w_ref, bf16[1024,4608]{1,0:T(8,128)(2,1)} %get-tuple-element.53.slope_ref), custom_call_target="tpu_custom_call" | custom-call | flops 10871635968 | bytes 31850496 | tf_op jit(solution)/shard_map/hidden_backward/pallas_call | solution.py:410
  321.5 23.3 %multiply_reduce_fusion = (f32[2,1152]{1,0:T(2,128)}, f32[2,512]{1,0:T(2,128)S(1)}, f32[2,512]{1,0:T(2,128)S(1)}, f32[2,1152]{1,0:T(2,128)}, f32[2,512,1152]{2,1,0:T(8,128)}) fusion(f32[2,512,1152]{2,1,0:T(8,128)} %copy-done.9, f32[2,512]{1,0:T(2,128)S(1)} %add_rsqrt_fusion, f32[2,512]{1,0:T(2,128)S(1)} %broadcast_multiply_fusion.4, ...), kind=kOutput, calls=%fused_computation.34 | convolution fusion | flops 10882246656 | bytes 29535232 | tf_op jit(solution)/shard_map/srn,nk->srk/dot_general | solution.py:350
  344.8 23.6 %fusion.17 = (f32[2,1152]{1,0:T(2,128)S(1)}, bf16[2,1,512,1152]{3,2,1,0:T(8,128)(2,1)}, f32[1152]{0:T(1024)S(1)}, bf16[2,512,1152]{2,1,0:T(8,128)(2,1)}, f32[2,512,1152]{2,1,0:T(8,128)}) fusion(bf16[2,1,512,1152]{3,2,1,0:T(8,128)(2,1)S(1)} %copy-done.42, f32[2,512,1152]{2,1,0:T(8,128)} %copy-done.9, f32[2,1152]{1,0:T(2,128)S(1)} %get-tuple-element.213, ...), kind=kOutput, calls=%fused_computation.26 | convolution fusion | flops 10894046208 | bytes 41350144 | tf_op jit(solution)/shard_map/srk,nk->srn/dot_general | solution.py:346
  368.4 24.0 %shard_outer.2 = (bf16[4,2,45,8,1152]{4,3,2,1,0:T(8,128)(2,1)}, bf16[4,2,45,8,1152]{4,3,2,1,0:T(8,128)(2,1)}) custom-call(s32[3]{0:T(128)} %pad_add_fusion.1.refs_0_.spots_ref, bf16[1024,4608]{1,0:T(8,128)(2,1)} %get-tuple-element.54.refs_0_, bf16[1024,1152]{1,0:T(8,128)(2,1)} %bitcast.277, bf16[1024,1152]{1,0:T(8,128)(2,1)} %bitcast.318, ...), custom_call_target="tpu_custom_call" | custom-call | flops 13589544960 | bytes 13271040 | tf_op jit(solution)/shard_map/shard_outer/pallas_call | solution.py:520
  403.5 9.3 %add_convert_fusion.refs_0_ = bf16[4,2,45,8,1152]{4,3,2,1,0:T(8,128)(2,1)} fusion(bf16[4,2,45,8,1152]{4,3,2,1,0:T(8,128)(2,1)} %collective-permute-done.19, bf16[4,2,45,8,1152]{4,3,2,1,0:T(8,128)(2,1)} %get-tuple-element.55), kind=kLoop, calls=%fused_computation.2 | loop fusion | flops 13271040 | bytes 19906560 | tf_op jit(solution)/shard_map/convert_element_type | solution.py:1003
  412.7 12.5 %reduce-scatter.8.cloned.1.call-done.refs_1_.refs_0_ = bf16[72,4608]{1,0:T(8,128)(2,1)} async-done(((bf16[1152,4608]{1,0:T(8,128)(2,1)}), bf16[72,4608]{1,0:T(8,128)(2,1)}) %reduce-scatter.8.cloned.1.call-update) | async-done | bytes 663568 | tf_op jit(solution)/shard_map/reduce_scatter | solution.py:249
  430.1 42.2 %attend_back.2 = (bf16[1,512,1152]{2,1,0:T(8,128)(2,1)}, bf16[1,1024,1152]{2,1,0:T(8,128)(2,1)}, bf16[1,1024,1152]{2,1,0:T(8,128)(2,1)}) custom-call(s32[1]{0:T(128)} %bitcast.17.refs_0_, s32[2]{0:T(128)} %pad_add_fusion.refs_1_, bf16[1,512,1152]{2,1,0:T(8,128)(2,1)} %fusion.27.refs_2_, bf16[1,1024,2304]{2,1,0:T(8,128)(2,1)} %fusion.9.refs_3_.refs_4_, ...), custom_call_target="tpu_custom_call" | custom-call | flops 10737418240 | bytes 14155776 | tf_op jit(solution)/shard_map/attend_back/pallas_call | solution.py:710
  481.0 42.5 %attend_back.3 = (bf16[1,512,1152]{2,1,0:T(8,128)(2,1)}, bf16[1,1024,1152]{2,1,0:T(8,128)(2,1)}, bf16[1,1024,1152]{2,1,0:T(8,128)(2,1)}) custom-call(s32[1]{0:T(128)} %bitcast.27.refs_0_, s32[2]{0:T(128)} %pad_add_fusion.refs_1_, bf16[1,512,1152]{2,1,0:T(8,128)(2,1)} %fusion.26.refs_2_, bf16[1,1024,2304]{2,1,0:T(8,128)(2,1)} %fusion.10.refs_3_.refs_4_.refs_1_, ...), custom_call_target="tpu_custom_call" | custom-call | flops 10737418240 | bytes 14155776 | tf_op jit(solution)/shard_map/attend_back/pallas_call | solution.py:710
  532.4 25.3 %shard_outer.3.refs_1_ = bf16[4,2,2,27,8,1152]{5,4,3,2,1,0:T(8,128)(2,1)} custom-call(s32[3]{0:T(128)} %pad_add_fusion.1.refs_0_.spots_ref, bf16[512,1152]{1,0:T(8,128)(2,1)} %bitcast.259, bf16[512,1152]{1,0:T(8,128)(2,1)} %bitcast.284, bf16[1024,1152]{1,0:T(8,128)(2,1)} %bitcast.316, bf16[1024,1152]{1,0:T(8,128)(2,1)} %bitcast.317, ...), custom_call_target="tpu_custom_call" | custom-call | flops 13589544960 | bytes 7962624 | tf_op jit(solution)/shard_map/shard_outer/pallas_call | solution.py:520
  590.3 25.4 %collective-permute-done.20 = bf16[512,1152]{1,0:T(8,128)(2,1)S(1)} collective-permute-done((bf16[512,1152]{1,0:T(8,128)(2,1)}, bf16[512,1152]{1,0:T(8,128)(2,1)S(1)}, u32[]{:S(2)}, u32[]{:S(2)}) %collective-permute-start.20) | collective-permute-done | bytes 1179680 | tf_op jit(solution)/shard_map/ppermute | solution.py:47
  700.9 15.3 %collective-permute-done.26.refs_0_ = f32[4,2,160,128]{3,2,1,0:T(8,128)S(1)} collective-permute-done((f32[4,2,160,128]{3,2,1,0:T(8,128)S(1)}, f32[4,2,160,128]{3,2,1,0:T(8,128)S(1)}, u32[]{:S(2)}, u32[]{:S(2)}) %collective-permute-start.26) | collective-permute-done | bytes 655392 | tf_op jit(solution)/shard_map/ppermute | solution.py:47
  764.7 13.2 %collective-permute-done.33.refs_0_ = f32[4,2,160,128]{3,2,1,0:T(8,128)S(1)} collective-permute-done((f32[4,2,160,128]{3,2,1,0:T(8,128)S(1)}, f32[4,2,160,128]{3,2,1,0:T(8,128)S(1)}, u32[]{:S(2)}, u32[]{:S(2)}) %collective-permute-start.33) | collective-permute-done | bytes 655392 | tf_op jit(solution)/shard_map/ppermute | solution.py:47
  783.9 11.0 %muon_apply.1 = (f32[72,2304]{1,0:T(8,128)}, f32[72,576]{1,0:T(8,128)}, f32[288,576]{1,0:T(8,128)}, f32[216,576]{1,0:T(8,128)}, f32[432,576]{1,0:T(8,128)}) custom-call(s32[3]{0:T(128)} %pad_add_fusion.1.refs_0_.spots_ref, f32[4,2,160,128]{3,2,1,0:T(8,128)} %copy-done.12, f32[4,2,160,128]{3,2,1,0:T(8,128)} %tie.97.refs_1_, f32[4,2,160,128]{3,2,1,0:T(8,128)} %tie.98.refs_2_, ...), custom_call_target="tpu_custom_call" | custom-call | tf_op jit(solution)/shard_map/muon_apply/pallas_call | solution.py:880
  (488 shorter events, 326.4 us)
Async XLA Ops:
  14.9 19.1 %all-to-all-start = ((f32[32,1,1656]{2,1,0:T(1,128)}), f32[32,1,1656]{2,1,0:T(1,128)S(1)}, u32[]{:S(2)}, u32[]{:S(2)}) async-start(f32[32,1,1656]{2,1,0:T(1,128)} %all_to_all.24), calls=%async_computation | async-start | bytes 425984 | tf_op jit(solution)/shard_map/all_to_all | solution.py:323
  21.1 22.5 %collective-permute-start.2 = (bf16[16,8,1152]{2,1,0:T(8,128)(2,1)S(1)}, bf16[16,8,1152]{2,1,0:T(8,128)(2,1)}, u32[]{:S(2)}, u32[]{:S(2)}) collective-permute-start(bf16[16,8,1152]{2,1,0:T(8,128)(2,1)S(1)} %get-tuple-element.201.refs_1_.refs_2_), channel_id=1, source_target_pairs={{0,8},{2,10},{4,12},{6,14},{8,16},{10,18},{12,20},{14,22},{16,24},... | collective-permute-start | bytes 884744 | tf_op jit(solution)/shard_map/ppermute | solution.py:47
  22.3 31.1 %collective-permute-start.1 = (bf16[16,8,1152]{2,1,0:T(8,128)(2,1)S(1)}, bf16[16,8,1152]{2,1,0:T(8,128)(2,1)S(1)}, u32[]{:S(2)}, u32[]{:S(2)}) collective-permute-start(bf16[16,8,1152]{2,1,0:T(8,128)(2,1)S(1)} %get-tuple-element.201.refs_1_.refs_2_), channel_id=1, source_target_pairs={{0,24},{2,26},{4,28},{6,30},{8,0},{10,2},{12,4},{14,6},{16,8},{18,... | collective-permute-start | bytes 884744 | tf_op jit(solution)/shard_map/ppermute | solution.py:47
  22.7 22.2 %collective-permute-start.4 = (bf16[20,8,1152]{2,1,0:T(8,128)(2,1)S(1)}, bf16[20,8,1152]{2,1,0:T(8,128)(2,1)S(1)}, u32[]{:S(2)}, u32[]{:S(2)}) collective-permute-start(bf16[20,8,1152]{2,1,0:T(8,128)(2,1)S(1)} %get-tuple-element.199.refs_3_), channel_id=1, source_target_pairs={{0,4},{2,6},{4,0},{6,2},{8,12},{10,14},{12,8},{14,10},{16,20},{18,... | collective-permute-start | bytes 1105928 | tf_op jit(solution)/shard_map/ppermute | solution.py:47
  39.1 16.5 %all-to-all-start.1 = ((f32[32,2,432]{2,1,0:T(2,128)}), f32[32,2,432]{2,1,0:T(2,128)S(1)}, u32[]{:S(2)}, u32[]{:S(2)}) async-start(f32[32,2,432]{2,1,0:T(2,128)} %bitcast.7), calls=%async_computation.1 | async-start | bytes 262144 | tf_op jit(solution)/shard_map/all_to_all | solution.py:323
  43.6 212.4 %all-gather.3.cloned.1.call-start = ((), (), s32[]{:S(2)}) async-start(), calls=%async_computation.7 | async-start | bytes 11280384 | tf_op jit(solution)/shard_map/all_gather | solution.py:939
  43.7 24.9 %collective-permute-start.3 = (bf16[16,8,1152]{2,1,0:T(8,128)(2,1)}, bf16[16,8,1152]{2,1,0:T(8,128)(2,1)}, u32[]{:S(2)}, u32[]{:S(2)}) collective-permute-start(bf16[16,8,1152]{2,1,0:T(8,128)(2,1)} %tie.53), channel_id=1, source_target_pairs={{0,8},{2,10},{4,12},{6,14},{8,16},{10,18},{12,20},{14,22},{16,24},... | collective-permute-start | bytes 884744 | tf_op jit(solution)/shard_map/ppermute | solution.py:47
  47.6 24.2 %collective-permute-start.5 = (bf16[2,20,8,1152]{3,2,1,0:T(8,128)(2,1)}, bf16[2,20,8,1152]{3,2,1,0:T(8,128)(2,1)}, u32[]{:S(2)}, u32[]{:S(2)}) collective-permute-start(bf16[2,20,8,1152]{3,2,1,0:T(8,128)(2,1)} %pad_maximum_fusion.5.refs_3_), channel_id=1, source_target_pairs={{0,24},{2,26},{4,28},{6,30},{8,0},{10,2},{12,4},{14,6},{16,8},{18,... | collective-permute-start | bytes 2211848 | tf_op jit(solution)/shard_map/ppermute | solution.py:47
  47.8 37.1 %collective-permute-start.9 = (bf16[2,20,8,1152]{3,2,1,0:T(8,128)(2,1)}, bf16[2,20,8,1152]{3,2,1,0:T(8,128)(2,1)}, u32[]{:S(2)}, u32[]{:S(2)}) collective-permute-start(bf16[2,20,8,1152]{3,2,1,0:T(8,128)(2,1)} %pad_maximum_fusion.5.refs_3_), channel_id=1, source_target_pairs={{0,8},{2,10},{4,12},{6,14},{8,16},{10,18},{12,20},{14,22},{16,24},... | collective-permute-start | bytes 2211848 | tf_op jit(solution)/shard_map/ppermute | solution.py:47
  52.2 52.7 %collective-permute-start.6 = (bf16[512,1152]{1,0:T(8,128)(2,1)}, bf16[512,1152]{1,0:T(8,128)(2,1)S(1)}, u32[]{:S(2)}, u32[]{:S(2)}) collective-permute-start(bf16[512,1152]{1,0:T(8,128)(2,1)} %tie.59), channel_id=1, source_target_pairs={{0,1},{1,0},{2,3},{3,2},{4,5},{5,4},{6,7},{7,6},{8,9},{9,8},{10,11... | collective-permute-start | bytes 3538952 | tf_op jit(solution)/shard_map/ppermute | solution.py:47
  54.2 50.8 %collective-permute-start.12 = (bf16[2,20,8,1152]{3,2,1,0:T(8,128)(2,1)}, bf16[2,20,8,1152]{3,2,1,0:T(8,128)(2,1)}, u32[]{:S(2)}, u32[]{:S(2)}) collective-permute-start(bf16[2,20,8,1152]{3,2,1,0:T(8,128)(2,1)} %pad_maximum_fusion.5.refs_3_), channel_id=1, source_target_pairs={{0,2},{2,0},{4,6},{6,4},{8,10},{10,8},{12,14},{14,12},{16,18},{18,... | collective-permute-start | bytes 2211848 | tf_op jit(solution)/shard_map/ppermute | solution.py:47
  69.9 26.5 %collective-permute-start.7 = (bf16[4,16,8,1152]{3,2,1,0:T(8,128)(2,1)S(1)}, bf16[4,16,8,1152]{3,2,1,0:T(8,128)(2,1)}, u32[]{:S(2)}, u32[]{:S(2)}) collective-permute-start(bf16[4,16,8,1152]{3,2,1,0:T(8,128)(2,1)S(1)} %pad_maximum_fusion.4.refs_1_.refs_2_), channel_id=1, source_target_pairs={{0,4},{2,6},{4,0},{6,2},{8,12},{10,14},{12,8},{14,10},{16,20},{18,... | collective-permute-start | bytes 3538952 | tf_op jit(solution)/shard_map/ppermute | solution.py:47
  71.8 35.6 %collective-permute-start.10 = (bf16[4,16,8,1152]{3,2,1,0:T(8,128)(2,1)S(1)}, bf16[4,16,8,1152]{3,2,1,0:T(8,128)(2,1)S(1)}, u32[]{:S(2)}, u32[]{:S(2)}) collective-permute-start(bf16[4,16,8,1152]{3,2,1,0:T(8,128)(2,1)S(1)} %pad_maximum_fusion.4.refs_1_.refs_2_), channel_id=1, source_target_pairs={{0,2},{2,0},{4,6},{6,4},{8,10},{10,8},{12,14},{14,12},{16,18},{18,... | collective-permute-start | bytes 3538952 | tf_op jit(solution)/shard_map/ppermute | solution.py:47
  84.9 18.8 %collective-permute-start.8 = (bf16[2,20,8,1152]{3,2,1,0:T(8,128)(2,1)}, bf16[2,20,8,1152]{3,2,1,0:T(8,128)(2,1)}, u32[]{:S(2)}, u32[]{:S(2)}) collective-permute-start(bf16[2,20,8,1152]{3,2,1,0:T(8,128)(2,1)} %tie.56.refs_2_.refs_4_.refs_3_), channel_id=1, source_target_pairs={{0,24},{2,26},{4,28},{6,30},{8,0},{10,2},{12,4},{14,6},{16,8},{18,... | collective-permute-start | bytes 2211848 | tf_op jit(solution)/shard_map/ppermute | solution.py:47
  122.8 178.5 %all-gather.5.cloned.1.call-start = ((), (), s32[]{:S(2)}) async-start(), calls=%async_computation.8 | async-start | bytes 11280384 | tf_op jit(solution)/shard_map/all_gather | solution.py:963
  133.4 46.3 %collective-permute-start.17 = (bf16[512,1152]{1,0:T(8,128)(2,1)}, bf16[512,1152]{1,0:T(8,128)(2,1)S(1)}, u32[]{:S(2)}, u32[]{:S(2)}) collective-permute-start(bf16[512,1152]{1,0:T(8,128)(2,1)} %tie.71), channel_id=1, source_target_pairs={{0,1},{1,0},{2,3},{3,2},{4,5},{5,4},{6,7},{7,6},{8,9},{9,8},{10,11... | collective-permute-start | bytes 3538952 | tf_op jit(solution)/shard_map/ppermute | solution.py:47
  180.7 17.5 %collective-permute-start.18 = (bf16[72,2304]{1,0:T(8,128)(2,1)}, bf16[72,2304]{1,0:T(8,128)(2,1)S(1)}, u32[]{:S(2)}, u32[]{:S(2)}) collective-permute-start(bf16[72,2304]{1,0:T(8,128)(2,1)} %tie.74), channel_id=1, source_target_pairs={{0,1},{1,0},{2,3},{3,2},{4,5},{5,4},{6,7},{7,6},{8,9},{9,8},{10,11... | collective-permute-start | bytes 995336 | tf_op jit(solution)/shard_map/ppermute | solution.py:47
  201.4 223.8 %reduce-scatter.8.cloned.1.call-start = ((), (), s32[]{:S(2)}) async-start(), calls=%async_computation.9 | async-start | bytes 11280384 | tf_op jit(solution)/shard_map/reduce_scatter | solution.py:249
  298.6 347.8 %reduce-scatter.10.cloned.1.call-start = ((), (), s32[]{:S(2)}) async-start(), calls=%async_computation.10 | async-start | bytes 7464960
  425.2 249.0 %reduce-scatter.12.cloned.1.call-start = ((), (), s32[]{:S(2)}) async-start(), calls=%async_computation.11 | async-start | bytes 8460288
  563.4 26.9 %collective-permute-start.21 = (bf16[512,1152]{1,0:T(8,128)(2,1)}, bf16[512,1152]{1,0:T(8,128)(2,1)S(1)}, u32[]{:S(2)}, u32[]{:S(2)}) collective-permute-start(bf16[512,1152]{1,0:T(8,128)(2,1)} %fusion.25.refs_10_), channel_id=1, source_target_pairs={{0,1},{1,0},{2,3},{3,2},{4,5},{5,4},{6,7},{7,6},{8,9},{9,8},{10,11... | collective-permute-start | bytes 3538952 | tf_op jit(solution)/shard_map/ppermute | solution.py:47
  564.7 51.0 %collective-permute-start.20 = (bf16[512,1152]{1,0:T(8,128)(2,1)}, bf16[512,1152]{1,0:T(8,128)(2,1)S(1)}, u32[]{:S(2)}, u32[]{:S(2)}) collective-permute-start(bf16[512,1152]{1,0:T(8,128)(2,1)} %fusion.24.refs_8_), channel_id=1, source_target_pairs={{0,1},{1,0},{2,3},{3,2},{4,5},{5,4},{6,7},{7,6},{8,9},{9,8},{10,11... | collective-permute-start | bytes 3538952 | tf_op jit(solution)/shard_map/ppermute | solution.py:47
  639.8 17.1 %all-to-all-start.3 = ((f32[32,1,1656]{2,1,0:T(1,128)}), f32[32,1,1656]{2,1,0:T(1,128)S(1)}, u32[]{:S(2)}, u32[]{:S(2)}) async-start(f32[32,1,1656]{2,1,0:T(1,128)} %all_to_all.22), calls=%async_computation.4 | async-start | bytes 425984 | tf_op jit(solution)/shard_map/all_to_all | solution.py:323
  763.9 18.3 %collective-permute-start.34 = (f32[4,2,160,128]{3,2,1,0:T(8,128)S(1)}, f32[4,2,160,128]{3,2,1,0:T(8,128)S(1)}, u32[]{:S(2)}, u32[]{:S(2)}) collective-permute-start(f32[4,2,160,128]{3,2,1,0:T(8,128)S(1)} %pad_maximum_fusion.6.refs_1_.refs_0_), channel_id=1, source_target_pairs={{0,2},{2,0},{4,6},{6,4},{8,10},{10,8},{12,14},{14,12},{16,18},{18,... | collective-permute-start | bytes 1966088 | tf_op jit(solution)/shard_map/ppermute | solution.py:47
  (117 other events, 906.7 us)
Sparse Core Ops, SparseCore 0:
  122.9 88.6 all-gather.2
  214.4 86.8 all-gather.4
  305.4 119.7 reduce-scatter.7
  428.7 122.7 reduce-scatter.9
  557.8 104.2 reduce-scatter.11
